TPU v7x, 32 devices: a whole 2x2x4 slice. The times are simulated.
32 devices in a mesh: dp: 2 (over core), row: 4 (over y, x), col: 4 (over z).
Axes of the slice: x: 2, y: 2, z: 4, core: 2. Of those that a mesh axis runs over, the one named last changes fastest.
Arguments:
- tokens: bfloat16 [2, 4608, 4096], P('dp', 'col', 'row'), may hold values from -6 to 6
- kept_index: int32 [2, 2048], P('dp'), may hold values from 0 to 4095, as said below
- w_query: bfloat16 [4608, 4096], P(('dp', 'row'), 'col'), may hold values from -0.125 to 0.125
- cotangent: bfloat16 [2, 4096, 2048], P('dp', 'col', 'row'), may hold values from -6 to 6
Outputs:
- queries: bfloat16 [2, 4096, 2048], P('dp', 'col', 'row')
- grad_kept: float32 [2, 4608, 2048], P('dp', 'col', 'row')
- grad_weight: float32 [4608, 4096], P(('dp', 'row'), 'col')
Inputs may be any that keep to these rules, and one draw needn't show every extreme that they name: `kept_index`: in each sequence the positions increase strictly. For every block b of 1024 positions (positions b * 1024 to (b + 1) * 1024 - 1), the number of kept positions before the block lies between b * 512 and b * 512 + 128; the upper end is reached in every sequence.
All inputs are finite; a program needn't handle non-finite values.
Results may differ from a plain program's by a relative error of at most 0.001.
Values may be sent and summed in bfloat16 or wider, within the bound.
No kernel may reach another device: no remote copies, remote signals or barrier semaphores. Data moves between devices by JAX's collectives and lax.ppermute only.
A program may use at most 128 MiB of HBM per device.

v0:
```python
import jax
import jax.numpy as jnp
from jax import lax
from jax.sharding import PartitionSpec as P


def passed_along(value, axis, steps):
    count = lax.axis_size(axis)
    initial, last = (max(0, -steps), min(count, count - steps))
    return lax.ppermute(value, axis, [(source, source + steps) for source in range(initial, last)])


def per_device(tokens, kept_index, w_query, cotangent):
    seq_x = tokens[0]
    seq_dev = seq_x.shape[1]
    keep_dev = cotangent.shape[2]
    drift = keep_dev // 4
    row_index = lax.axis_index("row")
    block_base = row_index * seq_dev
    own_keep = lax.dynamic_slice_in_dim(kept_index[0], row_index * keep_dev, keep_dev)
    next_keep = lax.dynamic_slice_in_dim(kept_index[0], (row_index + 1) * keep_dev, drift)
    position_ids = jnp.arange(seq_dev, dtype=jnp.int32)
    onehot_own = (position_ids[:, None] == (own_keep - block_base)[None, :]).astype(jnp.bfloat16)
    onehot_send = (position_ids[:, None] == (next_keep - block_base)[None, :]).astype(jnp.bfloat16)
    own_part = jnp.dot(seq_x, onehot_own, preferred_element_type=jnp.float32)
    leaving = jnp.dot(seq_x, onehot_send, preferred_element_type=jnp.float32).astype(jnp.bfloat16)
    arrived = passed_along(leaving, "row", 1)
    padded = jnp.pad(arrived.astype(jnp.float32), ((0, 0), (0, keep_dev - drift)))
    kept_panel = (own_part + padded).astype(jnp.bfloat16)
    full_panel = lax.all_gather(kept_panel, "col", axis=0, tiled=True)
    w_panel = lax.all_gather(w_query, ("dp", "row"), axis=0, tiled=True)
    queries = lax.dot_general(
        w_panel, full_panel, (((0,), (0,)), ((), ())), preferred_element_type=jnp.float32
    ).astype(jnp.bfloat16)
    head_grad = cotangent[0]
    grad_kept = lax.psum_scatter(
        jnp.dot(w_panel, head_grad, preferred_element_type=jnp.float32),
        "col",
        scatter_dimension=0,
        tiled=True,
    )
    grad_weight = lax.psum_scatter(
        lax.dot_general(
            full_panel, head_grad, (((1,), (1,)), ((), ())), preferred_element_type=jnp.float32
        ),
        ("dp", "row"),
        scatter_dimension=0,
        tiled=True,
    )
    return (queries[None], grad_kept[None], grad_weight)


def solution(mesh):
    in_specs = (
        P("dp", "col", "row"),
        P("dp", None),
        P(("dp", "row"), "col"),
        P("dp", "col", "row"),
    )
    out_specs = (P("dp", "col", "row"), P("dp", "col", "row"), P(("dp", "row"), "col"))
    return jax.shard_map(
        per_device, mesh=mesh, in_specs=in_specs, out_specs=out_specs, check_vma=False
    )
```

profile of v0, /device:TPU:18, one launch (start us, length us, event | category | flops | bytes accessed | tf_op | source)
XLA Modules:
  0.0 461.6 jit_solution(10764774549853595717)
XLA Ops:
  7.2 0.0 copy-start
  7.2 0.0 all-gather.5.cloned.1.call-start
  7.2 0.7 all-gather.5.cloned.1.call-update
  7.9 0.0 all-gather.3.cloned.1.call-start
  8.0 0.7 subtract_bitcast_fusion
  8.6 0.2 copy-done
  8.8 0.9 fusion.2
  9.7 3.4 collective-permute-start
  13.1 0.7 dynamic-slice_subtract_fusion
  13.8 6.5 %collective-permute-done = bf16[1152,128]{0,1:T(8,128)(2,1)S(1)} collective-permute-done((bf16[1152,128]{0,1:T(8,128)(2,1)S(1)}, bf16[1152,128]{0,1:T(8,128)(2,1)S(1)}, u32[]{:S(2)}, u32[]{:S(2)}) %collective-permute-start) | collective-permute-done | bytes 294944 | tf_op jit(solution)/shard_map/ppermute | solution.py:10
  20.4 0.0 copy-start.2
  20.4 0.7 copy-done.2
  21.1 0.0 copy-start.1
  21.1 3.6 add_convert_fusion
  24.7 0.0 all-gather.3.cloned.1.call-update
  24.8 0.0 reduce-scatter.3.cloned.1.call-start
  24.8 45.0 %all-gather.5.cloned.1.call-done = bf16[4608,1024]{1,0:T(8,128)(2,1)} async-done(((bf16[576,1024]{1,0:T(8,128)(2,1)}), bf16[4608,1024]{1,0:T(8,128)(2,1)}) %all-gather.5.cloned.1.call-update) | async-done | bytes 9437200 | tf_op jit(solution)/shard_map/all_gather | solution.py:31
  69.8 0.0 copy-done.1
  69.8 11.4 %fusion.14 = f32[4608,512]{1,0:T(8,128)} fusion(bf16[4608,1024]{1,0:T(8,128)(2,1)} %all-gather.5.cloned.1.call-done, bf16[1,1024,512]{2,1,0:T(8,128)(2,1)S(1)} %copy-done.1), kind=kOutput, calls=%fused_computation.12 | convolution fusion | flops 4831838208 | bytes 19922944 | tf_op jit(solution)/shard_map/dot_general | solution.py:37
  81.2 0.0 reduce-scatter.3.cloned.1.call-update
  81.2 0.0 reduce-scatter.5.cloned.1.call-start
  81.2 78.6 %all-gather.3.cloned.1.call-done = bf16[4608,512]{0,1:T(8,128)(2,1)} async-done(((bf16[1152,512]{0,1:T(8,128)(2,1)}), bf16[4608,512]{0,1:T(8,128)(2,1)}) %all-gather.3.cloned.1.call-update) | async-done | bytes 4718608 | tf_op jit(solution)/shard_map/all_gather | solution.py:30
  159.9 11.9 %fusion.12 = f32[4608,1024]{1,0:T(8,128)} fusion(bf16[4608,512]{0,1:T(8,128)(2,1)} %all-gather.3.cloned.1.call-done, bf16[1,1024,512]{2,1,0:T(8,128)(2,1)S(1)} %copy-done.1), kind=kOutput, calls=%fused_computation.10 | convolution fusion | flops 4831838208 | bytes 24641536 | tf_op jit(solution)/shard_map/dot_general | solution.py:43
  171.7 0.0 reduce-scatter.5.cloned.1.call-update
  171.8 9.0 %fusion.6 = bf16[1,1024,512]{1,2,0:T(8,128)(2,1)S(1)} fusion(bf16[4608,512]{0,1:T(8,128)(2,1)} %all-gather.3.cloned.1.call-done, bf16[4608,1024]{1,0:T(8,128)(2,1)} %all-gather.5.cloned.1.call-done), kind=kOutput, calls=%fused_computation.9 | convolution fusion | flops 4832362496 | bytes 15204352 | tf_op jit(solution)/shard_map/dot_general | solution.py:32
  180.8 1.3 copy.7
  182.1 142.8 %reduce-scatter.3.cloned.1.call-done = f32[1152,512]{1,0:T(8,128)} async-done(((f32[4608,512]{1,0:T(8,128)}), f32[1152,512]{1,0:T(8,128)}) %reduce-scatter.3.cloned.1.call-update) | async-done | bytes 2359312 | tf_op jit(solution)/shard_map/reduce_scatter | solution.py:36
  325.0 130.1 %reduce-scatter.5.cloned.1.call-done = f32[576,1024]{1,0:T(8,128)} async-done(((f32[4608,1024]{1,0:T(8,128)}), f32[576,1024]{1,0:T(8,128)}) %reduce-scatter.5.cloned.1.call-update) | async-done | bytes 2359312 | tf_op jit(solution)/shard_map/reduce_scatter | solution.py:42
Async XLA Ops:
  7.2 1.7 copy-start
  7.2 62.6 %all-gather.5.cloned.1.call-start = ((), (), s32[]{:S(2)}) async-start(), calls=%async_computation.3 | async-start | bytes 10616832 | tf_op jit(solution)/shard_map/all_gather | solution.py:31
  7.9 152.0 %all-gather.3.cloned.1.call-start = ((), (), s32[]{:S(2)}) async-start(), calls=%async_computation.2 | async-start | bytes 5898240 | tf_op jit(solution)/shard_map/all_gather | solution.py:30
  9.7 10.6 %collective-permute-start = (bf16[1152,128]{0,1:T(8,128)(2,1)S(1)}, bf16[1152,128]{0,1:T(8,128)(2,1)S(1)}, u32[]{:S(2)}, u32[]{:S(2)}) collective-permute-start(bf16[1152,128]{0,1:T(8,128)(2,1)S(1)} %fusion.2), channel_id=1, source_target_pairs={{0,4},{4,8},{8,12},{1,5},{5,9},{9,13},{2,6},{6,10},{10,14},{3,7},{... | collective-permute-start | bytes 884744 | tf_op jit(solution)/shard_map/ppermute | solution.py:10
  20.4 0.7 copy-start.2
  21.1 48.7 %copy-start.1 = (bf16[1,1024,512]{2,1,0:T(8,128)(2,1)S(1)}, bf16[1,1024,512]{2,1,0:T(8,128)(2,1)}, u32[]{:S(2)}) copy-start(bf16[1,1024,512]{2,1,0:T(8,128)(2,1)} %param.7) | copy-start | bytes 3145732
  24.8 300.2 %reduce-scatter.3.cloned.1.call-start = ((), (), s32[]{:S(2)}) async-start(), calls=%async_computation.4 | async-start | bytes 11796480 | tf_op jit(solution)/shard_map/reduce_scatter | solution.py:36
  81.2 373.8 %reduce-scatter.5.cloned.1.call-start = ((), (), s32[]{:S(2)}) async-start(), calls=%async_computation.5 | async-start | bytes 21233664 | tf_op jit(solution)/shard_map/reduce_scatter | solution.py:42
Sparse Core Ops, SparseCore 0:
  9.9 59.8 all-gather.4
  72.0 87.8 all-gather.2
  162.8 162.1 reduce-scatter.2
  329.0 125.9 reduce-scatter.4
where the time goes:
time: 464 us; the launch traced here: 462 us
  waiting for transfers between devices  404 us (87%)
  matrix products  36.8 us (8%)
  between operations  13.8 us (3%)
    reduce_scatter x1, waiting for transfers between devices, per_device(): lax.psum_scatter(jnp.dot(w_panel, head_grad, preferred_element_type=jnp.f...  143 us
    reduce_scatter x1, waiting for transfers between devices, per_device(): lax.psum_scatter(lax.dot_general(full_panel, head_grad, (((1,), (1,)), ((...  130 us
    all_gather x1, waiting for transfers between devices, per_device(): full_panel = lax.all_gather(kept_panel, 'col', axis=0, tiled=True)  78.6 us
    all_gather x1, waiting for transfers between devices, per_device(): w_panel = lax.all_gather(w_query, ('dp', 'row'), axis=0, tiled=True)  45 us
    dot_general x1, matrix products, per_device(): lax.dot_general(full_panel, head_grad, (((1,), (1,)), ((), ())), preferre...  11.9 us
    dot_general x1, matrix products, per_device(): jnp.dot(w_panel, head_grad, preferred_element_type=jnp.float32)  11.4 us
  transfers between devices with their start and end apart: 5, of which 5 were waited for; matrix products, arithmetic and copies ran while one was open for 9% of the time, Pallas kernels for 0%

commit v1 on v0

v1 whole, which is shorter than its diff:
```python
import jax
import jax.numpy as jnp
from jax import lax
from jax.sharding import PartitionSpec as P

HEADER = 16
OFFSET = 512.0
F32 = jnp.float32
F16 = jnp.float16


def mm(a, b, ca, cb):
    return lax.dot_general(a, b, (((ca,), (cb,)), ((), ())), preferred_element_type=F32)


def exponent(bound):
    return jnp.clip(jnp.floor(14.99 - jnp.log2(jnp.maximum(bound, 1e-30))), -100.0, 100.0)


def encode(values, expo):
    rows, cols = values.shape
    padded = jnp.pad(values, ((0, HEADER), (0, 0))) * jnp.exp2(expo)
    row = lax.broadcasted_iota(jnp.int32, (rows + HEADER, cols), 0)
    return jnp.where(row < rows, padded, expo + OFFSET).astype(F16)


def header(payload):
    code = payload[-1, 0].astype(F32)
    return code > 0.0, jnp.where(code > 0.0, code - OFFSET, 0.0)


def decode(payload):
    _, expo = header(payload)
    return payload[:-HEADER].astype(F32) * jnp.exp2(-expo)


def amax(values):
    return jnp.max(jnp.abs(values)).astype(F32)


def per_device(tokens, kept_index, w_query, cotangent):
    n_dp, n_row, n_col = (lax.axis_size(a) for a in ("dp", "row", "col"))
    dp, row, col = (lax.axis_index(a) for a in ("dp", "row", "col"))
    seq_x = tokens[0]
    cot = cotangent[0]
    d_dev, seq_dev = seq_x.shape
    w_rows = w_query.shape[0]
    keep_dev = cot.shape[1]
    heads = cot.shape[0]
    drift = keep_dev // 4
    parts = 2 if w_rows % 32 == 0 else 1
    sub = w_rows // parts
    blocks = d_dev // w_rows
    shard = blocks * sub
    half = (n_col // n_dp) * shard

    w_parts = [
        lax.all_gather(w_query[p * sub : (p + 1) * sub], ("dp", "row"), axis=0, tiled=True)
        for p in range(parts)
    ]

    block_base = row * seq_dev
    own_keep = lax.dynamic_slice_in_dim(kept_index[0], row * keep_dev, keep_dev)
    next_keep = lax.dynamic_slice_in_dim(kept_index[0], (row + 1) * keep_dev, drift)
    position_ids = jnp.arange(seq_dev, dtype=jnp.int32)
    onehot_own = (position_ids[:, None] == (own_keep - block_base)[None, :]).astype(jnp.bfloat16)
    onehot_send = (position_ids[:, None] == (next_keep - block_base)[None, :]).astype(jnp.bfloat16)
    leaving = mm(seq_x, onehot_send, 1, 0).astype(jnp.bfloat16)
    arrived = lax.ppermute(leaving, "row", [(r, r + 1) for r in range(n_row - 1)])
    own_part = mm(seq_x, onehot_own, 1, 0)
    padded = jnp.pad(arrived.astype(F32), ((0, 0), (0, keep_dev - drift)))
    kept = (own_part + padded).astype(jnp.bfloat16).reshape(blocks, parts, sub, keep_dev)

    def along(value, sources, step):
        return lax.ppermute(value, "col", [(c, c + step) for c in sources])

    panels = []
    for p in range(parts):
        own = kept[:, p].reshape(shard, keep_dev)
        from_left, from_right = [own], [own]
        for t in range(1, n_col):
            from_left.append(along(from_left[-1], range(t - 1, n_col - 1), 1))
            from_right.append(along(from_right[-1], range(1, n_col - t + 1), -1))
        line = jnp.concatenate(from_left[:0:-1] + [own] + from_right[1:], axis=0)
        panels.append(lax.dynamic_slice_in_dim(line, (n_col - 1 - col) * shard, n_col * shard))

    grads = []
    for p in range(parts):
        partial = mm(w_parts[p], cot, 1, 0)
        bound = amax(partial)

        def block_of(index):
            return lax.dynamic_slice_in_dim(partial, jnp.clip(index, 0, n_col - 1) * shard, shard)

        def one_way(step):
            payload = None
            for t in range(1, n_col):
                place = col if step > 0 else n_col - 1 - col
                target = n_col - t + place
                target = target if step > 0 else n_col - 1 - target
                value = block_of(target)
                total = bound
                if payload is not None:
                    came, expo = header(payload)
                    total = total + jnp.where(came, jnp.exp2(15.0 - expo), 0.0)
                    value = value + decode(payload)
                sources = range(t) if step > 0 else range(n_col - 1, n_col - 1 - t, -1)
                payload = along(encode(value, exponent(total)), sources, step)
            return decode(payload)

        grads.append(block_of(col) + (one_way(1) + one_way(-1)))
    grad_kept = jnp.stack([g.reshape(blocks, sub, keep_dev) for g in grads], axis=1)
    grad_kept = grad_kept.reshape(d_dev, keep_dev)

    swap = [(i, i ^ 1) for i in range(n_dp)]
    cot_other = lax.ppermute(cot, "dp", swap)
    weight_rows = []
    for p in range(parts):
        mine = lax.dynamic_slice_in_dim(panels[p], dp * half, half)
        give = lax.dynamic_slice_in_dim(panels[p], (n_dp - 1 - dp) * half, half)
        other = lax.ppermute(give, "dp", swap)
        partial = mm(mine, cot, 1, 1) + mm(other, cot_other, 1, 1)
        expo = exponent(amax(partial))
        total = lax.dynamic_slice_in_dim(partial, row * sub, sub)
        came = []
        for step in range(1, n_row):
            piece = lax.dynamic_slice_in_dim(partial, (row ^ step) * sub, sub)
            came.append(
                lax.ppermute(encode(piece, expo), "row", [(r, r ^ step) for r in range(n_row)])
            )
        for payload in came:
            total = total + decode(payload)
        weight_rows.append(total)
    grad_weight = jnp.concatenate(weight_rows, axis=0)

    queries = sum(mm(w_parts[p], panels[p], 0, 0) for p in range(parts))
    return (queries.astype(jnp.bfloat16)[None], grad_kept[None], grad_weight)


def solution(mesh):
    in_specs = (
        P("dp", "col", "row"),
        P("dp", None),
        P(("dp", "row"), "col"),
        P("dp", "col", "row"),
    )
    out_specs = (P("dp", "col", "row"), P("dp", "col", "row"), P(("dp", "row"), "col"))
    return jax.shard_map(
        per_device, mesh=mesh, in_specs=in_specs, out_specs=out_specs, check_vma=False
    )
```

time: 464 us -> 326 us (0.70)
  waiting for transfers between devices: 404 us -> 85 us
  starting transfers between devices: 3.56 us -> 72.8 us
  local copies, waits for them, and re-layouts: 2.26 us -> 45.1 us
  other arithmetic: 1.35 us -> 36.7 us
  between operations: 13.8 us -> 36.6 us
  matrix products: 36.8 us -> 47 us
    reduce_scatter x2 -> x0, waiting for transfers between devices: 273 us -> none  [the longest x1 143 us: per_device(): lax.psum_scatter(jnp.dot(w_panel, head_grad, preferred_element_type=jnp.f...]
    all_gather x2, waiting for transfers between devices: 124 us -> 0.02 us  [per_device(): lax.all_gather(w_query[p * sub:(p + 1) * sub], ('dp', 'row'), axis=0, til...]
    ppermute x1 -> x34, waiting for transfers between devices: 6.54 us -> 84.3 us  [the longest x24 54.7 us: along(): return lax.ppermute(value, 'col', [(c, c + step) for c in sources])]
    ppermute x1 -> x34, starting transfers between devices: 3.4 us -> 72.7 us  [the longest x24 61.7 us: along(): return lax.ppermute(value, 'col', [(c, c + step) for c in sources])]
    add x0 -> x12, other arithmetic: none -> 22.4 us  [the longest x8 14.2 us: one_way(): value = value + decode(payload)]
    slice x0 -> x20, local copies, waits for them, and re-layouts: none -> 20.7 us  [the longest x18 18.2 us: header(): code = payload[-1, 0].astype(F32)]
    convert_element_type x0 -> x9, other arithmetic: none -> 11.1 us  [encode(): return jnp.where(row < rows, padded, expo + OFFSET).astype(F16)]
    dot_general x5 -> x10, matrix products: 36.8 us -> 47 us  [mm(): lax.dot_general(a, b, (((ca,), (cb,)), ((), ())), preferred_element_type=...]
  transfers between devices with their start and end apart: 5 -> 36, of which waited for: 5 -> 16; matrix products, arithmetic and copies ran while one was open for 9% -> 36% of each run, Pallas kernels for 0% -> 0%
where the time goes in v1:
time: 326 us; the launch traced here: 323 us
  waiting for transfers between devices  85 us (26%)
  starting transfers between devices  72.8 us (22%)
  matrix products  47 us (14%)
  local copies, waits for them, and re-layouts  45.1 us (14%)
  other arithmetic  36.7 us (11%)
  between operations  36.6 us (11%)
    ppermute x24, starting transfers between devices, along(): return lax.ppermute(value, 'col', [(c, c + step) for c in sources])  61.7 us
    ppermute x24, waiting for transfers between devices, along(): return lax.ppermute(value, 'col', [(c, c + step) for c in sources])  54.7 us
    dot_general x10, matrix products, mm(): lax.dot_general(a, b, (((ca,), (cb,)), ((), ())), preferred_element_type=...  47 us
    ppermute x6, waiting for transfers between devices, per_device(): lax.ppermute(encode(piece, expo), 'row', [(r, r ^ step) for r in range(n_...  20.2 us
    slice x18, local copies, waits for them, and re-layouts, header(): code = payload[-1, 0].astype(F32)  18.2 us
    add x8, other arithmetic, one_way(): value = value + decode(payload)  14.2 us
    unnamed x49, local copies, waits for them, and re-layouts  12.2 us
    convert_element_type x9, other arithmetic, encode(): return jnp.where(row < rows, padded, expo + OFFSET).astype(F16)  11.1 us
  transfers between devices with their start and end apart: 36, of which 16 were waited for; matrix products, arithmetic and copies ran while one was open for 36% of the time, Pallas kernels for 0%

profile of v1, /device:TPU:18, one launch (start us, length us, event | category | flops | bytes accessed | tf_op | source)
XLA Modules:
  0.0 323.3 jit_solution(16974091064586012808)
XLA Ops:
  7.2 2.5 fusion.40
  12.1 3.4 %collective-permute-start = (bf16[1152,128]{0,1:T(8,128)(2,1)S(1)}, bf16[1152,128]{0,1:T(8,128)(2,1)S(1)}, u32[]{:S(2)}, u32[]{:S(2)}) collective-permute-start(bf16[1152,128]{0,1:T(8,128)(2,1)S(1)} %fusion.6), channel_id=1, source_target_pairs={{0,4},{4,8},{8,12},{1,5},{5,9},{9,13},{2,6},{6,10},{10,14},{3,7},{... | collective-permute-start | bytes 884744 | tf_op jit(solution)/shard_map/ppermute | solution.py:69
  16.1 9.4 %collective-permute-done = bf16[1152,128]{0,1:T(8,128)(2,1)S(1)} collective-permute-done((bf16[1152,128]{0,1:T(8,128)(2,1)S(1)}, bf16[1152,128]{0,1:T(8,128)(2,1)S(1)}, u32[]{:S(2)}, u32[]{:S(2)}) %collective-permute-start) | collective-permute-done | bytes 294944 | tf_op jit(solution)/shard_map/ppermute | solution.py:69
  26.2 2.5 add_convert_fusion
  29.5 3.7 %collective-permute-start.7 = (bf16[576,512]{1,0:T(8,128)(2,1)S(1)}, bf16[576,512]{1,0:T(8,128)(2,1)S(1)}, u32[]{:S(2)}, u32[]{:S(2)}) collective-permute-start(bf16[576,512]{1,0:T(8,128)(2,1)S(1)} %bitcast.87), channel_id=1, source_target_pairs={{0,1},{1,2},{2,3},{4,5},{5,6},{6,7},{8,9},{9,10},{10,11},{12,13},{... | collective-permute-start | bytes 1769480 | tf_op jit(solution)/shard_map/ppermute | solution.py:75
  33.2 2.3 collective-permute-start.10
  35.5 4.4 %collective-permute-start.1 = (bf16[576,512]{1,0:T(8,128)(2,1)S(1)}, bf16[576,512]{1,0:T(8,128)(2,1)S(1)}, u32[]{:S(2)}, u32[]{:S(2)}) collective-permute-start(bf16[576,512]{1,0:T(8,128)(2,1)S(1)} %bitcast.84), channel_id=1, source_target_pairs={{0,1},{1,2},{2,3},{4,5},{5,6},{6,7},{8,9},{9,10},{10,11},{12,13},{... | collective-permute-start | bytes 1769480 | tf_op jit(solution)/shard_map/ppermute | solution.py:75
  39.9 1.9 collective-permute-start.4
  41.9 5.9 %collective-permute-done.7 = bf16[576,512]{1,0:T(8,128)(2,1)S(1)} collective-permute-done((bf16[576,512]{1,0:T(8,128)(2,1)S(1)}, bf16[576,512]{1,0:T(8,128)(2,1)S(1)}, u32[]{:S(2)}, u32[]{:S(2)}) %collective-permute-start.7) | collective-permute-done | bytes 589856 | tf_op jit(solution)/shard_map/ppermute | solution.py:75
  47.8 3.6 %collective-permute-start.8 = (bf16[576,512]{1,0:T(8,128)(2,1)S(1)}, bf16[576,512]{1,0:T(8,128)(2,1)}, u32[]{:S(2)}, u32[]{:S(2)}) collective-permute-start(bf16[576,512]{1,0:T(8,128)(2,1)S(1)} %collective-permute-done.7), channel_id=1, source_target_pairs={{1,2},{2,3},{5,6},{6,7},{9,10},{10,11},{13,14},{14,15},{17,18},{18... | collective-permute-start | bytes 1769480 | tf_op jit(solution)/shard_map/ppermute | solution.py:75
  51.5 3.8 %collective-permute-start.11 = (bf16[576,512]{1,0:T(8,128)(2,1)}, bf16[576,512]{1,0:T(8,128)(2,1)}, u32[]{:S(2)}, u32[]{:S(2)}) collective-permute-start(bf16[576,512]{1,0:T(8,128)(2,1)} %collective-permute-done.10), channel_id=1, source_target_pairs={{1,0},{2,1},{5,4},{6,5},{9,8},{10,9},{13,12},{14,13},{17,16},{18,1... | collective-permute-start | bytes 1769480 | tf_op jit(solution)/shard_map/ppermute | solution.py:75
  55.3 5.2 %collective-permute-done.1 = bf16[576,512]{1,0:T(8,128)(2,1)S(1)} collective-permute-done((bf16[576,512]{1,0:T(8,128)(2,1)S(1)}, bf16[576,512]{1,0:T(8,128)(2,1)S(1)}, u32[]{:S(2)}, u32[]{:S(2)}) %collective-permute-start.1) | collective-permute-done | bytes 589856 | tf_op jit(solution)/shard_map/ppermute | solution.py:75
  60.4 3.6 %collective-permute-start.2 = (bf16[576,512]{1,0:T(8,128)(2,1)S(1)}, bf16[576,512]{1,0:T(8,128)(2,1)}, u32[]{:S(2)}, u32[]{:S(2)}) collective-permute-start(bf16[576,512]{1,0:T(8,128)(2,1)S(1)} %collective-permute-done.1), channel_id=1, source_target_pairs={{1,2},{2,3},{5,6},{6,7},{9,10},{10,11},{13,14},{14,15},{17,18},{18... | collective-permute-start | bytes 1769480 | tf_op jit(solution)/shard_map/ppermute | solution.py:75
  64.0 3.9 %collective-permute-start.5 = (bf16[576,512]{1,0:T(8,128)(2,1)S(1)}, bf16[576,512]{1,0:T(8,128)(2,1)}, u32[]{:S(2)}, u32[]{:S(2)}) collective-permute-start(bf16[576,512]{1,0:T(8,128)(2,1)S(1)} %collective-permute-done.4), channel_id=1, source_target_pairs={{1,0},{2,1},{5,4},{6,5},{9,8},{10,9},{13,12},{14,13},{17,16},{18,1... | collective-permute-start | bytes 1769480 | tf_op jit(solution)/shard_map/ppermute | solution.py:75
  67.9 5.3 %collective-permute-done.8 = bf16[576,512]{1,0:T(8,128)(2,1)} collective-permute-done((bf16[576,512]{1,0:T(8,128)(2,1)S(1)}, bf16[576,512]{1,0:T(8,128)(2,1)}, u32[]{:S(2)}, u32[]{:S(2)}) %collective-permute-start.8) | collective-permute-done | bytes 589856 | tf_op jit(solution)/shard_map/ppermute | solution.py:75
  73.2 4.4 %collective-permute-start.9 = (bf16[576,512]{1,0:T(8,128)(2,1)}, bf16[576,512]{1,0:T(8,128)(2,1)}, u32[]{:S(2)}, u32[]{:S(2)}) collective-permute-start(bf16[576,512]{1,0:T(8,128)(2,1)} %collective-permute-done.8), channel_id=1, source_target_pairs={{2,3},{6,7},{10,11},{14,15},{18,19},{22,23},{26,27},{30,31}} | collective-permute-start | bytes 1769480 | tf_op jit(solution)/shard_map/ppermute | solution.py:75
  78.5 6.4 %collective-permute-done.2 = bf16[576,512]{1,0:T(8,128)(2,1)} collective-permute-done((bf16[576,512]{1,0:T(8,128)(2,1)S(1)}, bf16[576,512]{1,0:T(8,128)(2,1)}, u32[]{:S(2)}, u32[]{:S(2)}) %collective-permute-start.2) | collective-permute-done | bytes 589856 | tf_op jit(solution)/shard_map/ppermute | solution.py:75
  84.9 4.5 %collective-permute-start.3 = (bf16[576,512]{1,0:T(8,128)(2,1)}, bf16[576,512]{1,0:T(8,128)(2,1)S(1)}, u32[]{:S(2)}, u32[]{:S(2)}) collective-permute-start(bf16[576,512]{1,0:T(8,128)(2,1)} %collective-permute-done.2), channel_id=1, source_target_pairs={{2,3},{6,7},{10,11},{14,15},{18,19},{22,23},{26,27},{30,31}} | collective-permute-start | bytes 1769480 | tf_op jit(solution)/shard_map/ppermute | solution.py:75
  90.1 7.5 %collective-permute-done.9 = bf16[576,512]{1,0:T(8,128)(2,1)} collective-permute-done((bf16[576,512]{1,0:T(8,128)(2,1)}, bf16[576,512]{1,0:T(8,128)(2,1)}, u32[]{:S(2)}, u32[]{:S(2)}) %collective-permute-start.9) | collective-permute-done | bytes 589856 | tf_op jit(solution)/shard_map/ppermute | solution.py:75
  103.9 2.2 collective-permute-done.3
  108.5 1.9 copy-done.6
  111.8 7.3 %abs_reduce_fusion.3 = (f32[]{:T(128)}, f32[2304,512]{1,0:T(8,128)}) fusion(bf16[2304,1024]{1,0:T(8,128)(2,1)} %all-gather.3.cloned.1.call-done, bf16[1,1024,512]{2,1,0:T(8,128)(2,1)S(1)} %copy-done.3), kind=kOutput, calls=%fused_computation.5 | convolution fusion | flops 2418278400 | bytes 10485764 | tf_op jit(solution)/shard_map/dot_general | solution.py:13
  122.1 3.0 fusion.42
  125.1 5.5 %abs_reduce_fusion = (f32[]{:T(128)}, f32[1152,1024]{1,0:T(8,128)}) fusion(f32[1152,1024]{1,0:T(8,128)S(1)} %fusion.42, bf16[1,1024,512]{2,1,0:T(8,128)(2,1)S(1)} %copy-done.3, bf16[4032,512]{1,0:T(8,128)(2,1)} %copy-done.4, s32[]{:T(128)S(6)} %dynamic_slice.116), kind=kOutput, calls=%fused_computation.2 | convolution fusion | flops 1211498496 | bytes 11665416 | tf_op jit(solution)/shard_map/dot_general | solution.py:13
  136.1 7.3 %abs_reduce_fusion.2 = (f32[]{:T(128)}, f32[2304,512]{1,0:T(8,128)}) fusion(bf16[2304,1024]{1,0:T(8,128)(2,1)} %all-gather.5.cloned.1.call-done, bf16[1,1024,512]{2,1,0:T(8,128)(2,1)S(1)} %copy-done.3), kind=kOutput, calls=%fused_computation.4 | convolution fusion | flops 2418278400 | bytes 10485764 | tf_op jit(solution)/shard_map/dot_general | solution.py:13
  145.5 13.3 %collective-permute-done.14 = f16[592,512]{1,0:T(8,128)(2,1)} collective-permute-done((f16[592,512]{1,0:T(8,128)(2,1)S(1)}, f16[592,512]{1,0:T(8,128)(2,1)}, u32[]{:S(2)}, u32[]{:S(2)}) %collective-permute-start.14) | collective-permute-done | bytes 606240 | tf_op jit(solution)/shard_map/ppermute | solution.py:75
  161.5 2.1 multiply_add_fusion.8
  166.4 3.0 fusion.41
  169.5 5.6 %abs_reduce_fusion.1 = (f32[]{:T(128)}, f32[1152,1024]{1,0:T(8,128)}) fusion(f32[1152,1024]{1,0:T(8,128)S(1)} %fusion.41, bf16[1,1024,512]{2,1,0:T(8,128)(2,1)S(1)} %copy-done.3, bf16[4032,512]{1,0:T(8,128)(2,1)} %copy-done.6, s32[]{:T(128)S(6)} %dynamic_slice.116), kind=kOutput, calls=%fused_computation.3 | convolution fusion | flops 1211498496 | bytes 11665416 | tf_op jit(solution)/shard_map/dot_general | solution.py:13
  176.5 5.3 %collective-permute-done.16 = f16[592,512]{1,0:T(8,128)(2,1)S(1)} collective-permute-done((f16[592,512]{1,0:T(8,128)(2,1)S(1)}, f16[592,512]{1,0:T(8,128)(2,1)S(1)}, u32[]{:S(2)}, u32[]{:S(2)}) %collective-permute-start.16) | collective-permute-done | bytes 606240 | tf_op jit(solution)/shard_map/ppermute | solution.py:75
  186.4 1.9 collective-permute-start.17
  188.4 4.2 %constant_dynamic-slice_fusion.2 = (f32[288,1024]{1,0:T(8,128)S(1)}, f32[288,1024]{1,0:T(8,128)S(1)}, f32[288,1024]{1,0:T(8,128)S(1)}, f32[288,1024]{1,0:T(8,128)}, f32[288,1024]{1,0:T(8,128)}, /*index=5*/f32[288,1024]{1,0:T(8,128)}) fusion(f32[1152,1024]{1,0:T(8,128)} %get-tuple-element.43, s32[]{:T(128)S(6)} %select_n.269, s32[]{:T(128)S(6)} %select_n.275, ...), kind=kLoop, calls=%fused_computation.74 | loop fusion | bytes 14155788 | tf_op jit(solution)/shard_map/dynamic_slice | solution.py:127
  194.0 4.5 %select_convert_fusion.5 = (f16[304,1024]{1,0:T(8,128)(2,1)}, f16[304,1024]{1,0:T(8,128)(2,1)}, f16[304,1024]{1,0:T(8,128)(2,1)}, f16[304,1024]{1,0:T(8,128)(2,1...) fusion(f32[288,1024]{1,0:T(8,128)} %get-tuple-element.46, f32[]{:T(128)S(6)} %add.361, f32[]{:T(128)S(6)} %exp2.301, ...), kind=kLoop, calls=%fused_computation.27 | loop fusion | flops 5603328 | bytes 10813760 | tf_op jit(solution)/shard_map/convert_element_type | solution.py:24
  198.4 2.3 collective-permute-start.33
  213.2 2.4 collective-permute-start.29
  220.0 10.0 %collective-permute-done.32 = f16[304,1024]{1,0:T(8,128)(2,1)} collective-permute-done((f16[304,1024]{1,0:T(8,128)(2,1)}, f16[304,1024]{1,0:T(8,128)(2,1)}, u32[]{:S(2)}, u32[]{:S(2)}) %collective-permute-start.32) | collective-permute-done | bytes 622624 | tf_op jit(solution)/shard_map/ppermute | solution.py:129
  235.3 2.1 multiply_add_fusion.4
  240.7 2.2 multiply_add_fusion
  245.2 8.6 %collective-permute-done.28 = f16[304,1024]{1,0:T(8,128)(2,1)} collective-permute-done((f16[304,1024]{1,0:T(8,128)(2,1)}, f16[304,1024]{1,0:T(8,128)(2,1)}, u32[]{:S(2)}, u32[]{:S(2)}) %collective-permute-start.28) | collective-permute-done | bytes 622624 | tf_op jit(solution)/shard_map/ppermute | solution.py:129
  257.7 2.2 multiply_add_fusion.1
  266.5 2.3 collective-permute-start.23
  268.8 6.3 %fusion.2 = f32[512,1024]{1,0:T(8,128)} fusion(bf16[2304,1024]{1,0:T(8,128)(2,1)} %all-gather.5.cloned.1.call-done, bf16[4032,512]{1,0:T(8,128)(2,1)S(1)} %copy-done.5, s32[]{:T(128)S(6)} %select_n.223), kind=kOutput, calls=%fused_computation.12 | convolution fusion | flops 2415919104 | bytes 9175044 | tf_op jit(solution)/shard_map/dot_general | solution.py:13
  275.1 3.9 %collective-permute-start.15 = (f16[592,512]{1,0:T(8,128)(2,1)}, f16[592,512]{1,0:T(8,128)(2,1)}, u32[]{:S(2)}, u32[]{:S(2)}) collective-permute-start(f16[592,512]{1,0:T(8,128)(2,1)} %get-tuple-element.23), channel_id=1, source_target_pairs={{0,1},{1,2},{2,3},{4,5},{5,6},{6,7},{8,9},{9,10},{10,11},{12,13},{... | collective-permute-start | bytes 1818632 | tf_op jit(solution)/shard_map/ppermute | solution.py:75
  279.1 1.9 collective-permute-start.18
  281.0 4.8 %collective-permute-start.21 = (f16[592,512]{1,0:T(8,128)(2,1)S(1)}, f16[592,512]{1,0:T(8,128)(2,1)}, u32[]{:S(2)}, u32[]{:S(2)}) collective-permute-start(f16[592,512]{1,0:T(8,128)(2,1)S(1)} %copy-done.10), channel_id=1, source_target_pairs={{0,1},{1,2},{2,3},{4,5},{5,6},{6,7},{8,9},{9,10},{10,11},{12,13},{... | collective-permute-start | bytes 1818632 | tf_op jit(solution)/shard_map/ppermute | solution.py:75
  290.6 1.9 collective-permute-start.24
  292.5 5.6 %fusion.12 = bf16[1,1024,512]{1,2,0:T(8,128)(2,1)S(1)} fusion(f32[512,1024]{1,0:T(8,128)} %fusion.2, bf16[2304,1024]{1,0:T(8,128)(2,1)} %all-gather.3.cloned.1.call-done, bf16[4032,512]{1,0:T(8,128)(2,1)S(1)} %copy-done.7, s32[]{:T(128)S(6)} %select_n.223), kind=kOutput, calls=%fused_computation.21 | convolution fusion | flops 2416967680 | bytes 10223620 | tf_op jit(solution)/shard_map/dot_general | solution.py:13
  307.8 2.6 collective-permute-done.24
  (141 shorter events, 76.3 us)
Async XLA Ops:
  7.2 4.0 %copy-start = (bf16[1,1152,1024]{2,1,0:T(8,128)(2,1)S(1)}, bf16[1,1152,1024]{2,1,0:T(8,128)(2,1)}, u32[]{:S(2)}) copy-start(bf16[1,1152,1024]{2,1,0:T(8,128)(2,1)} %param.4) | copy-start | bytes 7077892
  7.2 104.6 %all-gather.3.cloned.1.call-start = ((), (), s32[]{:S(2)}) async-start(), calls=%async_computation | async-start | bytes 5308416 | tf_op jit(solution)/shard_map/all_gather | solution.py:58
  9.7 126.3 %all-gather.5.cloned.1.call-start = ((), (), s32[]{:S(2)}) async-start(), calls=%async_computation.1 | async-start | bytes 5308416 | tf_op jit(solution)/shard_map/all_gather | solution.py:58
  12.1 13.5 %collective-permute-start = (bf16[1152,128]{0,1:T(8,128)(2,1)S(1)}, bf16[1152,128]{0,1:T(8,128)(2,1)S(1)}, u32[]{:S(2)}, u32[]{:S(2)}) collective-permute-start(bf16[1152,128]{0,1:T(8,128)(2,1)S(1)} %fusion.6), channel_id=1, source_target_pairs={{0,4},{4,8},{8,12},{1,5},{5,9},{9,13},{2,6},{6,10},{10,14},{3,7},{... | collective-permute-start | bytes 884744 | tf_op jit(solution)/shard_map/ppermute | solution.py:69
  29.4 48.2 %copy-start.3 = (bf16[1,1024,512]{2,1,0:T(8,128)(2,1)S(1)}, bf16[1,1024,512]{2,1,0:T(8,128)(2,1)}, u32[]{:S(2)}) copy-start(bf16[1,1024,512]{2,1,0:T(8,128)(2,1)} %param.7) | copy-start | bytes 3145732
  29.5 18.3 %collective-permute-start.7 = (bf16[576,512]{1,0:T(8,128)(2,1)S(1)}, bf16[576,512]{1,0:T(8,128)(2,1)S(1)}, u32[]{:S(2)}, u32[]{:S(2)}) collective-permute-start(bf16[576,512]{1,0:T(8,128)(2,1)S(1)} %bitcast.87), channel_id=1, source_target_pairs={{0,1},{1,2},{2,3},{4,5},{5,6},{6,7},{8,9},{9,10},{10,11},{12,13},{... | collective-permute-start | bytes 1769480 | tf_op jit(solution)/shard_map/ppermute | solution.py:75
  33.2 18.3 %collective-permute-start.10 = (bf16[576,512]{1,0:T(8,128)(2,1)S(1)}, bf16[576,512]{1,0:T(8,128)(2,1)}, u32[]{:S(2)}, u32[]{:S(2)}) collective-permute-start(bf16[576,512]{1,0:T(8,128)(2,1)S(1)} %bitcast.88), channel_id=1, source_target_pairs={{1,0},{2,1},{3,2},{5,4},{6,5},{7,6},{9,8},{10,9},{11,10},{13,12},{... | collective-permute-start | bytes 1769480 | tf_op jit(solution)/shard_map/ppermute | solution.py:75
  35.5 24.9 %collective-permute-start.1 = (bf16[576,512]{1,0:T(8,128)(2,1)S(1)}, bf16[576,512]{1,0:T(8,128)(2,1)S(1)}, u32[]{:S(2)}, u32[]{:S(2)}) collective-permute-start(bf16[576,512]{1,0:T(8,128)(2,1)S(1)} %bitcast.84), channel_id=1, source_target_pairs={{0,1},{1,2},{2,3},{4,5},{5,6},{6,7},{8,9},{9,10},{10,11},{12,13},{... | collective-permute-start | bytes 1769480 | tf_op jit(solution)/shard_map/ppermute | solution.py:75
  39.9 24.1 %collective-permute-start.4 = (bf16[576,512]{1,0:T(8,128)(2,1)S(1)}, bf16[576,512]{1,0:T(8,128)(2,1)S(1)}, u32[]{:S(2)}, u32[]{:S(2)}) collective-permute-start(bf16[576,512]{1,0:T(8,128)(2,1)S(1)} %bitcast.85), channel_id=1, source_target_pairs={{1,0},{2,1},{3,2},{5,4},{6,5},{7,6},{9,8},{10,9},{11,10},{13,12},{... | collective-permute-start | bytes 1769480 | tf_op jit(solution)/shard_map/ppermute | solution.py:75
  47.8 29.8 %copy-start.11 = (bf16[576,512]{1,0:T(8,128)(2,1)}, bf16[576,512]{1,0:T(8,128)(2,1)S(1)}, u32[]{:S(2)}) copy-start(bf16[576,512]{1,0:T(8,128)(2,1)S(1)} %collective-permute-done.7) | copy-start | bytes 1769476
  47.8 25.4 %collective-permute-start.8 = (bf16[576,512]{1,0:T(8,128)(2,1)S(1)}, bf16[576,512]{1,0:T(8,128)(2,1)}, u32[]{:S(2)}, u32[]{:S(2)}) collective-permute-start(bf16[576,512]{1,0:T(8,128)(2,1)S(1)} %collective-permute-done.7), channel_id=1, source_target_pairs={{1,2},{2,3},{5,6},{6,7},{9,10},{10,11},{13,14},{14,15},{17,18},{18... | collective-permute-start | bytes 1769480 | tf_op jit(solution)/shard_map/ppermute | solution.py:75
  51.5 26.1 %collective-permute-start.11 = (bf16[576,512]{1,0:T(8,128)(2,1)}, bf16[576,512]{1,0:T(8,128)(2,1)}, u32[]{:S(2)}, u32[]{:S(2)}) collective-permute-start(bf16[576,512]{1,0:T(8,128)(2,1)} %collective-permute-done.10), channel_id=1, source_target_pairs={{1,0},{2,1},{5,4},{6,5},{9,8},{10,9},{13,12},{14,13},{17,16},{18,1... | collective-permute-start | bytes 1769480 | tf_op jit(solution)/shard_map/ppermute | solution.py:75
  60.4 24.5 %collective-permute-start.2 = (bf16[576,512]{1,0:T(8,128)(2,1)S(1)}, bf16[576,512]{1,0:T(8,128)(2,1)}, u32[]{:S(2)}, u32[]{:S(2)}) collective-permute-start(bf16[576,512]{1,0:T(8,128)(2,1)S(1)} %collective-permute-done.1), channel_id=1, source_target_pairs={{1,2},{2,3},{5,6},{6,7},{9,10},{10,11},{13,14},{14,15},{17,18},{18... | collective-permute-start | bytes 1769480 | tf_op jit(solution)/shard_map/ppermute | solution.py:75
  64.0 25.4 %collective-permute-start.5 = (bf16[576,512]{1,0:T(8,128)(2,1)S(1)}, bf16[576,512]{1,0:T(8,128)(2,1)}, u32[]{:S(2)}, u32[]{:S(2)}) collective-permute-start(bf16[576,512]{1,0:T(8,128)(2,1)S(1)} %collective-permute-done.4), channel_id=1, source_target_pairs={{1,0},{2,1},{5,4},{6,5},{9,8},{10,9},{13,12},{14,13},{17,16},{18,1... | collective-permute-start | bytes 1769480 | tf_op jit(solution)/shard_map/ppermute | solution.py:75
  73.2 24.5 %collective-permute-start.9 = (bf16[576,512]{1,0:T(8,128)(2,1)}, bf16[576,512]{1,0:T(8,128)(2,1)}, u32[]{:S(2)}, u32[]{:S(2)}) collective-permute-start(bf16[576,512]{1,0:T(8,128)(2,1)} %collective-permute-done.8), channel_id=1, source_target_pairs={{2,3},{6,7},{10,11},{14,15},{18,19},{22,23},{26,27},{30,31}} | collective-permute-start | bytes 1769480 | tf_op jit(solution)/shard_map/ppermute | solution.py:75
  77.6 44.5 %collective-permute-start.26 = (bf16[1024,512]{1,0:T(8,128)(2,1)S(1)}, bf16[1024,512]{1,0:T(8,128)(2,1)}, u32[]{:S(2)}, u32[]{:S(2)}) collective-permute-start(bf16[1024,512]{1,0:T(8,128)(2,1)S(1)} %bitcast.82), channel_id=1, source_target_pairs={{0,16},{16,0},{1,17},{17,1},{2,18},{18,2},{3,19},{19,3},{4,20},{20... | collective-permute-start | bytes 3145736 | tf_op jit(solution)/shard_map/ppermute | solution.py:116
  77.6 22.3 %copy-start.12 = (bf16[576,512]{1,0:T(8,128)(2,1)S(1)}, bf16[576,512]{1,0:T(8,128)(2,1)}, u32[]{:S(2)}) copy-start(bf16[576,512]{1,0:T(8,128)(2,1)} %copy-done.11) | copy-start | bytes 1769476
  77.6 24.6 %collective-permute-start.12 = (bf16[576,512]{1,0:T(8,128)(2,1)}, bf16[576,512]{1,0:T(8,128)(2,1)S(1)}, u32[]{:S(2)}, u32[]{:S(2)}) collective-permute-start(bf16[576,512]{1,0:T(8,128)(2,1)} %collective-permute-done.11), channel_id=1, source_target_pairs={{1,0},{5,4},{9,8},{13,12},{17,16},{21,20},{25,24},{29,28}} | collective-permute-start | bytes 1769480 | tf_op jit(solution)/shard_map/ppermute | solution.py:75
  84.9 21.1 %collective-permute-start.3 = (bf16[576,512]{1,0:T(8,128)(2,1)}, bf16[576,512]{1,0:T(8,128)(2,1)S(1)}, u32[]{:S(2)}, u32[]{:S(2)}) collective-permute-start(bf16[576,512]{1,0:T(8,128)(2,1)} %collective-permute-done.2), channel_id=1, source_target_pairs={{2,3},{6,7},{10,11},{14,15},{18,19},{22,23},{26,27},{30,31}} | collective-permute-start | bytes 1769480 | tf_op jit(solution)/shard_map/ppermute | solution.py:75
  89.4 19.0 %collective-permute-start.6 = (bf16[576,512]{1,0:T(8,128)(2,1)}, bf16[576,512]{1,0:T(8,128)(2,1)S(1)}, u32[]{:S(2)}, u32[]{:S(2)}) collective-permute-start(bf16[576,512]{1,0:T(8,128)(2,1)} %collective-permute-done.5), channel_id=1, source_target_pairs={{1,0},{5,4},{9,8},{13,12},{17,16},{21,20},{25,24},{29,28}} | collective-permute-start | bytes 1769480 | tf_op jit(solution)/shard_map/ppermute | solution.py:75
  102.2 5.1 %copy-start.4 = (bf16[4032,512]{1,0:T(8,128)(2,1)}, bf16[4032,512]{1,0:T(8,128)(2,1)S(1)}, u32[]{:S(2)}) copy-start(bf16[4032,512]{1,0:T(8,128)(2,1)S(1)} %constant_dynamic-update-slice_fusion.7) | copy-start | bytes 12386308
  103.9 18.2 %collective-permute-start.30 = (bf16[1152,512]{1,0:T(8,128)(2,1)}, bf16[1152,512]{1,0:T(8,128)(2,1)}, u32[]{:S(2)}, u32[]{:S(2)}) collective-permute-start(bf16[1152,512]{1,0:T(8,128)(2,1)} %constant_dynamic-slice_fusion.3), channel_id=1, source_target_pairs={{0,16},{16,0},{1,17},{17,1},{2,18},{18,2},{3,19},{19,3},{4,20},{20... | collective-permute-start | bytes 3538952 | tf_op jit(solution)/shard_map/ppermute | solution.py:121
  111.7 54.7 %collective-permute-start.25 = (bf16[1152,512]{1,0:T(8,128)(2,1)}, bf16[1152,512]{1,0:T(8,128)(2,1)}, u32[]{:S(2)}, u32[]{:S(2)}) collective-permute-start(bf16[1152,512]{1,0:T(8,128)(2,1)} %constant_dynamic-slice_fusion.7), channel_id=1, source_target_pairs={{0,16},{16,0},{1,17},{17,1},{2,18},{18,2},{3,19},{19,3},{4,20},{20... | collective-permute-start | bytes 3538952 | tf_op jit(solution)/shard_map/ppermute | solution.py:121
  121.4 9.2 %collective-permute-start.13 = (f16[592,512]{1,0:T(8,128)(2,1)S(1)}, f16[592,512]{1,0:T(8,128)(2,1)S(1)}, u32[]{:S(2)}, u32[]{:S(2)}) collective-permute-start(f16[592,512]{1,0:T(8,128)(2,1)S(1)} %select_convert_fusion.17), channel_id=1, source_target_pairs={{0,1},{4,5},{8,9},{12,13},{16,17},{20,21},{24,25},{28,29}} | collective-permute-start | bytes 1818632 | tf_op jit(solution)/shard_map/ppermute | solution.py:75
  134.6 24.3 %collective-permute-start.14 = (f16[592,512]{1,0:T(8,128)(2,1)S(1)}, f16[592,512]{1,0:T(8,128)(2,1)}, u32[]{:S(2)}, u32[]{:S(2)}) collective-permute-start(f16[592,512]{1,0:T(8,128)(2,1)S(1)} %select_convert_fusion.16), channel_id=1, source_target_pairs={{0,1},{1,2},{4,5},{5,6},{8,9},{9,10},{12,13},{13,14},{16,17},{17,1... | collective-permute-start | bytes 1818632 | tf_op jit(solution)/shard_map/ppermute | solution.py:75
  165.1 16.6 %collective-permute-start.16 = (f16[592,512]{1,0:T(8,128)(2,1)S(1)}, f16[592,512]{1,0:T(8,128)(2,1)S(1)}, u32[]{:S(2)}, u32[]{:S(2)}) collective-permute-start(f16[592,512]{1,0:T(8,128)(2,1)S(1)} %get-tuple-element.24), channel_id=1, source_target_pairs={{3,2},{7,6},{11,10},{15,14},{19,18},{23,22},{27,26},{31,30}} | collective-permute-start | bytes 1818632 | tf_op jit(solution)/shard_map/ppermute | solution.py:75
  175.0 26.9 %collective-permute-start.19 = (f16[592,512]{1,0:T(8,128)(2,1)}, f16[592,512]{1,0:T(8,128)(2,1)}, u32[]{:S(2)}, u32[]{:S(2)}) collective-permute-start(f16[592,512]{1,0:T(8,128)(2,1)} %get-tuple-element.25), channel_id=1, source_target_pairs={{0,1},{4,5},{8,9},{12,13},{16,17},{20,21},{24,25},{28,29}} | collective-permute-start | bytes 1818632 | tf_op jit(solution)/shard_map/ppermute | solution.py:75
  183.8 4.6 %copy-start.2 = (f32[1152,1024]{1,0:T(8,128)S(1)}, f32[1152,1024]{1,0:T(8,128)}, u32[]{:S(2)}) copy-start(f32[1152,1024]{1,0:T(8,128)} %get-tuple-element.41) | copy-start | bytes 14155780
  186.4 19.8 %collective-permute-start.17 = (f16[592,512]{1,0:T(8,128)(2,1)}, f16[592,512]{1,0:T(8,128)(2,1)}, u32[]{:S(2)}, u32[]{:S(2)}) collective-permute-start(f16[592,512]{1,0:T(8,128)(2,1)} %select_convert_fusion.13), channel_id=1, source_target_pairs={{3,2},{2,1},{7,6},{6,5},{11,10},{10,9},{15,14},{14,13},{19,18},{18... | collective-permute-start | bytes 1818632 | tf_op jit(solution)/shard_map/ppermute | solution.py:75
  198.4 18.2 %collective-permute-start.33 = (f16[304,1024]{1,0:T(8,128)(2,1)}, f16[304,1024]{1,0:T(8,128)(2,1)}, u32[]{:S(2)}, u32[]{:S(2)}) collective-permute-start(f16[304,1024]{1,0:T(8,128)(2,1)} %get-tuple-element.33), channel_id=1, source_target_pairs={{0,12},{4,8},{8,4},{12,0},{1,13},{5,9},{9,5},{13,1},{2,14},{6,10},... | collective-permute-start | bytes 1867784 | tf_op jit(solution)/shard_map/ppermute | solution.py:129
  200.7 29.3 %collective-permute-start.32 = (f16[304,1024]{1,0:T(8,128)(2,1)}, f16[304,1024]{1,0:T(8,128)(2,1)}, u32[]{:S(2)}, u32[]{:S(2)}) collective-permute-start(f16[304,1024]{1,0:T(8,128)(2,1)} %get-tuple-element.32), channel_id=1, source_target_pairs={{0,8},{4,12},{8,0},{12,4},{1,9},{5,13},{9,1},{13,5},{2,10},{6,14},... | collective-permute-start | bytes 1867784 | tf_op jit(solution)/shard_map/ppermute | solution.py:129
  200.7 31.3 %collective-permute-start.31 = (f16[304,1024]{1,0:T(8,128)(2,1)}, f16[304,1024]{1,0:T(8,128)(2,1)}, u32[]{:S(2)}, u32[]{:S(2)}) collective-permute-start(f16[304,1024]{1,0:T(8,128)(2,1)} %get-tuple-element.31), channel_id=1, source_target_pairs={{0,4},{4,0},{8,12},{12,8},{1,5},{5,1},{9,13},{13,9},{2,6},{6,2},{1... | collective-permute-start | bytes 1867784 | tf_op jit(solution)/shard_map/ppermute | solution.py:129
  210.5 19.5 %copy-start.8 = (f16[304,1024]{1,0:T(8,128)(2,1)S(1)}, f16[304,1024]{1,0:T(8,128)(2,1)}, u32[]{:S(2)}) copy-start(f16[304,1024]{1,0:T(8,128)(2,1)} %get-tuple-element.30) | copy-start | bytes 1867780
  211.9 22.1 %collective-permute-start.20 = (f16[592,512]{1,0:T(8,128)(2,1)}, f16[592,512]{1,0:T(8,128)(2,1)S(1)}, u32[]{:S(2)}, u32[]{:S(2)}) collective-permute-start(f16[592,512]{1,0:T(8,128)(2,1)} %get-tuple-element.27), channel_id=1, source_target_pairs={{0,1},{1,2},{4,5},{5,6},{8,9},{9,10},{12,13},{13,14},{16,17},{17,1... | collective-permute-start | bytes 1818632 | tf_op jit(solution)/shard_map/ppermute | solution.py:75
  213.2 30.2 %collective-permute-start.29 = (f16[304,1024]{1,0:T(8,128)(2,1)}, f16[304,1024]{1,0:T(8,128)(2,1)}, u32[]{:S(2)}, u32[]{:S(2)}) collective-permute-start(f16[304,1024]{1,0:T(8,128)(2,1)} %get-tuple-element.35), channel_id=1, source_target_pairs={{0,12},{4,8},{8,4},{12,0},{1,13},{5,9},{9,5},{13,1},{2,14},{6,10},... | collective-permute-start | bytes 1867784 | tf_op jit(solution)/shard_map/ppermute | solution.py:129
  216.6 37.2 %collective-permute-start.28 = (f16[304,1024]{1,0:T(8,128)(2,1)}, f16[304,1024]{1,0:T(8,128)(2,1)}, u32[]{:S(2)}, u32[]{:S(2)}) collective-permute-start(f16[304,1024]{1,0:T(8,128)(2,1)} %get-tuple-element.34), channel_id=1, source_target_pairs={{0,8},{4,12},{8,0},{12,4},{1,9},{5,13},{9,1},{13,5},{2,10},{6,14},... | collective-permute-start | bytes 1867784 | tf_op jit(solution)/shard_map/ppermute | solution.py:129
  230.0 25.6 %collective-permute-start.27 = (f16[304,1024]{1,0:T(8,128)(2,1)S(1)}, f16[304,1024]{1,0:T(8,128)(2,1)}, u32[]{:S(2)}, u32[]{:S(2)}) collective-permute-start(f16[304,1024]{1,0:T(8,128)(2,1)S(1)} %copy-done.8), channel_id=1, source_target_pairs={{0,4},{4,0},{8,12},{12,8},{1,5},{5,1},{9,13},{13,9},{2,6},{6,2},{1... | collective-permute-start | bytes 1867784 | tf_op jit(solution)/shard_map/ppermute | solution.py:129
  239.4 22.2 %collective-permute-start.22 = (f16[592,512]{1,0:T(8,128)(2,1)S(1)}, f16[592,512]{1,0:T(8,128)(2,1)S(1)}, u32[]{:S(2)}, u32[]{:S(2)}) collective-permute-start(f16[592,512]{1,0:T(8,128)(2,1)S(1)} %get-tuple-element.29), channel_id=1, source_target_pairs={{3,2},{7,6},{11,10},{15,14},{19,18},{23,22},{27,26},{31,30}} | collective-permute-start | bytes 1818632 | tf_op jit(solution)/shard_map/ppermute | solution.py:75
  264.5 4.3 %copy-start.5 = (bf16[4032,512]{1,0:T(8,128)(2,1)S(1)}, bf16[4032,512]{1,0:T(8,128)(2,1)}, u32[]{:S(2)}) copy-start(bf16[4032,512]{1,0:T(8,128)(2,1)} %copy-done.4) | copy-start | bytes 12386308
  266.5 12.6 %copy-start.9 = (f16[592,512]{1,0:T(8,128)(2,1)S(1)}, f16[592,512]{1,0:T(8,128)(2,1)}, u32[]{:S(2)}) copy-start(f16[592,512]{1,0:T(8,128)(2,1)} %get-tuple-element.26) | copy-start | bytes 1818628
  266.5 14.5 %copy-start.10 = (f16[592,512]{1,0:T(8,128)(2,1)S(1)}, f16[592,512]{1,0:T(8,128)(2,1)}, u32[]{:S(2)}) copy-start(f16[592,512]{1,0:T(8,128)(2,1)} %get-tuple-element.28) | copy-start | bytes 1818628
  266.5 19.3 %collective-permute-start.23 = (f16[592,512]{1,0:T(8,128)(2,1)S(1)}, f16[592,512]{1,0:T(8,128)(2,1)S(1)}, u32[]{:S(2)}, u32[]{:S(2)}) collective-permute-start(f16[592,512]{1,0:T(8,128)(2,1)S(1)} %select_convert_fusion.7), channel_id=1, source_target_pairs={{3,2},{2,1},{7,6},{6,5},{11,10},{10,9},{15,14},{14,13},{19,18},{18... | collective-permute-start | bytes 1818632 | tf_op jit(solution)/shard_map/ppermute | solution.py:75
  275.1 24.3 %collective-permute-start.15 = (f16[592,512]{1,0:T(8,128)(2,1)}, f16[592,512]{1,0:T(8,128)(2,1)}, u32[]{:S(2)}, u32[]{:S(2)}) collective-permute-start(f16[592,512]{1,0:T(8,128)(2,1)} %get-tuple-element.23), channel_id=1, source_target_pairs={{0,1},{1,2},{2,3},{4,5},{5,6},{6,7},{8,9},{9,10},{10,11},{12,13},{... | collective-permute-start | bytes 1818632 | tf_op jit(solution)/shard_map/ppermute | solution.py:75
  279.1 22.2 %collective-permute-start.18 = (f16[592,512]{1,0:T(8,128)(2,1)S(1)}, f16[592,512]{1,0:T(8,128)(2,1)}, u32[]{:S(2)}, u32[]{:S(2)}) collective-permute-start(f16[592,512]{1,0:T(8,128)(2,1)S(1)} %copy-done.9), channel_id=1, source_target_pairs={{3,2},{2,1},{1,0},{7,6},{6,5},{5,4},{11,10},{10,9},{9,8},{15,14},{... | collective-permute-start | bytes 1818632 | tf_op jit(solution)/shard_map/ppermute | solution.py:75
  281.0 24.9 %collective-permute-start.21 = (f16[592,512]{1,0:T(8,128)(2,1)S(1)}, f16[592,512]{1,0:T(8,128)(2,1)}, u32[]{:S(2)}, u32[]{:S(2)}) collective-permute-start(f16[592,512]{1,0:T(8,128)(2,1)S(1)} %copy-done.10), channel_id=1, source_target_pairs={{0,1},{1,2},{2,3},{4,5},{5,6},{6,7},{8,9},{9,10},{10,11},{12,13},{... | collective-permute-start | bytes 1818632 | tf_op jit(solution)/shard_map/ppermute | solution.py:75
  287.8 4.7 %copy-start.7 = (bf16[4032,512]{1,0:T(8,128)(2,1)S(1)}, bf16[4032,512]{1,0:T(8,128)(2,1)}, u32[]{:S(2)}) copy-start(bf16[4032,512]{1,0:T(8,128)(2,1)} %copy-done.6) | copy-start | bytes 12386308
  290.6 19.8 %collective-permute-start.24 = (f16[592,512]{1,0:T(8,128)(2,1)}, f16[592,512]{1,0:T(8,128)(2,1)}, u32[]{:S(2)}, u32[]{:S(2)}) collective-permute-start(f16[592,512]{1,0:T(8,128)(2,1)} %select_convert_fusion.6), channel_id=1, source_target_pairs={{3,2},{2,1},{1,0},{7,6},{6,5},{5,4},{11,10},{10,9},{9,8},{15,14},{... | collective-permute-start | bytes 1818632 | tf_op jit(solution)/shard_map/ppermute | solution.py:75
  314.1 2.3 copy-start.1
  (6 other events, 8.7 us)
Sparse Core Ops, SparseCore 0:
  10.5 41.6 all-gather.2
  54.0 38.9 all-gather.4

commit v2 on v0

v2 whole, which is shorter than its diff:
```python
import functools

import jax
import jax.numpy as jnp
from jax import lax
from jax.experimental import pallas as pl
from jax.experimental.pallas import tpu as pltpu
from jax.sharding import PartitionSpec as P

HEADER = 16
OFFSET = 128.0
F32 = jnp.float32
BF16 = jnp.bfloat16
MIB = 1 << 20
ANY = pl.BlockSpec(memory_space=pl.ANY)
VMEM = pl.BlockSpec(memory_space=pltpu.VMEM)
SMEM = pl.BlockSpec(memory_space=pltpu.SMEM)


def shape(dims, dtype):
    return jax.ShapeDtypeStruct(dims, dtype)


def params(mib):
    return pltpu.CompilerParams(vmem_limit_bytes=mib * MIB)


def cost(flops, moved):
    return pl.CostEstimate(flops=int(flops), bytes_accessed=int(moved), transcendentals=0)


def dot(a, b, ca, cb):
    return lax.dot_general(a, b, (((ca,), (cb,)), ((), ())), preferred_element_type=F32)


def exponent(bound):
    return jnp.clip(jnp.floor(14.99 - jnp.log2(jnp.maximum(bound, 1e-30))), -100.0, 100.0)


def power(values, scale):
    v = values * scale
    square = v * v
    fourth = square * square
    return (fourth * square * (v * jnp.abs(v))).astype(BF16)


def root(code, scale):
    y = code.astype(F32)
    quarter = lax.rsqrt(lax.rsqrt(jnp.maximum(jnp.abs(y), 1e-37)))
    size = quarter * lax.rsqrt(quarter) * scale
    return jnp.where(y > 0.0, size, jnp.where(y < 0.0, -size, 0.0))


def tile_max(values):
    most = jnp.max(jnp.abs(values), axis=0, keepdims=True)
    return jnp.broadcast_to(jnp.max(most, axis=1, keepdims=True), (8, 128))


def write_payload(out_ref, values, bound):
    rows = out_ref.shape[0] - HEADER
    expo = exponent(bound)
    out_ref[:rows, :] = power(values, jnp.exp2(expo)[0:1, 0:1])
    code = jnp.broadcast_to((expo + OFFSET)[0:1, 0:1], (HEADER, out_ref.shape[1]))
    out_ref[rows:, :] = code.astype(BF16)


def read_header(rows):
    code = rows[0:8, 0:128].astype(F32)
    came = code > 0.0
    expo = jnp.where(came, code - OFFSET, 0.0)
    return jnp.exp2(-expo), jnp.where(came, jnp.exp2(15.0 - expo), 0.0)


def pick_kernel(index_ref, x_ref, out_ref):
    onehot = lax.broadcasted_iota(jnp.int32, (x_ref.shape[1], index_ref.shape[1]), 0) == index_ref[...]
    out_ref[...] = dot(x_ref[...], onehot.astype(F32).astype(BF16), 1, 0).astype(BF16)


def pick_parts_kernel(blocks, sub, index_ref, x_ref, dep_ref, *out_refs):
    onehot = lax.broadcasted_iota(jnp.int32, (x_ref.shape[1], index_ref.shape[1]), 0) == index_ref[...]
    onehot = onehot.astype(F32).astype(BF16)
    parts = len(out_refs)
    for b in range(blocks):
        for p, out_ref in enumerate(out_refs):
            rows = x_ref[pl.ds((b * parts + p) * sub, sub), :]
            out_ref[pl.ds(b * sub, sub), :] = dot(rows, onehot, 1, 0).astype(BF16)


def add_arrived_kernel(blocks, sub, parts, arrived_ref, *refs):
    in_refs, out_refs = refs[:parts], refs[parts:]
    for b in range(blocks):
        for p in range(parts):
            rows = pl.ds(b * sub, sub)
            came = arrived_ref[pl.ds((b * parts + p) * sub, sub), :]
            out_refs[p][rows, :] = in_refs[p][rows, :] + came


def kept_tokens(seq_x, own, leaving_index, blocks, parts, sub, row_pairs):
    d_dev, seq_dev = seq_x.shape
    keep_dev, drift = own.shape[1], leaving_index.shape[1]
    leaving = pl.pallas_call(
        pick_kernel,
        out_shape=shape((d_dev, drift), BF16),
        in_specs=[VMEM, VMEM],
        out_specs=VMEM,
        compiler_params=params(32),
        cost_estimate=cost(2 * d_dev * seq_dev * drift, 2 * d_dev * seq_dev),
        name="pick_leaving",
    )(leaving_index, seq_x)
    arrived = lax.ppermute(leaving, "row", row_pairs)
    picked = pl.pallas_call(
        functools.partial(pick_parts_kernel, blocks, sub),
        out_shape=[shape((blocks * sub, keep_dev), BF16)] * parts,
        in_specs=[VMEM, VMEM, ANY],
        out_specs=[VMEM] * parts,
        compiler_params=params(32),
        cost_estimate=cost(2 * d_dev * seq_dev * keep_dev, 2 * d_dev * seq_dev),
        name="pick_own",
    )(own, seq_x, leaving)
    window = pl.BlockSpec((blocks * sub, drift), lambda i: (0, 0))
    kept = pl.pallas_call(
        functools.partial(add_arrived_kernel, blocks, sub, parts),
        grid=(1,),
        out_shape=[shape((blocks * sub, keep_dev), BF16)] * parts,
        in_specs=[pl.BlockSpec((d_dev, drift), lambda i: (0, 0))] + [window] * parts,
        out_specs=[window] * parts,
        input_output_aliases={1 + p: p for p in range(parts)},
        compiler_params=params(16),
        cost_estimate=cost(0, 6 * d_dev * drift),
        name="add_arrived",
    )(arrived, *picked)
    return kept, leaving


def split_kernel(sub, dep_ref, w_ref, *refs):
    out_refs, sem = refs[:-1], refs[-1]
    copies = [
        pltpu.make_async_copy(w_ref.at[pl.ds(p * sub, sub), :], out_ref, sem.at[p])
        for p, out_ref in enumerate(out_refs)
    ]
    for copy in copies:
        copy.start()
    for copy in copies:
        copy.wait()


def split_rows(array, parts, dep):
    if parts == 1:
        return [array]
    sub = array.shape[0] // parts
    return pl.pallas_call(
        functools.partial(split_kernel, sub),
        out_shape=[shape((sub, array.shape[1]), array.dtype)] * parts,
        in_specs=[ANY, ANY],
        out_specs=[ANY] * parts,
        scratch_shapes=[pltpu.SemaphoreType.DMA((parts,))],
        cost_estimate=cost(0, 4 * array.size),
        name="split_rows",
    )(dep, array)


def partial_kernel(w_ref, cot_ref, dep_ref, out_ref, bound_ref, right_ref, left_ref):
    value = dot(w_ref[...], cot_ref[...], 1, 0)
    out_ref[...] = value
    bound = tile_max(value)
    bound_ref[...] = bound

    @pl.when(pl.program_id(0) == 0)
    def _():
        write_payload(left_ref, value, bound)

    @pl.when(pl.program_id(0) == pl.num_programs(0) - 1)
    def _():
        write_payload(right_ref, value, bound)


def first_sums(w_part, cot, n_col, dep):
    rows, heads = w_part.shape
    shard = rows // n_col
    keep = cot.shape[1]
    payload = pl.BlockSpec((shard + HEADER, keep), lambda i: (0, 0))
    return pl.pallas_call(
        partial_kernel,
        grid=(n_col,),
        out_shape=[
            shape((rows, keep), F32),
            shape((n_col * 8, 128), F32),
            shape((shard + HEADER, keep), BF16),
            shape((shard + HEADER, keep), BF16),
        ],
        in_specs=[
            pl.BlockSpec((shard, heads), lambda i: (i, 0)),
            pl.BlockSpec((heads, keep), lambda i: (0, 0)),
            ANY,
        ],
        out_specs=[
            pl.BlockSpec((shard, keep), lambda i: (i, 0)),
            pl.BlockSpec((8, 128), lambda i: (i, 0)),
            payload,
            payload,
        ],
        compiler_params=params(32),
        cost_estimate=cost(2 * rows * heads * keep, 2 * rows * heads + 4 * rows * keep),
        name="grad_kept_partial",
    )(w_part, cot, dep)


def pass_on_kernel(at_ref, g_r, b_r, came_r, g_l, b_l, came_l, dep_ref, out_r, out_l):
    for g, b, came, out in ((g_r, b_r, came_r, out_r), (g_l, b_l, came_l, out_l)):
        rows = came.shape[0] - HEADER
        undo, bound = read_header(came[rows:, :])
        value = g[...] + root(came[:rows, :], undo[0:1, 0:1])
        write_payload(out, value, b[...] + bound)


def pass_on(at, sums, bounds, came_r, came_l, dep):
    shard = came_r.shape[0] - HEADER
    keep = came_r.shape[1]
    whole = pl.BlockSpec((shard + HEADER, keep), lambda i, at: (0, 0))

    def own(n):
        return [
            pl.BlockSpec((shard, keep), lambda i, at: (at[n], 0)),
            pl.BlockSpec((8, 128), lambda i, at: (at[n], 0)),
        ]

    return pl.pallas_call(
        pass_on_kernel,
        grid_spec=pltpu.PrefetchScalarGridSpec(
            num_scalar_prefetch=1,
            grid=(1,),
            in_specs=own(0) + [whole] + own(1) + [whole, ANY],
            out_specs=[whole, whole],
        ),
        out_shape=[shape((shard + HEADER, keep), BF16)] * 2,
        compiler_params=params(24),
        cost_estimate=cost(0, 16 * shard * keep),
        name="grad_kept_pass_on",
    )(at, sums, bounds, came_r, sums, bounds, came_l, dep)


def last_kernel(at_ref, g_ref, r_ref, rh_ref, l_ref, lh_ref, base_ref, out_ref):
    undo_r, _ = read_header(rh_ref[...])
    undo_l, _ = read_header(lh_ref[...])
    total = root(r_ref[...], undo_r[0:1, 0:1]) + root(l_ref[...], undo_l[0:1, 0:1])
    out_ref[0] = g_ref[...] + total


def last_sums(at, sums, came_r, came_l, base, part, parts, blocks):
    shard = came_r.shape[0] - HEADER
    keep = came_r.shape[1]
    sub = shard // blocks
    rows = pl.BlockSpec((sub, keep), lambda b, at: (b, 0))
    head = pl.BlockSpec((HEADER, keep), lambda b, at: (shard // HEADER, 0))
    return pl.pallas_call(
        last_kernel,
        grid_spec=pltpu.PrefetchScalarGridSpec(
            num_scalar_prefetch=1,
            grid=(blocks,),
            in_specs=[
                pl.BlockSpec((sub, keep), lambda b, at: (at[0] * blocks + b, 0)),
                rows,
                head,
                rows,
                head,
                ANY,
            ],
            out_specs=pl.BlockSpec((1, sub, keep), lambda b, at: (b * parts + part, 0, 0)),
        ),
        out_shape=shape((blocks * parts, sub, keep), F32),
        input_output_aliases={6: 0} if part else {},
        compiler_params=params(24),
        cost_estimate=cost(0, 12 * shard * keep),
        name="grad_kept_last",
    )(at, sums, came_r, came_r, came_l, came_l, base)


def fetch(refs, source, target, sem):
    for j, ref in enumerate(refs):

        @pl.when(source == j)
        def _():
            pltpu.make_async_copy(ref, target, sem).start()

    return pltpu.make_async_copy(refs[0], target, sem)


def give_kernel(n_col, n_half, where_ref, *refs):
    sources, (out_ref, sem) = refs[: 2 * n_col - 1], refs[2 * n_col - 1 :]
    other = 1 - where_ref[0]
    shard = sources[0].shape[0]
    waits = [
        fetch(
            sources,
            other * n_half + i - where_ref[2] + n_col - 1,
            out_ref.at[pl.ds(i * shard, shard), :],
            sem.at[i],
        )
        for i in range(n_half)
    ]
    for wait in waits:
        wait.wait()


def other_half(where, line, n_col, n_half):
    shard, keep = line[0].shape
    return pl.pallas_call(
        functools.partial(give_kernel, n_col, n_half),
        out_shape=shape((n_half * shard, keep), BF16),
        in_specs=[SMEM] + [ANY] * len(line),
        out_specs=ANY,
        scratch_shapes=[pltpu.SemaphoreType.DMA((n_half,))],
        cost_estimate=cost(0, 4 * n_half * shard * keep),
        name="half_for_other_core",
    )(where, *line)


def weight_kernel(n_col, n_half, n_row, where_ref, cot_ref, cot_other_ref, other_ref, dep_ref, *refs):
    sources = refs[: 2 * n_col - 1]
    own_ref, send_refs = refs[2 * n_col - 1], refs[2 * n_col : 2 * n_col + n_row - 1]
    mine_ref, total_ref, sem = refs[2 * n_col + n_row - 1 :]
    dp, row, col = where_ref[0], where_ref[1], where_ref[2]
    shard = sources[0].shape[0]
    waits = [
        fetch(
            sources,
            dp * n_half + i - col + n_col - 1,
            mine_ref.at[pl.ds(i * shard, shard), :],
            sem.at[i],
        )
        for i in range(n_half)
    ]
    for wait in waits:
        wait.wait()
    sub = own_ref.shape[0]
    bound = jnp.zeros((8, 128), F32)
    for step in range(n_row):
        rows = pl.ds(pl.multiple_of((row ^ step) * sub, 16), sub)
        value = dot(mine_ref[rows, :], cot_ref[...], 1, 1) + dot(other_ref[rows, :], cot_other_ref[...], 1, 1)
        if step == 0:
            own_ref[...] = value
        else:
            total_ref[step - 1] = value
            bound = jnp.maximum(bound, tile_max(value))
    for step in range(1, n_row):
        write_payload(send_refs[step - 1], total_ref[step - 1], bound)


def weight_partial(where, cot, cot_other, other, line, n_col, n_half, n_row, dep):
    half, keep = other.shape
    heads = cot.shape[0]
    sub = half // n_row
    return pl.pallas_call(
        functools.partial(weight_kernel, n_col, n_half, n_row),
        out_shape=[shape((sub, heads), F32)] + [shape((sub + HEADER, heads), BF16)] * (n_row - 1),
        in_specs=[SMEM, VMEM, VMEM, VMEM, ANY] + [ANY] * len(line),
        out_specs=[VMEM] * n_row,
        scratch_shapes=[
            pltpu.VMEM((half, keep), BF16),
            pltpu.VMEM((n_row - 1, sub, heads), F32),
            pltpu.SemaphoreType.DMA((n_half,)),
        ],
        compiler_params=params(40),
        cost_estimate=cost(4 * half * keep * heads, 4 * half * (keep + heads)),
        name="grad_weight_partial",
    )(where, cot, cot_other, other, dep, *line)


def weight_last_kernel(n_came, *refs):
    own_ref, came_refs, out_ref = refs[0], refs[1 : 1 + n_came], refs[-1]
    rows = own_ref.shape[0]
    total = own_ref[...]
    for came in came_refs:
        undo, _ = read_header(came[rows:, :])
        total = total + root(came[:rows, :], undo[0:1, 0:1])
    out_ref[...] = total


def weight_last(own, came, base, part, parts):
    sub, heads = own.shape
    tile = 256
    rows = pl.BlockSpec((sub, tile), lambda i: (0, i))
    whole = pl.BlockSpec((sub + HEADER, tile), lambda i: (0, i))
    return pl.pallas_call(
        functools.partial(weight_last_kernel, len(came)),
        grid=(heads // tile,),
        out_shape=shape((sub * parts, heads), F32),
        in_specs=[rows] + [whole] * len(came) + [ANY],
        out_specs=pl.BlockSpec((sub, tile), lambda i: (part, i)),
        input_output_aliases={1 + len(came): 0} if part else {},
        compiler_params=params(24),
        cost_estimate=cost(0, 14 * sub * heads),
        name="grad_weight_last",
    )(own, *came, base)


def query_kernel(n_col, parts, where_ref, dep_ref, *refs):
    w_refs = refs[:parts]
    count = 2 * n_col - 1
    lines = [refs[parts + p * count : parts + (p + 1) * count] for p in range(parts)]
    out_ref, panel_ref, sem = refs[parts + parts * count :]
    shard = lines[0][0].shape[0]

    @pl.when(pl.program_id(0) == 0)
    def _():
        waits = [
            fetch(
                lines[p],
                i - where_ref[2] + n_col - 1,
                panel_ref.at[p, pl.ds(i * shard, shard), :],
                sem.at[p, i],
            )
            for p in range(parts)
            for i in range(n_col)
        ]
        for wait in waits:
            wait.wait()

    total = dot(w_refs[0][...], panel_ref[0], 0, 0)
    for p in range(1, parts):
        total = total + dot(w_refs[p][...], panel_ref[p], 0, 0)
    out_ref[...] = total.astype(BF16)


def all_queries(where, w_parts, lines, n_col, dep):
    parts = len(w_parts)
    rows, heads = w_parts[0].shape
    shard, keep = lines[0][0].shape
    tile = 256
    return pl.pallas_call(
        functools.partial(query_kernel, n_col, parts),
        grid=(heads // tile,),
        out_shape=shape((heads, keep), BF16),
        in_specs=[SMEM, ANY]
        + [pl.BlockSpec((rows, tile), lambda i: (0, i))] * parts
        + [ANY] * (len(lines[0]) * parts),
        out_specs=pl.BlockSpec((tile, keep), lambda i: (i, 0)),
        scratch_shapes=[
            pltpu.VMEM((parts, rows, keep), BF16),
            pltpu.SemaphoreType.DMA((parts, n_col)),
        ],
        compiler_params=params(48),
        cost_estimate=cost(2 * parts * rows * heads * keep, 2 * parts * rows * (heads + keep)),
        name="queries",
    )(where, dep, *w_parts, *[piece for line in lines for piece in line])


def per_device(tokens, kept_index, w_query, cotangent):
    n_dp, n_row, n_col = (lax.axis_size(a) for a in ("dp", "row", "col"))
    dp, row, col = (lax.axis_index(a) for a in ("dp", "row", "col"))
    where = jnp.stack([dp, row, col]).astype(jnp.int32)
    seq_x = tokens[0]
    cot = cotangent[0]
    d_dev, seq_dev = seq_x.shape
    w_rows = w_query.shape[0]
    keep_dev = cot.shape[1]
    drift = keep_dev // 4
    parts = 2 if w_rows % 32 == 0 else 1
    sub = w_rows // parts
    blocks = d_dev // w_rows
    n_half = n_col // n_dp

    base = row * seq_dev
    own = lax.dynamic_slice_in_dim(kept_index, row * keep_dev, keep_dev, axis=1) - base
    leaving_index = lax.dynamic_slice_in_dim(kept_index, (row + 1) * keep_dev, drift, axis=1) - base
    row_pairs = [(r, r + 1) for r in range(n_row - 1)]
    kept, leaving = kept_tokens(seq_x, own, leaving_index, blocks, parts, sub, row_pairs)

    w_parts = [
        lax.all_gather(w, ("dp", "row"), axis=0, tiled=True) for w in split_rows(w_query, parts, leaving)
    ]
    swap = [(i, i ^ 1) for i in range(n_dp)]
    cot_other = lax.ppermute(cot, "dp", swap)

    def along(value, sources, step):
        return lax.ppermute(value, "col", [(c, c + step) for c in sources])

    from_left = [[k] for k in kept]
    from_right = [[k] for k in kept]

    def gather_step(p, t):
        from_left[p].append(along(from_left[p][-1], range(t - 1, n_col - 1), 1))
        from_right[p].append(along(from_right[p][-1], range(1, n_col - t + 1), -1))

    def reduce_send(right, left, t):
        return (
            along(right, range(t), 1),
            along(left, range(n_col - 1, n_col - 1 - t, -1), -1),
        )

    for t in range(1, n_col):
        for p in range(parts):
            gather_step(p, t)
    lines = [from_left[p][:0:-1] + [kept[p]] + from_right[p][1:] for p in range(parts)]

    grad_kept = None
    dep = kept[0]
    at_end = col.reshape(1).astype(jnp.int32)
    for p in range(parts):
        sums, bounds, right, left = first_sums(w_parts[p], cot, n_col, dep)
        for t in range(1, n_col):
            if t > 1:
                at = jnp.stack([n_col - t + col, t - 1 - (n_col - 1 - col)])
                at = jnp.clip(at, 0, n_col - 1).astype(jnp.int32)
                right, left = pass_on(at, sums, bounds, right, left, lines[p][n_col - 1 - t + 1])
            right, left = reduce_send(right, left, t)
        if grad_kept is None:
            grad_kept = last_sums(at_end, sums, right, left, dep, p, parts, blocks)
        else:
            grad_kept = last_sums(at_end, sums, right, left, grad_kept, p, parts, blocks)

    grad_weight = dep
    for p in range(parts):
        give = other_half(where, lines[p], n_col, n_half)
        other = lax.ppermute(give, "dp", swap)
        total, *sends = weight_partial(where, cot, cot_other, other, lines[p], n_col, n_half, n_row, dep)
        came = [
            lax.ppermute(send, "row", [(r, r ^ step) for r in range(n_row)])
            for step, send in enumerate(sends, 1)
        ]
        grad_weight = weight_last(total, came, grad_weight, p, parts)

    queries = all_queries(where, w_parts, lines, n_col, total)
    return (queries[None], grad_kept.reshape(1, d_dev, keep_dev), grad_weight)


def solution(mesh):
    in_specs = (
        P("dp", "col", "row"),
        P("dp", None),
        P(("dp", "row"), "col"),
        P("dp", "col", "row"),
    )
    out_specs = (P("dp", "col", "row"), P("dp", "col", "row"), P(("dp", "row"), "col"))
    return jax.shard_map(
        per_device, mesh=mesh, in_specs=in_specs, out_specs=out_specs, check_vma=False
    )
```

time: 464 us -> 388 us (0.84); the launches traced: 462 us -> 380 us
  waiting for transfers between devices: 404 us -> 69.3 us
  Pallas kernels: 0 us -> 186 us
  starting transfers between devices: 3.56 us -> 78.1 us
  matrix products: 36.8 us -> 0 us
  local copies, waits for them, and re-layouts: 2.26 us -> 29.1 us
    reduce_scatter x2 -> x0, waiting for transfers between devices: 273 us -> none  [the longest x1 143 us: per_device(): lax.psum_scatter(jnp.dot(w_panel, head_grad, preferred_element_type=jnp.f...]
    pallas_call x0 -> x19, Pallas kernels: none -> 186 us  [the longest x2 75 us: other_half(): pl.pallas_call(functools.partial(give_kernel, n_col, n_half), out_shape=s...]
    all_gather x2, waiting for transfers between devices: 124 us -> 0.04 us  [per_device(): lax.all_gather(w, ('dp', 'row'), axis=0, tiled=True)]
    ppermute x1 -> x34, starting transfers between devices: 3.4 us -> 78 us  [the longest x24 67.2 us: along(): return lax.ppermute(value, 'col', [(c, c + step) for c in sources])]
    ppermute x1 -> x34, waiting for transfers between devices: 6.54 us -> 68.5 us  [the longest x24 36.3 us: along(): return lax.ppermute(value, 'col', [(c, c + step) for c in sources])]
    dot_general x5 -> x0, matrix products: 36.8 us -> none  [the longest x1 11.9 us: per_device(): lax.dot_general(full_panel, head_grad, (((1,), (1,)), ((), ())), preferre...]
    unnamed x7 -> x110, local copies, waits for them, and re-layouts: 2.26 us -> 29.1 us
  transfers between devices with their start and end apart: 5 -> 36, of which waited for: 5 -> 8; matrix products, arithmetic and copies ran while one was open for 9% -> 0% of each run, Pallas kernels for 0% -> 38%
where the time goes in v2:
time: 388 us; the launch traced here: 380 us
  Pallas kernels  186 us (48%)
  starting transfers between devices  78.1 us (20%)
  waiting for transfers between devices  69.3 us (18%)
  local copies, waits for them, and re-layouts  29.1 us (8%)
  between operations  15.3 us (4%)
    pallas_call x2, Pallas kernels, other_half(): pl.pallas_call(functools.partial(give_kernel, n_col, n_half), out_shape=s...  75 us
    ppermute x24, starting transfers between devices, along(): return lax.ppermute(value, 'col', [(c, c + step) for c in sources])  67.2 us
    pallas_call x1, Pallas kernels, split_rows(): pl.pallas_call(functools.partial(split_kernel, sub), out_shape=[shape((su...  36.9 us
    ppermute x24, waiting for transfers between devices, along(): return lax.ppermute(value, 'col', [(c, c + step) for c in sources])  36.3 us
    unnamed x110, local copies, waits for them, and re-layouts  29.1 us
    ppermute x6, waiting for transfers between devices, per_device(): lax.ppermute(send, 'row', [(r, r ^ step) for r in range(n_row)])  25.8 us
    pallas_call x4, Pallas kernels, pass_on(): pl.pallas_call(pass_on_kernel, grid_spec=pltpu.PrefetchScalarGridSpec(num...  19.8 us
    pallas_call x2, Pallas kernels, weight_partial(): pl.pallas_call(functools.partial(weight_kernel, n_col, n_half, n_row), ou...  15.3 us
  transfers between devices with their start and end apart: 36, of which 8 were waited for; matrix products, arithmetic and copies ran while one was open for 0% of the time, Pallas kernels for 38%

profile of v2, /device:TPU:18, one launch (start us, length us, event | category | flops | bytes accessed | tf_op | source)
XLA Modules:
  0.0 380.3 jit_solution(10555186442947468473)
XLA Ops:
  11.0 36.9 %split_rows.1 = (bf16[288,1024]{1,0:T(8,128)(2,1)}, bf16[288,1024]{1,0:T(8,128)(2,1)}) custom-call(bf16[1152,128]{1,0:T(8,128)(2,1)} %copy-done.32, bf16[576,1024]{1,0:T(8,128)(2,1)} %w_ref.1), custom_call_target="tpu_custom_call" | custom-call | bytes 2359296 | tf_op jit(solution)/shard_map/split_rows/pallas_call | solution.py:151
  48.7 3.4 collective-permute-start.1
  55.2 6.4 %collective-permute-done.1.arrived_ref = bf16[1152,128]{1,0:T(8,128)(2,1)S(1)} collective-permute-done((bf16[1152,128]{1,0:T(8,128)(2,1)}, bf16[1152,128]{1,0:T(8,128)(2,1)S(1)}, u32[]{:S(2)}, u32[]{:S(2)}) %collective-permute-start.1) | collective-permute-done | bytes 294944 | tf_op jit(solution)/shard_map/ppermute | solution.py:110
  61.8 2.1 collective-permute-start.12
  63.9 3.8 collective-permute-start.9
  67.7 8.2 %collective-permute-done.12.refs_6_.refs_4_ = bf16[576,512]{1,0:T(8,128)(2,1)S(1)} collective-permute-done((bf16[576,512]{1,0:T(8,128)(2,1)S(1)}, bf16[576,512]{1,0:T(8,128)(2,1)S(1)}, u32[]{:S(2)}, u32[]{:S(2)}) %collective-permute-start.12) | collective-permute-done | bytes 589856 | tf_op jit(solution)/shard_map/ppermute | solution.py:476
  75.8 3.2 collective-permute-start.13
  79.0 2.4 collective-permute-start.10
  81.4 3.4 collective-permute-start.5
  84.9 3.2 collective-permute-start.2
  88.1 3.8 %collective-permute-done.13.refs_7_.refs_5_ = bf16[576,512]{1,0:T(8,128)(2,1)} collective-permute-done((bf16[576,512]{1,0:T(8,128)(2,1)S(1)}, bf16[576,512]{1,0:T(8,128)(2,1)}, u32[]{:S(2)}, u32[]{:S(2)}) %collective-permute-start.13) | collective-permute-done | bytes 589856 | tf_op jit(solution)/shard_map/ppermute | solution.py:476
  93.4 3.7 collective-permute-done.10.refs_3_.dep_ref.refs_1_
  97.1 3.3 collective-permute-start.11
  100.4 7.4 %collective-permute-start.6 = (bf16[576,512]{1,0:T(8,128)(2,1)}, bf16[576,512]{1,0:T(8,128)(2,1)}, u32[]{:S(2)}, u32[]{:S(2)}) collective-permute-start(bf16[576,512]{1,0:T(8,128)(2,1)} %collective-permute-done.5.refs_4_.refs_13_), channel_id=1, source_target_pairs={{1,0},{2,1},{5,4},{6,5},{9,8},{10,9},{13,12},{14,13},{17,16},{18,1... | collective-permute-start | bytes 1769480 | tf_op jit(solution)/shard_map/ppermute | solution.py:476
  107.8 4.4 %collective-permute-start.3 = (bf16[576,512]{1,0:T(8,128)(2,1)S(1)}, bf16[576,512]{1,0:T(8,128)(2,1)S(1)}, u32[]{:S(2)}, u32[]{:S(2)}) collective-permute-start(bf16[576,512]{1,0:T(8,128)(2,1)S(1)} %collective-permute-done.2.refs_2_.refs_11_.dep_ref), channel_id=1, source_target_pairs={{1,2},{2,3},{5,6},{6,7},{9,10},{10,11},{13,14},{14,15},{17,18},{18... | collective-permute-start | bytes 1769480 | tf_op jit(solution)/shard_map/ppermute | solution.py:476
  112.9 7.6 %collective-permute-done.11.refs_2_.refs_0_ = bf16[576,512]{1,0:T(8,128)(2,1)} collective-permute-done((bf16[576,512]{1,0:T(8,128)(2,1)S(1)}, bf16[576,512]{1,0:T(8,128)(2,1)}, u32[]{:S(2)}, u32[]{:S(2)}) %collective-permute-start.11) | collective-permute-done | bytes 589856 | tf_op jit(solution)/shard_map/ppermute | solution.py:476
  120.5 37.5 %half_for_other_core.3 = bf16[1152,512]{1,0:T(8,128)(2,1)} custom-call(s32[3]{0:T(128)} %pad_add_fusion.where_ref, bf16[576,512]{1,0:T(8,128)(2,1)} %collective-permute-done.11.refs_2_.refs_0_, bf16[576,512]{1,0:T(8,128)(2,1)} %copy-done.8, bf16[576,512]{1,0:T(8,128)(2,1)} %copy-done.6, bf16[576,512]{1,0:T(8,128)(2,1)} %copy-done.4, ...), custom_call_target="tpu_custom_call" | custom-call | bytes 2359296 | tf_op jit(solution)/shard_map/half_for_other_core/pallas_call | solution.py:307
  159.3 4.5 %collective-permute-start.4 = (bf16[576,512]{1,0:T(8,128)(2,1)S(1)}, bf16[576,512]{1,0:T(8,128)(2,1)S(1)}, u32[]{:S(2)}, u32[]{:S(2)}) collective-permute-start(bf16[576,512]{1,0:T(8,128)(2,1)S(1)} %collective-permute-done.3.refs_1_.refs_10_.dep_ref), channel_id=1, source_target_pairs={{2,3},{6,7},{10,11},{14,15},{18,19},{22,23},{26,27},{30,31}} | collective-permute-start | bytes 1769480 | tf_op jit(solution)/shard_map/ppermute | solution.py:476
  163.9 12.9 %collective-permute-done.4.refs_0_.refs_9_ = bf16[576,512]{1,0:T(8,128)(2,1)S(1)} collective-permute-done((bf16[576,512]{1,0:T(8,128)(2,1)S(1)}, bf16[576,512]{1,0:T(8,128)(2,1)S(1)}, u32[]{:S(2)}, u32[]{:S(2)}) %collective-permute-start.4) | collective-permute-done | bytes 589856 | tf_op jit(solution)/shard_map/ppermute | solution.py:476
  177.6 37.5 %half_for_other_core.2 = bf16[1152,512]{1,0:T(8,128)(2,1)} custom-call(s32[3]{0:T(128)} %pad_add_fusion.where_ref, bf16[576,512]{1,0:T(8,128)(2,1)} %copy-done.25, bf16[576,512]{1,0:T(8,128)(2,1)} %copy-done.12, bf16[576,512]{1,0:T(8,128)(2,1)} %copy-done.10, bf16[576,512]{1,0:T(8,128)(2,1)} %copy-done.14, ...), custom_call_target="tpu_custom_call" | custom-call | bytes 2359296 | tf_op jit(solution)/shard_map/half_for_other_core/pallas_call | solution.py:307
  215.3 2.3 copy-done.18
  218.8 5.1 %grad_kept_partial.2 = (f32[2304,512]{1,0:T(8,128)S(1)}, f32[32,128]{1,0:T(8,128)S(1)}, bf16[592,512]{1,0:T(8,128)(2,1)}, bf16[592,512]{1,0:T(8,128)(2,1)}) custom-call(bf16[2304,1024]{1,0:T(8,128)(2,1)S(1)} %copy-done.18, bf16[1024,512]{1,0:T(8,128)(2,1)S(1)} %bitcast.20, bf16[576,512]{1,0:T(8,128)(2,1)S(1)} %copy-done.5), custom_call_target="tpu_custom_call" | custom-call | flops 2415919104 | bytes 9437184 | tf_op jit(solution)/shard_map/grad_kept_partial/pallas_call | solution.py:182
  224.0 2.2 copy-done.1
  229.1 2.3 copy-done.19
  232.7 5.1 %grad_kept_partial.3 = (f32[2304,512]{1,0:T(8,128)S(1)}, f32[32,128]{1,0:T(8,128)S(1)}, bf16[592,512]{1,0:T(8,128)(2,1)}, bf16[592,512]{1,0:T(8,128)(2,1)}) custom-call(bf16[2304,1024]{1,0:T(8,128)(2,1)S(1)} %copy-done.19, bf16[1024,512]{1,0:T(8,128)(2,1)S(1)} %bitcast.21, bf16[576,512]{1,0:T(8,128)(2,1)S(1)} %copy-done.5), custom_call_target="tpu_custom_call" | custom-call | flops 2415919104 | bytes 9437184 | tf_op jit(solution)/shard_map/grad_kept_partial/pallas_call | solution.py:182
  237.8 2.1 copy-done
  244.0 7.7 %grad_weight_partial.3 = (f32[288,1024]{1,0:T(8,128)S(1)}, bf16[304,1024]{1,0:T(8,128)(2,1)S(1)}, bf16[304,1024]{1,0:T(8,128)(2,1)}, bf16[304,1024]{1,0:T(8,128)(2,1)}) custom-call(s32[3]{0:T(128)S(1)} %copy-done.44, bf16[1024,512]{1,0:T(8,128)(2,1)S(1)} %bitcast.22, bf16[1024,512]{1,0:T(8,128)(2,1)} %collective-permute-done.cot_other_ref, ...), custom_call_target="tpu_custom_call" | custom-call | flops 2415919104 | bytes 7077888 | tf_op jit(solution)/shard_map/grad_weight_partial/pallas_call | solution.py:353
  251.9 5.7 %grad_kept_pass_on.4 = (bf16[592,512]{1,0:T(8,128)(2,1)S(1)}, bf16[592,512]{1,0:T(8,128)(2,1)S(1)}) custom-call(s32[2]{0:T(128)S(1)} %add_clamp_fusion.1.at_ref, f32[2304,512]{1,0:T(8,128)S(1)} %bitcast.16, f32[32,128]{1,0:T(8,128)S(1)} %get-tuple-element.41.b_r.b_l, bf16[592,512]{1,0:T(8,128)(2,1)} %collective-permute-done.15.came_r, ...), custom_call_target="tpu_custom_call" | custom-call | bytes 4718592 | tf_op jit(solution)/shard_map/grad_kept_pass_on/pallas_call | solution.py:227
  258.9 4.6 %collective-permute-start.18 = (bf16[592,512]{1,0:T(8,128)(2,1)S(1)}, bf16[592,512]{1,0:T(8,128)(2,1)S(1)}, u32[]{:S(2)}, u32[]{:S(2)}) collective-permute-start(bf16[592,512]{1,0:T(8,128)(2,1)S(1)} %get-tuple-element.45), channel_id=1, source_target_pairs={{3,2},{2,1},{7,6},{6,5},{11,10},{10,9},{15,14},{14,13},{19,18},{18... | collective-permute-start | bytes 1818632 | tf_op jit(solution)/shard_map/ppermute | solution.py:476
  263.6 5.5 %grad_kept_pass_on.6 = (bf16[592,512]{1,0:T(8,128)(2,1)S(1)}, bf16[592,512]{1,0:T(8,128)(2,1)S(1)}) custom-call(s32[2]{0:T(128)S(1)} %add_clamp_fusion.1.at_ref, f32[2304,512]{1,0:T(8,128)S(1)} %bitcast.12, f32[32,128]{1,0:T(8,128)S(1)} %get-tuple-element.49.b_r.b_l, bf16[592,512]{1,0:T(8,128)(2,1)} %collective-permute-done.21.came_r, ...), custom_call_target="tpu_custom_call" | custom-call | bytes 4718592 | tf_op jit(solution)/shard_map/grad_kept_pass_on/pallas_call | solution.py:227
  270.4 4.6 %collective-permute-start.24 = (bf16[592,512]{1,0:T(8,128)(2,1)S(1)}, bf16[592,512]{1,0:T(8,128)(2,1)S(1)}, u32[]{:S(2)}, u32[]{:S(2)}) collective-permute-start(bf16[592,512]{1,0:T(8,128)(2,1)S(1)} %get-tuple-element.53), channel_id=1, source_target_pairs={{3,2},{2,1},{7,6},{6,5},{11,10},{10,9},{15,14},{14,13},{19,18},{18... | collective-permute-start | bytes 1818632 | tf_op jit(solution)/shard_map/ppermute | solution.py:476
  275.0 7.6 %grad_weight_partial.2 = (f32[288,1024]{1,0:T(8,128)S(1)}, bf16[304,1024]{1,0:T(8,128)(2,1)}, bf16[304,1024]{1,0:T(8,128)(2,1)}, bf16[304,1024]{1,0:T(8,128)(2,1)}) custom-call(s32[3]{0:T(128)S(1)} %copy-done.44, bf16[1024,512]{1,0:T(8,128)(2,1)S(1)} %bitcast.23, bf16[1024,512]{1,0:T(8,128)(2,1)} %collective-permute-done.cot_other_ref, ...), custom_call_target="tpu_custom_call" | custom-call | flops 2415919104 | bytes 7077888 | tf_op jit(solution)/shard_map/grad_weight_partial/pallas_call | solution.py:353
  284.5 2.7 collective-permute-start.32
  291.2 2.0 collective-permute-start.28
  294.7 2.3 copy-done.2
  299.2 3.9 %grad_kept_pass_on.5 = (bf16[592,512]{1,0:T(8,128)(2,1)}, bf16[592,512]{1,0:T(8,128)(2,1)S(1)}) custom-call(s32[2]{0:T(128)S(1)} %add_clamp_fusion.at_ref, f32[2304,512]{1,0:T(8,128)S(1)} %copy-done.2, f32[32,128]{1,0:T(8,128)S(1)} %get-tuple-element.41.b_r.b_l, bf16[592,512]{1,0:T(8,128)(2,1)S(1)} %copy-done.37, f32[2304,512]{1,0:T(8,128)S(1)} %copy-done.2, ...), custom_call_target="tpu_custom_call" | custom-call | bytes 4718592 | tf_op jit(solution)/shard_map/grad_kept_pass_on/pallas_call | solution.py:227
  303.1 4.7 %grad_kept_pass_on.7 = (bf16[592,512]{1,0:T(8,128)(2,1)}, bf16[592,512]{1,0:T(8,128)(2,1)}) custom-call(s32[2]{0:T(128)S(1)} %add_clamp_fusion.at_ref, f32[2304,512]{1,0:T(8,128)S(1)} %bitcast.14, f32[32,128]{1,0:T(8,128)S(1)} %get-tuple-element.49.b_r.b_l, bf16[592,512]{1,0:T(8,128)(2,1)S(1)} %copy-done.41, f32[2304,512]{1,0:T(8,128)S(1)} %bitcast.14, ...), custom_call_target="tpu_custom_call" | custom-call | bytes 4718592 | tf_op jit(solution)/shard_map/grad_kept_pass_on/pallas_call | solution.py:227
  307.9 7.8 %collective-permute-done.32.refs_2_ = bf16[304,1024]{1,0:T(8,128)(2,1)} collective-permute-done((bf16[304,1024]{1,0:T(8,128)(2,1)}, bf16[304,1024]{1,0:T(8,128)(2,1)}, u32[]{:S(2)}, u32[]{:S(2)}) %collective-permute-start.32) | collective-permute-done | bytes 622624 | tf_op jit(solution)/shard_map/ppermute | solution.py:518
  315.7 2.0 collective-permute-start.19
  319.6 3.9 %collective-permute-start.26 = (bf16[592,512]{1,0:T(8,128)(2,1)}, bf16[592,512]{1,0:T(8,128)(2,1)S(1)}, u32[]{:S(2)}, u32[]{:S(2)}) collective-permute-start(bf16[592,512]{1,0:T(8,128)(2,1)} %get-tuple-element.55), channel_id=1, source_target_pairs={{3,2},{2,1},{1,0},{7,6},{6,5},{5,4},{11,10},{10,9},{9,8},{15,14},{... | collective-permute-start | bytes 1818632 | tf_op jit(solution)/shard_map/ppermute | solution.py:476
  323.6 17.9 %collective-permute-done.28.refs_2_ = bf16[304,1024]{1,0:T(8,128)(2,1)} collective-permute-done((bf16[304,1024]{1,0:T(8,128)(2,1)}, bf16[304,1024]{1,0:T(8,128)(2,1)}, u32[]{:S(2)}, u32[]{:S(2)}) %collective-permute-start.28) | collective-permute-done | bytes 622624 | tf_op jit(solution)/shard_map/ppermute | solution.py:518
  341.5 2.2 collective-permute-start.20
  343.7 5.2 %grad_weight_last.2.refs_4_ = f32[576,1024]{1,0:T(8,128)} custom-call(f32[288,1024]{1,0:T(8,128)S(1)} %copy-done.31, bf16[304,1024]{1,0:T(8,128)(2,1)S(1)} %copy-done.35, bf16[304,1024]{1,0:T(8,128)(2,1)} %collective-permute-done.32.refs_2_, bf16[304,1024]{1,0:T(8,128)(2,1)} %collective-permute-done.33.refs_3_, bf16[576,512]{1,0:T(8,128)(2,1)S(1)} %copy-done.5), custom_call_target="tpu_custom_call" | custom-call | bytes 4128768 | tf_op jit(solution)/shard_map/grad_weight_last/pallas_call | solution.py:384
  349.0 5.3 %grad_weight_last.3 = f32[576,1024]{1,0:T(8,128)} custom-call(f32[288,1024]{1,0:T(8,128)S(1)} %copy-done.17, bf16[304,1024]{1,0:T(8,128)(2,1)} %collective-permute-done.27.refs_1_, bf16[304,1024]{1,0:T(8,128)(2,1)} %collective-permute-done.28.refs_2_, bf16[304,1024]{1,0:T(8,128)(2,1)} %collective-permute-done.29.refs_3_, ...), custom_call_target="tpu_custom_call", output_to_operand_aliasing={{}: (4, {})} | custom-call | bytes 4128768 | tf_op jit(solution)/shard_map/grad_weight_last/pallas_call | solution.py:384
  354.3 10.7 %queries.1 = bf16[1024,512]{1,0:T(8,128)(2,1)} custom-call(s32[3]{0:T(128)S(1)} %copy-done.44, f32[288,1024]{1,0:T(8,128)} %copy-done.16, bf16[2304,1024]{1,0:T(8,128)(2,1)} %all-gather.3.cloned.1.call-done.refs_0_.w_ref, bf16[2304,1024]{1,0:T(8,128)(2,1)} %all-gather.5.cloned.1.call-done.refs_1_.w_ref, ...), custom_call_target="tpu_custom_call" | custom-call | flops 4831838208 | bytes 14155776 | tf_op jit(solution)/shard_map/queries/pallas_call | solution.py:430
  365.0 2.8 grad_kept_last.2.base_ref
  367.9 2.3 copy-done.3
  370.2 2.8 grad_kept_last.3
  (163 shorter events, 35.9 us)
Async XLA Ops:
  7.2 208.1 %all-gather.5.cloned.1.call-start = ((), (), s32[]{:S(2)}) async-start(), calls=%async_computation.1 | async-start | bytes 5308416 | tf_op jit(solution)/shard_map/all_gather | solution.py:470
  9.5 43.2 %copy-start.29 = (bf16[1,1152,1024]{2,1,0:T(8,128)(2,1)S(1)}, bf16[1,1152,1024]{2,1,0:T(8,128)(2,1)}, u32[]{:S(2)}) copy-start(bf16[1,1152,1024]{2,1,0:T(8,128)(2,1)} %param.4) | copy-start | bytes 7077892
  47.9 181.2 %all-gather.3.cloned.1.call-start = ((), (), s32[]{:S(2)}) async-start(), calls=%async_computation | async-start | bytes 5308416 | tf_op jit(solution)/shard_map/all_gather | solution.py:470
  48.7 12.9 %collective-permute-start.1 = (bf16[1152,128]{1,0:T(8,128)(2,1)}, bf16[1152,128]{1,0:T(8,128)(2,1)S(1)}, u32[]{:S(2)}, u32[]{:S(2)}) collective-permute-start(bf16[1152,128]{1,0:T(8,128)(2,1)} %copy-done.32), channel_id=1, source_target_pairs={{0,4},{4,8},{8,12},{1,5},{5,9},{9,13},{2,6},{6,10},{10,14},{3,7},{... | collective-permute-start | bytes 884744 | tf_op jit(solution)/shard_map/ppermute | solution.py:110
  61.7 46.1 %copy-start.14 = (bf16[576,512]{1,0:T(8,128)(2,1)}, bf16[576,512]{1,0:T(8,128)(2,1)S(1)}, u32[]{:S(2)}) copy-start(bf16[576,512]{1,0:T(8,128)(2,1)S(1)} %get-tuple-element.35.refs_3_.refs_12_) | copy-start | bytes 1769476
  61.7 58.7 %copy-start.4 = (bf16[576,512]{1,0:T(8,128)(2,1)}, bf16[576,512]{1,0:T(8,128)(2,1)S(1)}, u32[]{:S(2)}) copy-start(bf16[576,512]{1,0:T(8,128)(2,1)S(1)} %get-tuple-element.36.dep_ref.refs_5_.base_ref.refs_3_.refs_4_) | copy-start | bytes 1769476
  61.8 14.0 %collective-permute-start.12 = (bf16[576,512]{1,0:T(8,128)(2,1)S(1)}, bf16[576,512]{1,0:T(8,128)(2,1)S(1)}, u32[]{:S(2)}, u32[]{:S(2)}) collective-permute-start(bf16[576,512]{1,0:T(8,128)(2,1)S(1)} %get-tuple-element.36.dep_ref.refs_5_.base_ref.refs_3_.refs_4_), channel_id=1, source_target_pairs={{1,0},{2,1},{3,2},{5,4},{6,5},{7,6},{9,8},{10,9},{11,10},{13,12},{... | collective-permute-start | bytes 1769480 | tf_op jit(solution)/shard_map/ppermute | solution.py:476
  63.9 15.1 %collective-permute-start.9 = (bf16[576,512]{1,0:T(8,128)(2,1)S(1)}, bf16[576,512]{1,0:T(8,128)(2,1)S(1)}, u32[]{:S(2)}, u32[]{:S(2)}) collective-permute-start(bf16[576,512]{1,0:T(8,128)(2,1)S(1)} %get-tuple-element.36.dep_ref.refs_5_.base_ref.refs_3_.refs_4_), channel_id=1, source_target_pairs={{0,1},{1,2},{2,3},{4,5},{5,6},{6,7},{8,9},{9,10},{10,11},{12,13},{... | collective-permute-start | bytes 1769480 | tf_op jit(solution)/shard_map/ppermute | solution.py:476
  75.8 32.0 %copy-start.20 = (bf16[576,512]{1,0:T(8,128)(2,1)}, bf16[576,512]{1,0:T(8,128)(2,1)S(1)}, u32[]{:S(2)}) copy-start(bf16[576,512]{1,0:T(8,128)(2,1)S(1)} %collective-permute-done.12.refs_6_.refs_4_) | copy-start | bytes 1769476
  75.8 16.1 %collective-permute-start.13 = (bf16[576,512]{1,0:T(8,128)(2,1)S(1)}, bf16[576,512]{1,0:T(8,128)(2,1)}, u32[]{:S(2)}, u32[]{:S(2)}) collective-permute-start(bf16[576,512]{1,0:T(8,128)(2,1)S(1)} %collective-permute-done.12.refs_6_.refs_4_), channel_id=1, source_target_pairs={{1,0},{2,1},{5,4},{6,5},{9,8},{10,9},{13,12},{14,13},{17,16},{18,1... | collective-permute-start | bytes 1769480 | tf_op jit(solution)/shard_map/ppermute | solution.py:476
  79.0 41.5 %copy-start.6 = (bf16[576,512]{1,0:T(8,128)(2,1)}, bf16[576,512]{1,0:T(8,128)(2,1)S(1)}, u32[]{:S(2)}) copy-start(bf16[576,512]{1,0:T(8,128)(2,1)S(1)} %collective-permute-done.9.refs_4_.dep_ref.refs_2_) | copy-start | bytes 1769476
  79.0 18.1 %collective-permute-start.10 = (bf16[576,512]{1,0:T(8,128)(2,1)S(1)}, bf16[576,512]{1,0:T(8,128)(2,1)S(1)}, u32[]{:S(2)}, u32[]{:S(2)}) collective-permute-start(bf16[576,512]{1,0:T(8,128)(2,1)S(1)} %collective-permute-done.9.refs_4_.dep_ref.refs_2_), channel_id=1, source_target_pairs={{1,2},{2,3},{5,6},{6,7},{9,10},{10,11},{13,14},{14,15},{17,18},{18... | collective-permute-start | bytes 1769480 | tf_op jit(solution)/shard_map/ppermute | solution.py:476
  81.4 19.0 %collective-permute-start.5 = (bf16[576,512]{1,0:T(8,128)(2,1)S(1)}, bf16[576,512]{1,0:T(8,128)(2,1)}, u32[]{:S(2)}, u32[]{:S(2)}) collective-permute-start(bf16[576,512]{1,0:T(8,128)(2,1)S(1)} %get-tuple-element.35.refs_3_.refs_12_), channel_id=1, source_target_pairs={{1,0},{2,1},{3,2},{5,4},{6,5},{7,6},{9,8},{10,9},{11,10},{13,12},{... | collective-permute-start | bytes 1769480 | tf_op jit(solution)/shard_map/ppermute | solution.py:476
  84.9 23.0 %collective-permute-start.2 = (bf16[576,512]{1,0:T(8,128)(2,1)S(1)}, bf16[576,512]{1,0:T(8,128)(2,1)S(1)}, u32[]{:S(2)}, u32[]{:S(2)}) collective-permute-start(bf16[576,512]{1,0:T(8,128)(2,1)S(1)} %get-tuple-element.35.refs_3_.refs_12_), channel_id=1, source_target_pairs={{0,1},{1,2},{2,3},{4,5},{5,6},{6,7},{8,9},{9,10},{10,11},{12,13},{... | collective-permute-start | bytes 1769480 | tf_op jit(solution)/shard_map/ppermute | solution.py:476
  91.9 20.9 %collective-permute-start.14 = (bf16[576,512]{1,0:T(8,128)(2,1)}, bf16[576,512]{1,0:T(8,128)(2,1)}, u32[]{:S(2)}, u32[]{:S(2)}) collective-permute-start(bf16[576,512]{1,0:T(8,128)(2,1)} %collective-permute-done.13.refs_7_.refs_5_), channel_id=1, source_target_pairs={{1,0},{5,4},{9,8},{13,12},{17,16},{21,20},{25,24},{29,28}} | collective-permute-start | bytes 1769480 | tf_op jit(solution)/shard_map/ppermute | solution.py:476
  97.1 23.3 %copy-start.8 = (bf16[576,512]{1,0:T(8,128)(2,1)}, bf16[576,512]{1,0:T(8,128)(2,1)S(1)}, u32[]{:S(2)}) copy-start(bf16[576,512]{1,0:T(8,128)(2,1)S(1)} %collective-permute-done.10.refs_3_.dep_ref.refs_1_) | copy-start | bytes 1769476
  97.1 23.3 %collective-permute-start.11 = (bf16[576,512]{1,0:T(8,128)(2,1)S(1)}, bf16[576,512]{1,0:T(8,128)(2,1)}, u32[]{:S(2)}, u32[]{:S(2)}) collective-permute-start(bf16[576,512]{1,0:T(8,128)(2,1)S(1)} %collective-permute-done.10.refs_3_.dep_ref.refs_1_), channel_id=1, source_target_pairs={{2,3},{6,7},{10,11},{14,15},{18,19},{22,23},{26,27},{30,31}} | collective-permute-start | bytes 1769480 | tf_op jit(solution)/shard_map/ppermute | solution.py:476
  100.4 58.2 %collective-permute-start.6 = (bf16[576,512]{1,0:T(8,128)(2,1)}, bf16[576,512]{1,0:T(8,128)(2,1)}, u32[]{:S(2)}, u32[]{:S(2)}) collective-permute-start(bf16[576,512]{1,0:T(8,128)(2,1)} %collective-permute-done.5.refs_4_.refs_13_), channel_id=1, source_target_pairs={{1,0},{2,1},{5,4},{6,5},{9,8},{10,9},{13,12},{14,13},{17,16},{18,1... | collective-permute-start | bytes 1769480 | tf_op jit(solution)/shard_map/ppermute | solution.py:476
  107.8 50.2 %copy-start.10 = (bf16[576,512]{1,0:T(8,128)(2,1)}, bf16[576,512]{1,0:T(8,128)(2,1)S(1)}, u32[]{:S(2)}) copy-start(bf16[576,512]{1,0:T(8,128)(2,1)S(1)} %collective-permute-done.2.refs_2_.refs_11_.dep_ref) | copy-start | bytes 1769476
  107.8 51.5 %collective-permute-start.3 = (bf16[576,512]{1,0:T(8,128)(2,1)S(1)}, bf16[576,512]{1,0:T(8,128)(2,1)S(1)}, u32[]{:S(2)}, u32[]{:S(2)}) collective-permute-start(bf16[576,512]{1,0:T(8,128)(2,1)S(1)} %collective-permute-done.2.refs_2_.refs_11_.dep_ref), channel_id=1, source_target_pairs={{1,2},{2,3},{5,6},{6,7},{9,10},{10,11},{13,14},{14,15},{17,18},{18... | collective-permute-start | bytes 1769480 | tf_op jit(solution)/shard_map/ppermute | solution.py:476
  158.0 83.4 %collective-permute-start.30 = (bf16[1152,512]{1,0:T(8,128)(2,1)}, bf16[1152,512]{1,0:T(8,128)(2,1)}, u32[]{:S(2)}, u32[]{:S(2)}) collective-permute-start(bf16[1152,512]{1,0:T(8,128)(2,1)} %half_for_other_core.3), channel_id=1, source_target_pairs={{0,16},{16,0},{1,17},{17,1},{2,18},{18,2},{3,19},{19,3},{4,20},{20... | collective-permute-start | bytes 3538952 | tf_op jit(solution)/shard_map/ppermute | solution.py:515
  158.1 57.2 %copy-start.5 = (bf16[576,512]{1,0:T(8,128)(2,1)S(1)}, bf16[576,512]{1,0:T(8,128)(2,1)}, u32[]{:S(2)}) copy-start(bf16[576,512]{1,0:T(8,128)(2,1)} %copy-done.4) | copy-start | bytes 1769476
  158.1 81.8 %collective-permute-start = (bf16[1024,512]{1,0:T(8,128)(2,1)}, bf16[1024,512]{1,0:T(8,128)(2,1)}, u32[]{:S(2)}, u32[]{:S(2)}) collective-permute-start(bf16[1024,512]{1,0:T(8,128)(2,1)} %bitcast.19), channel_id=1, source_target_pairs={{0,16},{16,0},{1,17},{17,1},{2,18},{18,2},{3,19},{19,3},{4,20},{20... | collective-permute-start | bytes 3145736 | tf_op jit(solution)/shard_map/ppermute | solution.py:473
  158.6 5.3 %collective-permute-start.7 = (bf16[576,512]{1,0:T(8,128)(2,1)}, bf16[576,512]{1,0:T(8,128)(2,1)S(1)}, u32[]{:S(2)}, u32[]{:S(2)}) collective-permute-start(bf16[576,512]{1,0:T(8,128)(2,1)} %collective-permute-done.6.refs_5_.refs_14_), channel_id=1, source_target_pairs={{1,0},{5,4},{9,8},{13,12},{17,16},{21,20},{25,24},{29,28}} | collective-permute-start | bytes 1769480 | tf_op jit(solution)/shard_map/ppermute | solution.py:476
  159.3 17.5 %copy-start.12 = (bf16[576,512]{1,0:T(8,128)(2,1)}, bf16[576,512]{1,0:T(8,128)(2,1)S(1)}, u32[]{:S(2)}) copy-start(bf16[576,512]{1,0:T(8,128)(2,1)S(1)} %collective-permute-done.3.refs_1_.refs_10_.dep_ref) | copy-start | bytes 1769476
  159.3 17.5 %collective-permute-start.4 = (bf16[576,512]{1,0:T(8,128)(2,1)S(1)}, bf16[576,512]{1,0:T(8,128)(2,1)S(1)}, u32[]{:S(2)}, u32[]{:S(2)}) collective-permute-start(bf16[576,512]{1,0:T(8,128)(2,1)S(1)} %collective-permute-done.3.refs_1_.refs_10_.dep_ref), channel_id=1, source_target_pairs={{2,3},{6,7},{10,11},{14,15},{18,19},{22,23},{26,27},{30,31}} | collective-permute-start | bytes 1769480 | tf_op jit(solution)/shard_map/ppermute | solution.py:476
  215.1 55.2 %collective-permute-start.8 = (bf16[1152,512]{1,0:T(8,128)(2,1)}, bf16[1152,512]{1,0:T(8,128)(2,1)}, u32[]{:S(2)}, u32[]{:S(2)}) collective-permute-start(bf16[1152,512]{1,0:T(8,128)(2,1)} %half_for_other_core.2), channel_id=1, source_target_pairs={{0,16},{16,0},{1,17},{17,1},{2,18},{18,2},{3,19},{19,3},{4,20},{20... | collective-permute-start | bytes 3538952 | tf_op jit(solution)/shard_map/ppermute | solution.py:515
  226.2 25.5 %collective-permute-start.15 = (bf16[592,512]{1,0:T(8,128)(2,1)}, bf16[592,512]{1,0:T(8,128)(2,1)}, u32[]{:S(2)}, u32[]{:S(2)}) collective-permute-start(bf16[592,512]{1,0:T(8,128)(2,1)} %get-tuple-element.42), channel_id=1, source_target_pairs={{0,1},{4,5},{8,9},{12,13},{16,17},{20,21},{24,25},{28,29}} | collective-permute-start | bytes 1818632 | tf_op jit(solution)/shard_map/ppermute | solution.py:476
  227.7 24.2 %collective-permute-start.16 = (bf16[592,512]{1,0:T(8,128)(2,1)}, bf16[592,512]{1,0:T(8,128)(2,1)}, u32[]{:S(2)}, u32[]{:S(2)}) collective-permute-start(bf16[592,512]{1,0:T(8,128)(2,1)} %get-tuple-element.43), channel_id=1, source_target_pairs={{3,2},{7,6},{11,10},{15,14},{19,18},{23,22},{27,26},{31,30}} | collective-permute-start | bytes 1818632 | tf_op jit(solution)/shard_map/ppermute | solution.py:476
  239.9 19.0 %collective-permute-start.21 = (bf16[592,512]{1,0:T(8,128)(2,1)}, bf16[592,512]{1,0:T(8,128)(2,1)}, u32[]{:S(2)}, u32[]{:S(2)}) collective-permute-start(bf16[592,512]{1,0:T(8,128)(2,1)} %get-tuple-element.50), channel_id=1, source_target_pairs={{0,1},{4,5},{8,9},{12,13},{16,17},{20,21},{24,25},{28,29}} | collective-permute-start | bytes 1818632 | tf_op jit(solution)/shard_map/ppermute | solution.py:476
  241.4 22.1 %collective-permute-start.22 = (bf16[592,512]{1,0:T(8,128)(2,1)}, bf16[592,512]{1,0:T(8,128)(2,1)}, u32[]{:S(2)}, u32[]{:S(2)}) collective-permute-start(bf16[592,512]{1,0:T(8,128)(2,1)} %get-tuple-element.51), channel_id=1, source_target_pairs={{3,2},{7,6},{11,10},{15,14},{19,18},{23,22},{27,26},{31,30}} | collective-permute-start | bytes 1818632 | tf_op jit(solution)/shard_map/ppermute | solution.py:476
  251.7 32.0 %collective-permute-start.31 = (bf16[304,1024]{1,0:T(8,128)(2,1)S(1)}, bf16[304,1024]{1,0:T(8,128)(2,1)S(1)}, u32[]{:S(2)}, u32[]{:S(2)}) collective-permute-start(bf16[304,1024]{1,0:T(8,128)(2,1)S(1)} %get-tuple-element.60), channel_id=1, source_target_pairs={{0,4},{4,0},{8,12},{12,8},{1,5},{5,1},{9,13},{13,9},{2,6},{6,2},{1... | collective-permute-start | bytes 1867784 | tf_op jit(solution)/shard_map/ppermute | solution.py:518
  257.6 29.6 %collective-permute-start.17 = (bf16[592,512]{1,0:T(8,128)(2,1)S(1)}, bf16[592,512]{1,0:T(8,128)(2,1)S(1)}, u32[]{:S(2)}, u32[]{:S(2)}) collective-permute-start(bf16[592,512]{1,0:T(8,128)(2,1)S(1)} %get-tuple-element.44), channel_id=1, source_target_pairs={{0,1},{1,2},{4,5},{5,6},{8,9},{9,10},{12,13},{13,14},{16,17},{17,1... | collective-permute-start | bytes 1818632 | tf_op jit(solution)/shard_map/ppermute | solution.py:476
  258.9 29.6 %collective-permute-start.18 = (bf16[592,512]{1,0:T(8,128)(2,1)S(1)}, bf16[592,512]{1,0:T(8,128)(2,1)S(1)}, u32[]{:S(2)}, u32[]{:S(2)}) collective-permute-start(bf16[592,512]{1,0:T(8,128)(2,1)S(1)} %get-tuple-element.45), channel_id=1, source_target_pairs={{3,2},{2,1},{7,6},{6,5},{11,10},{10,9},{15,14},{14,13},{19,18},{18... | collective-permute-start | bytes 1818632 | tf_op jit(solution)/shard_map/ppermute | solution.py:476
  269.1 21.2 %collective-permute-start.23 = (bf16[592,512]{1,0:T(8,128)(2,1)S(1)}, bf16[592,512]{1,0:T(8,128)(2,1)S(1)}, u32[]{:S(2)}, u32[]{:S(2)}) collective-permute-start(bf16[592,512]{1,0:T(8,128)(2,1)S(1)} %get-tuple-element.52), channel_id=1, source_target_pairs={{0,1},{1,2},{4,5},{5,6},{8,9},{9,10},{12,13},{13,14},{16,17},{17,1... | collective-permute-start | bytes 1818632 | tf_op jit(solution)/shard_map/ppermute | solution.py:476
  270.4 22.8 %collective-permute-start.24 = (bf16[592,512]{1,0:T(8,128)(2,1)S(1)}, bf16[592,512]{1,0:T(8,128)(2,1)S(1)}, u32[]{:S(2)}, u32[]{:S(2)}) collective-permute-start(bf16[592,512]{1,0:T(8,128)(2,1)S(1)} %get-tuple-element.53), channel_id=1, source_target_pairs={{3,2},{2,1},{7,6},{6,5},{11,10},{10,9},{15,14},{14,13},{19,18},{18... | collective-permute-start | bytes 1818632 | tf_op jit(solution)/shard_map/ppermute | solution.py:476
  275.0 28.1 %slice-start.2 = ((s8[4718592]{0:T(1024)(128)(4,1)}), s8[524288]{0:T(1024)(128)(4,1)S(1)}, s32[]{:S(2)}) async-start(s8[4718592]{0:T(1024)(128)(4,1)} %bitcast.13), calls=%async_computation.4 | async-start | bytes 1048576
  284.5 31.2 %collective-permute-start.32 = (bf16[304,1024]{1,0:T(8,128)(2,1)}, bf16[304,1024]{1,0:T(8,128)(2,1)}, u32[]{:S(2)}, u32[]{:S(2)}) collective-permute-start(bf16[304,1024]{1,0:T(8,128)(2,1)} %get-tuple-element.61), channel_id=1, source_target_pairs={{0,8},{4,12},{8,0},{12,4},{1,9},{5,13},{9,1},{13,5},{2,10},{6,14},... | collective-permute-start | bytes 1867784 | tf_op jit(solution)/shard_map/ppermute | solution.py:518
  288.0 29.7 %collective-permute-start.33 = (bf16[304,1024]{1,0:T(8,128)(2,1)}, bf16[304,1024]{1,0:T(8,128)(2,1)}, u32[]{:S(2)}, u32[]{:S(2)}) collective-permute-start(bf16[304,1024]{1,0:T(8,128)(2,1)} %get-tuple-element.62), channel_id=1, source_target_pairs={{0,12},{4,8},{8,4},{12,0},{1,13},{5,9},{9,5},{13,1},{2,14},{6,10},... | collective-permute-start | bytes 1867784 | tf_op jit(solution)/shard_map/ppermute | solution.py:518
  289.4 30.2 %collective-permute-start.27 = (bf16[304,1024]{1,0:T(8,128)(2,1)}, bf16[304,1024]{1,0:T(8,128)(2,1)}, u32[]{:S(2)}, u32[]{:S(2)}) collective-permute-start(bf16[304,1024]{1,0:T(8,128)(2,1)} %get-tuple-element.56), channel_id=1, source_target_pairs={{0,4},{4,0},{8,12},{12,8},{1,5},{5,1},{9,13},{13,9},{2,6},{6,2},{1... | collective-permute-start | bytes 1867784 | tf_op jit(solution)/shard_map/ppermute | solution.py:518
  291.2 50.3 %collective-permute-start.28 = (bf16[304,1024]{1,0:T(8,128)(2,1)}, bf16[304,1024]{1,0:T(8,128)(2,1)}, u32[]{:S(2)}, u32[]{:S(2)}) collective-permute-start(bf16[304,1024]{1,0:T(8,128)(2,1)} %get-tuple-element.57), channel_id=1, source_target_pairs={{0,8},{4,12},{8,0},{12,4},{1,9},{5,13},{9,1},{13,5},{2,10},{6,14},... | collective-permute-start | bytes 1867784 | tf_op jit(solution)/shard_map/ppermute | solution.py:518
  294.1 54.9 %collective-permute-start.29 = (bf16[304,1024]{1,0:T(8,128)(2,1)}, bf16[304,1024]{1,0:T(8,128)(2,1)}, u32[]{:S(2)}, u32[]{:S(2)}) collective-permute-start(bf16[304,1024]{1,0:T(8,128)(2,1)} %get-tuple-element.58), channel_id=1, source_target_pairs={{0,12},{4,8},{8,4},{12,0},{1,13},{5,9},{9,5},{13,1},{2,14},{6,10},... | collective-permute-start | bytes 1867784 | tf_op jit(solution)/shard_map/ppermute | solution.py:518
  303.1 40.6 %copy-start.31 = (f32[288,1024]{1,0:T(8,128)S(1)}, f32[288,1024]{1,0:T(8,128)}, u32[]{:S(2)}) copy-start(f32[288,1024]{1,0:T(8,128)} %copy-done.30) | copy-start | bytes 3538948
  303.1 40.6 %copy-start.35 = (bf16[304,1024]{1,0:T(8,128)(2,1)S(1)}, bf16[304,1024]{1,0:T(8,128)(2,1)}, u32[]{:S(2)}) copy-start(bf16[304,1024]{1,0:T(8,128)(2,1)} %copy-done.34) | copy-start | bytes 1867780
  315.7 52.1 %collective-permute-start.19 = (bf16[592,512]{1,0:T(8,128)(2,1)}, bf16[592,512]{1,0:T(8,128)(2,1)S(1)}, u32[]{:S(2)}, u32[]{:S(2)}) collective-permute-start(bf16[592,512]{1,0:T(8,128)(2,1)} %get-tuple-element.46), channel_id=1, source_target_pairs={{0,1},{1,2},{2,3},{4,5},{5,6},{6,7},{8,9},{9,10},{10,11},{12,13},{... | collective-permute-start | bytes 1818632 | tf_op jit(solution)/shard_map/ppermute | solution.py:476
  317.7 47.3 %collective-permute-start.25 = (bf16[592,512]{1,0:T(8,128)(2,1)}, bf16[592,512]{1,0:T(8,128)(2,1)S(1)}, u32[]{:S(2)}, u32[]{:S(2)}) collective-permute-start(bf16[592,512]{1,0:T(8,128)(2,1)} %get-tuple-element.54), channel_id=1, source_target_pairs={{0,1},{1,2},{2,3},{4,5},{5,6},{6,7},{8,9},{9,10},{10,11},{12,13},{... | collective-permute-start | bytes 1818632 | tf_op jit(solution)/shard_map/ppermute | solution.py:476
  319.6 45.4 %collective-permute-start.26 = (bf16[592,512]{1,0:T(8,128)(2,1)}, bf16[592,512]{1,0:T(8,128)(2,1)S(1)}, u32[]{:S(2)}, u32[]{:S(2)}) collective-permute-start(bf16[592,512]{1,0:T(8,128)(2,1)} %get-tuple-element.55), channel_id=1, source_target_pairs={{3,2},{2,1},{1,0},{7,6},{6,5},{5,4},{11,10},{10,9},{9,8},{15,14},{... | collective-permute-start | bytes 1818632 | tf_op jit(solution)/shard_map/ppermute | solution.py:476
  341.5 26.3 %collective-permute-start.20 = (bf16[592,512]{1,0:T(8,128)(2,1)S(1)}, bf16[592,512]{1,0:T(8,128)(2,1)S(1)}, u32[]{:S(2)}, u32[]{:S(2)}) collective-permute-start(bf16[592,512]{1,0:T(8,128)(2,1)S(1)} %get-tuple-element.47), channel_id=1, source_target_pairs={{3,2},{2,1},{1,0},{7,6},{6,5},{5,4},{11,10},{10,9},{9,8},{15,14},{... | collective-permute-start | bytes 1818632 | tf_op jit(solution)/shard_map/ppermute | solution.py:476
  (43 other events, 236.0 us)
Sparse Core Ops, SparseCore 0:
  48.0 40.8 all-gather.4
  90.9 38.9 all-gather.2

commit v3 on v2

--- a/solution.py
+++ b/solution.py
@@ -21,8 +21,7 @@
     return jax.ShapeDtypeStruct(dims, dtype)
 
 
-def params(mib):
-    return pltpu.CompilerParams(vmem_limit_bytes=mib * MIB)
+PARAMS = pltpu.CompilerParams(vmem_limit_bytes=60 * MIB)
 
 
 def cost(flops, moved):
@@ -60,6 +59,11 @@
     rows = out_ref.shape[0] - HEADER
     expo = exponent(bound)
     out_ref[:rows, :] = power(values, jnp.exp2(expo)[0:1, 0:1])
+    write_header(out_ref, expo)
+
+
+def write_header(out_ref, expo):
+    rows = out_ref.shape[0] - HEADER
     code = jnp.broadcast_to((expo + OFFSET)[0:1, 0:1], (HEADER, out_ref.shape[1]))
     out_ref[rows:, :] = code.astype(BF16)
 
@@ -71,19 +75,41 @@
     return jnp.exp2(-expo), jnp.where(came, jnp.exp2(15.0 - expo), 0.0)
 
 
-def pick_kernel(index_ref, x_ref, out_ref):
-    onehot = lax.broadcasted_iota(jnp.int32, (x_ref.shape[1], index_ref.shape[1]), 0) == index_ref[...]
-    out_ref[...] = dot(x_ref[...], onehot.astype(F32).astype(BF16), 1, 0).astype(BF16)
-
-
-def pick_parts_kernel(blocks, sub, index_ref, x_ref, dep_ref, *out_refs):
-    onehot = lax.broadcasted_iota(jnp.int32, (x_ref.shape[1], index_ref.shape[1]), 0) == index_ref[...]
-    onehot = onehot.astype(F32).astype(BF16)
-    parts = len(out_refs)
-    for b in range(blocks):
-        for p, out_ref in enumerate(out_refs):
-            rows = x_ref[pl.ds((b * parts + p) * sub, sub), :]
-            out_ref[pl.ds(b * sub, sub), :] = dot(rows, onehot, 1, 0).astype(BF16)
+def onehot_of(index_ref, first, count, seq_dev):
+    row = lax.axis_index("row")
+    index = index_ref[:, pl.ds(pl.multiple_of(first, 128), count)] - row * seq_dev
+    positions = lax.broadcasted_iota(jnp.int32, (seq_dev, count), 0)
+    return (positions == index).astype(F32).astype(BF16)
+
+
+def pick_kernel(keep_dev, n_row, index_ref, x_ref, out_ref, onehot_ref):
+    count = out_ref.shape[1]
+
+    @pl.when(pl.program_id(0) == 0)
+    def _():
+        after = jnp.minimum(lax.axis_index("row") + 1, n_row - 1) * keep_dev
+        onehot_ref[...] = onehot_of(index_ref, after, count, x_ref.shape[1])
+
+    out_ref[...] = dot(x_ref[...], onehot_ref[...], 1, 0).astype(BF16)
+
+
+def pick_parts_kernel(parts, index_ref, x_ref, dep_ref, *refs):
+    out_refs, onehot_ref = refs[:parts], refs[parts]
+    i = pl.program_id(0)
+    sub, seq_dev = x_ref.shape
+    keep_dev = onehot_ref.shape[1]
+
+    @pl.when(i == 0)
+    def _():
+        onehot_ref[...] = onehot_of(index_ref, lax.axis_index("row") * keep_dev, keep_dev, seq_dev)
+
+    picked = dot(x_ref[...], onehot_ref[...], 1, 0).astype(BF16)
+    rows = pl.ds(pl.multiple_of((i // parts) * sub, 16), sub)
+    for p, out_ref in enumerate(out_refs):
+
+        @pl.when(i % parts == p)
+        def _():
+            out_ref[rows, :] = picked
 
 
 def add_arrived_kernel(blocks, sub, parts, arrived_ref, *refs):
@@ -95,28 +121,33 @@
             out_refs[p][rows, :] = in_refs[p][rows, :] + came
 
 
-def kept_tokens(seq_x, own, leaving_index, blocks, parts, sub, row_pairs):
+def kept_tokens(seq_x, kept_index, keep_dev, drift, blocks, parts, sub, n_row):
     d_dev, seq_dev = seq_x.shape
-    keep_dev, drift = own.shape[1], leaving_index.shape[1]
+    index = pl.BlockSpec(kept_index.shape, lambda i: (0, 0))
+    rows = pl.BlockSpec((sub, seq_dev), lambda i: (i, 0))
     leaving = pl.pallas_call(
-        pick_kernel,
+        functools.partial(pick_kernel, keep_dev, n_row),
+        grid=(d_dev // sub,),
         out_shape=shape((d_dev, drift), BF16),
-        in_specs=[VMEM, VMEM],
-        out_specs=VMEM,
-        compiler_params=params(32),
+        in_specs=[index, rows],
+        out_specs=pl.BlockSpec((sub, drift), lambda i: (i, 0)),
+        scratch_shapes=[pltpu.VMEM((seq_dev, drift), BF16)],
+        compiler_params=PARAMS,
         cost_estimate=cost(2 * d_dev * seq_dev * drift, 2 * d_dev * seq_dev),
         name="pick_leaving",
-    )(leaving_index, seq_x)
-    arrived = lax.ppermute(leaving, "row", row_pairs)
+    )(kept_index, seq_x)
+    arrived = lax.ppermute(leaving, "row", [(r, r + 1) for r in range(n_row - 1)])
     picked = pl.pallas_call(
-        functools.partial(pick_parts_kernel, blocks, sub),
+        functools.partial(pick_parts_kernel, parts),
+        grid=(d_dev // sub,),
         out_shape=[shape((blocks * sub, keep_dev), BF16)] * parts,
-        in_specs=[VMEM, VMEM, ANY],
-        out_specs=[VMEM] * parts,
-        compiler_params=params(32),
+        in_specs=[index, rows, ANY],
+        out_specs=[pl.BlockSpec((blocks * sub, keep_dev), lambda i: (0, 0))] * parts,
+        scratch_shapes=[pltpu.VMEM((seq_dev, keep_dev), BF16)],
+        compiler_params=PARAMS,
         cost_estimate=cost(2 * d_dev * seq_dev * keep_dev, 2 * d_dev * seq_dev),
         name="pick_own",
-    )(own, seq_x, leaving)
+    )(kept_index, seq_x, leaving)
     window = pl.BlockSpec((blocks * sub, drift), lambda i: (0, 0))
     kept = pl.pallas_call(
         functools.partial(add_arrived_kernel, blocks, sub, parts),
@@ -125,7 +156,7 @@
         in_specs=[pl.BlockSpec((d_dev, drift), lambda i: (0, 0))] + [window] * parts,
         out_specs=[window] * parts,
         input_output_aliases={1 + p: p for p in range(parts)},
-        compiler_params=params(16),
+        compiler_params=PARAMS,
         cost_estimate=cost(0, 6 * d_dev * drift),
         name="add_arrived",
     )(arrived, *picked)
@@ -152,8 +183,9 @@
         functools.partial(split_kernel, sub),
         out_shape=[shape((sub, array.shape[1]), array.dtype)] * parts,
         in_specs=[ANY, ANY],
-        out_specs=[ANY] * parts,
+        out_specs=[VMEM] * parts,
         scratch_shapes=[pltpu.SemaphoreType.DMA((parts,))],
+        compiler_params=PARAMS,
         cost_estimate=cost(0, 4 * array.size),
         name="split_rows",
     )(dep, array)
@@ -199,54 +231,66 @@
             payload,
             payload,
         ],
-        compiler_params=params(32),
+        compiler_params=PARAMS,
         cost_estimate=cost(2 * rows * heads * keep, 2 * rows * heads + 4 * rows * keep),
         name="grad_kept_partial",
     )(w_part, cot, dep)
 
 
-def pass_on_kernel(at_ref, g_r, b_r, came_r, g_l, b_l, came_l, dep_ref, out_r, out_l):
-    for g, b, came, out in ((g_r, b_r, came_r, out_r), (g_l, b_l, came_l, out_l)):
-        rows = came.shape[0] - HEADER
-        undo, bound = read_header(came[rows:, :])
-        value = g[...] + root(came[:rows, :], undo[0:1, 0:1])
-        write_payload(out, value, b[...] + bound)
-
-
-def pass_on(at, sums, bounds, came_r, came_l, dep):
+def pass_on_kernel(blocks, at_ref, g_r, b_r, came_r, head_r, g_l, b_l, came_l, head_l, dep_ref, out_r, out_l):
+    i = pl.program_id(0)
+    sub = came_r.shape[0]
+    rows = pl.ds(pl.multiple_of(i * sub, 16), sub)
+    for g, b, came, head, out in ((g_r, b_r, came_r, head_r, out_r), (g_l, b_l, came_l, head_l, out_l)):
+        undo, bound = read_header(head[...])
+        value = g[...] + root(came[...], undo[0:1, 0:1])
+        expo = exponent(b[...] + bound)
+        out[rows, :] = power(value, jnp.exp2(expo)[0:1, 0:1])
+
+        @pl.when(i == 0)
+        def _():
+            write_header(out, expo)
+
+
+def pass_on(numbers, first, sums, bounds, came_r, came_l, dep, blocks):
     shard = came_r.shape[0] - HEADER
     keep = came_r.shape[1]
+    sub = shard // blocks
     whole = pl.BlockSpec((shard + HEADER, keep), lambda i, at: (0, 0))
+    came = [
+        pl.BlockSpec((sub, keep), lambda i, at: (i, 0)),
+        pl.BlockSpec((HEADER, keep), lambda i, at: (shard // HEADER, 0)),
+    ]
 
     def own(n):
         return [
-            pl.BlockSpec((shard, keep), lambda i, at: (at[n], 0)),
+            pl.BlockSpec((sub, keep), lambda i, at: (at[n] * blocks + i, 0)),
             pl.BlockSpec((8, 128), lambda i, at: (at[n], 0)),
         ]
 
     return pl.pallas_call(
-        pass_on_kernel,
+        functools.partial(pass_on_kernel, blocks),
         grid_spec=pltpu.PrefetchScalarGridSpec(
             num_scalar_prefetch=1,
-            grid=(1,),
-            in_specs=own(0) + [whole] + own(1) + [whole, ANY],
+            grid=(blocks,),
+            in_specs=own(first) + came + own(first + 1) + came + [ANY],
             out_specs=[whole, whole],
         ),
         out_shape=[shape((shard + HEADER, keep), BF16)] * 2,
-        compiler_params=params(24),
+        compiler_params=PARAMS,
         cost_estimate=cost(0, 16 * shard * keep),
         name="grad_kept_pass_on",
-    )(at, sums, bounds, came_r, sums, bounds, came_l, dep)
-
-
-def last_kernel(at_ref, g_ref, r_ref, rh_ref, l_ref, lh_ref, base_ref, out_ref):
+    )(numbers, sums, bounds, came_r, came_r, sums, bounds, came_l, came_l, dep)
+
+
+def last_kernel(at_ref, g_ref, r_ref, rh_ref, l_ref, lh_ref, base_ref, dep_ref, out_ref):
     undo_r, _ = read_header(rh_ref[...])
     undo_l, _ = read_header(lh_ref[...])
     total = root(r_ref[...], undo_r[0:1, 0:1]) + root(l_ref[...], undo_l[0:1, 0:1])
     out_ref[0] = g_ref[...] + total
 
 
-def last_sums(at, sums, came_r, came_l, base, part, parts, blocks):
+def last_sums(numbers, sums, came_r, came_l, base, dep, part, parts, blocks):
     shard = came_r.shape[0] - HEADER
     keep = came_r.shape[1]
     sub = shard // blocks
@@ -258,21 +302,22 @@
             num_scalar_prefetch=1,
             grid=(blocks,),
             in_specs=[
-                pl.BlockSpec((sub, keep), lambda b, at: (at[0] * blocks + b, 0)),
+                pl.BlockSpec((sub, keep), lambda b, at: (at[2] * blocks + b, 0)),
                 rows,
                 head,
                 rows,
                 head,
+                ANY,
                 ANY,
             ],
             out_specs=pl.BlockSpec((1, sub, keep), lambda b, at: (b * parts + part, 0, 0)),
         ),
         out_shape=shape((blocks * parts, sub, keep), F32),
         input_output_aliases={6: 0} if part else {},
-        compiler_params=params(24),
+        compiler_params=PARAMS,
         cost_estimate=cost(0, 12 * shard * keep),
         name="grad_kept_last",
-    )(at, sums, came_r, came_r, came_l, came_l, base)
+    )(numbers, sums, came_r, came_r, came_l, came_l, base, dep)
 
 
 def fetch(refs, source, target, sem):
@@ -285,7 +330,7 @@
     return pltpu.make_async_copy(refs[0], target, sem)
 
 
-def give_kernel(n_col, n_half, where_ref, *refs):
+def give_kernel(n_col, n_half, where_ref, dep_ref, *refs):
     sources, (out_ref, sem) = refs[: 2 * n_col - 1], refs[2 * n_col - 1 :]
     other = 1 - where_ref[0]
     shard = sources[0].shape[0]
@@ -302,17 +347,18 @@
         wait.wait()
 
 
-def other_half(where, line, n_col, n_half):
+def other_half(where, line, n_col, n_half, dep):
     shard, keep = line[0].shape
     return pl.pallas_call(
         functools.partial(give_kernel, n_col, n_half),
         out_shape=shape((n_half * shard, keep), BF16),
-        in_specs=[SMEM] + [ANY] * len(line),
-        out_specs=ANY,
+        in_specs=[SMEM, ANY] + [ANY] * len(line),
+        out_specs=VMEM,
         scratch_shapes=[pltpu.SemaphoreType.DMA((n_half,))],
+        compiler_params=PARAMS,
         cost_estimate=cost(0, 4 * n_half * shard * keep),
         name="half_for_other_core",
-    )(where, *line)
+    )(where, dep, *line)
 
 
 def weight_kernel(n_col, n_half, n_row, where_ref, cot_ref, cot_other_ref, other_ref, dep_ref, *refs):
@@ -360,7 +406,7 @@
             pltpu.VMEM((n_row - 1, sub, heads), F32),
             pltpu.SemaphoreType.DMA((n_half,)),
         ],
-        compiler_params=params(40),
+        compiler_params=PARAMS,
         cost_estimate=cost(4 * half * keep * heads, 4 * half * (keep + heads)),
         name="grad_weight_partial",
     )(where, cot, cot_other, other, dep, *line)
@@ -376,7 +422,7 @@
     out_ref[...] = total
 
 
-def weight_last(own, came, base, part, parts):
+def weight_last(own, came, base, dep, part, parts):
     sub, heads = own.shape
     tile = 256
     rows = pl.BlockSpec((sub, tile), lambda i: (0, i))
@@ -385,13 +431,13 @@
         functools.partial(weight_last_kernel, len(came)),
         grid=(heads // tile,),
         out_shape=shape((sub * parts, heads), F32),
-        in_specs=[rows] + [whole] * len(came) + [ANY],
+        in_specs=[rows] + [whole] * len(came) + [ANY, ANY],
         out_specs=pl.BlockSpec((sub, tile), lambda i: (part, i)),
         input_output_aliases={1 + len(came): 0} if part else {},
-        compiler_params=params(24),
+        compiler_params=PARAMS,
         cost_estimate=cost(0, 14 * sub * heads),
         name="grad_weight_last",
-    )(own, *came, base)
+    )(own, *came, base, dep)
 
 
 def query_kernel(n_col, parts, where_ref, dep_ref, *refs):
@@ -439,19 +485,35 @@
             pltpu.VMEM((parts, rows, keep), BF16),
             pltpu.SemaphoreType.DMA((parts, n_col)),
         ],
-        compiler_params=params(48),
+        compiler_params=PARAMS,
         cost_estimate=cost(2 * parts * rows * heads * keep, 2 * parts * rows * (heads + keep)),
         name="queries",
     )(where, dep, *w_parts, *[piece for line in lines for piece in line])
 
 
+def nothing_kernel(*refs):
+    pass
+
+
+def after(values, deps):
+    return pl.pallas_call(
+        nothing_kernel,
+        out_shape=[shape(v.shape, v.dtype) for v in values],
+        in_specs=[ANY] * (len(values) + len(deps)),
+        out_specs=[ANY] * len(values),
+        input_output_aliases={i: i for i in range(len(values))},
+        compiler_params=PARAMS,
+        cost_estimate=cost(0, 0),
+        name="after",
+    )(*values, *deps)
+
+
 def per_device(tokens, kept_index, w_query, cotangent):
     n_dp, n_row, n_col = (lax.axis_size(a) for a in ("dp", "row", "col"))
     dp, row, col = (lax.axis_index(a) for a in ("dp", "row", "col"))
-    where = jnp.stack([dp, row, col]).astype(jnp.int32)
     seq_x = tokens[0]
     cot = cotangent[0]
-    d_dev, seq_dev = seq_x.shape
+    d_dev = seq_x.shape[0]
     w_rows = w_query.shape[0]
     keep_dev = cot.shape[1]
     drift = keep_dev // 4
@@ -460,12 +522,12 @@
     blocks = d_dev // w_rows
     n_half = n_col // n_dp
 
-    base = row * seq_dev
-    own = lax.dynamic_slice_in_dim(kept_index, row * keep_dev, keep_dev, axis=1) - base
-    leaving_index = lax.dynamic_slice_in_dim(kept_index, (row + 1) * keep_dev, drift, axis=1) - base
-    row_pairs = [(r, r + 1) for r in range(n_row - 1)]
-    kept, leaving = kept_tokens(seq_x, own, leaving_index, blocks, parts, sub, row_pairs)
-
+    numbers = [dp, row, col]
+    for t in range(2, n_col):
+        numbers += [jnp.clip(b, 0, n_col - 1) for b in (n_col - t + col, t - n_col + col)]
+    numbers = jnp.stack(numbers).astype(jnp.int32)
+
+    kept, leaving = kept_tokens(seq_x, kept_index, keep_dev, drift, blocks, parts, sub, n_row)
     w_parts = [
         lax.all_gather(w, ("dp", "row"), axis=0, tiled=True) for w in split_rows(w_query, parts, leaving)
     ]
@@ -477,50 +539,65 @@
 
     from_left = [[k] for k in kept]
     from_right = [[k] for k in kept]
+    sums, bounds, right, left = ([None] * parts for _ in range(4))
+    sent = []
 
     def gather_step(p, t):
+        if t > 2:
+            held = after([from_left[p][-1], from_right[p][-1]], sent[-1:])
+            from_left[p][-1], from_right[p][-1] = held
         from_left[p].append(along(from_left[p][-1], range(t - 1, n_col - 1), 1))
         from_right[p].append(along(from_right[p][-1], range(1, n_col - t + 1), -1))
 
-    def reduce_send(right, left, t):
-        return (
-            along(right, range(t), 1),
-            along(left, range(n_col - 1, n_col - 1 - t, -1), -1),
-        )
-
-    for t in range(1, n_col):
-        for p in range(parts):
-            gather_step(p, t)
-    lines = [from_left[p][:0:-1] + [kept[p]] + from_right[p][1:] for p in range(parts)]
-
-    grad_kept = None
-    dep = kept[0]
-    at_end = col.reshape(1).astype(jnp.int32)
-    for p in range(parts):
-        sums, bounds, right, left = first_sums(w_parts[p], cot, n_col, dep)
-        for t in range(1, n_col):
-            if t > 1:
-                at = jnp.stack([n_col - t + col, t - 1 - (n_col - 1 - col)])
-                at = jnp.clip(at, 0, n_col - 1).astype(jnp.int32)
-                right, left = pass_on(at, sums, bounds, right, left, lines[p][n_col - 1 - t + 1])
-            right, left = reduce_send(right, left, t)
-        if grad_kept is None:
-            grad_kept = last_sums(at_end, sums, right, left, dep, p, parts, blocks)
+    def reduce_step(p, t, dep):
+        if t == 1:
+            sums[p], bounds[p], right[p], left[p] = first_sums(w_parts[p], cot, n_col, dep)
         else:
-            grad_kept = last_sums(at_end, sums, right, left, grad_kept, p, parts, blocks)
-
-    grad_weight = dep
-    for p in range(parts):
-        give = other_half(where, lines[p], n_col, n_half)
+            at = 3 + 2 * (t - 2)
+            right[p], left[p] = pass_on(numbers, at, sums[p], bounds[p], right[p], left[p], dep, blocks)
+        sent.append(right[p])
+        right[p] = along(right[p], range(t), 1)
+        left[p] = along(left[p], range(n_col - 1, n_col - 1 - t, -1), -1)
+
+    def weight_step(p, dep):
+        line = from_left[p][:0:-1] + [kept[p]] + from_right[p][1:]
+        give = other_half(numbers, line, n_col, n_half, dep)
         other = lax.ppermute(give, "dp", swap)
-        total, *sends = weight_partial(where, cot, cot_other, other, lines[p], n_col, n_half, n_row, dep)
+        own, *sends = weight_partial(numbers, cot, cot_other, other, line, n_col, n_half, n_row, sent[-1])
         came = [
             lax.ppermute(send, "row", [(r, r ^ step) for r in range(n_row)])
             for step, send in enumerate(sends, 1)
         ]
-        grad_weight = weight_last(total, came, grad_weight, p, parts)
-
-    queries = all_queries(where, w_parts, lines, n_col, total)
+        return line, own, came
+
+    for t in (1, 2):
+        for p in range(parts):
+            gather_step(p, t)
+    reduce_step(0, 1, from_left[-1][1])
+    for t in range(3, n_col):
+        for p in range(parts):
+            gather_step(p, t)
+            if t - 1 + p < n_col:
+                reduce_step(0, t - 1 + p, from_left[p][t - 1])
+    for t in range(len(sent) + 1, n_col):
+        reduce_step(0, t, sent[-1])
+    lines, owns, cames = [], [], []
+    for p in range(parts):
+        if p > 0:
+            reduce_step(p, 1, sent[-1])
+        line, own, came = weight_step(p, sent[-1])
+        lines.append(line)
+        owns.append(own)
+        cames.append(came)
+        if p > 0:
+            for t in range(2, n_col):
+                reduce_step(p, t, own if t > 2 else sent[-1])
+    queries = all_queries(numbers, w_parts, lines, n_col, sent[-1])
+    grad_kept, grad_weight = kept[0], kept[0]
+    for p in range(parts):
+        dep = queries if p == parts - 1 else sent[-1]
+        grad_kept = last_sums(numbers, sums[p], right[p], left[p], grad_kept, dep, p, parts, blocks)
+        grad_weight = weight_last(owns[p], cames[p], grad_weight, dep, p, parts)
     return (queries[None], grad_kept.reshape(1, d_dev, keep_dev), grad_weight)
 
 

time: 388 us -> 278 us (0.72); the launches traced: 380 us -> 276 us
  Pallas kernels: 186 us -> 110 us
  local copies, waits for them, and re-layouts: 29.1 us -> 10.1 us
  starting transfers between devices: 78.1 us -> 72.2 us
    pallas_call x2, Pallas kernels: 75 us -> 6.15 us  [other_half(): pl.pallas_call(functools.partial(give_kernel, n_col, n_half), out_shape=s...]
    pallas_call x1, Pallas kernels: 36.9 us -> 2.32 us  [split_rows(): pl.pallas_call(functools.partial(split_kernel, sub), out_shape=[shape((su...]
    unnamed x110 -> x62, local copies, waits for them, and re-layouts: 29.1 us -> 9.38 us
    pallas_call x6 -> x8, Pallas kernels: 22 us -> 35.3 us  [the longest x4 26.2 us: pass_on(): pl.pallas_call(functools.partial(pass_on_kernel, blocks), grid_spec=pltpu...]
    ppermute x24, waiting for transfers between devices: 36.3 us -> 42.5 us  [along(): return lax.ppermute(value, 'col', [(c, c + step) for c in sources])]
    ppermute x9, waiting for transfers between devices: 32.2 us -> 26.2 us  [the longest x6 22.2 us: weight_step(): lax.ppermute(send, 'row', [(r, r ^ step) for r in range(n_row)])]
    pallas_call x2, Pallas kernels: 10.2 us -> 16.2 us  [first_sums(): pl.pallas_call(partial_kernel, grid=(n_col,), out_shape=[shape((rows, kee...]
    ppermute x24, starting transfers between devices: 67.2 us -> 61.8 us  [along(): return lax.ppermute(value, 'col', [(c, c + step) for c in sources])]
  transfers between devices with their start and end apart: 36 -> 36, of which waited for: 8 -> 9; matrix products, arithmetic and copies ran while one was open for 0% -> 0% of each run, Pallas kernels for 38% -> 36%
where the time goes in v3:
time: 278 us; the launch traced here: 276 us
  Pallas kernels  110 us (40%)
  starting transfers between devices  72.2 us (26%)
  waiting for transfers between devices  69.3 us (25%)
  between operations  14.6 us (5%)
  local copies, waits for them, and re-layouts  10.1 us (4%)
    ppermute x24, starting transfers between devices, along(): return lax.ppermute(value, 'col', [(c, c + step) for c in sources])  61.8 us
    ppermute x24, waiting for transfers between devices, along(): return lax.ppermute(value, 'col', [(c, c + step) for c in sources])  42.5 us
    pallas_call x4, Pallas kernels, pass_on(): pl.pallas_call(functools.partial(pass_on_kernel, blocks), grid_spec=pltpu...  26.2 us
    ppermute x6, waiting for transfers between devices, weight_step(): lax.ppermute(send, 'row', [(r, r ^ step) for r in range(n_row)])  22.2 us
    pallas_call x2, Pallas kernels, weight_partial(): pl.pallas_call(functools.partial(weight_kernel, n_col, n_half, n_row), ou...  17.3 us
    pallas_call x2, Pallas kernels, first_sums(): pl.pallas_call(partial_kernel, grid=(n_col,), out_shape=[shape((rows, kee...  16.2 us
    pallas_call x1, Pallas kernels, all_queries(): pl.pallas_call(functools.partial(query_kernel, n_col, parts), grid=(heads...  11 us
    pallas_call x2, Pallas kernels, weight_last(): pl.pallas_call(functools.partial(weight_last_kernel, len(came)), grid=(he...  10.7 us
  transfers between devices with their start and end apart: 36, of which 9 were waited for; matrix products, arithmetic and copies ran while one was open for 0% of the time, Pallas kernels for 36%

profile of v3, /device:TPU:18, one launch (start us, length us, event | category | flops | bytes accessed | tf_op | source)
XLA Modules:
  0.0 276.4 jit_solution(11613700514941873717)
XLA Ops:
  7.2 4.2 %pick_leaving.1.dep_ref = bf16[1152,128]{1,0:T(8,128)(2,1)} custom-call(s32[1,2048]{1,0:T(1,128)} %index_ref.3, bf16[1152,1024]{1,0:T(8,128)(2,1)} %bitcast.13), custom_call_target="tpu_custom_call" | custom-call | flops 301989888 | bytes 2359296 | tf_op jit(solution)/shard_map/pick_leaving/pallas_call | solution.py:128
  11.4 2.3 split_rows.1
  14.5 3.4 %collective-permute-start = (bf16[1152,128]{1,0:T(8,128)(2,1)S(1)}, bf16[1152,128]{1,0:T(8,128)(2,1)S(1)}, u32[]{:S(2)}, u32[]{:S(2)}) collective-permute-start(bf16[1152,128]{1,0:T(8,128)(2,1)S(1)} %copy-done.25), channel_id=1, source_target_pairs={{0,4},{4,8},{8,12},{1,5},{5,9},{9,13},{2,6},{6,10},{10,14},{3,7},{... | collective-permute-start | bytes 884744 | tf_op jit(solution)/shard_map/ppermute | solution.py:139
  17.9 4.9 %pick_own.1 = (bf16[576,512]{1,0:T(8,128)(2,1)}, bf16[576,512]{1,0:T(8,128)(2,1)}) custom-call(s32[1,2048]{1,0:T(1,128)} %index_ref.3, bf16[1152,1024]{1,0:T(8,128)(2,1)} %bitcast.14, bf16[1152,128]{1,0:T(8,128)(2,1)} %pick_leaving.1.dep_ref), custom_call_target="tpu_custom_call" | custom-call | flops 1207959552 | bytes 2359296 | tf_op jit(solution)/shard_map/pick_own/pallas_call | solution.py:140
  22.8 4.0 %collective-permute-done.arrived_ref = bf16[1152,128]{1,0:T(8,128)(2,1)S(1)} collective-permute-done((bf16[1152,128]{1,0:T(8,128)(2,1)S(1)}, bf16[1152,128]{1,0:T(8,128)(2,1)S(1)}, u32[]{:S(2)}, u32[]{:S(2)}) %collective-permute-start) | collective-permute-done | bytes 294944 | tf_op jit(solution)/shard_map/ppermute | solution.py:139
  27.5 1.9 add_arrived.1
  29.3 3.7 %collective-permute-start.4 = (bf16[576,512]{1,0:T(8,128)(2,1)}, bf16[576,512]{1,0:T(8,128)(2,1)S(1)}, u32[]{:S(2)}, u32[]{:S(2)}) collective-permute-start(bf16[576,512]{1,0:T(8,128)(2,1)} %get-tuple-element.46.refs_5_.base_ref.refs_3_.refs_4_), channel_id=1, source_target_pairs={{0,1},{1,2},{2,3},{4,5},{5,6},{6,7},{8,9},{9,10},{10,11},{12,13},{... | collective-permute-start | bytes 1769480 | tf_op jit(solution)/shard_map/ppermute | solution.py:538
  33.0 1.9 collective-permute-start.1
  34.9 3.9 %collective-permute-start.6 = (bf16[576,512]{1,0:T(8,128)(2,1)}, bf16[576,512]{1,0:T(8,128)(2,1)}, u32[]{:S(2)}, u32[]{:S(2)}) collective-permute-start(bf16[576,512]{1,0:T(8,128)(2,1)} %get-tuple-element.46.refs_5_.base_ref.refs_3_.refs_4_), channel_id=1, source_target_pairs={{1,0},{2,1},{3,2},{5,4},{6,5},{7,6},{9,8},{10,9},{11,10},{13,12},{... | collective-permute-start | bytes 1769480 | tf_op jit(solution)/shard_map/ppermute | solution.py:538
  38.9 8.8 %collective-permute-done.4.refs_4_.refs_2_ = bf16[576,512]{1,0:T(8,128)(2,1)S(1)} collective-permute-done((bf16[576,512]{1,0:T(8,128)(2,1)}, bf16[576,512]{1,0:T(8,128)(2,1)S(1)}, u32[]{:S(2)}, u32[]{:S(2)}) %collective-permute-start.4) | collective-permute-done | bytes 589856 | tf_op jit(solution)/shard_map/ppermute | solution.py:538
  47.7 3.7 %collective-permute-start.5 = (bf16[576,512]{1,0:T(8,128)(2,1)S(1)}, bf16[576,512]{1,0:T(8,128)(2,1)S(1)}, u32[]{:S(2)}, u32[]{:S(2)}) collective-permute-start(bf16[576,512]{1,0:T(8,128)(2,1)S(1)} %collective-permute-done.4.refs_4_.refs_2_), channel_id=1, source_target_pairs={{1,2},{2,3},{5,6},{6,7},{9,10},{10,11},{13,14},{14,15},{17,18},{18... | collective-permute-start | bytes 1769480 | tf_op jit(solution)/shard_map/ppermute | solution.py:538
  51.4 9.0 %collective-permute-done.1.dep_ref.refs_2_.refs_11_ = bf16[576,512]{1,0:T(8,128)(2,1)S(1)} collective-permute-done((bf16[576,512]{1,0:T(8,128)(2,1)}, bf16[576,512]{1,0:T(8,128)(2,1)S(1)}, u32[]{:S(2)}, u32[]{:S(2)}) %collective-permute-start.1) | collective-permute-done | bytes 589856 | tf_op jit(solution)/shard_map/ppermute | solution.py:538
  61.2 8.1 %grad_kept_partial.2 = (f32[2304,512]{1,0:T(8,128)}, f32[32,128]{1,0:T(8,128)}, bf16[592,512]{1,0:T(8,128)(2,1)}, bf16[592,512]{1,0:T(8,128)(2,1)}) custom-call(bf16[2304,1024]{1,0:T(8,128)(2,1)} %all-gather.5.cloned.1.call-done.w_ref.refs_0_, bf16[1024,512]{1,0:T(8,128)(2,1)} %bitcast.15, bf16[576,512]{1,0:T(8,128)(2,1)} %copy-done.21), custom_call_target="tpu_custom_call" | custom-call | flops 2415919104 | bytes 9437184 | tf_op jit(solution)/shard_map/grad_kept_partial/pallas_call | solution.py:214
  70.0 1.3 collective-permute-start.3
  71.3 2.4 collective-permute-start.7
  73.8 4.6 %collective-permute-start.11 = (bf16[576,512]{1,0:T(8,128)(2,1)S(1)}, bf16[576,512]{1,0:T(8,128)(2,1)S(1)}, u32[]{:S(2)}, u32[]{:S(2)}) collective-permute-start(bf16[576,512]{1,0:T(8,128)(2,1)S(1)} %copy-done.8), channel_id=1, source_target_pairs={{1,0},{2,1},{3,2},{5,4},{6,5},{7,6},{9,8},{10,9},{11,10},{13,12},{... | collective-permute-start | bytes 1769480 | tf_op jit(solution)/shard_map/ppermute | solution.py:538
  78.3 1.9 collective-permute-start.10
  80.9 6.6 %collective-permute-done.7.refs_1_ = bf16[576,512]{1,0:T(8,128)(2,1)S(1)} collective-permute-done((bf16[576,512]{1,0:T(8,128)(2,1)}, bf16[576,512]{1,0:T(8,128)(2,1)S(1)}, u32[]{:S(2)}, u32[]{:S(2)}) %collective-permute-start.7) | collective-permute-done | bytes 589856 | tf_op jit(solution)/shard_map/ppermute | solution.py:538
  89.2 6.6 %grad_kept_pass_on.4 = (bf16[592,512]{1,0:T(8,128)(2,1)}, bf16[592,512]{1,0:T(8,128)(2,1)}) custom-call(s32[7]{0:T(128)} %stack.31.at_ref.where_ref, f32[2304,512]{1,0:T(8,128)} %get-tuple-element.42.g_r.g_l.g_ref, f32[32,128]{1,0:T(8,128)} %get-tuple-element.43.b_r.b_l, bf16[592,512]{1,0:T(8,128)(2,1)} %copy-done.9, bf16[592,512]{1,0:T(8,128)(2,1)} %copy-done.9, ...), custom_call_target="tpu_custom_call" | custom-call | bytes 4718592 | tf_op jit(solution)/shard_map/grad_kept_pass_on/pallas_call | solution.py:271
  97.1 4.9 %collective-permute-start.9 = (bf16[592,512]{1,0:T(8,128)(2,1)}, bf16[592,512]{1,0:T(8,128)(2,1)}, u32[]{:S(2)}, u32[]{:S(2)}) collective-permute-start(bf16[592,512]{1,0:T(8,128)(2,1)} %get-tuple-element.49), channel_id=1, source_target_pairs={{3,2},{2,1},{7,6},{6,5},{11,10},{10,9},{15,14},{14,13},{19,18},{18... | collective-permute-start | bytes 1818632 | tf_op jit(solution)/shard_map/ppermute | solution.py:538
  102.1 1.3 collective-permute-start.12
  103.4 2.1 collective-permute-start.21
  105.6 1.5 collective-permute-start.22
  107.0 12.4 %collective-permute-done.12.refs_1_ = bf16[576,512]{1,0:T(8,128)(2,1)S(1)} collective-permute-done((bf16[576,512]{1,0:T(8,128)(2,1)S(1)}, bf16[576,512]{1,0:T(8,128)(2,1)S(1)}, u32[]{:S(2)}, u32[]{:S(2)}) %collective-permute-start.12) | collective-permute-done | bytes 589856 | tf_op jit(solution)/shard_map/ppermute | solution.py:538
  121.1 6.5 %grad_kept_pass_on.5 = (bf16[592,512]{1,0:T(8,128)(2,1)}, bf16[592,512]{1,0:T(8,128)(2,1)}) custom-call(s32[7]{0:T(128)} %stack.31.at_ref.where_ref, f32[2304,512]{1,0:T(8,128)} %get-tuple-element.42.g_r.g_l.g_ref, f32[32,128]{1,0:T(8,128)} %get-tuple-element.43.b_r.b_l, bf16[592,512]{1,0:T(8,128)(2,1)} %copy-done.15, bf16[592,512]{1,0:T(8,128)(2,1)} %copy-done.15, ...), custom_call_target="tpu_custom_call" | custom-call | bytes 4718592 | tf_op jit(solution)/shard_map/grad_kept_pass_on/pallas_call | solution.py:271
  127.6 3.1 %half_for_other_core.3 = bf16[1152,512]{1,0:T(8,128)(2,1)} custom-call(s32[7]{0:T(128)} %stack.31.at_ref.where_ref, bf16[592,512]{1,0:T(8,128)(2,1)} %get-tuple-element.51.dep_ref, bf16[576,512]{1,0:T(8,128)(2,1)} %collective-permute-done.21.refs_2_.refs_0_, bf16[576,512]{1,0:T(8,128)(2,1)} %get-tuple-element.47.dep_ref.refs_3_.refs_1_, ...), custom_call_target="tpu_custom_call" | custom-call | bytes 2359296 | tf_op jit(solution)/shard_map/half_for_other_core/pallas_call | solution.py:352
  130.8 1.3 collective-permute-start.18
  133.3 8.0 %grad_kept_partial.3 = (f32[2304,512]{1,0:T(8,128)}, f32[32,128]{1,0:T(8,128)}, bf16[592,512]{1,0:T(8,128)(2,1)}, bf16[592,512]{1,0:T(8,128)(2,1)}) custom-call(bf16[2304,1024]{1,0:T(8,128)(2,1)} %all-gather.3.cloned.1.call-done.w_ref.refs_1_, bf16[1024,512]{1,0:T(8,128)(2,1)} %bitcast.17, bf16[592,512]{1,0:T(8,128)(2,1)} %get-tuple-element.51.dep_ref), custom_call_target="tpu_custom_call" | custom-call | flops 2415919104 | bytes 9437184 | tf_op jit(solution)/shard_map/grad_kept_partial/pallas_call | solution.py:214
  141.4 4.2 %collective-permute-done.18.refs_0_.refs_9_ = bf16[576,512]{1,0:T(8,128)(2,1)S(1)} collective-permute-done((bf16[576,512]{1,0:T(8,128)(2,1)S(1)}, bf16[576,512]{1,0:T(8,128)(2,1)S(1)}, u32[]{:S(2)}, u32[]{:S(2)}) %collective-permute-start.18) | collective-permute-done | bytes 589856 | tf_op jit(solution)/shard_map/ppermute | solution.py:538
  146.6 3.1 %half_for_other_core.2 = bf16[1152,512]{1,0:T(8,128)(2,1)} custom-call(s32[7]{0:T(128)} %stack.31.at_ref.where_ref, bf16[592,512]{1,0:T(8,128)(2,1)} %get-tuple-element.54.dep_ref, bf16[576,512]{1,0:T(8,128)(2,1)} %copy-done.23, bf16[576,512]{1,0:T(8,128)(2,1)} %get-tuple-element.50.dep_ref.refs_1_.refs_10_, bf16[576,512]{1,0:T(8,128)(2,1)} %copy-done.21, ...), custom_call_target="tpu_custom_call" | custom-call | bytes 2359296 | tf_op jit(solution)/shard_map/half_for_other_core/pallas_call | solution.py:352
  151.8 4.6 %collective-permute-start.25 = (bf16[592,512]{1,0:T(8,128)(2,1)}, bf16[592,512]{1,0:T(8,128)(2,1)S(1)}, u32[]{:S(2)}, u32[]{:S(2)}) collective-permute-start(bf16[592,512]{1,0:T(8,128)(2,1)} %get-tuple-element.51.dep_ref), channel_id=1, source_target_pairs={{0,1},{1,2},{2,3},{4,5},{5,6},{6,7},{8,9},{9,10},{10,11},{12,13},{... | collective-permute-start | bytes 1818632 | tf_op jit(solution)/shard_map/ppermute | solution.py:538
  156.4 2.5 collective-permute-start.26
  158.8 8.6 %grad_weight_partial.3 = (f32[288,1024]{1,0:T(8,128)}, bf16[304,1024]{1,0:T(8,128)(2,1)}, bf16[304,1024]{1,0:T(8,128)(2,1)}, bf16[304,1024]{1,0:T(8,128)(2,1)}) custom-call(s32[7]{0:T(128)} %stack.31.at_ref.where_ref, bf16[1024,512]{1,0:T(8,128)(2,1)} %bitcast.18, bf16[1024,512]{1,0:T(8,128)(2,1)} %collective-permute-done.17.cot_other_ref, ...), custom_call_target="tpu_custom_call" | custom-call | flops 2415919104 | bytes 7077888 | tf_op jit(solution)/shard_map/grad_weight_partial/pallas_call | solution.py:399
  169.9 6.6 %grad_kept_pass_on.6 = (bf16[592,512]{1,0:T(8,128)(2,1)}, bf16[592,512]{1,0:T(8,128)(2,1)}) custom-call(s32[7]{0:T(128)} %stack.31.at_ref.where_ref, f32[2304,512]{1,0:T(8,128)} %get-tuple-element.52.g_r.g_l.g_ref, f32[32,128]{1,0:T(8,128)} %get-tuple-element.53.b_r.b_l, bf16[592,512]{1,0:T(8,128)(2,1)} %copy-done.16, bf16[592,512]{1,0:T(8,128)(2,1)} %copy-done.16, ...), custom_call_target="tpu_custom_call" | custom-call | bytes 4718592 | tf_op jit(solution)/shard_map/grad_kept_pass_on/pallas_call | solution.py:271
  177.8 8.4 %collective-permute-start.16 = (bf16[592,512]{1,0:T(8,128)(2,1)}, bf16[592,512]{1,0:T(8,128)(2,1)S(1)}, u32[]{:S(2)}, u32[]{:S(2)}) collective-permute-start(bf16[592,512]{1,0:T(8,128)(2,1)} %get-tuple-element.57), channel_id=1, source_target_pairs={{3,2},{2,1},{7,6},{6,5},{11,10},{10,9},{15,14},{14,13},{19,18},{18... | collective-permute-start | bytes 1818632 | tf_op jit(solution)/shard_map/ppermute | solution.py:538
  186.6 1.5 collective-permute-start.33
  188.1 8.6 %grad_weight_partial.2 = (f32[288,1024]{1,0:T(8,128)}, bf16[304,1024]{1,0:T(8,128)(2,1)}, bf16[304,1024]{1,0:T(8,128)(2,1)}, bf16[304,1024]{1,0:T(8,128)(2,1)}) custom-call(s32[7]{0:T(128)} %stack.31.at_ref.where_ref, bf16[1024,512]{1,0:T(8,128)(2,1)} %bitcast.19, bf16[1024,512]{1,0:T(8,128)(2,1)} %collective-permute-done.17.cot_other_ref, ...), custom_call_target="tpu_custom_call" | custom-call | flops 2415919104 | bytes 7077888 | tf_op jit(solution)/shard_map/grad_weight_partial/pallas_call | solution.py:399
  196.8 1.8 collective-permute-start.27
  199.6 1.5 collective-permute-start.29
  201.1 6.5 %grad_kept_pass_on.7 = (bf16[592,512]{1,0:T(8,128)(2,1)}, bf16[592,512]{1,0:T(8,128)(2,1)}) custom-call(s32[7]{0:T(128)} %stack.31.at_ref.where_ref, f32[2304,512]{1,0:T(8,128)} %get-tuple-element.52.g_r.g_l.g_ref, f32[32,128]{1,0:T(8,128)} %get-tuple-element.53.b_r.b_l, bf16[592,512]{1,0:T(8,128)(2,1)} %copy-done.12, bf16[592,512]{1,0:T(8,128)(2,1)} %copy-done.12, ...), custom_call_target="tpu_custom_call" | custom-call | bytes 4718592 | tf_op jit(solution)/shard_map/grad_kept_pass_on/pallas_call | solution.py:271
  207.6 22.2 %collective-permute-done.32.refs_2_ = bf16[304,1024]{1,0:T(8,128)(2,1)} collective-permute-done((bf16[304,1024]{1,0:T(8,128)(2,1)S(1)}, bf16[304,1024]{1,0:T(8,128)(2,1)}, u32[]{:S(2)}, u32[]{:S(2)}) %collective-permute-start.32) | collective-permute-done | bytes 622624 | tf_op jit(solution)/shard_map/ppermute | solution.py:568
  229.8 1.9 collective-permute-start.23
  231.7 3.9 %collective-permute-start.24 = (bf16[592,512]{1,0:T(8,128)(2,1)}, bf16[592,512]{1,0:T(8,128)(2,1)S(1)}, u32[]{:S(2)}, u32[]{:S(2)}) collective-permute-start(bf16[592,512]{1,0:T(8,128)(2,1)} %get-tuple-element.62), channel_id=1, source_target_pairs={{3,2},{2,1},{1,0},{7,6},{6,5},{5,4},{11,10},{10,9},{9,8},{15,14},{... | collective-permute-start | bytes 1818632 | tf_op jit(solution)/shard_map/ppermute | solution.py:538
  235.6 4.7 %grad_kept_last.2.base_ref = f32[4,288,512]{2,1,0:T(8,128)} custom-call(s32[7]{0:T(128)} %stack.31.at_ref.where_ref, f32[2304,512]{1,0:T(8,128)} %get-tuple-element.42.g_r.g_l.g_ref, bf16[592,512]{1,0:T(8,128)(2,1)} %copy-done.18, bf16[592,512]{1,0:T(8,128)(2,1)} %copy-done.18, bf16[592,512]{1,0:T(8,128)(2,1)} %copy-done.19, bf16[592,512]{1,0:T(8,128)(2,1)} %copy-done.19, ...), custom_call_target="tpu_custom_call" | custom-call | bytes 3538944 | tf_op jit(solution)/shard_map/grad_kept_last/pallas_call | solution.py:299
  240.4 11.0 %queries.1.dep_ref.refs_5_ = bf16[1024,512]{1,0:T(8,128)(2,1)} custom-call(s32[7]{0:T(128)} %stack.31.at_ref.where_ref, bf16[592,512]{1,0:T(8,128)(2,1)} %get-tuple-element.60.dep_ref.refs_5_, bf16[2304,1024]{1,0:T(8,128)(2,1)} %all-gather.5.cloned.1.call-done.w_ref.refs_0_, bf16[2304,1024]{1,0:T(8,128)(2,1)} %all-gather.3.cloned.1.call-done.w_ref.refs_1_, ...), custom_call_target="tpu_custom_call" | custom-call | flops 4831838208 | bytes 14155776 | tf_op jit(solution)/shard_map/queries/pallas_call | solution.py:476
  251.4 5.4 %grad_weight_last.2.refs_4_ = f32[576,1024]{1,0:T(8,128)} custom-call(f32[288,1024]{1,0:T(8,128)} %get-tuple-element.67.refs_0_, bf16[304,1024]{1,0:T(8,128)(2,1)} %collective-permute-done.31.refs_1_, bf16[304,1024]{1,0:T(8,128)(2,1)} %collective-permute-done.32.refs_2_, bf16[304,1024]{1,0:T(8,128)(2,1)} %collective-permute-done.33.refs_3_, ...), custom_call_target="tpu_custom_call" | custom-call | bytes 4128768 | tf_op jit(solution)/shard_map/grad_weight_last/pallas_call | solution.py:430
  257.8 5.4 %grad_weight_last.3 = f32[576,1024]{1,0:T(8,128)} custom-call(f32[288,1024]{1,0:T(8,128)} %get-tuple-element.59.dep_ref.refs_0_, bf16[304,1024]{1,0:T(8,128)(2,1)} %copy-done.26, bf16[304,1024]{1,0:T(8,128)(2,1)} %copy-done.27, bf16[304,1024]{1,0:T(8,128)(2,1)} %collective-permute-done.29.refs_3_, ...), custom_call_target="tpu_custom_call", output_to_operand_aliasing={{}: (4, {})} | custom-call | bytes 4128768 | tf_op jit(solution)/shard_map/grad_weight_last/pallas_call | solution.py:430
  264.8 4.7 %grad_kept_last.3 = f32[4,288,512]{2,1,0:T(8,128)} custom-call(s32[7]{0:T(128)} %stack.31.at_ref.where_ref, f32[2304,512]{1,0:T(8,128)} %get-tuple-element.52.g_r.g_l.g_ref, bf16[592,512]{1,0:T(8,128)(2,1)} %copy-done.11, bf16[592,512]{1,0:T(8,128)(2,1)} %copy-done.11, bf16[592,512]{1,0:T(8,128)(2,1)} %copy-done.13, ...), custom_call_target="tpu_custom_call", output_to_operand_aliasing={{}: (6, {})} | custom-call | bytes 3538944 | tf_op jit(solution)/shard_map/grad_kept_last/pallas_call | solution.py:299
  (110 shorter events, 20.5 us)
Async XLA Ops:
  7.2 53.2 %all-gather.5.cloned.1.call-start = ((), (), s32[]{:S(2)}) async-start(), calls=%async_computation.1 | async-start | bytes 5308416 | tf_op jit(solution)/shard_map/all_gather | solution.py:532
  13.7 119.6 %all-gather.3.cloned.1.call-start = ((), (), s32[]{:S(2)}) async-start(), calls=%async_computation | async-start | bytes 5308416 | tf_op jit(solution)/shard_map/all_gather | solution.py:532
  14.5 12.3 %collective-permute-start = (bf16[1152,128]{1,0:T(8,128)(2,1)S(1)}, bf16[1152,128]{1,0:T(8,128)(2,1)S(1)}, u32[]{:S(2)}, u32[]{:S(2)}) collective-permute-start(bf16[1152,128]{1,0:T(8,128)(2,1)S(1)} %copy-done.25), channel_id=1, source_target_pairs={{0,4},{4,8},{8,12},{1,5},{5,9},{9,13},{2,6},{6,10},{10,14},{3,7},{... | collective-permute-start | bytes 884744 | tf_op jit(solution)/shard_map/ppermute | solution.py:139
  29.3 18.4 %collective-permute-start.4 = (bf16[576,512]{1,0:T(8,128)(2,1)}, bf16[576,512]{1,0:T(8,128)(2,1)S(1)}, u32[]{:S(2)}, u32[]{:S(2)}) collective-permute-start(bf16[576,512]{1,0:T(8,128)(2,1)} %get-tuple-element.46.refs_5_.base_ref.refs_3_.refs_4_), channel_id=1, source_target_pairs={{0,1},{1,2},{2,3},{4,5},{5,6},{6,7},{8,9},{9,10},{10,11},{12,13},{... | collective-permute-start | bytes 1769480 | tf_op jit(solution)/shard_map/ppermute | solution.py:538
  33.0 27.3 %collective-permute-start.1 = (bf16[576,512]{1,0:T(8,128)(2,1)}, bf16[576,512]{1,0:T(8,128)(2,1)S(1)}, u32[]{:S(2)}, u32[]{:S(2)}) collective-permute-start(bf16[576,512]{1,0:T(8,128)(2,1)} %get-tuple-element.41.refs_3_.refs_12_), channel_id=1, source_target_pairs={{0,1},{1,2},{2,3},{4,5},{5,6},{6,7},{8,9},{9,10},{10,11},{12,13},{... | collective-permute-start | bytes 1769480 | tf_op jit(solution)/shard_map/ppermute | solution.py:538
  34.9 36.4 %collective-permute-start.6 = (bf16[576,512]{1,0:T(8,128)(2,1)}, bf16[576,512]{1,0:T(8,128)(2,1)}, u32[]{:S(2)}, u32[]{:S(2)}) collective-permute-start(bf16[576,512]{1,0:T(8,128)(2,1)} %get-tuple-element.46.refs_5_.base_ref.refs_3_.refs_4_), channel_id=1, source_target_pairs={{1,0},{2,1},{3,2},{5,4},{6,5},{7,6},{9,8},{10,9},{11,10},{13,12},{... | collective-permute-start | bytes 1769480 | tf_op jit(solution)/shard_map/ppermute | solution.py:538
  47.7 21.6 %copy-start.20 = (bf16[576,512]{1,0:T(8,128)(2,1)}, bf16[576,512]{1,0:T(8,128)(2,1)S(1)}, u32[]{:S(2)}) copy-start(bf16[576,512]{1,0:T(8,128)(2,1)S(1)} %collective-permute-done.4.refs_4_.refs_2_) | copy-start | bytes 1769476
  47.7 30.6 %collective-permute-start.5 = (bf16[576,512]{1,0:T(8,128)(2,1)S(1)}, bf16[576,512]{1,0:T(8,128)(2,1)S(1)}, u32[]{:S(2)}, u32[]{:S(2)}) collective-permute-start(bf16[576,512]{1,0:T(8,128)(2,1)S(1)} %collective-permute-done.4.refs_4_.refs_2_), channel_id=1, source_target_pairs={{1,2},{2,3},{5,6},{6,7},{9,10},{10,11},{13,14},{14,15},{17,18},{18... | collective-permute-start | bytes 1769480 | tf_op jit(solution)/shard_map/ppermute | solution.py:538
  61.2 12.6 %copy-start.8 = (bf16[576,512]{1,0:T(8,128)(2,1)S(1)}, bf16[576,512]{1,0:T(8,128)(2,1)}, u32[]{:S(2)}) copy-start(bf16[576,512]{1,0:T(8,128)(2,1)} %get-tuple-element.41.refs_3_.refs_12_) | copy-start | bytes 1769476
  69.3 19.1 %collective-permute-start.2 = (bf16[592,512]{1,0:T(8,128)(2,1)}, bf16[592,512]{1,0:T(8,128)(2,1)S(1)}, u32[]{:S(2)}, u32[]{:S(2)}) collective-permute-start(bf16[592,512]{1,0:T(8,128)(2,1)} %get-tuple-element.44.refs_2_), channel_id=1, source_target_pairs={{0,1},{4,5},{8,9},{12,13},{16,17},{20,21},{24,25},{28,29}} | collective-permute-start | bytes 1818632 | tf_op jit(solution)/shard_map/ppermute | solution.py:538
  70.0 18.4 %collective-permute-start.3 = (bf16[592,512]{1,0:T(8,128)(2,1)}, bf16[592,512]{1,0:T(8,128)(2,1)}, u32[]{:S(2)}, u32[]{:S(2)}) collective-permute-start(bf16[592,512]{1,0:T(8,128)(2,1)} %get-tuple-element.45), channel_id=1, source_target_pairs={{3,2},{7,6},{11,10},{15,14},{19,18},{23,22},{27,26},{31,30}} | collective-permute-start | bytes 1818632 | tf_op jit(solution)/shard_map/ppermute | solution.py:538
  71.3 16.2 %collective-permute-start.7 = (bf16[576,512]{1,0:T(8,128)(2,1)}, bf16[576,512]{1,0:T(8,128)(2,1)S(1)}, u32[]{:S(2)}, u32[]{:S(2)}) collective-permute-start(bf16[576,512]{1,0:T(8,128)(2,1)} %collective-permute-done.6.refs_6_.refs_4_), channel_id=1, source_target_pairs={{1,0},{2,1},{5,4},{6,5},{9,8},{10,9},{13,12},{14,13},{17,16},{18,1... | collective-permute-start | bytes 1769480 | tf_op jit(solution)/shard_map/ppermute | solution.py:538
  73.8 28.3 %collective-permute-start.11 = (bf16[576,512]{1,0:T(8,128)(2,1)S(1)}, bf16[576,512]{1,0:T(8,128)(2,1)S(1)}, u32[]{:S(2)}, u32[]{:S(2)}) collective-permute-start(bf16[576,512]{1,0:T(8,128)(2,1)S(1)} %copy-done.8), channel_id=1, source_target_pairs={{1,0},{2,1},{3,2},{5,4},{6,5},{7,6},{9,8},{10,9},{11,10},{13,12},{... | collective-permute-start | bytes 1769480 | tf_op jit(solution)/shard_map/ppermute | solution.py:538
  78.3 9.3 %copy-start.2 = (bf16[576,512]{1,0:T(8,128)(2,1)}, bf16[576,512]{1,0:T(8,128)(2,1)S(1)}, u32[]{:S(2)}) copy-start(bf16[576,512]{1,0:T(8,128)(2,1)S(1)} %collective-permute-done.5.refs_0_) | copy-start | bytes 1769476
  78.3 27.2 %collective-permute-start.10 = (bf16[576,512]{1,0:T(8,128)(2,1)}, bf16[576,512]{1,0:T(8,128)(2,1)S(1)}, u32[]{:S(2)}, u32[]{:S(2)}) collective-permute-start(bf16[576,512]{1,0:T(8,128)(2,1)} %copy-done.21), channel_id=1, source_target_pairs={{1,2},{2,3},{5,6},{6,7},{9,10},{10,11},{13,14},{14,15},{17,18},{18... | collective-permute-start | bytes 1769480 | tf_op jit(solution)/shard_map/ppermute | solution.py:538
  89.2 14.2 %copy-start.3 = (bf16[576,512]{1,0:T(8,128)(2,1)S(1)}, bf16[576,512]{1,0:T(8,128)(2,1)}, u32[]{:S(2)}) copy-start(bf16[576,512]{1,0:T(8,128)(2,1)} %get-tuple-element.47.dep_ref.refs_3_.refs_1_) | copy-start | bytes 1769476
  89.2 16.3 %copy-start.5 = (bf16[576,512]{1,0:T(8,128)(2,1)S(1)}, bf16[576,512]{1,0:T(8,128)(2,1)}, u32[]{:S(2)}) copy-start(bf16[576,512]{1,0:T(8,128)(2,1)} %get-tuple-element.61.refs_7_.refs_5_) | copy-start | bytes 1769476
  95.8 24.4 %collective-permute-start.8 = (bf16[592,512]{1,0:T(8,128)(2,1)}, bf16[592,512]{1,0:T(8,128)(2,1)S(1)}, u32[]{:S(2)}, u32[]{:S(2)}) collective-permute-start(bf16[592,512]{1,0:T(8,128)(2,1)} %get-tuple-element.48.refs_2_), channel_id=1, source_target_pairs={{0,1},{1,2},{4,5},{5,6},{8,9},{9,10},{12,13},{13,14},{16,17},{17,1... | collective-permute-start | bytes 1818632 | tf_op jit(solution)/shard_map/ppermute | solution.py:538
  97.1 23.1 %collective-permute-start.9 = (bf16[592,512]{1,0:T(8,128)(2,1)}, bf16[592,512]{1,0:T(8,128)(2,1)}, u32[]{:S(2)}, u32[]{:S(2)}) collective-permute-start(bf16[592,512]{1,0:T(8,128)(2,1)} %get-tuple-element.49), channel_id=1, source_target_pairs={{3,2},{2,1},{7,6},{6,5},{11,10},{10,9},{15,14},{14,13},{19,18},{18... | collective-permute-start | bytes 1818632 | tf_op jit(solution)/shard_map/ppermute | solution.py:538
  102.1 25.5 %copy-start.22 = (bf16[576,512]{1,0:T(8,128)(2,1)}, bf16[576,512]{1,0:T(8,128)(2,1)S(1)}, u32[]{:S(2)}) copy-start(bf16[576,512]{1,0:T(8,128)(2,1)S(1)} %collective-permute-done.11.refs_4_.refs_13_) | copy-start | bytes 1769476
  102.1 17.3 %collective-permute-start.12 = (bf16[576,512]{1,0:T(8,128)(2,1)S(1)}, bf16[576,512]{1,0:T(8,128)(2,1)S(1)}, u32[]{:S(2)}, u32[]{:S(2)}) collective-permute-start(bf16[576,512]{1,0:T(8,128)(2,1)S(1)} %collective-permute-done.11.refs_4_.refs_13_), channel_id=1, source_target_pairs={{1,0},{2,1},{5,4},{6,5},{9,8},{10,9},{13,12},{14,13},{17,16},{18,1... | collective-permute-start | bytes 1769480 | tf_op jit(solution)/shard_map/ppermute | solution.py:538
  103.4 24.1 %collective-permute-start.21 = (bf16[576,512]{1,0:T(8,128)(2,1)S(1)}, bf16[576,512]{1,0:T(8,128)(2,1)}, u32[]{:S(2)}, u32[]{:S(2)}) collective-permute-start(bf16[576,512]{1,0:T(8,128)(2,1)S(1)} %copy-done.3), channel_id=1, source_target_pairs={{2,3},{6,7},{10,11},{14,15},{18,19},{22,23},{26,27},{30,31}} | collective-permute-start | bytes 1769480 | tf_op jit(solution)/shard_map/ppermute | solution.py:538
  105.6 13.9 %copy-start = (bf16[576,512]{1,0:T(8,128)(2,1)}, bf16[576,512]{1,0:T(8,128)(2,1)S(1)}, u32[]{:S(2)}) copy-start(bf16[576,512]{1,0:T(8,128)(2,1)S(1)} %collective-permute-done.10.refs_0_) | copy-start | bytes 1769476
  105.6 22.0 %collective-permute-start.22 = (bf16[576,512]{1,0:T(8,128)(2,1)S(1)}, bf16[576,512]{1,0:T(8,128)(2,1)}, u32[]{:S(2)}, u32[]{:S(2)}) collective-permute-start(bf16[576,512]{1,0:T(8,128)(2,1)S(1)} %copy-done.5), channel_id=1, source_target_pairs={{1,0},{5,4},{9,8},{13,12},{17,16},{21,20},{25,24},{29,28}} | collective-permute-start | bytes 1769480 | tf_op jit(solution)/shard_map/ppermute | solution.py:538
  127.6 4.5 %copy-start.7 = (bf16[576,512]{1,0:T(8,128)(2,1)S(1)}, bf16[576,512]{1,0:T(8,128)(2,1)}, u32[]{:S(2)}) copy-start(bf16[576,512]{1,0:T(8,128)(2,1)} %get-tuple-element.58.refs_5_.refs_14_) | copy-start | bytes 1769476
  130.7 25.7 %collective-permute-start.30 = (bf16[1152,512]{1,0:T(8,128)(2,1)}, bf16[1152,512]{1,0:T(8,128)(2,1)}, u32[]{:S(2)}, u32[]{:S(2)}) collective-permute-start(bf16[1152,512]{1,0:T(8,128)(2,1)} %half_for_other_core.3), channel_id=1, source_target_pairs={{0,16},{16,0},{1,17},{17,1},{2,18},{18,2},{3,19},{19,3},{4,20},{20... | collective-permute-start | bytes 3538952 | tf_op jit(solution)/shard_map/ppermute | solution.py:565
  130.8 14.8 %collective-permute-start.18 = (bf16[576,512]{1,0:T(8,128)(2,1)S(1)}, bf16[576,512]{1,0:T(8,128)(2,1)S(1)}, u32[]{:S(2)}, u32[]{:S(2)}) collective-permute-start(bf16[576,512]{1,0:T(8,128)(2,1)S(1)} %copy-done.1), channel_id=1, source_target_pairs={{2,3},{6,7},{10,11},{14,15},{18,19},{22,23},{26,27},{30,31}} | collective-permute-start | bytes 1769480 | tf_op jit(solution)/shard_map/ppermute | solution.py:538
  132.1 13.4 %collective-permute-start.19 = (bf16[576,512]{1,0:T(8,128)(2,1)S(1)}, bf16[576,512]{1,0:T(8,128)(2,1)S(1)}, u32[]{:S(2)}, u32[]{:S(2)}) collective-permute-start(bf16[576,512]{1,0:T(8,128)(2,1)S(1)} %copy-done.7), channel_id=1, source_target_pairs={{1,0},{5,4},{9,8},{13,12},{17,16},{21,20},{25,24},{29,28}} | collective-permute-start | bytes 1769480 | tf_op jit(solution)/shard_map/ppermute | solution.py:538
  132.8 18.9 %collective-permute-start.17 = (bf16[1024,512]{1,0:T(8,128)(2,1)}, bf16[1024,512]{1,0:T(8,128)(2,1)}, u32[]{:S(2)}, u32[]{:S(2)}) collective-permute-start(bf16[1024,512]{1,0:T(8,128)(2,1)} %bitcast.16), channel_id=1, source_target_pairs={{0,16},{16,0},{1,17},{17,1},{2,18},{18,2},{3,19},{19,3},{4,20},{20... | collective-permute-start | bytes 3145736 | tf_op jit(solution)/shard_map/ppermute | solution.py:535
  149.6 37.0 %collective-permute-start.20 = (bf16[1152,512]{1,0:T(8,128)(2,1)}, bf16[1152,512]{1,0:T(8,128)(2,1)}, u32[]{:S(2)}, u32[]{:S(2)}) collective-permute-start(bf16[1152,512]{1,0:T(8,128)(2,1)} %half_for_other_core.2), channel_id=1, source_target_pairs={{0,16},{16,0},{1,17},{17,1},{2,18},{18,2},{3,19},{19,3},{4,20},{20... | collective-permute-start | bytes 3538952 | tf_op jit(solution)/shard_map/ppermute | solution.py:565
  149.7 17.7 %collective-permute-start.13 = (bf16[592,512]{1,0:T(8,128)(2,1)S(1)}, bf16[592,512]{1,0:T(8,128)(2,1)S(1)}, u32[]{:S(2)}, u32[]{:S(2)}) collective-permute-start(bf16[592,512]{1,0:T(8,128)(2,1)S(1)} %copy-done.10), channel_id=1, source_target_pairs={{0,1},{4,5},{8,9},{12,13},{16,17},{20,21},{24,25},{28,29}} | collective-permute-start | bytes 1818632 | tf_op jit(solution)/shard_map/ppermute | solution.py:538
  150.4 18.6 %collective-permute-start.14 = (bf16[592,512]{1,0:T(8,128)(2,1)}, bf16[592,512]{1,0:T(8,128)(2,1)S(1)}, u32[]{:S(2)}, u32[]{:S(2)}) collective-permute-start(bf16[592,512]{1,0:T(8,128)(2,1)} %get-tuple-element.55), channel_id=1, source_target_pairs={{3,2},{7,6},{11,10},{15,14},{19,18},{23,22},{27,26},{31,30}} | collective-permute-start | bytes 1818632 | tf_op jit(solution)/shard_map/ppermute | solution.py:538
  151.8 26.0 %collective-permute-start.25 = (bf16[592,512]{1,0:T(8,128)(2,1)}, bf16[592,512]{1,0:T(8,128)(2,1)S(1)}, u32[]{:S(2)}, u32[]{:S(2)}) collective-permute-start(bf16[592,512]{1,0:T(8,128)(2,1)} %get-tuple-element.51.dep_ref), channel_id=1, source_target_pairs={{0,1},{1,2},{2,3},{4,5},{5,6},{6,7},{8,9},{9,10},{10,11},{12,13},{... | collective-permute-start | bytes 1818632 | tf_op jit(solution)/shard_map/ppermute | solution.py:538
  156.4 29.9 %collective-permute-start.26 = (bf16[592,512]{1,0:T(8,128)(2,1)}, bf16[592,512]{1,0:T(8,128)(2,1)S(1)}, u32[]{:S(2)}, u32[]{:S(2)}) collective-permute-start(bf16[592,512]{1,0:T(8,128)(2,1)} %get-tuple-element.63), channel_id=1, source_target_pairs={{3,2},{2,1},{1,0},{7,6},{6,5},{5,4},{11,10},{10,9},{9,8},{15,14},{... | collective-permute-start | bytes 1818632 | tf_op jit(solution)/shard_map/ppermute | solution.py:538
  167.5 32.2 %collective-permute-start.31 = (bf16[304,1024]{1,0:T(8,128)(2,1)}, bf16[304,1024]{1,0:T(8,128)(2,1)}, u32[]{:S(2)}, u32[]{:S(2)}) collective-permute-start(bf16[304,1024]{1,0:T(8,128)(2,1)} %get-tuple-element.68), channel_id=1, source_target_pairs={{0,4},{4,0},{8,12},{12,8},{1,5},{5,1},{9,13},{13,9},{2,6},{6,2},{1... | collective-permute-start | bytes 1867784 | tf_op jit(solution)/shard_map/ppermute | solution.py:568
  169.9 16.4 %copy-start.30 = (bf16[304,1024]{1,0:T(8,128)(2,1)S(1)}, bf16[304,1024]{1,0:T(8,128)(2,1)}, u32[]{:S(2)}) copy-start(bf16[304,1024]{1,0:T(8,128)(2,1)} %get-tuple-element.69) | copy-start | bytes 1867780
  169.9 16.7 %copy-start.29 = (bf16[304,1024]{1,0:T(8,128)(2,1)S(1)}, bf16[304,1024]{1,0:T(8,128)(2,1)}, u32[]{:S(2)}) copy-start(bf16[304,1024]{1,0:T(8,128)(2,1)} %get-tuple-element.70) | copy-start | bytes 1867780
  176.5 20.2 %collective-permute-start.15 = (bf16[592,512]{1,0:T(8,128)(2,1)}, bf16[592,512]{1,0:T(8,128)(2,1)S(1)}, u32[]{:S(2)}, u32[]{:S(2)}) collective-permute-start(bf16[592,512]{1,0:T(8,128)(2,1)} %get-tuple-element.56), channel_id=1, source_target_pairs={{0,1},{1,2},{4,5},{5,6},{8,9},{9,10},{12,13},{13,14},{16,17},{17,1... | collective-permute-start | bytes 1818632 | tf_op jit(solution)/shard_map/ppermute | solution.py:538
  177.8 18.9 %copy-start.18 = (bf16[592,512]{1,0:T(8,128)(2,1)}, bf16[592,512]{1,0:T(8,128)(2,1)S(1)}, u32[]{:S(2)}) copy-start(bf16[592,512]{1,0:T(8,128)(2,1)S(1)} %collective-permute-done.25.r_ref.rh_ref) | copy-start | bytes 1818628
  177.8 21.3 %collective-permute-start.16 = (bf16[592,512]{1,0:T(8,128)(2,1)}, bf16[592,512]{1,0:T(8,128)(2,1)S(1)}, u32[]{:S(2)}, u32[]{:S(2)}) collective-permute-start(bf16[592,512]{1,0:T(8,128)(2,1)} %get-tuple-element.57), channel_id=1, source_target_pairs={{3,2},{2,1},{7,6},{6,5},{11,10},{10,9},{15,14},{14,13},{19,18},{18... | collective-permute-start | bytes 1818632 | tf_op jit(solution)/shard_map/ppermute | solution.py:538
  186.2 10.5 %copy-start.19 = (bf16[592,512]{1,0:T(8,128)(2,1)}, bf16[592,512]{1,0:T(8,128)(2,1)S(1)}, u32[]{:S(2)}) copy-start(bf16[592,512]{1,0:T(8,128)(2,1)S(1)} %collective-permute-done.26.l_ref.lh_ref) | copy-start | bytes 1818628
  186.3 43.5 %collective-permute-start.32 = (bf16[304,1024]{1,0:T(8,128)(2,1)S(1)}, bf16[304,1024]{1,0:T(8,128)(2,1)}, u32[]{:S(2)}, u32[]{:S(2)}) collective-permute-start(bf16[304,1024]{1,0:T(8,128)(2,1)S(1)} %copy-done.30), channel_id=1, source_target_pairs={{0,8},{4,12},{8,0},{12,4},{1,9},{5,13},{9,1},{13,5},{2,10},{6,14},... | collective-permute-start | bytes 1867784 | tf_op jit(solution)/shard_map/ppermute | solution.py:568
  186.6 45.1 %collective-permute-start.33 = (bf16[304,1024]{1,0:T(8,128)(2,1)S(1)}, bf16[304,1024]{1,0:T(8,128)(2,1)}, u32[]{:S(2)}, u32[]{:S(2)}) collective-permute-start(bf16[304,1024]{1,0:T(8,128)(2,1)S(1)} %copy-done.29), channel_id=1, source_target_pairs={{0,12},{4,8},{8,4},{12,0},{1,13},{5,9},{9,5},{13,1},{2,14},{6,10},... | collective-permute-start | bytes 1867784 | tf_op jit(solution)/shard_map/ppermute | solution.py:568
  196.8 60.0 %collective-permute-start.27 = (bf16[304,1024]{1,0:T(8,128)(2,1)}, bf16[304,1024]{1,0:T(8,128)(2,1)S(1)}, u32[]{:S(2)}, u32[]{:S(2)}) collective-permute-start(bf16[304,1024]{1,0:T(8,128)(2,1)} %get-tuple-element.64), channel_id=1, source_target_pairs={{0,4},{4,0},{8,12},{12,8},{1,5},{5,1},{9,13},{13,9},{2,6},{6,2},{1... | collective-permute-start | bytes 1867784 | tf_op jit(solution)/shard_map/ppermute | solution.py:568
  199.1 57.7 %collective-permute-start.28 = (bf16[304,1024]{1,0:T(8,128)(2,1)}, bf16[304,1024]{1,0:T(8,128)(2,1)S(1)}, u32[]{:S(2)}, u32[]{:S(2)}) collective-permute-start(bf16[304,1024]{1,0:T(8,128)(2,1)} %get-tuple-element.65), channel_id=1, source_target_pairs={{0,8},{4,12},{8,0},{12,4},{1,9},{5,13},{9,1},{13,5},{2,10},{6,14},... | collective-permute-start | bytes 1867784 | tf_op jit(solution)/shard_map/ppermute | solution.py:568
  199.6 57.2 %collective-permute-start.29 = (bf16[304,1024]{1,0:T(8,128)(2,1)}, bf16[304,1024]{1,0:T(8,128)(2,1)}, u32[]{:S(2)}, u32[]{:S(2)}) collective-permute-start(bf16[304,1024]{1,0:T(8,128)(2,1)} %get-tuple-element.66), channel_id=1, source_target_pairs={{0,12},{4,8},{8,4},{12,0},{1,13},{5,9},{9,5},{13,1},{2,14},{6,10},... | collective-permute-start | bytes 1867784 | tf_op jit(solution)/shard_map/ppermute | solution.py:568
  229.8 33.4 %collective-permute-start.23 = (bf16[592,512]{1,0:T(8,128)(2,1)}, bf16[592,512]{1,0:T(8,128)(2,1)S(1)}, u32[]{:S(2)}, u32[]{:S(2)}) collective-permute-start(bf16[592,512]{1,0:T(8,128)(2,1)} %get-tuple-element.60.dep_ref.refs_5_), channel_id=1, source_target_pairs={{0,1},{1,2},{2,3},{4,5},{5,6},{6,7},{8,9},{9,10},{10,11},{12,13},{... | collective-permute-start | bytes 1818632 | tf_op jit(solution)/shard_map/ppermute | solution.py:538
  231.7 31.5 %collective-permute-start.24 = (bf16[592,512]{1,0:T(8,128)(2,1)}, bf16[592,512]{1,0:T(8,128)(2,1)S(1)}, u32[]{:S(2)}, u32[]{:S(2)}) collective-permute-start(bf16[592,512]{1,0:T(8,128)(2,1)} %get-tuple-element.62), channel_id=1, source_target_pairs={{3,2},{2,1},{1,0},{7,6},{6,5},{5,4},{11,10},{10,9},{9,8},{15,14},{... | collective-permute-start | bytes 1818632 | tf_op jit(solution)/shard_map/ppermute | solution.py:538
  (19 other events, 28.4 us)
Sparse Core Ops, SparseCore 0:
  13.8 40.6 all-gather.4
  56.5 38.9 all-gather.2

commit v4 on v0

v4 whole, which is shorter than its diff:
```python
import functools

import jax
import jax.numpy as jnp
from jax import lax
from jax.experimental import pallas as pl
from jax.experimental.pallas import tpu as pltpu
from jax.sharding import PartitionSpec as P

HEADER = 16
OFFSET = 128.0
F32 = jnp.float32
BF16 = jnp.bfloat16
ANY = pl.BlockSpec(memory_space=pl.ANY)
VMEM = pl.BlockSpec(memory_space=pltpu.VMEM)
SMEM = pl.BlockSpec(memory_space=pltpu.SMEM)


def call(kernel, name, out_shape, in_specs, args, out_specs=None, scratch=(), aliases=None, flops=0, mib=14):
    moved = sum(a.size * a.dtype.itemsize for a, s in zip(args, in_specs) if s is VMEM)
    return pl.pallas_call(
        kernel,
        out_shape=out_shape,
        in_specs=in_specs,
        out_specs=out_specs if out_specs is not None else [VMEM] * len(out_shape),
        scratch_shapes=scratch,
        input_output_aliases=aliases or {},
        compiler_params=pltpu.CompilerParams(vmem_limit_bytes=mib * 2**20),
        cost_estimate=pl.CostEstimate(flops=int(flops), bytes_accessed=int(moved), transcendentals=0),
        name=name,
    )(*args)


def shape(dims, dtype):
    return jax.ShapeDtypeStruct(dims, dtype)


def dot(a, b, ca, cb):
    return lax.dot_general(a, b, (((ca,), (cb,)), ((), ())), preferred_element_type=F32)


def span(start, size):
    return pl.ds(pl.multiple_of(start, 16), size)


def chunks(rows):
    size = 32 if rows % 32 == 0 else 16
    return size, rows // size


def exponent(bound):
    return jnp.clip(jnp.floor(14.99 - jnp.log2(jnp.maximum(bound, 1e-30))), -100.0, 100.0)


def power(values, scale):
    v = values * scale
    square = v * v
    fourth = square * square
    return (fourth * square * (v * jnp.abs(v))).astype(BF16)


def root(code, scale):
    y = code.astype(F32)
    quarter = lax.rsqrt(lax.rsqrt(jnp.maximum(jnp.abs(y), 1e-37)))
    size = quarter * lax.rsqrt(quarter) * scale
    return jnp.where(y > 0.0, size, jnp.where(y < 0.0, -size, 0.0))


def tile_max(values):
    most = jnp.max(jnp.abs(values), axis=0, keepdims=True)
    return jnp.broadcast_to(jnp.max(most, axis=1, keepdims=True), (8, 128))


def write_header(out_ref, expo):
    rows = out_ref.shape[0] - HEADER
    code = jnp.broadcast_to((expo + OFFSET)[0:1, 0:1], (HEADER, out_ref.shape[1]))
    out_ref[rows:, :] = code.astype(BF16)


def write_payload(out_ref, value_of, bound):
    expo = exponent(bound)
    scale = jnp.exp2(expo)[0:1, 0:1]
    size, count = chunks(out_ref.shape[0] - HEADER)

    @pl.loop(0, count)
    def _(i):
        out_ref[span(i * size, size), :] = power(value_of(i * size, size), scale)

    write_header(out_ref, expo)


def read_header(came_ref):
    rows = came_ref.shape[0] - HEADER
    code = came_ref[rows:, :][0:8, 0:128].astype(F32)
    came = code > 0.0
    expo = jnp.where(came, code - OFFSET, 0.0)
    return jnp.exp2(-expo)[0:1, 0:1], jnp.where(came, jnp.exp2(15.0 - expo), 0.0)


def pick_kernel(blocks, n_row, index_ref, x_ref, leaving_ref, *refs):
    parts = len(refs) - 3
    out_refs, (rows_ref, onehot_ref, sem) = refs[:parts], refs[parts:]
    d_dev, seq_dev = rows_ref.shape
    drift, keep_dev = leaving_ref.shape[1], out_refs[0].shape[1]
    sub = d_dev // (blocks * parts)

    def copy(i):
        rows = pl.ds(i * sub, sub)
        return pltpu.make_async_copy(x_ref.at[rows, :], rows_ref.at[rows, :], sem.at[i])

    for i in range(blocks * parts):
        copy(i).start()
    row = lax.axis_index("row")

    def onehot(first, count):
        index = index_ref[:, pl.ds(pl.multiple_of(first, 128), count)] - row * seq_dev
        positions = lax.broadcasted_iota(jnp.int32, (seq_dev, count), 0)
        return (positions == index).astype(F32).astype(BF16)

    onehot_ref[:, :keep_dev] = onehot(row * keep_dev, keep_dev)
    onehot_ref[:, keep_dev:] = onehot(jnp.minimum(row + 1, n_row - 1) * keep_dev, drift)
    for i in range(blocks * parts):
        copy(i).wait()
        picked = dot(rows_ref[pl.ds(i * sub, sub), :], onehot_ref[...], 1, 0).astype(BF16)
        out_refs[i % parts][pl.ds((i // parts) * sub, sub), :] = picked[:, :keep_dev]
        leaving_ref[pl.ds(i * sub, sub), :] = picked[:, keep_dev:]


def add_arrived_kernel(blocks, arrived_ref, *refs):
    parts = len(refs) // 2
    in_refs, out_refs = refs[:parts], refs[parts:]
    drift = arrived_ref.shape[1]
    sub = in_refs[0].shape[0] // blocks
    for b in range(blocks):
        for p in range(parts):
            rows = pl.ds(b * sub, sub)
            came = arrived_ref[pl.ds((b * parts + p) * sub, sub), :]
            out_refs[p][rows, :drift] = in_refs[p][rows, :drift] + came


def split_kernel(w_ref, dep_ref, *refs):
    out_refs, sem = refs[:-1], refs[-1]
    sub = out_refs[0].shape[0]
    copies = [
        pltpu.make_async_copy(w_ref.at[pl.ds(p * sub, sub), :], out_ref, sem.at[p])
        for p, out_ref in enumerate(out_refs)
    ]
    for copy in copies:
        copy.start()
    for copy in copies:
        copy.wait()


def nothing_kernel(*refs):
    pass


def after(values, deps):
    return call(
        nothing_kernel,
        "after",
        [shape(v.shape, v.dtype) for v in values],
        [ANY] * (len(values) + len(deps)),
        (*values, *deps),
        out_specs=[ANY] * len(values),
        aliases={i: i for i in range(len(values))},
        mib=1,
    )


def first_kernel(n_dp, n_row, n_col, *refs):
    pieces, (cot_ref, w_ref, sums_ref, bounds_ref, right_ref, left_ref) = refs[: n_dp * n_row], refs[-6:]
    dp, row = lax.axis_index("dp"), lax.axis_index("row")
    sub = pieces[0].shape[0]
    for n, piece in enumerate(pieces):
        block = (dp if n < n_row else 1 - dp) * n_row + (row ^ (n % n_row))
        w_ref[span(block * sub, sub), :] = piece[...]
    shard = w_ref.shape[0] // n_col
    for i in range(n_col):
        rows = pl.ds(i * shard, shard)
        value = dot(w_ref[rows, :], cot_ref[...], 1, 0)
        sums_ref[rows, :] = value
        bounds_ref[pl.ds(i * 8, 8), :] = tile_max(value)
    for out_ref, i in ((right_ref, n_col - 1), (left_ref, 0)):
        write_payload(
            out_ref,
            lambda first, size, i=i: sums_ref[span(i * shard + first, size), :],
            bounds_ref[pl.ds(i * 8, 8), :],
        )


def first_sums(pieces, cot, n_dp, n_row, n_col, deps):
    sub, heads = pieces[0].shape
    keep = cot.shape[1]
    rows = sub * n_dp * n_row
    payload = shape((rows // n_col + HEADER, keep), BF16)

    def kernel(*refs):
        first_kernel(n_dp, n_row, n_col, *refs[: n_dp * n_row], refs[n_dp * n_row], *refs[-5:])

    return call(
        kernel,
        "grad_kept_first",
        [shape((rows, heads), BF16), shape((rows, keep), F32), shape((n_col * 8, 128), F32), payload, payload],
        [VMEM] * (len(pieces) + 1) + [ANY] * len(deps),
        (*pieces, cot, *deps),
        flops=2 * rows * heads * keep,
    )


def pass_on_kernel(n_col, t, sums_ref, bounds_ref, came_r, came_l, dep_ref, out_r, out_l):
    shard = came_r.shape[0] - HEADER
    col = lax.axis_index("col")
    for block, came, out in ((n_col - t + col, came_r, out_r), (t - n_col + col, came_l, out_l)):
        block = jnp.clip(block, 0, n_col - 1)
        undo, bound = read_header(came)
        write_payload(
            out,
            lambda first, size, block=block, came=came, undo=undo: (
                sums_ref[span(block * shard + first, size), :] + root(came[span(first, size), :], undo)
            ),
            bounds_ref[pl.ds(pl.multiple_of(block * 8, 8), 8), :] + bound,
        )


def pass_on(n_col, t, sums, bounds, came_r, came_l, dep):
    payload = shape(came_r.shape, BF16)
    return call(
        functools.partial(pass_on_kernel, n_col, t),
        "grad_kept_pass_on",
        [payload, payload],
        [VMEM] * 4 + [ANY],
        (sums, bounds, came_r, came_l, dep),
        flops=20 * came_r.size,
    )


def last_kernel(part, parts, blocks, sums_ref, r_ref, l_ref, base_ref, dep_ref, out_ref, total_ref, sem):
    shard = r_ref.shape[0] - HEADER
    sub = shard // blocks
    first = lax.axis_index("col") * shard
    undo_r, _ = read_header(r_ref)
    undo_l, _ = read_header(l_ref)
    size, count = chunks(sub)
    copies = []
    for b in range(blocks):

        @pl.loop(0, count)
        def _(i):
            at = b * sub + i * size
            rows = span(at, size)
            came = root(r_ref[rows, :], undo_r) + root(l_ref[rows, :], undo_l)
            total_ref[rows, :] = sums_ref[span(first + at, size), :] + came

        copies.append(
            pltpu.make_async_copy(
                total_ref.at[pl.ds(b * sub, sub), :], out_ref.at[b * parts + part], sem.at[b]
            )
        )
        copies[-1].start()
    for copy in copies:
        copy.wait()


def last_sums(sums, came_r, came_l, base, dep, part, parts, blocks):
    shard, keep = came_r.shape[0] - HEADER, came_r.shape[1]
    return call(
        functools.partial(last_kernel, part, parts, blocks),
        "grad_kept_last",
        shape((blocks * parts, shard // blocks, keep), F32),
        [VMEM] * 3 + [ANY] * 2,
        (sums, came_r, came_l, base, dep),
        out_specs=ANY,
        scratch=[pltpu.VMEM((shard, keep), F32), pltpu.SemaphoreType.DMA((blocks,))],
        aliases={3: 0} if part else None,
        flops=20 * shard * keep,
    )


def each_shard(line):
    n_col = (len(line) + 1) // 2
    col = lax.axis_index("col")
    for n, ref in enumerate(line):
        shard = col + n - (n_col - 1)
        yield (shard >= 0) & (shard < n_col), shard, ref


def half_kernel(n_half, *refs):
    line, out_ref = refs[:-2], refs[-1]
    other = 1 - lax.axis_index("dp")
    for came, shard, ref in each_shard(line):
        rows = ref.shape[0]

        @pl.when(came & (shard >= other * n_half) & (shard < (other + 1) * n_half))
        def _():
            out_ref[span((shard - other * n_half) * rows, rows), :] = ref[...]


def other_half(line, n_half, dep):
    rows, keep = line[0].shape
    return call(
        functools.partial(half_kernel, n_half),
        "half_for_other_core",
        shape((n_half * rows, keep), BF16),
        [VMEM] * len(line) + [ANY],
        (*line, dep),
        out_specs=VMEM,
    )


def weight_kernel(n_half, n_row, cot_ref, cot_other_ref, other_ref, *refs):
    count = len(refs) - n_row - 3
    line, own_ref, send_refs = refs[:count], refs[count + 1], refs[count + 2 : count + 1 + n_row]
    mine_ref, total_ref = refs[-2:]
    dp, row = lax.axis_index("dp"), lax.axis_index("row")
    for came, shard, ref in each_shard(line):
        rows = ref.shape[0]

        @pl.when(came & (shard >= dp * n_half) & (shard < (dp + 1) * n_half))
        def _():
            mine_ref[span((shard - dp * n_half) * rows, rows), :] = ref[...]

    sub = own_ref.shape[0]
    bound = jnp.zeros((8, 128), F32)
    for step in range(n_row):
        rows = span((row ^ step) * sub, sub)
        value = dot(mine_ref[rows, :], cot_ref[...], 1, 1) + dot(other_ref[rows, :], cot_other_ref[...], 1, 1)
        if step == 0:
            own_ref[...] = value
        else:
            total_ref[step - 1] = value
            bound = jnp.maximum(bound, tile_max(value))
    for step in range(1, n_row):
        write_payload(
            send_refs[step - 1],
            lambda first, size, step=step: total_ref[step - 1, span(first, size), :],
            bound,
        )


def weight_partial(cot, cot_other, other, line, n_half, n_row, dep):
    half, keep = other.shape
    heads = cot.shape[0]
    sub = half // n_row
    return call(
        functools.partial(weight_kernel, n_half, n_row),
        "grad_weight_partial",
        [shape((sub, heads), F32)] + [shape((sub + HEADER, heads), BF16)] * (n_row - 1),
        [VMEM] * (3 + len(line)) + [ANY],
        (cot, cot_other, other, *line, dep),
        scratch=[pltpu.VMEM((half, keep), BF16), pltpu.VMEM((n_row - 1, sub, heads), F32)],
        flops=4 * half * keep * heads,
        mib=20,
    )


def weight_last_kernel(n_came, part, own_ref, *refs):
    came_refs, (out_ref, total_ref, sem) = refs[:n_came], refs[-3:]
    sub = own_ref.shape[0]
    undo = [read_header(came)[0] for came in came_refs]
    size = 16
    steps = sub // size
    copies = []
    for first, last in ((0, steps // 2), (steps // 2, steps)):

        @pl.loop(first, last)
        def _(i):
            rows = span(i * size, size)
            total = own_ref[rows, :]
            for came, scale in zip(came_refs, undo):
                total = total + root(came[rows, :], scale)
            total_ref[rows, :] = total

        rows = pl.ds(first * size, (last - first) * size)
        target = out_ref.at[pl.ds(part * sub + first * size, (last - first) * size), :]
        copies.append(pltpu.make_async_copy(total_ref.at[rows, :], target, sem.at[len(copies)]))
        copies[-1].start()
    for copy in copies:
        copy.wait()


def weight_last(own, came, base, dep, part, parts):
    sub, heads = own.shape
    return call(
        functools.partial(weight_last_kernel, len(came), part),
        "grad_weight_last",
        shape((sub * parts, heads), F32),
        [VMEM] * (1 + len(came)) + [ANY] * 2,
        (own, *came, base, dep),
        out_specs=ANY,
        scratch=[pltpu.VMEM((sub, heads), F32), pltpu.SemaphoreType.DMA((2,))],
        aliases={1 + len(came): 0} if part else None,
        flops=20 * sub * heads * len(came),
    )


def query_kernel(parts, *refs):
    w_refs = refs[:parts]
    count = (len(refs) - parts - 3) // parts
    lines = [refs[parts + p * count : parts + (p + 1) * count] for p in range(parts)]
    out_ref, panel_ref = refs[-2:]
    for p, line in enumerate(lines):
        for came, shard, ref in each_shard(line):
            rows = ref.shape[0]

            @pl.when(came)
            def _():
                panel_ref[p, span(shard * rows, rows), :] = ref[...]

    tile = 256
    for i in range(out_ref.shape[0] // tile):
        heads = pl.ds(i * tile, tile)
        total = dot(w_refs[0][:, heads], panel_ref[0], 0, 0)
        for p in range(1, parts):
            total = total + dot(w_refs[p][:, heads], panel_ref[p], 0, 0)
        out_ref[heads, :] = total.astype(BF16)


def all_queries(w_parts, lines, dep):
    parts = len(w_parts)
    rows, heads = w_parts[0].shape
    keep = lines[0][0].shape[1]
    return call(
        functools.partial(query_kernel, parts),
        "queries",
        shape((heads, keep), BF16),
        [VMEM] * (parts + len(lines[0]) * parts) + [ANY],
        (*w_parts, *[piece for line in lines for piece in line], dep),
        out_specs=VMEM,
        scratch=[pltpu.VMEM((parts, rows, keep), BF16)],
        flops=2 * parts * rows * heads * keep,
        mib=20,
    )


def per_device(tokens, kept_index, w_query, cotangent):
    n_dp, n_row, n_col = (lax.axis_size(a) for a in ("dp", "row", "col"))
    seq_x = tokens[0]
    cot = cotangent[0]
    d_dev, seq_dev = seq_x.shape
    w_rows, heads = w_query.shape
    keep_dev = cot.shape[1]
    drift = keep_dev // 4
    parts = 2 if w_rows % 32 == 0 else 1
    sub = w_rows // parts
    blocks = d_dev // w_rows
    shard = blocks * sub
    n_half = n_col // n_dp

    def to_row(value, step):
        return lax.ppermute(value, "row", [(r, r ^ step) for r in range(n_row)])

    def to_core(value):
        return lax.ppermute(value, "dp", [(i, i ^ 1) for i in range(n_dp)])

    def along(value, sources, step):
        return lax.ppermute(value, "col", [(c, c + step) for c in sources])

    leaving, *picked = call(
        functools.partial(pick_kernel, blocks, n_row),
        "pick",
        [shape((d_dev, drift), BF16)] + [shape((shard, keep_dev), BF16)] * parts,
        [VMEM, ANY],
        (kept_index, seq_x),
        scratch=[
            pltpu.VMEM((d_dev, seq_dev), BF16),
            pltpu.VMEM((seq_dev, keep_dev + drift), BF16),
            pltpu.SemaphoreType.DMA((blocks * parts,)),
        ],
        flops=2 * d_dev * seq_dev * (keep_dev + drift),
    )
    arrived = lax.ppermute(leaving, "row", [(r, r + 1) for r in range(n_row - 1)])
    own_w = list(call(
        split_kernel,
        "split_rows",
        [shape((sub, heads), BF16)] * parts,
        [ANY, ANY],
        (w_query, leaving),
        scratch=[pltpu.SemaphoreType.DMA((parts,))],
    ))
    cot_other = to_core(cot)
    pieces = []
    for p in range(parts):
        if p > 0:
            (own_w[p],) = after([own_w[p]], pieces[0][1:n_row])
        mine = [own_w[p]] + [to_row(own_w[p], step) for step in range(1, n_row)]
        pieces.append(mine + [to_core(m) for m in mine])
    kept = call(
        functools.partial(add_arrived_kernel, blocks),
        "add_arrived",
        [shape((shard, keep_dev), BF16)] * parts,
        [VMEM] * (1 + parts),
        (arrived, *picked),
        aliases={1 + p: p for p in range(parts)},
    )

    from_left = [[k] for k in kept]
    from_right = [[k] for k in kept]
    w_parts, sums, bounds, right, left, owns, cames = ([None] * parts for _ in range(7))
    token = None

    def line_of(p):
        return from_left[p][:0:-1] + [kept[p]] + from_right[p][1:]

    def gather(p, t):
        nonlocal token
        if t > 2:
            held = after([from_left[p][-1], from_right[p][-1]], [token])
            from_left[p][-1], from_right[p][-1] = held
            token = held[0]
        from_left[p].append(along(from_left[p][-1], range(t - 1, n_col - 1), 1))
        from_right[p].append(along(from_right[p][-1], range(1, n_col - t + 1), -1))

    def pass_sums(p, t):
        nonlocal token
        if t == 1:
            deps = [token] if token is not None else [f[q][1] for q in range(parts) for f in (from_left, from_right)]
            w_parts[p], sums[p], bounds[p], right[p], left[p] = first_sums(
                pieces[p], cot, n_dp, n_row, n_col, deps
            )
        else:
            right[p], left[p] = pass_on(n_col, t, sums[p], bounds[p], right[p], left[p], token)
        token = right[p]
        right[p] = along(right[p], range(t), 1)
        left[p] = along(left[p], range(n_col - 1, n_col - 1 - t, -1), -1)

    def weigh(p):
        nonlocal token
        give = other_half(line_of(p), n_half, token)
        owns[p], *sends = weight_partial(cot, cot_other, to_core(give), line_of(p), n_half, n_row, give)
        token = owns[p]
        cames[p] = [to_row(send, step) for step, send in enumerate(sends, 1)]

    last = parts - 1
    for t in (1, 2):
        for p in range(parts):
            gather(p, t)
    pass_sums(0, 1)
    for t in range(3, n_col):
        gather(0, t)
        pass_sums(0, t - 1)
        if parts > 1:
            gather(1, t)
            pass_sums(1, t - 2)
    pass_sums(0, n_col - 1)
    weigh(0)
    if parts > 1:
        pass_sums(1, n_col - 2)
        weigh(1)
        pass_sums(1, n_col - 1)
    queries = all_queries(w_parts, [line_of(p) for p in range(parts)], token)
    grad_kept, grad_weight = leaving, leaving
    for p in range(parts):
        grad_kept = last_sums(sums[p], right[p], left[p], grad_kept, queries, p, parts, blocks)
        grad_weight = weight_last(owns[p], cames[p], grad_weight, queries, p, parts)
    return (queries[None], grad_kept.reshape(1, d_dev, keep_dev), grad_weight)


def solution(mesh):
    in_specs = (
        P("dp", "col", "row"),
        P("dp", None),
        P(("dp", "row"), "col"),
        P("dp", "col", "row"),
    )
    out_specs = (P("dp", "col", "row"), P("dp", "col", "row"), P(("dp", "row"), "col"))
    return jax.shard_map(
        per_device, mesh=mesh, in_specs=in_specs, out_specs=out_specs, check_vma=False
    )
```

time: 464 us -> 224 us (0.48)
  waiting for transfers between devices: 404 us -> 91.2 us
  starting transfers between devices: 3.56 us -> 72.9 us
  Pallas kernels: 0 us -> 52.2 us
  matrix products: 36.8 us -> 0 us
  between operations: 13.8 us -> 1.44 us
    reduce_scatter x2 -> x0, waiting for transfers between devices: 273 us -> none  [the longest x1 143 us: per_device(): lax.psum_scatter(jnp.dot(w_panel, head_grad, preferred_element_type=jnp.f...]
    all_gather x2 -> x0, waiting for transfers between devices: 124 us -> none  [the longest x1 78.6 us: per_device(): full_panel = lax.all_gather(kept_panel, 'col', axis=0, tiled=True)]
    ppermute x1 -> x48, waiting for transfers between devices: 6.54 us -> 91.2 us  [the longest x24 60.1 us: along(): return lax.ppermute(value, 'col', [(c, c + step) for c in sources])]
    ppermute x1 -> x48, starting transfers between devices: 3.4 us -> 72.9 us  [the longest x24 56.9 us: along(): return lax.ppermute(value, 'col', [(c, c + step) for c in sources])]
    pallas_call x0 -> x21, Pallas kernels: none -> 52.2 us  [call(): pl.pallas_call(kernel, out_shape=out_shape, in_specs=in_specs, out_specs=...]
    dot_general x5 -> x0, matrix products: 36.8 us -> none  [the longest x1 11.9 us: per_device(): lax.dot_general(full_panel, head_grad, (((1,), (1,)), ((), ())), preferre...]
  transfers between devices with their start and end apart: 5 -> 48, of which waited for: 5 -> 17; matrix products, arithmetic and copies ran while one was open for 9% -> 0% of each run, Pallas kernels for 0% -> 20%
where the time goes in v4:
time: 224 us
  waiting for transfers between devices  91.2 us (41%)
  starting transfers between devices  72.9 us (33%)
  Pallas kernels  52.2 us (23%)
  local copies, waits for them, and re-layouts  5.88 us (3%)
    ppermute x24, waiting for transfers between devices, along(): return lax.ppermute(value, 'col', [(c, c + step) for c in sources])  60.1 us
    ppermute x24, starting transfers between devices, along(): return lax.ppermute(value, 'col', [(c, c + step) for c in sources])  56.9 us
    pallas_call x21, Pallas kernels, call(): pl.pallas_call(kernel, out_shape=out_shape, in_specs=in_specs, out_specs=...  52.2 us
    ppermute x1, waiting for transfers between devices, per_device(): lax.ppermute(leaving, 'row', [(r, r + 1) for r in range(n_row - 1)])  17 us
    ppermute x12, waiting for transfers between devices, to_row(): return lax.ppermute(value, 'row', [(r, r ^ step) for r in range(n_row)])  14 us
    ppermute x12, starting transfers between devices, to_row(): return lax.ppermute(value, 'row', [(r, r ^ step) for r in range(n_row)])  10.5 us
    unnamed x20, local copies, waits for them, and re-layouts  5.88 us
  transfers between devices with their start and end apart: 48, of which 17 were waited for; matrix products, arithmetic and copies ran while one was open for 0% of the time, Pallas kernels for 20%

profile of v4, /device:TPU:18, one launch (start us, length us, event | category | flops | bytes accessed | tf_op | source)
XLA Modules:
  0.0 223.6 jit_solution(8859306804771048893)
XLA Ops:
  0.6 1.7 copy-done.3
  3.0 3.9 %pick.1 = (bf16[1152,128]{1,0:T(8,128)(2,1)S(1)}, bf16[576,512]{1,0:T(8,128)(2,1)S(1)}, bf16[576,512]{1,0:T(8,128)(2,1)S(1)}) custom-call(s32[1,2048]{1,0:T(1,128)S(1)} %copy-done.9, bf16[1152,1024]{1,0:T(8,128)(2,1)S(1)} %bitcast.5), custom_call_target="tpu_custom_call" | custom-call | flops 1509949440 | bytes 8192 | tf_op jit(solution)/shard_map/pick/pallas_call | solution.py:21
  9.3 4.3 %collective-permute-start.7 = (bf16[1152,128]{1,0:T(8,128)(2,1)S(1)}, bf16[1152,128]{1,0:T(8,128)(2,1)S(1)}, u32[]{:S(2)}, u32[]{:S(2)}) collective-permute-start(bf16[1152,128]{1,0:T(8,128)(2,1)S(1)} %get-tuple-element.40.dep_ref.base_ref.refs_3_), channel_id=1, source_target_pairs={{0,4},{4,8},{8,12},{1,5},{5,9},{9,13},{2,6},{6,10},{10,14},{3,7},{... | collective-permute-start | bytes 884744 | tf_op jit(solution)/shard_map/ppermute | solution.py:472
  13.8 17.0 %collective-permute-done.7.arrived_ref = bf16[1152,128]{1,0:T(8,128)(2,1)S(1)} collective-permute-done((bf16[1152,128]{1,0:T(8,128)(2,1)S(1)}, bf16[1152,128]{1,0:T(8,128)(2,1)S(1)}, u32[]{:S(2)}, u32[]{:S(2)}) %collective-permute-start.7) | collective-permute-done | bytes 294944 | tf_op jit(solution)/shard_map/ppermute | solution.py:472
  30.9 2.4 %collective-permute-start.9 = (bf16[576,512]{1,0:T(8,128)(2,1)S(1)}, bf16[576,512]{1,0:T(8,128)(2,1)S(1)}, u32[]{:S(2)}, u32[]{:S(2)}) collective-permute-start(bf16[576,512]{1,0:T(8,128)(2,1)S(1)} %get-tuple-element.44.refs_3_.refs_5_), channel_id=1, source_target_pairs={{1,0},{2,1},{3,2},{5,4},{6,5},{7,6},{9,8},{10,9},{11,10},{13,12},{... | collective-permute-start | bytes 1769480 | tf_op jit(solution)/shard_map/ppermute | solution.py:457
  33.3 3.5 %collective-permute-start.8 = (bf16[576,512]{1,0:T(8,128)(2,1)S(1)}, bf16[576,512]{1,0:T(8,128)(2,1)S(1)}, u32[]{:S(2)}, u32[]{:S(2)}) collective-permute-start(bf16[576,512]{1,0:T(8,128)(2,1)S(1)} %get-tuple-element.44.refs_3_.refs_5_), channel_id=1, source_target_pairs={{0,1},{1,2},{2,3},{4,5},{5,6},{6,7},{8,9},{9,10},{10,11},{12,13},{... | collective-permute-start | bytes 1769480 | tf_op jit(solution)/shard_map/ppermute | solution.py:457
  36.8 2.3 %collective-permute-start.11 = (bf16[576,512]{1,0:T(8,128)(2,1)S(1)}, bf16[576,512]{1,0:T(8,128)(2,1)S(1)}, u32[]{:S(2)}, u32[]{:S(2)}) collective-permute-start(bf16[576,512]{1,0:T(8,128)(2,1)S(1)} %get-tuple-element.45.refs_3_.refs_12_), channel_id=1, source_target_pairs={{1,0},{2,1},{3,2},{5,4},{6,5},{7,6},{9,8},{10,9},{11,10},{13,12},{... | collective-permute-start | bytes 1769480 | tf_op jit(solution)/shard_map/ppermute | solution.py:457
  39.1 3.5 %collective-permute-start.10 = (bf16[576,512]{1,0:T(8,128)(2,1)S(1)}, bf16[576,512]{1,0:T(8,128)(2,1)S(1)}, u32[]{:S(2)}, u32[]{:S(2)}) collective-permute-start(bf16[576,512]{1,0:T(8,128)(2,1)S(1)} %get-tuple-element.45.refs_3_.refs_12_), channel_id=1, source_target_pairs={{0,1},{1,2},{2,3},{4,5},{5,6},{6,7},{8,9},{9,10},{10,11},{12,13},{... | collective-permute-start | bytes 1769480 | tf_op jit(solution)/shard_map/ppermute | solution.py:457
  43.0 6.1 %collective-permute-done.9.refs_10_.refs_4_.refs_6_ = bf16[576,512]{1,0:T(8,128)(2,1)S(1)} collective-permute-done((bf16[576,512]{1,0:T(8,128)(2,1)S(1)}, bf16[576,512]{1,0:T(8,128)(2,1)S(1)}, u32[]{:S(2)}, u32[]{:S(2)}) %collective-permute-start.9) | collective-permute-done | bytes 589856 | tf_op jit(solution)/shard_map/ppermute | solution.py:457
  49.1 2.4 %collective-permute-done.8.refs_9_.refs_2_.refs_4_ = bf16[576,512]{1,0:T(8,128)(2,1)S(1)} collective-permute-done((bf16[576,512]{1,0:T(8,128)(2,1)S(1)}, bf16[576,512]{1,0:T(8,128)(2,1)S(1)}, u32[]{:S(2)}, u32[]{:S(2)}) %collective-permute-start.8) | collective-permute-done | bytes 589856 | tf_op jit(solution)/shard_map/ppermute | solution.py:457
  51.4 8.4 %collective-permute-done.11.refs_12_.refs_4_.refs_13_ = bf16[576,512]{1,0:T(8,128)(2,1)S(1)} collective-permute-done((bf16[576,512]{1,0:T(8,128)(2,1)S(1)}, bf16[576,512]{1,0:T(8,128)(2,1)S(1)}, u32[]{:S(2)}, u32[]{:S(2)}) %collective-permute-start.11) | collective-permute-done | bytes 589856 | tf_op jit(solution)/shard_map/ppermute | solution.py:457
  59.9 2.1 collective-permute-done.10.refs_11_.refs_2_
  63.4 2.1 collective-permute-start.12
  65.5 2.4 %collective-permute-start.24 = (bf16[576,512]{1,0:T(8,128)(2,1)S(1)}, bf16[576,512]{1,0:T(8,128)(2,1)S(1)}, u32[]{:S(2)}, u32[]{:S(2)}) collective-permute-start(bf16[576,512]{1,0:T(8,128)(2,1)S(1)} %collective-permute-done.9.refs_10_.refs_4_.refs_6_), channel_id=1, source_target_pairs={{1,0},{2,1},{5,4},{6,5},{9,8},{10,9},{13,12},{14,13},{17,16},{18,1... | collective-permute-start | bytes 1769480 | tf_op jit(solution)/shard_map/ppermute | solution.py:457
  67.9 5.0 %grad_kept_first.2 = (bf16[2304,1024]{1,0:T(8,128)(2,1)S(1)}, f32[2304,512]{1,0:T(8,128)S(1)}, f32[32,128]{1,0:T(8,128)S(1)}, bf16[592,512]{1,0:T(8,128)(2,1)S(1)}, bf16[592,512]{1,0:T(8,128)(2,1)S(1)}) custom-call(bf16[288,1024]{1,0:T(8,128)(2,1)S(1)} %get-tuple-element.41.refs_0_, bf16[288,1024]{1,0:T(8,128)(2,1)S(1)} %collective-permute-done.refs_1_, ...), custom_call_target="tpu_custom_call" | custom-call | flops 2415919104 | bytes 5767168 | tf_op jit(solution)/shard_map/grad_kept_first/pallas_call | solution.py:21
  74.2 4.9 %collective-permute-done.14.refs_3_ = bf16[288,1024]{1,0:T(8,128)(2,1)S(1)} collective-permute-done((bf16[288,1024]{1,0:T(8,128)(2,1)S(1)}, bf16[288,1024]{1,0:T(8,128)(2,1)S(1)}, u32[]{:S(2)}, u32[]{:S(2)}) %collective-permute-start.14) | collective-permute-done | bytes 589856 | tf_op jit(solution)/shard_map/ppermute | solution.py:451
  79.1 3.5 %collective-permute-start.23 = (bf16[576,512]{1,0:T(8,128)(2,1)S(1)}, bf16[576,512]{1,0:T(8,128)(2,1)S(1)}, u32[]{:S(2)}, u32[]{:S(2)}) collective-permute-start(bf16[576,512]{1,0:T(8,128)(2,1)S(1)} %collective-permute-done.8.refs_9_.refs_2_.refs_4_), channel_id=1, source_target_pairs={{1,2},{2,3},{5,6},{6,7},{9,10},{10,11},{13,14},{14,15},{17,18},{18... | collective-permute-start | bytes 1769480 | tf_op jit(solution)/shard_map/ppermute | solution.py:457
  82.6 6.5 %collective-permute-done.13.refs_2_ = bf16[288,1024]{1,0:T(8,128)(2,1)S(1)} collective-permute-done((bf16[288,1024]{1,0:T(8,128)(2,1)S(1)}, bf16[288,1024]{1,0:T(8,128)(2,1)S(1)}, u32[]{:S(2)}, u32[]{:S(2)}) %collective-permute-start.13) | collective-permute-done | bytes 589856 | tf_op jit(solution)/shard_map/ppermute | solution.py:451
  89.9 3.0 %collective-permute-start.20 = (bf16[576,512]{1,0:T(8,128)(2,1)S(1)}, bf16[576,512]{1,0:T(8,128)(2,1)S(1)}, u32[]{:S(2)}, u32[]{:S(2)}) collective-permute-start(bf16[576,512]{1,0:T(8,128)(2,1)S(1)} %collective-permute-done.11.refs_12_.refs_4_.refs_13_), channel_id=1, source_target_pairs={{1,0},{2,1},{5,4},{6,5},{9,8},{10,9},{13,12},{14,13},{17,16},{18,1... | collective-permute-start | bytes 1769480 | tf_op jit(solution)/shard_map/ppermute | solution.py:457
  92.9 1.9 collective-permute-start.19
  95.5 2.7 %grad_kept_pass_on.4 = (bf16[592,512]{1,0:T(8,128)(2,1)S(1)}, bf16[592,512]{1,0:T(8,128)(2,1)S(1)}) custom-call(f32[2304,512]{1,0:T(8,128)S(1)} %get-tuple-element.48.sums_ref, f32[32,128]{1,0:T(8,128)S(1)} %get-tuple-element.49.bounds_ref, bf16[592,512]{1,0:T(8,128)(2,1)S(1)} %collective-permute-done.21.came_r, ...), custom_call_target="tpu_custom_call" | custom-call | flops 6062080 | bytes 5947392 | tf_op jit(solution)/shard_map/grad_kept_pass_on/pallas_call | solution.py:21
  98.1 7.4 %collective-permute-done.20.refs_1_ = bf16[576,512]{1,0:T(8,128)(2,1)S(1)} collective-permute-done((bf16[576,512]{1,0:T(8,128)(2,1)S(1)}, bf16[576,512]{1,0:T(8,128)(2,1)S(1)}, u32[]{:S(2)}, u32[]{:S(2)}) %collective-permute-start.20) | collective-permute-done | bytes 589856 | tf_op jit(solution)/shard_map/ppermute | solution.py:457
  105.6 6.1 %collective-permute-start.33 = (bf16[592,512]{1,0:T(8,128)(2,1)S(1)}, bf16[592,512]{1,0:T(8,128)(2,1)S(1)}, u32[]{:S(2)}, u32[]{:S(2)}) collective-permute-start(bf16[592,512]{1,0:T(8,128)(2,1)S(1)} %get-tuple-element.62), channel_id=1, source_target_pairs={{3,2},{2,1},{7,6},{6,5},{11,10},{10,9},{15,14},{14,13},{19,18},{18... | collective-permute-start | bytes 1818632 | tf_op jit(solution)/shard_map/ppermute | solution.py:457
  115.4 5.0 %grad_kept_first.3 = (bf16[2304,1024]{1,0:T(8,128)(2,1)S(1)}, f32[2304,512]{1,0:T(8,128)S(1)}, f32[32,128]{1,0:T(8,128)S(1)}, bf16[592,512]{1,0:T(8,128)(2,1)S(1)}, bf16[592,512]{1,0:T(8,128)(2,1)S(1)}) custom-call(bf16[288,1024]{1,0:T(8,128)(2,1)S(1)} %after.3.refs_0_, bf16[288,1024]{1,0:T(8,128)(2,1)S(1)} %collective-permute-done.12.refs_1_, ...), custom_call_target="tpu_custom_call" | custom-call | flops 2415919104 | bytes 5767168 | tf_op jit(solution)/shard_map/grad_kept_first/pallas_call | solution.py:21
  120.4 4.9 %collective-permute-done.33.came_l = bf16[592,512]{1,0:T(8,128)(2,1)S(1)} collective-permute-done((bf16[592,512]{1,0:T(8,128)(2,1)S(1)}, bf16[592,512]{1,0:T(8,128)(2,1)S(1)}, u32[]{:S(2)}, u32[]{:S(2)}) %collective-permute-start.33) | collective-permute-done | bytes 606240 | tf_op jit(solution)/shard_map/ppermute | solution.py:457
  125.3 4.1 %collective-permute-done.32.came_r = bf16[592,512]{1,0:T(8,128)(2,1)S(1)} collective-permute-done((bf16[592,512]{1,0:T(8,128)(2,1)S(1)}, bf16[592,512]{1,0:T(8,128)(2,1)S(1)}, u32[]{:S(2)}, u32[]{:S(2)}) %collective-permute-start.32) | collective-permute-done | bytes 606240 | tf_op jit(solution)/shard_map/ppermute | solution.py:457
  129.4 2.7 %grad_kept_pass_on.5 = (bf16[592,512]{1,0:T(8,128)(2,1)S(1)}, bf16[592,512]{1,0:T(8,128)(2,1)S(1)}) custom-call(f32[2304,512]{1,0:T(8,128)S(1)} %get-tuple-element.48.sums_ref, f32[32,128]{1,0:T(8,128)S(1)} %get-tuple-element.49.bounds_ref, bf16[592,512]{1,0:T(8,128)(2,1)S(1)} %collective-permute-done.32.came_r, ...), custom_call_target="tpu_custom_call" | custom-call | flops 6062080 | bytes 5947392 | tf_op jit(solution)/shard_map/grad_kept_pass_on/pallas_call | solution.py:21
  135.1 4.6 %collective-permute-start.27 = (bf16[576,512]{1,0:T(8,128)(2,1)S(1)}, bf16[576,512]{1,0:T(8,128)(2,1)S(1)}, u32[]{:S(2)}, u32[]{:S(2)}) collective-permute-start(bf16[576,512]{1,0:T(8,128)(2,1)S(1)} %get-tuple-element.54.refs_9_.refs_1_.refs_10_), channel_id=1, source_target_pairs={{2,3},{6,7},{10,11},{14,15},{18,19},{22,23},{26,27},{30,31}} | collective-permute-start | bytes 1769480 | tf_op jit(solution)/shard_map/ppermute | solution.py:457
  139.7 5.3 %grad_weight_partial.2 = (f32[288,1024]{1,0:T(8,128)S(1)}, bf16[304,1024]{1,0:T(8,128)(2,1)}, bf16[304,1024]{1,0:T(8,128)(2,1)}, bf16[304,1024]{1,0:T(8,128)(2,1)}) custom-call(bf16[1024,512]{1,0:T(8,128)(2,1)S(1)} %bitcast.9, bf16[1024,512]{1,0:T(8,128)(2,1)S(1)} %collective-permute-done.31.cot_other_ref, ...), custom_call_target="tpu_custom_call" | custom-call | flops 2415919104 | bytes 7405568 | tf_op jit(solution)/shard_map/grad_weight_partial/pallas_call | solution.py:21
  145.0 5.3 %collective-permute-done.30.came_l = bf16[592,512]{1,0:T(8,128)(2,1)S(1)} collective-permute-done((bf16[592,512]{1,0:T(8,128)(2,1)S(1)}, bf16[592,512]{1,0:T(8,128)(2,1)S(1)}, u32[]{:S(2)}, u32[]{:S(2)}) %collective-permute-start.30) | collective-permute-done | bytes 606240 | tf_op jit(solution)/shard_map/ppermute | solution.py:457
  150.3 2.7 %grad_kept_pass_on.6 = (bf16[592,512]{1,0:T(8,128)(2,1)S(1)}, bf16[592,512]{1,0:T(8,128)(2,1)S(1)}) custom-call(f32[2304,512]{1,0:T(8,128)S(1)} %get-tuple-element.58.sums_ref, f32[32,128]{1,0:T(8,128)S(1)} %get-tuple-element.59.bounds_ref, bf16[592,512]{1,0:T(8,128)(2,1)S(1)} %collective-permute-done.29.came_r, ...), custom_call_target="tpu_custom_call" | custom-call | flops 6062080 | bytes 5947392 | tf_op jit(solution)/shard_map/grad_kept_pass_on/pallas_call | solution.py:21
  153.2 2.4 %collective-permute-start.41 = (bf16[592,512]{1,0:T(8,128)(2,1)S(1)}, bf16[592,512]{1,0:T(8,128)(2,1)S(1)}, u32[]{:S(2)}, u32[]{:S(2)}) collective-permute-start(bf16[592,512]{1,0:T(8,128)(2,1)S(1)} %get-tuple-element.70), channel_id=1, source_target_pairs={{3,2},{2,1},{1,0},{7,6},{6,5},{5,4},{11,10},{10,9},{9,8},{15,14},{... | collective-permute-start | bytes 1818632 | tf_op jit(solution)/shard_map/ppermute | solution.py:457
  155.6 3.6 %collective-permute-start.40 = (bf16[592,512]{1,0:T(8,128)(2,1)S(1)}, bf16[592,512]{1,0:T(8,128)(2,1)S(1)}, u32[]{:S(2)}, u32[]{:S(2)}) collective-permute-start(bf16[592,512]{1,0:T(8,128)(2,1)S(1)} %get-tuple-element.63.refs_7_), channel_id=1, source_target_pairs={{0,1},{1,2},{2,3},{4,5},{5,6},{6,7},{8,9},{9,10},{10,11},{12,13},{... | collective-permute-start | bytes 1818632 | tf_op jit(solution)/shard_map/ppermute | solution.py:457
  159.3 2.0 collective-permute-start.46
  161.3 9.9 %collective-permute-done.41.l_ref = bf16[592,512]{1,0:T(8,128)(2,1)S(1)} collective-permute-done((bf16[592,512]{1,0:T(8,128)(2,1)S(1)}, bf16[592,512]{1,0:T(8,128)(2,1)S(1)}, u32[]{:S(2)}, u32[]{:S(2)}) %collective-permute-start.41) | collective-permute-done | bytes 606240 | tf_op jit(solution)/shard_map/ppermute | solution.py:457
  173.2 2.5 %collective-permute-start.36 = (bf16[592,512]{1,0:T(8,128)(2,1)S(1)}, bf16[592,512]{1,0:T(8,128)(2,1)S(1)}, u32[]{:S(2)}, u32[]{:S(2)}) collective-permute-start(bf16[592,512]{1,0:T(8,128)(2,1)S(1)} %get-tuple-element.66), channel_id=1, source_target_pairs={{3,2},{2,1},{7,6},{6,5},{11,10},{10,9},{15,14},{14,13},{19,18},{18... | collective-permute-start | bytes 1818632 | tf_op jit(solution)/shard_map/ppermute | solution.py:457
  179.3 4.9 %grad_weight_partial.3 = (f32[288,1024]{1,0:T(8,128)S(1)}, bf16[304,1024]{1,0:T(8,128)(2,1)}, bf16[304,1024]{1,0:T(8,128)(2,1)}, bf16[304,1024]{1,0:T(8,128)(2,1)S(1)}) custom-call(bf16[1024,512]{1,0:T(8,128)(2,1)S(1)} %bitcast.10, bf16[1024,512]{1,0:T(8,128)(2,1)S(1)} %copy-done.8, bf16[1152,512]{1,0:T(8,128)(2,1)S(1)} %copy-done.5, ...), custom_call_target="tpu_custom_call" | custom-call | flops 2415919104 | bytes 7405568 | tf_op jit(solution)/shard_map/grad_weight_partial/pallas_call | solution.py:21
  184.2 5.7 %collective-permute-done.36.came_l = bf16[592,512]{1,0:T(8,128)(2,1)S(1)} collective-permute-done((bf16[592,512]{1,0:T(8,128)(2,1)S(1)}, bf16[592,512]{1,0:T(8,128)(2,1)S(1)}, u32[]{:S(2)}, u32[]{:S(2)}) %collective-permute-start.36) | collective-permute-done | bytes 606240 | tf_op jit(solution)/shard_map/ppermute | solution.py:457
  189.9 3.2 %collective-permute-done.35.came_r = bf16[592,512]{1,0:T(8,128)(2,1)S(1)} collective-permute-done((bf16[592,512]{1,0:T(8,128)(2,1)S(1)}, bf16[592,512]{1,0:T(8,128)(2,1)S(1)}, u32[]{:S(2)}, u32[]{:S(2)}) %collective-permute-start.35) | collective-permute-done | bytes 606240 | tf_op jit(solution)/shard_map/ppermute | solution.py:457
  194.6 2.7 %grad_kept_pass_on.7 = (bf16[592,512]{1,0:T(8,128)(2,1)S(1)}, bf16[592,512]{1,0:T(8,128)(2,1)S(1)}) custom-call(f32[2304,512]{1,0:T(8,128)S(1)} %get-tuple-element.58.sums_ref, f32[32,128]{1,0:T(8,128)S(1)} %get-tuple-element.59.bounds_ref, bf16[592,512]{1,0:T(8,128)(2,1)S(1)} %collective-permute-done.35.came_r, ...), custom_call_target="tpu_custom_call" | custom-call | flops 6062080 | bytes 5947392 | tf_op jit(solution)/shard_map/grad_kept_pass_on/pallas_call | solution.py:21
  197.2 1.9 collective-permute-start.39
  199.2 4.0 %collective-permute-start.38 = (bf16[592,512]{1,0:T(8,128)(2,1)S(1)}, bf16[592,512]{1,0:T(8,128)(2,1)S(1)}, u32[]{:S(2)}, u32[]{:S(2)}) collective-permute-start(bf16[592,512]{1,0:T(8,128)(2,1)S(1)} %get-tuple-element.68.refs_16_), channel_id=1, source_target_pairs={{0,1},{1,2},{2,3},{4,5},{5,6},{6,7},{8,9},{9,10},{10,11},{12,13},{... | collective-permute-start | bytes 1818632 | tf_op jit(solution)/shard_map/ppermute | solution.py:457
  203.1 6.4 %queries.1.dep_ref.refs_4_ = bf16[1024,512]{1,0:T(8,128)(2,1)} custom-call(bf16[2304,1024]{1,0:T(8,128)(2,1)S(1)} %get-tuple-element.46.refs_0_, bf16[2304,1024]{1,0:T(8,128)(2,1)S(1)} %get-tuple-element.55.refs_1_, bf16[576,512]{1,0:T(8,128)(2,1)S(1)} %collective-permute-done.25.refs_0_.refs_2_, ...), custom_call_target="tpu_custom_call" | custom-call | flops 4831838208 | bytes 17694720 | tf_op jit(solution)/shard_map/queries/pallas_call | solution.py:21
  210.8 2.3 %grad_kept_last.2.base_ref = f32[4,288,512]{2,1,0:T(8,128)} custom-call(f32[2304,512]{1,0:T(8,128)S(1)} %get-tuple-element.48.sums_ref, bf16[592,512]{1,0:T(8,128)(2,1)S(1)} %collective-permute-done.40.r_ref, bf16[592,512]{1,0:T(8,128)(2,1)S(1)} %collective-permute-done.41.l_ref, bf16[1152,128]{1,0:T(8,128)(2,1)S(1)} %get-tuple-element.40.dep_ref.base_ref.refs_3_, ...), custom_call_target="tpu_custom_call" | custom-call | flops 5898240 | bytes 5931008 | tf_op jit(solution)/shard_map/grad_kept_last/pallas_call | solution.py:21
  213.1 2.8 %grad_weight_last.2.refs_3_ = f32[576,1024]{1,0:T(8,128)} custom-call(f32[288,1024]{1,0:T(8,128)S(1)} %get-tuple-element.64.dep_ref.own_ref, bf16[304,1024]{1,0:T(8,128)(2,1)S(1)} %collective-permute-done.45.refs_0_, bf16[304,1024]{1,0:T(8,128)(2,1)S(1)} %collective-permute-done.46.refs_1_, bf16[304,1024]{1,0:T(8,128)(2,1)S(1)} %collective-permute-done.47.refs_2_, ...), custom_call_target="tpu_custom_call" | custom-call | flops 17694720 | bytes 3047424 | tf_op jit(solution)/shard_map/grad_weight_last/pallas_call | solution.py:21
  216.0 2.3 %grad_kept_last.3 = f32[4,288,512]{2,1,0:T(8,128)} custom-call(f32[2304,512]{1,0:T(8,128)S(1)} %get-tuple-element.58.sums_ref, bf16[592,512]{1,0:T(8,128)(2,1)S(1)} %collective-permute-done.38.r_ref, bf16[592,512]{1,0:T(8,128)(2,1)S(1)} %collective-permute-done.39.l_ref, f32[4,288,512]{2,1,0:T(8,128)} %grad_kept_last.2.base_ref, ...), custom_call_target="tpu_custom_call", output_to_operand_aliasing={{}: (3, {})} | custom-call | flops 5898240 | bytes 5931008 | tf_op jit(solution)/shard_map/grad_kept_last/pallas_call | solution.py:21
  218.3 2.3 %collective-permute-done.43.refs_1_ = bf16[304,1024]{1,0:T(8,128)(2,1)S(1)} collective-permute-done((bf16[304,1024]{1,0:T(8,128)(2,1)}, bf16[304,1024]{1,0:T(8,128)(2,1)S(1)}, u32[]{:S(2)}, u32[]{:S(2)}) %collective-permute-start.43) | collective-permute-done | bytes 622624 | tf_op jit(solution)/shard_map/ppermute | solution.py:451
  220.6 2.8 %grad_weight_last.3 = f32[576,1024]{1,0:T(8,128)} custom-call(f32[288,1024]{1,0:T(8,128)S(1)} %get-tuple-element.67.dep_ref.own_ref, bf16[304,1024]{1,0:T(8,128)(2,1)S(1)} %collective-permute-done.42.refs_0_, bf16[304,1024]{1,0:T(8,128)(2,1)S(1)} %collective-permute-done.43.refs_1_, ...), custom_call_target="tpu_custom_call", output_to_operand_aliasing={{}: (4, {})} | custom-call | flops 17694720 | bytes 3047424 | tf_op jit(solution)/shard_map/grad_weight_last/pallas_call | solution.py:21
  (89 shorter events, 22.7 us)
Async XLA Ops:
  7.2 26.1 %collective-permute-start.3 = (bf16[288,1024]{1,0:T(8,128)(2,1)S(1)}, bf16[288,1024]{1,0:T(8,128)(2,1)S(1)}, u32[]{:S(2)}, u32[]{:S(2)}) collective-permute-start(bf16[288,1024]{1,0:T(8,128)(2,1)S(1)} %get-tuple-element.41.refs_0_), channel_id=1, source_target_pairs={{0,16},{16,0},{1,17},{17,1},{2,18},{18,2},{3,19},{19,3},{4,20},{20... | collective-permute-start | bytes 1769480 | tf_op jit(solution)/shard_map/ppermute | solution.py:454
  7.3 29.5 %collective-permute-start.2 = (bf16[288,1024]{1,0:T(8,128)(2,1)S(1)}, bf16[288,1024]{1,0:T(8,128)(2,1)S(1)}, u32[]{:S(2)}, u32[]{:S(2)}) collective-permute-start(bf16[288,1024]{1,0:T(8,128)(2,1)S(1)} %get-tuple-element.41.refs_0_), channel_id=1, source_target_pairs={{0,12},{4,8},{8,4},{12,0},{1,13},{5,9},{9,5},{13,1},{2,14},{6,10},... | collective-permute-start | bytes 1769480 | tf_op jit(solution)/shard_map/ppermute | solution.py:451
  8.8 30.3 %collective-permute-start.1 = (bf16[288,1024]{1,0:T(8,128)(2,1)S(1)}, bf16[288,1024]{1,0:T(8,128)(2,1)S(1)}, u32[]{:S(2)}, u32[]{:S(2)}) collective-permute-start(bf16[288,1024]{1,0:T(8,128)(2,1)S(1)} %get-tuple-element.41.refs_0_), channel_id=1, source_target_pairs={{0,8},{4,12},{8,0},{12,4},{1,9},{5,13},{9,1},{13,5},{2,10},{6,14},... | collective-permute-start | bytes 1769480 | tf_op jit(solution)/shard_map/ppermute | solution.py:451
  9.3 21.5 %collective-permute-start.7 = (bf16[1152,128]{1,0:T(8,128)(2,1)S(1)}, bf16[1152,128]{1,0:T(8,128)(2,1)S(1)}, u32[]{:S(2)}, u32[]{:S(2)}) collective-permute-start(bf16[1152,128]{1,0:T(8,128)(2,1)S(1)} %get-tuple-element.40.dep_ref.base_ref.refs_3_), channel_id=1, source_target_pairs={{0,4},{4,8},{8,12},{1,5},{5,9},{9,13},{2,6},{6,10},{10,14},{3,7},{... | collective-permute-start | bytes 884744 | tf_op jit(solution)/shard_map/ppermute | solution.py:472
  13.7 29.3 %collective-permute-start = (bf16[288,1024]{1,0:T(8,128)(2,1)S(1)}, bf16[288,1024]{1,0:T(8,128)(2,1)S(1)}, u32[]{:S(2)}, u32[]{:S(2)}) collective-permute-start(bf16[288,1024]{1,0:T(8,128)(2,1)S(1)} %get-tuple-element.41.refs_0_), channel_id=1, source_target_pairs={{0,4},{4,0},{8,12},{12,8},{1,5},{5,1},{9,13},{13,9},{2,6},{6,2},{1... | collective-permute-start | bytes 1769480 | tf_op jit(solution)/shard_map/ppermute | solution.py:451
  30.9 18.2 %collective-permute-start.9 = (bf16[576,512]{1,0:T(8,128)(2,1)S(1)}, bf16[576,512]{1,0:T(8,128)(2,1)S(1)}, u32[]{:S(2)}, u32[]{:S(2)}) collective-permute-start(bf16[576,512]{1,0:T(8,128)(2,1)S(1)} %get-tuple-element.44.refs_3_.refs_5_), channel_id=1, source_target_pairs={{1,0},{2,1},{3,2},{5,4},{6,5},{7,6},{9,8},{10,9},{11,10},{13,12},{... | collective-permute-start | bytes 1769480 | tf_op jit(solution)/shard_map/ppermute | solution.py:457
  33.3 18.2 %collective-permute-start.8 = (bf16[576,512]{1,0:T(8,128)(2,1)S(1)}, bf16[576,512]{1,0:T(8,128)(2,1)S(1)}, u32[]{:S(2)}, u32[]{:S(2)}) collective-permute-start(bf16[576,512]{1,0:T(8,128)(2,1)S(1)} %get-tuple-element.44.refs_3_.refs_5_), channel_id=1, source_target_pairs={{0,1},{1,2},{2,3},{4,5},{5,6},{6,7},{8,9},{9,10},{10,11},{12,13},{... | collective-permute-start | bytes 1769480 | tf_op jit(solution)/shard_map/ppermute | solution.py:457
  36.8 23.1 %collective-permute-start.11 = (bf16[576,512]{1,0:T(8,128)(2,1)S(1)}, bf16[576,512]{1,0:T(8,128)(2,1)S(1)}, u32[]{:S(2)}, u32[]{:S(2)}) collective-permute-start(bf16[576,512]{1,0:T(8,128)(2,1)S(1)} %get-tuple-element.45.refs_3_.refs_12_), channel_id=1, source_target_pairs={{1,0},{2,1},{3,2},{5,4},{6,5},{7,6},{9,8},{10,9},{11,10},{13,12},{... | collective-permute-start | bytes 1769480 | tf_op jit(solution)/shard_map/ppermute | solution.py:457
  39.1 22.8 %collective-permute-start.10 = (bf16[576,512]{1,0:T(8,128)(2,1)S(1)}, bf16[576,512]{1,0:T(8,128)(2,1)S(1)}, u32[]{:S(2)}, u32[]{:S(2)}) collective-permute-start(bf16[576,512]{1,0:T(8,128)(2,1)S(1)} %get-tuple-element.45.refs_3_.refs_12_), channel_id=1, source_target_pairs={{0,1},{1,2},{2,3},{4,5},{5,6},{6,7},{8,9},{9,10},{10,11},{12,13},{... | collective-permute-start | bytes 1769480 | tf_op jit(solution)/shard_map/ppermute | solution.py:457
  43.0 20.4 %collective-permute-start.6 = (bf16[288,1024]{1,0:T(8,128)(2,1)S(1)}, bf16[288,1024]{1,0:T(8,128)(2,1)S(1)}, u32[]{:S(2)}, u32[]{:S(2)}) collective-permute-start(bf16[288,1024]{1,0:T(8,128)(2,1)S(1)} %collective-permute-done.2.refs_3_), channel_id=1, source_target_pairs={{0,16},{16,0},{1,17},{17,1},{2,18},{18,2},{3,19},{19,3},{4,20},{20... | collective-permute-start | bytes 1769480 | tf_op jit(solution)/shard_map/ppermute | solution.py:454
  49.0 14.4 %collective-permute-start.5 = (bf16[288,1024]{1,0:T(8,128)(2,1)S(1)}, bf16[288,1024]{1,0:T(8,128)(2,1)S(1)}, u32[]{:S(2)}, u32[]{:S(2)}) collective-permute-start(bf16[288,1024]{1,0:T(8,128)(2,1)S(1)} %collective-permute-done.1.refs_2_), channel_id=1, source_target_pairs={{0,16},{16,0},{1,17},{17,1},{2,18},{18,2},{3,19},{19,3},{4,20},{20... | collective-permute-start | bytes 1769480 | tf_op jit(solution)/shard_map/ppermute | solution.py:454
  51.4 14.0 %collective-permute-start.4 = (bf16[288,1024]{1,0:T(8,128)(2,1)S(1)}, bf16[288,1024]{1,0:T(8,128)(2,1)S(1)}, u32[]{:S(2)}, u32[]{:S(2)}) collective-permute-start(bf16[288,1024]{1,0:T(8,128)(2,1)S(1)} %collective-permute-done.refs_1_), channel_id=1, source_target_pairs={{0,16},{16,0},{1,17},{17,1},{2,18},{18,2},{3,19},{19,3},{4,20},{20... | collective-permute-start | bytes 1769480 | tf_op jit(solution)/shard_map/ppermute | solution.py:454
  59.9 13.0 %collective-permute-start.15 = (bf16[288,1024]{1,0:T(8,128)(2,1)S(1)}, bf16[288,1024]{1,0:T(8,128)(2,1)S(1)}, u32[]{:S(2)}, u32[]{:S(2)}) collective-permute-start(bf16[288,1024]{1,0:T(8,128)(2,1)S(1)} %after.3.refs_0_), channel_id=1, source_target_pairs={{0,16},{16,0},{1,17},{17,1},{2,18},{18,2},{3,19},{19,3},{4,20},{20... | collective-permute-start | bytes 1769480 | tf_op jit(solution)/shard_map/ppermute | solution.py:454
  62.0 17.2 %collective-permute-start.14 = (bf16[288,1024]{1,0:T(8,128)(2,1)S(1)}, bf16[288,1024]{1,0:T(8,128)(2,1)S(1)}, u32[]{:S(2)}, u32[]{:S(2)}) collective-permute-start(bf16[288,1024]{1,0:T(8,128)(2,1)S(1)} %after.3.refs_0_), channel_id=1, source_target_pairs={{0,12},{4,8},{8,4},{12,0},{1,13},{5,9},{9,5},{13,1},{2,14},{6,10},... | collective-permute-start | bytes 1769480 | tf_op jit(solution)/shard_map/ppermute | solution.py:451
  63.4 25.8 %collective-permute-start.13 = (bf16[288,1024]{1,0:T(8,128)(2,1)S(1)}, bf16[288,1024]{1,0:T(8,128)(2,1)S(1)}, u32[]{:S(2)}, u32[]{:S(2)}) collective-permute-start(bf16[288,1024]{1,0:T(8,128)(2,1)S(1)} %after.3.refs_0_), channel_id=1, source_target_pairs={{0,8},{4,12},{8,0},{12,4},{1,9},{5,13},{9,1},{13,5},{2,10},{6,14},... | collective-permute-start | bytes 1769480 | tf_op jit(solution)/shard_map/ppermute | solution.py:451
  63.4 26.4 %collective-permute-start.12 = (bf16[288,1024]{1,0:T(8,128)(2,1)S(1)}, bf16[288,1024]{1,0:T(8,128)(2,1)S(1)}, u32[]{:S(2)}, u32[]{:S(2)}) collective-permute-start(bf16[288,1024]{1,0:T(8,128)(2,1)S(1)} %after.3.refs_0_), channel_id=1, source_target_pairs={{0,4},{4,0},{8,12},{12,8},{1,5},{5,1},{9,13},{13,9},{2,6},{6,2},{1... | collective-permute-start | bytes 1769480 | tf_op jit(solution)/shard_map/ppermute | solution.py:451
  65.5 27.4 %collective-permute-start.24 = (bf16[576,512]{1,0:T(8,128)(2,1)S(1)}, bf16[576,512]{1,0:T(8,128)(2,1)S(1)}, u32[]{:S(2)}, u32[]{:S(2)}) collective-permute-start(bf16[576,512]{1,0:T(8,128)(2,1)S(1)} %collective-permute-done.9.refs_10_.refs_4_.refs_6_), channel_id=1, source_target_pairs={{1,0},{2,1},{5,4},{6,5},{9,8},{10,9},{13,12},{14,13},{17,16},{18,1... | collective-permute-start | bytes 1769480 | tf_op jit(solution)/shard_map/ppermute | solution.py:457
  72.9 22.0 %collective-permute-start.22 = (bf16[592,512]{1,0:T(8,128)(2,1)S(1)}, bf16[592,512]{1,0:T(8,128)(2,1)S(1)}, u32[]{:S(2)}, u32[]{:S(2)}) collective-permute-start(bf16[592,512]{1,0:T(8,128)(2,1)S(1)} %get-tuple-element.51), channel_id=1, source_target_pairs={{3,2},{7,6},{11,10},{15,14},{19,18},{23,22},{27,26},{31,30}} | collective-permute-start | bytes 1818632 | tf_op jit(solution)/shard_map/ppermute | solution.py:457
  79.1 15.7 %collective-permute-start.23 = (bf16[576,512]{1,0:T(8,128)(2,1)S(1)}, bf16[576,512]{1,0:T(8,128)(2,1)S(1)}, u32[]{:S(2)}, u32[]{:S(2)}) collective-permute-start(bf16[576,512]{1,0:T(8,128)(2,1)S(1)} %collective-permute-done.8.refs_9_.refs_2_.refs_4_), channel_id=1, source_target_pairs={{1,2},{2,3},{5,6},{6,7},{9,10},{10,11},{13,14},{14,15},{17,18},{18... | collective-permute-start | bytes 1769480 | tf_op jit(solution)/shard_map/ppermute | solution.py:457
  89.2 6.2 %collective-permute-start.21 = (bf16[592,512]{1,0:T(8,128)(2,1)S(1)}, bf16[592,512]{1,0:T(8,128)(2,1)S(1)}, u32[]{:S(2)}, u32[]{:S(2)}) collective-permute-start(bf16[592,512]{1,0:T(8,128)(2,1)S(1)} %get-tuple-element.50.refs_2_), channel_id=1, source_target_pairs={{0,1},{4,5},{8,9},{12,13},{16,17},{20,21},{24,25},{28,29}} | collective-permute-start | bytes 1818632 | tf_op jit(solution)/shard_map/ppermute | solution.py:457
  89.9 15.7 %collective-permute-start.20 = (bf16[576,512]{1,0:T(8,128)(2,1)S(1)}, bf16[576,512]{1,0:T(8,128)(2,1)S(1)}, u32[]{:S(2)}, u32[]{:S(2)}) collective-permute-start(bf16[576,512]{1,0:T(8,128)(2,1)S(1)} %collective-permute-done.11.refs_12_.refs_4_.refs_13_), channel_id=1, source_target_pairs={{1,0},{2,1},{5,4},{6,5},{9,8},{10,9},{13,12},{14,13},{17,16},{18,1... | collective-permute-start | bytes 1769480 | tf_op jit(solution)/shard_map/ppermute | solution.py:457
  92.9 18.8 %collective-permute-start.19 = (bf16[576,512]{1,0:T(8,128)(2,1)S(1)}, bf16[576,512]{1,0:T(8,128)(2,1)S(1)}, u32[]{:S(2)}, u32[]{:S(2)}) collective-permute-start(bf16[576,512]{1,0:T(8,128)(2,1)S(1)} %collective-permute-done.10.refs_11_.refs_2_), channel_id=1, source_target_pairs={{1,2},{2,3},{5,6},{6,7},{9,10},{10,11},{13,14},{14,15},{17,18},{18... | collective-permute-start | bytes 1769480 | tf_op jit(solution)/shard_map/ppermute | solution.py:457
  94.8 18.2 %collective-permute-start.18 = (bf16[288,1024]{1,0:T(8,128)(2,1)S(1)}, bf16[288,1024]{1,0:T(8,128)(2,1)S(1)}, u32[]{:S(2)}, u32[]{:S(2)}) collective-permute-start(bf16[288,1024]{1,0:T(8,128)(2,1)S(1)} %collective-permute-done.14.refs_3_), channel_id=1, source_target_pairs={{0,16},{16,0},{1,17},{17,1},{2,18},{18,2},{3,19},{19,3},{4,20},{20... | collective-permute-start | bytes 1769480 | tf_op jit(solution)/shard_map/ppermute | solution.py:454
  94.9 18.8 %collective-permute-start.17 = (bf16[288,1024]{1,0:T(8,128)(2,1)S(1)}, bf16[288,1024]{1,0:T(8,128)(2,1)S(1)}, u32[]{:S(2)}, u32[]{:S(2)}) collective-permute-start(bf16[288,1024]{1,0:T(8,128)(2,1)S(1)} %collective-permute-done.13.refs_2_), channel_id=1, source_target_pairs={{0,16},{16,0},{1,17},{17,1},{2,18},{18,2},{3,19},{19,3},{4,20},{20... | collective-permute-start | bytes 1769480 | tf_op jit(solution)/shard_map/ppermute | solution.py:454
  95.4 19.7 %collective-permute-start.16 = (bf16[288,1024]{1,0:T(8,128)(2,1)S(1)}, bf16[288,1024]{1,0:T(8,128)(2,1)S(1)}, u32[]{:S(2)}, u32[]{:S(2)}) collective-permute-start(bf16[288,1024]{1,0:T(8,128)(2,1)S(1)} %collective-permute-done.12.refs_1_), channel_id=1, source_target_pairs={{0,16},{16,0},{1,17},{17,1},{2,18},{18,2},{3,19},{19,3},{4,20},{20... | collective-permute-start | bytes 1769480 | tf_op jit(solution)/shard_map/ppermute | solution.py:454
  105.6 19.7 %collective-permute-start.33 = (bf16[592,512]{1,0:T(8,128)(2,1)S(1)}, bf16[592,512]{1,0:T(8,128)(2,1)S(1)}, u32[]{:S(2)}, u32[]{:S(2)}) collective-permute-start(bf16[592,512]{1,0:T(8,128)(2,1)S(1)} %get-tuple-element.62), channel_id=1, source_target_pairs={{3,2},{2,1},{7,6},{6,5},{11,10},{10,9},{15,14},{14,13},{19,18},{18... | collective-permute-start | bytes 1818632 | tf_op jit(solution)/shard_map/ppermute | solution.py:457
  111.7 17.7 %collective-permute-start.32 = (bf16[592,512]{1,0:T(8,128)(2,1)S(1)}, bf16[592,512]{1,0:T(8,128)(2,1)S(1)}, u32[]{:S(2)}, u32[]{:S(2)}) collective-permute-start(bf16[592,512]{1,0:T(8,128)(2,1)S(1)} %get-tuple-element.53.refs_2_), channel_id=1, source_target_pairs={{0,1},{1,2},{4,5},{5,6},{8,9},{9,10},{12,13},{13,14},{16,17},{17,1... | collective-permute-start | bytes 1818632 | tf_op jit(solution)/shard_map/ppermute | solution.py:457
  113.0 19.1 %collective-permute-start.26 = (bf16[576,512]{1,0:T(8,128)(2,1)S(1)}, bf16[576,512]{1,0:T(8,128)(2,1)S(1)}, u32[]{:S(2)}, u32[]{:S(2)}) collective-permute-start(bf16[576,512]{1,0:T(8,128)(2,1)S(1)} %get-tuple-element.56.refs_5_.refs_7_), channel_id=1, source_target_pairs={{1,0},{5,4},{9,8},{13,12},{17,16},{21,20},{25,24},{29,28}} | collective-permute-start | bytes 1769480 | tf_op jit(solution)/shard_map/ppermute | solution.py:457
  113.7 18.4 %collective-permute-start.25 = (bf16[576,512]{1,0:T(8,128)(2,1)S(1)}, bf16[576,512]{1,0:T(8,128)(2,1)S(1)}, u32[]{:S(2)}, u32[]{:S(2)}) collective-permute-start(bf16[576,512]{1,0:T(8,128)(2,1)S(1)} %get-tuple-element.52.dep_ref.refs_1_.refs_3_), channel_id=1, source_target_pairs={{2,3},{6,7},{10,11},{14,15},{18,19},{22,23},{26,27},{30,31}} | collective-permute-start | bytes 1769480 | tf_op jit(solution)/shard_map/ppermute | solution.py:457
  115.1 20.0 %collective-permute-start.31 = (bf16[1024,512]{1,0:T(8,128)(2,1)S(1)}, bf16[1024,512]{1,0:T(8,128)(2,1)S(1)}, u32[]{:S(2)}, u32[]{:S(2)}) collective-permute-start(bf16[1024,512]{1,0:T(8,128)(2,1)S(1)} %bitcast.7), channel_id=1, source_target_pairs={{0,16},{16,0},{1,17},{17,1},{2,18},{18,2},{3,19},{19,3},{4,20},{20... | collective-permute-start | bytes 3145736 | tf_op jit(solution)/shard_map/ppermute | solution.py:454
  132.2 7.4 %collective-permute-start.34 = (bf16[1152,512]{1,0:T(8,128)(2,1)S(1)}, bf16[1152,512]{1,0:T(8,128)(2,1)S(1)}, u32[]{:S(2)}, u32[]{:S(2)}) collective-permute-start(bf16[1152,512]{1,0:T(8,128)(2,1)S(1)} %half_for_other_core.2.refs_7_), channel_id=1, source_target_pairs={{0,16},{16,0},{1,17},{17,1},{2,18},{18,2},{3,19},{19,3},{4,20},{20... | collective-permute-start | bytes 3538952 | tf_op jit(solution)/shard_map/ppermute | solution.py:454
  132.3 18.0 %collective-permute-start.30 = (bf16[592,512]{1,0:T(8,128)(2,1)S(1)}, bf16[592,512]{1,0:T(8,128)(2,1)S(1)}, u32[]{:S(2)}, u32[]{:S(2)}) collective-permute-start(bf16[592,512]{1,0:T(8,128)(2,1)S(1)} %get-tuple-element.61), channel_id=1, source_target_pairs={{3,2},{7,6},{11,10},{15,14},{19,18},{23,22},{27,26},{31,30}} | collective-permute-start | bytes 1818632 | tf_op jit(solution)/shard_map/ppermute | solution.py:457
  133.6 16.7 %collective-permute-start.29 = (bf16[592,512]{1,0:T(8,128)(2,1)S(1)}, bf16[592,512]{1,0:T(8,128)(2,1)S(1)}, u32[]{:S(2)}, u32[]{:S(2)}) collective-permute-start(bf16[592,512]{1,0:T(8,128)(2,1)S(1)} %get-tuple-element.60.dep_ref), channel_id=1, source_target_pairs={{0,1},{4,5},{8,9},{12,13},{16,17},{20,21},{24,25},{28,29}} | collective-permute-start | bytes 1818632 | tf_op jit(solution)/shard_map/ppermute | solution.py:457
  134.3 18.6 %collective-permute-start.28 = (bf16[576,512]{1,0:T(8,128)(2,1)S(1)}, bf16[576,512]{1,0:T(8,128)(2,1)S(1)}, u32[]{:S(2)}, u32[]{:S(2)}) collective-permute-start(bf16[576,512]{1,0:T(8,128)(2,1)S(1)} %get-tuple-element.57.refs_5_.refs_14_), channel_id=1, source_target_pairs={{1,0},{5,4},{9,8},{13,12},{17,16},{21,20},{25,24},{29,28}} | collective-permute-start | bytes 1769480 | tf_op jit(solution)/shard_map/ppermute | solution.py:457
  135.1 17.9 %collective-permute-start.27 = (bf16[576,512]{1,0:T(8,128)(2,1)S(1)}, bf16[576,512]{1,0:T(8,128)(2,1)S(1)}, u32[]{:S(2)}, u32[]{:S(2)}) collective-permute-start(bf16[576,512]{1,0:T(8,128)(2,1)S(1)} %get-tuple-element.54.refs_9_.refs_1_.refs_10_), channel_id=1, source_target_pairs={{2,3},{6,7},{10,11},{14,15},{18,19},{22,23},{26,27},{30,31}} | collective-permute-start | bytes 1769480 | tf_op jit(solution)/shard_map/ppermute | solution.py:457
  153.1 22.5 %collective-permute-start.37 = (bf16[1152,512]{1,0:T(8,128)(2,1)S(1)}, bf16[1152,512]{1,0:T(8,128)(2,1)S(1)}, u32[]{:S(2)}, u32[]{:S(2)}) collective-permute-start(bf16[1152,512]{1,0:T(8,128)(2,1)S(1)} %half_for_other_core.3.refs_7_), channel_id=1, source_target_pairs={{0,16},{16,0},{1,17},{17,1},{2,18},{18,2},{3,19},{19,3},{4,20},{20... | collective-permute-start | bytes 3538952 | tf_op jit(solution)/shard_map/ppermute | solution.py:454
  153.2 18.0 %collective-permute-start.41 = (bf16[592,512]{1,0:T(8,128)(2,1)S(1)}, bf16[592,512]{1,0:T(8,128)(2,1)S(1)}, u32[]{:S(2)}, u32[]{:S(2)}) collective-permute-start(bf16[592,512]{1,0:T(8,128)(2,1)S(1)} %get-tuple-element.70), channel_id=1, source_target_pairs={{3,2},{2,1},{1,0},{7,6},{6,5},{5,4},{11,10},{10,9},{9,8},{15,14},{... | collective-permute-start | bytes 1818632 | tf_op jit(solution)/shard_map/ppermute | solution.py:457
  155.6 17.6 %collective-permute-start.40 = (bf16[592,512]{1,0:T(8,128)(2,1)S(1)}, bf16[592,512]{1,0:T(8,128)(2,1)S(1)}, u32[]{:S(2)}, u32[]{:S(2)}) collective-permute-start(bf16[592,512]{1,0:T(8,128)(2,1)S(1)} %get-tuple-element.63.refs_7_), channel_id=1, source_target_pairs={{0,1},{1,2},{2,3},{4,5},{5,6},{6,7},{8,9},{9,10},{10,11},{12,13},{... | collective-permute-start | bytes 1818632 | tf_op jit(solution)/shard_map/ppermute | solution.py:457
  159.2 34.4 %collective-permute-start.45 = (bf16[304,1024]{1,0:T(8,128)(2,1)}, bf16[304,1024]{1,0:T(8,128)(2,1)S(1)}, u32[]{:S(2)}, u32[]{:S(2)}) collective-permute-start(bf16[304,1024]{1,0:T(8,128)(2,1)} %get-tuple-element.74), channel_id=1, source_target_pairs={{0,4},{4,0},{8,12},{12,8},{1,5},{5,1},{9,13},{13,9},{2,6},{6,2},{1... | collective-permute-start | bytes 1867784 | tf_op jit(solution)/shard_map/ppermute | solution.py:451
  159.3 37.9 %collective-permute-start.46 = (bf16[304,1024]{1,0:T(8,128)(2,1)}, bf16[304,1024]{1,0:T(8,128)(2,1)S(1)}, u32[]{:S(2)}, u32[]{:S(2)}) collective-permute-start(bf16[304,1024]{1,0:T(8,128)(2,1)} %get-tuple-element.75), channel_id=1, source_target_pairs={{0,8},{4,12},{8,0},{12,4},{1,9},{5,13},{9,1},{13,5},{2,10},{6,14},... | collective-permute-start | bytes 1867784 | tf_op jit(solution)/shard_map/ppermute | solution.py:451
  171.2 28.0 %collective-permute-start.47 = (bf16[304,1024]{1,0:T(8,128)(2,1)}, bf16[304,1024]{1,0:T(8,128)(2,1)S(1)}, u32[]{:S(2)}, u32[]{:S(2)}) collective-permute-start(bf16[304,1024]{1,0:T(8,128)(2,1)} %get-tuple-element.76), channel_id=1, source_target_pairs={{0,12},{4,8},{8,4},{12,0},{1,13},{5,9},{9,5},{13,1},{2,14},{6,10},... | collective-permute-start | bytes 1867784 | tf_op jit(solution)/shard_map/ppermute | solution.py:451
  173.2 16.7 %collective-permute-start.36 = (bf16[592,512]{1,0:T(8,128)(2,1)S(1)}, bf16[592,512]{1,0:T(8,128)(2,1)S(1)}, u32[]{:S(2)}, u32[]{:S(2)}) collective-permute-start(bf16[592,512]{1,0:T(8,128)(2,1)S(1)} %get-tuple-element.66), channel_id=1, source_target_pairs={{3,2},{2,1},{7,6},{6,5},{11,10},{10,9},{15,14},{14,13},{19,18},{18... | collective-permute-start | bytes 1818632 | tf_op jit(solution)/shard_map/ppermute | solution.py:457
  176.7 16.4 %collective-permute-start.35 = (bf16[592,512]{1,0:T(8,128)(2,1)S(1)}, bf16[592,512]{1,0:T(8,128)(2,1)S(1)}, u32[]{:S(2)}, u32[]{:S(2)}) collective-permute-start(bf16[592,512]{1,0:T(8,128)(2,1)S(1)} %get-tuple-element.65.refs_7_), channel_id=1, source_target_pairs={{0,1},{1,2},{4,5},{5,6},{8,9},{9,10},{12,13},{13,14},{16,17},{17,1... | collective-permute-start | bytes 1818632 | tf_op jit(solution)/shard_map/ppermute | solution.py:457
  189.9 28.4 %collective-permute-start.42 = (bf16[304,1024]{1,0:T(8,128)(2,1)}, bf16[304,1024]{1,0:T(8,128)(2,1)S(1)}, u32[]{:S(2)}, u32[]{:S(2)}) collective-permute-start(bf16[304,1024]{1,0:T(8,128)(2,1)} %get-tuple-element.71), channel_id=1, source_target_pairs={{0,4},{4,0},{8,12},{12,8},{1,5},{5,1},{9,13},{13,9},{2,6},{6,2},{1... | collective-permute-start | bytes 1867784 | tf_op jit(solution)/shard_map/ppermute | solution.py:451
  193.1 27.5 %collective-permute-start.43 = (bf16[304,1024]{1,0:T(8,128)(2,1)}, bf16[304,1024]{1,0:T(8,128)(2,1)S(1)}, u32[]{:S(2)}, u32[]{:S(2)}) collective-permute-start(bf16[304,1024]{1,0:T(8,128)(2,1)} %get-tuple-element.72), channel_id=1, source_target_pairs={{0,8},{4,12},{8,0},{12,4},{1,9},{5,13},{9,1},{13,5},{2,10},{6,14},... | collective-permute-start | bytes 1867784 | tf_op jit(solution)/shard_map/ppermute | solution.py:451
  193.6 27.0 %collective-permute-start.44 = (bf16[304,1024]{1,0:T(8,128)(2,1)S(1)}, bf16[304,1024]{1,0:T(8,128)(2,1)S(1)}, u32[]{:S(2)}, u32[]{:S(2)}) collective-permute-start(bf16[304,1024]{1,0:T(8,128)(2,1)S(1)} %get-tuple-element.73), channel_id=1, source_target_pairs={{0,12},{4,8},{8,4},{12,0},{1,13},{5,9},{9,5},{13,1},{2,14},{6,10},... | collective-permute-start | bytes 1867784 | tf_op jit(solution)/shard_map/ppermute | solution.py:451
  197.2 18.7 %collective-permute-start.39 = (bf16[592,512]{1,0:T(8,128)(2,1)S(1)}, bf16[592,512]{1,0:T(8,128)(2,1)S(1)}, u32[]{:S(2)}, u32[]{:S(2)}) collective-permute-start(bf16[592,512]{1,0:T(8,128)(2,1)S(1)} %get-tuple-element.69), channel_id=1, source_target_pairs={{3,2},{2,1},{1,0},{7,6},{6,5},{5,4},{11,10},{10,9},{9,8},{15,14},{... | collective-permute-start | bytes 1818632 | tf_op jit(solution)/shard_map/ppermute | solution.py:457
  199.2 16.8 %collective-permute-start.38 = (bf16[592,512]{1,0:T(8,128)(2,1)S(1)}, bf16[592,512]{1,0:T(8,128)(2,1)S(1)}, u32[]{:S(2)}, u32[]{:S(2)}) collective-permute-start(bf16[592,512]{1,0:T(8,128)(2,1)S(1)} %get-tuple-element.68.refs_16_), channel_id=1, source_target_pairs={{0,1},{1,2},{2,3},{4,5},{5,6},{6,7},{8,9},{9,10},{10,11},{12,13},{... | collective-permute-start | bytes 1818632 | tf_op jit(solution)/shard_map/ppermute | solution.py:457
  (10 other events, 107.8 us)

commit v5 on v4

v5 whole, which is shorter than its diff:
```python
import functools

import jax
import jax.numpy as jnp
from jax import lax
from jax.experimental import pallas as pl
from jax.experimental.pallas import tpu as pltpu
from jax.sharding import PartitionSpec as P

HEADER = 16
OFFSET = 128.0
F32 = jnp.float32
BF16 = jnp.bfloat16
ANY = pl.BlockSpec(memory_space=pl.ANY)
VMEM = pl.BlockSpec(memory_space=pltpu.VMEM)
SMEM = pl.BlockSpec(memory_space=pltpu.SMEM)


def call(kernel, name, out_shape, in_specs, args, out_specs=None, scratch=(), aliases=None, flops=0, mib=14):
    moved = sum(a.size * a.dtype.itemsize for a, s in zip(args, in_specs) if s is VMEM)
    return pl.pallas_call(
        kernel,
        out_shape=out_shape,
        in_specs=in_specs,
        out_specs=out_specs if out_specs is not None else [VMEM] * len(out_shape),
        scratch_shapes=scratch,
        input_output_aliases=aliases or {},
        compiler_params=pltpu.CompilerParams(vmem_limit_bytes=mib * 2**20),
        cost_estimate=pl.CostEstimate(flops=1, bytes_accessed=1, transcendentals=0),
        name=name,
    )(*args)


def shape(dims, dtype):
    return jax.ShapeDtypeStruct(dims, dtype)


def dot(a, b, ca, cb):
    return lax.dot_general(a, b, (((ca,), (cb,)), ((), ())), preferred_element_type=F32)


def span(start, size):
    return pl.ds(pl.multiple_of(start, 16), size)


def chunks(rows):
    size = 32 if rows % 32 == 0 else 16
    return size, rows // size


def exponent(bound):
    return jnp.clip(jnp.floor(14.99 - jnp.log2(jnp.maximum(bound, 1e-30))), -100.0, 100.0)


def power(values, scale):
    v = values * scale
    square = v * v
    fourth = square * square
    return (fourth * square * (v * jnp.abs(v))).astype(BF16)


def root(code, scale):
    y = code.astype(F32)
    quarter = lax.rsqrt(lax.rsqrt(jnp.maximum(jnp.abs(y), 1e-37)))
    size = quarter * lax.rsqrt(quarter) * scale
    return jnp.where(y > 0.0, size, jnp.where(y < 0.0, -size, 0.0))


def tile_max(values):
    most = jnp.max(jnp.abs(values), axis=0, keepdims=True)
    return jnp.broadcast_to(jnp.max(most, axis=1, keepdims=True), (8, 128))


def write_header(out_ref, expo):
    rows = out_ref.shape[0] - HEADER
    code = jnp.broadcast_to((expo + OFFSET)[0:1, 0:1], (HEADER, out_ref.shape[1]))
    out_ref[rows:, :] = code.astype(BF16)


def write_payload(out_ref, value_of, bound):
    expo = exponent(bound)
    scale = jnp.exp2(expo)[0:1, 0:1]
    size, count = chunks(out_ref.shape[0] - HEADER)

    @pl.loop(0, count)
    def _(i):
        out_ref[span(i * size, size), :] = power(value_of(i * size, size), scale)

    write_header(out_ref, expo)


def read_header(came_ref):
    rows = came_ref.shape[0] - HEADER
    code = came_ref[rows:, :][0:8, 0:128].astype(F32)
    came = code > 0.0
    expo = jnp.where(came, code - OFFSET, 0.0)
    return jnp.exp2(-expo)[0:1, 0:1], jnp.where(came, jnp.exp2(15.0 - expo), 0.0)


def part_rows(sizes, blocks):
    start = 0
    for size in sizes:
        yield start, size, start * blocks, size * blocks
        start += size


def onehot_of(index_ref, first, count, seq_dev):
    index = index_ref[:, pl.ds(pl.multiple_of(first, 128), count)] - lax.axis_index("row") * seq_dev
    positions = lax.broadcasted_iota(jnp.int32, (seq_dev, count), 0)
    return (positions == index).astype(F32).astype(BF16)


def pick_leaving_kernel(blocks, sizes, n_row, keep_dev, index_ref, x_ref, leaving_ref, rows_ref, onehot_ref, sem):
    d_dev, seq_dev = rows_ref.shape
    step = d_dev // blocks

    def copy(b):
        rows = pl.ds(b * step, step)
        return pltpu.make_async_copy(x_ref.at[rows, :], rows_ref.at[rows, :], sem.at[b])

    for b in range(blocks):
        copy(b).start()
    after = jnp.minimum(lax.axis_index("row") + 1, n_row - 1) * keep_dev
    onehot_ref[...] = onehot_of(index_ref, after, leaving_ref.shape[1], seq_dev)
    for b in range(blocks):
        copy(b).wait()
        for start, size, offset, _ in part_rows(sizes, blocks):
            picked = dot(rows_ref[pl.ds(b * step + start, size), :], onehot_ref[...], 1, 0)
            leaving_ref[pl.ds(offset + b * size, size), :] = picked.astype(BF16)


def pick_own_kernel(blocks, sizes, index_ref, rows_ref, kept_ref, onehot_ref):
    d_dev, seq_dev = rows_ref.shape
    keep_dev = kept_ref.shape[1]
    onehot_ref[...] = onehot_of(index_ref, lax.axis_index("row") * keep_dev, keep_dev, seq_dev)
    for b in range(blocks):
        for start, size, offset, _ in part_rows(sizes, blocks):
            picked = dot(rows_ref[pl.ds(b * (d_dev // blocks) + start, size), :], onehot_ref[...], 1, 0)
            kept_ref[pl.ds(offset + b * size, size), :] = picked.astype(BF16)


def add_arrived_kernel(arrived_ref, in_ref, out_ref):
    drift = arrived_ref.shape[1]
    out_ref[:, :drift] = in_ref[:, :drift] + arrived_ref[...]


def split_kernel(sizes, w_ref, dep_ref, *refs):
    out_refs, sem = refs[:-1], refs[-1]
    copies = [
        pltpu.make_async_copy(w_ref.at[pl.ds(start, size), :], out_refs[p], sem.at[p])
        for p, (start, size, _, _) in enumerate(part_rows(sizes, 1))
    ]
    for copy in copies:
        copy.start()
    for copy in copies:
        copy.wait()


def nothing_kernel(*refs):
    pass


def after(values, deps):
    return call(
        nothing_kernel,
        "after",
        [shape(v.shape, v.dtype) for v in values],
        [ANY] * (len(values) + len(deps)),
        (*values, *deps),
        out_specs=[ANY] * len(values),
        aliases={i: i for i in range(len(values))},
        mib=1,
    )


def collect_kernel(n_row, *refs):
    pieces, out_ref = refs[:n_row], refs[-1]
    row = lax.axis_index("row")
    size = pieces[0].shape[0]
    for step, piece in enumerate(pieces):
        out_ref[span((row ^ step) * size, size), :] = piece[...]


def collect(pieces):
    size, heads = pieces[0].shape
    n_row = len(pieces)
    return call(
        functools.partial(collect_kernel, n_row),
        "collect_rows",
        shape((n_row * size, heads), BF16),
        [VMEM] * n_row,
        pieces,
        out_specs=VMEM,
    )


def partial_into(out_ref, block, n_half, mine_ref, other_ref, cot_ref):
    shard = out_ref.shape[0]
    rows = span((block % n_half) * shard, shard)
    here = block // n_half == lax.axis_index("dp")

    @pl.when(here)
    def _():
        out_ref[...] = dot(mine_ref[rows, :], cot_ref[...], 1, 0)

    @pl.when(jnp.logical_not(here))
    def _():
        out_ref[...] = dot(other_ref[rows, :], cot_ref[...], 1, 0)


def step_kernel(n_col, n_half, t, offset, mine_ref, other_ref, cot_ref, came_r, came_l, dep_ref, out_r, out_l, term_ref):
    shard = out_r.shape[0] - HEADER
    col = lax.axis_index("col")
    ways = ((col, n_col - t + col, came_r, out_r), (n_col - 1 - col, t - n_col + col, came_l, out_l))
    for place, block, came, out in ways:

        @pl.when(place >= t)
        def _():
            out[:shard, :] = came[pl.ds(offset, shard), :]

        @pl.when(place < t)
        def _():
            partial_into(term_ref, block, n_half, mine_ref, other_ref, cot_ref)
            bound = tile_max(term_ref[...])
            if t == 1:
                write_payload(out, lambda first, size: term_ref[span(first, size), :], bound)
            else:
                undo, came_bound = read_header(came)

                def total(first, size):
                    rows = span(first, size)
                    return term_ref[rows, :] + root(came[rows, :], undo)

                write_payload(out, total, bound + came_bound)


def line_step(n_col, n_half, t, offset, shard, mine, other, cot, came_r, came_l, dep):
    keep = cot.shape[1]
    payload = shape((shard + HEADER, keep), BF16)
    return call(
        functools.partial(step_kernel, n_col, n_half, t, offset),
        "line_step",
        [payload, payload],
        [VMEM] * 5 + [ANY],
        (mine, other, cot, came_r, came_l, dep),
        scratch=[pltpu.VMEM((shard, keep), F32)],
    )


def last_kernel(start, size, blocks, n_half, mine_ref, other_ref, cot_ref, r_ref, l_ref, base_ref, dep_ref, out_ref, total_ref, sem):
    step = out_ref.shape[0] // blocks
    partial_into(total_ref, lax.axis_index("col"), n_half, mine_ref, other_ref, cot_ref)
    undo_r, _ = read_header(r_ref)
    undo_l, _ = read_header(l_ref)
    few, count = chunks(size)
    copies = []
    for b in range(blocks):

        @pl.loop(0, count)
        def _(i):
            rows = span(b * size + i * few, few)
            came = root(r_ref[rows, :], undo_r) + root(l_ref[rows, :], undo_l)
            total_ref[rows, :] = total_ref[rows, :] + came

        target = out_ref.at[pl.ds(b * step + start, size), :]
        copies.append(pltpu.make_async_copy(total_ref.at[pl.ds(b * size, size), :], target, sem.at[b]))
        copies[-1].start()
    for copy in copies:
        copy.wait()


def last_sums(mine, other, cot, came_r, came_l, base, dep, start, size, blocks, n_half, d_dev):
    shard, keep = came_r.shape[0] - HEADER, came_r.shape[1]
    return call(
        functools.partial(last_kernel, start, size, blocks, n_half),
        "grad_kept_last",
        shape((d_dev, keep), F32),
        [VMEM] * 5 + [ANY] * 2,
        (mine, other, cot, came_r, came_l, base, dep),
        out_specs=ANY,
        scratch=[pltpu.VMEM((shard, keep), F32), pltpu.SemaphoreType.DMA((blocks,))],
        aliases={5: 0} if start else None,
    )


def each_shard(line, offset, rows):
    n_col = (len(line) + 1) // 2
    col = lax.axis_index("col")
    for n, ref in enumerate(line):
        shard = col + n - (n_col - 1)
        whole = abs(n - (n_col - 1)) < 2
        yield (shard >= 0) & (shard < n_col), shard, ref.at[pl.ds(offset if whole else 0, rows), :]


def half_kernel(n_half, offset, rows, *refs):
    line, out_ref = refs[:-2], refs[-1]
    other = 1 - lax.axis_index("dp")
    for came, shard, ref in each_shard(line, offset, rows):

        @pl.when(came & (shard >= other * n_half) & (shard < (other + 1) * n_half))
        def _():
            out_ref[span((shard - other * n_half) * rows, rows), :] = ref[...]


def other_half(line, n_half, offset, rows, dep):
    keep = line[0].shape[1]
    return call(
        functools.partial(half_kernel, n_half, offset, rows),
        "half_for_other_core",
        shape((n_half * rows, keep), BF16),
        [VMEM] * len(line) + [ANY],
        (*line, dep),
        out_specs=VMEM,
    )


def weight_kernel(n_half, n_row, offset, cot_ref, cot_other_ref, other_ref, *refs):
    count = len(refs) - n_row - 3
    line, own_ref, send_refs = refs[:count], refs[count + 1], refs[count + 2 : count + 1 + n_row]
    mine_ref, total_ref = refs[-2:]
    dp, row = lax.axis_index("dp"), lax.axis_index("row")
    rows = mine_ref.shape[0] // n_half
    for came, shard, ref in each_shard(line, offset, rows):

        @pl.when(came & (shard >= dp * n_half) & (shard < (dp + 1) * n_half))
        def _():
            mine_ref[span((shard - dp * n_half) * rows, rows), :] = ref[...]

    sub = own_ref.shape[0]
    bound = jnp.zeros((8, 128), F32)
    for step in range(n_row):
        rows = span((row ^ step) * sub, sub)
        value = dot(mine_ref[rows, :], cot_ref[...], 1, 1) + dot(other_ref[rows, :], cot_other_ref[...], 1, 1)
        if step == 0:
            own_ref[...] = value
        else:
            total_ref[step - 1] = value
            bound = jnp.maximum(bound, tile_max(value))
    for step in range(1, n_row):
        write_payload(
            send_refs[step - 1],
            lambda first, size, step=step: total_ref[step - 1, span(first, size), :],
            bound,
        )


def weight_partial(cot, cot_other, other, line, n_half, n_row, offset, dep):
    half, keep = other.shape
    heads = cot.shape[0]
    sub = half // n_row
    return call(
        functools.partial(weight_kernel, n_half, n_row, offset),
        "grad_weight_partial",
        [shape((sub, heads), F32)] + [shape((sub + HEADER, heads), BF16)] * (n_row - 1),
        [VMEM] * (3 + len(line)) + [ANY],
        (cot, cot_other, other, *line, dep),
        scratch=[pltpu.VMEM((half, keep), BF16), pltpu.VMEM((n_row - 1, sub, heads), F32)],
        flops=4 * half * keep * heads,
        mib=20,
    )


def weight_last_kernel(n_came, start, own_ref, *refs):
    came_refs, (out_ref, total_ref, sem) = refs[:n_came], refs[-3:]
    sub = own_ref.shape[0]
    undo = [read_header(came)[0] for came in came_refs]
    size = 16
    steps = sub // size
    copies = []
    for first, last in ((0, steps // 2), (steps // 2, steps)):

        @pl.loop(first, last)
        def _(i):
            rows = span(i * size, size)
            total = own_ref[rows, :]
            for came, scale in zip(came_refs, undo):
                total = total + root(came[rows, :], scale)
            total_ref[rows, :] = total

        rows = pl.ds(first * size, (last - first) * size)
        target = out_ref.at[pl.ds(start + first * size, (last - first) * size), :]
        copies.append(pltpu.make_async_copy(total_ref.at[rows, :], target, sem.at[len(copies)]))
        copies[-1].start()
    for copy in copies:
        copy.wait()


def weight_last(own, came, base, dep, start, w_rows):
    sub, heads = own.shape
    return call(
        functools.partial(weight_last_kernel, len(came), start),
        "grad_weight_last",
        shape((w_rows, heads), F32),
        [VMEM] * (1 + len(came)) + [ANY] * 2,
        (own, *came, base, dep),
        out_specs=ANY,
        scratch=[pltpu.VMEM((sub, heads), F32), pltpu.SemaphoreType.DMA((2,))],
        aliases={1 + len(came): 0} if start else None,
        flops=20 * sub * heads * len(came),
    )


def query_kernel(sizes, blocks, n_half, *refs):
    parts = len(sizes)
    w_refs = refs[: 2 * parts]
    out_ref, tile_ref, sem, *panels = refs[-3 - parts :]
    pieces = refs[2 * parts : -4 - parts]
    middle, outer = pieces[:3], pieces[3:]
    per_part = len(outer) // parts
    dp = lax.axis_index("dp")
    for p, (_, _, offset, rows) in enumerate(part_rows(sizes, blocks)):
        mine = outer[p * per_part : (p + 1) * per_part]
        line = mine[: per_part // 2] + middle + mine[per_part // 2 :]
        for came, shard, ref in each_shard(line, offset, rows):

            @pl.when(came)
            def _():
                place = (shard // n_half ^ dp) * n_half + shard % n_half
                panels[p][span(place * rows, rows), :] = ref[...]

    tile = tile_ref.shape[1]
    copies = []
    for i in range(out_ref.shape[0] // tile):
        heads = pl.ds(i * tile, tile)
        total = jnp.zeros(tile_ref.shape[1:], F32)
        for p in range(parts):
            for n in range(2):
                w_ref = w_refs[2 * p + n]
                half = w_ref.shape[0]
                total = total + dot(w_ref[:, heads], panels[p][pl.ds(n * half, half), :], 0, 0)
        tile_ref[i] = total.astype(BF16)
        copies.append(pltpu.make_async_copy(tile_ref.at[i], out_ref.at[heads, :], sem.at[i]))
        copies[-1].start()
    for copy in copies:
        copy.wait()


def all_queries(w_halves, lines, sizes, blocks, n_half, dep):
    heads = w_halves[0].shape[1]
    keep = lines[0][0].shape[1]
    middle = len(lines[0]) // 2
    pieces = lines[0][middle - 1 : middle + 2]
    for line in lines:
        pieces = pieces + line[: middle - 1] + line[middle + 2 :]
    tile = 256
    return call(
        functools.partial(query_kernel, sizes, blocks, n_half),
        "queries",
        shape((heads, keep), BF16),
        [VMEM] * (len(w_halves) + len(pieces)) + [ANY],
        (*w_halves, *pieces, dep),
        out_specs=ANY,
        scratch=[pltpu.VMEM((heads // tile, tile, keep), BF16), pltpu.SemaphoreType.DMA((heads // tile,))]
        + [pltpu.VMEM((2 * w.shape[0], keep), BF16) for w in w_halves[::2]],
        mib=20,
    )


def per_device(tokens, kept_index, w_query, cotangent):
    n_dp, n_row, n_col = (lax.axis_size(a) for a in ("dp", "row", "col"))
    seq_x = tokens[0]
    cot = cotangent[0]
    d_dev, seq_dev = seq_x.shape
    w_rows, heads = w_query.shape
    keep_dev = cot.shape[1]
    drift = keep_dev // 4
    sizes = part_sizes(w_rows)
    parts = len(sizes)
    blocks = d_dev // w_rows
    n_half = n_col // n_dp
    layout = list(part_rows(sizes, blocks))

    def to_row(value, step):
        return lax.ppermute(value, "row", [(r, r ^ step) for r in range(n_row)])

    def to_core(value):
        return lax.ppermute(value, "dp", [(i, i ^ 1) for i in range(n_dp)])

    def along(value, sources, step):
        return lax.ppermute(value, "col", [(c, c + step) for c in sources])

    leaving, rows = call(
        functools.partial(pick_leaving_kernel, blocks, sizes, n_row, keep_dev),
        "pick_leaving",
        [shape((d_dev, drift), BF16), shape((d_dev, seq_dev), BF16)],
        [VMEM, ANY],
        (kept_index, seq_x),
        scratch=[pltpu.VMEM((seq_dev, drift), BF16), pltpu.SemaphoreType.DMA((blocks,))],
        mib=40,
    )
    arrived = lax.ppermute(leaving, "row", [(r, r + 1) for r in range(n_row - 1)])
    picked = call(
        functools.partial(pick_own_kernel, blocks, sizes),
        "pick_own",
        shape((d_dev, keep_dev), BF16),
        [VMEM] * 2,
        (kept_index, rows),
        out_specs=VMEM,
        scratch=[pltpu.VMEM((seq_dev, keep_dev), BF16)],
    )
    kept = call(
        add_arrived_kernel,
        "add_arrived",
        shape((d_dev, keep_dev), BF16),
        [VMEM] * 2,
        (arrived, picked),
        out_specs=VMEM,
        aliases={1: 0},
    )

    own_w = list(
        call(
            functools.partial(split_kernel, sizes),
            "split_rows",
            [shape((size, heads), BF16) for size in sizes],
            [ANY, ANY],
            (w_query, leaving),
            scratch=[pltpu.SemaphoreType.DMA((parts,))],
        )
    )
    mine, other = [], []
    for p in range(parts):
        if p > 0:
            (own_w[p],) = after([own_w[p]], mine[-1:])
        pieces = [own_w[p]] + [to_row(own_w[p], step) for step in range(1, n_row)]
        mine.append(collect(pieces))
        other.append(to_core(mine[p]))

    owns, cames = [None] * parts, [None] * parts
    right = [[along(kept, range(n_col - 1), 1)] for _ in range(parts)]
    left = [[along(kept, range(1, n_col), -1)] for _ in range(parts)]
    for p in range(1, parts):
        right[p][0], left[p][0] = right[0][0], left[0][0]
    token = kept

    def line_of(p):
        return right[p][n_col - 2 :: -1] + [kept] + left[p][: n_col - 1]

    def step(p, t):
        nonlocal token
        offset = layout[p][2] if t == 1 else 0
        out_r, out_l = line_step(
            n_col, n_half, t, offset, layout[p][3], mine[p], other[p], cot, right[p][-1], left[p][-1], token
        )
        token = out_r
        right[p].append(along(out_r, range(n_col - 1), 1))
        left[p].append(along(out_l, range(1, n_col), -1))

    def give(p):
        nonlocal token
        token = other_half(line_of(p), n_half, layout[p][2], layout[p][3], token)
        return to_core(token)

    def weigh(p, theirs):
        nonlocal token
        owns[p], *sends = weight_partial(
            cot, cot_other, theirs, line_of(p), n_half, n_row, layout[p][2], token
        )
        token = owns[p]
        cames[p] = [to_row(send, step) for step, send in enumerate(sends, 1)]

    grad_kept, grad_weight = leaving, leaving

    def finish_kept(p):
        nonlocal grad_kept, token
        start, size = layout[p][:2]
        grad_kept = last_sums(
            mine[p], other[p], cot, right[p][-1], left[p][-1], grad_kept, token, start, size, blocks, n_half, d_dev
        )
        token = grad_kept

    def finish_weight(p):
        nonlocal grad_weight, token
        grad_weight = weight_last(owns[p], cames[p], grad_weight, token, layout[p][0], w_rows)
        token = grad_weight

    step(0, 1)
    (cot_for_core,) = after([cot], [token])
    cot_other = to_core(cot_for_core)
    if parts == 1:
        for t in range(2, n_col):
            step(0, t)
        weigh(0, give(0))
    else:
        for t in range(2, n_col):
            step(1, t - 1)
            step(0, t)
            if t == n_col - 1:
                theirs = give(0)
        weigh(0, theirs)
        theirs = give(1)
        step(1, n_col - 1)
        weigh(1, theirs)
    queries = all_queries(
        [h for p in range(parts) for h in (mine[p], other[p])],
        [line_of(p) for p in range(parts)],
        sizes,
        blocks,
        n_half,
        token,
    )
    token = queries
    for p in range(parts):
        finish_kept(p)
        finish_weight(p)
    return (queries[None], grad_kept[None], grad_weight)


def part_sizes(w_rows):
    return (w_rows // 2, w_rows // 2) if w_rows % 32 == 0 else (w_rows,)


def solution(mesh):
    in_specs = (
        P("dp", "col", "row"),
        P("dp", None),
        P(("dp", "row"), "col"),
        P("dp", "col", "row"),
    )
    out_specs = (P("dp", "col", "row"), P("dp", "col", "row"), P(("dp", "row"), "col"))
    return jax.shard_map(
        per_device, mesh=mesh, in_specs=in_specs, out_specs=out_specs, check_vma=False
    )
```

time: 224 us -> 247 us (1.10); the launches traced: 224 us -> 242 us
  waiting for transfers between devices: 91.2 us -> 125 us
  starting transfers between devices: 72.9 us -> 62.7 us
  Pallas kernels: 52.2 us -> 44.6 us
  local copies, waits for them, and re-layouts: 5.88 us -> 8.64 us
    ppermute x12, waiting for transfers between devices: 14 us -> 58.3 us  [to_row(): return lax.ppermute(value, 'row', [(r, r ^ step) for r in range(n_row)])]
    ppermute x24 -> x14, starting transfers between devices: 56.9 us -> 43.2 us  [along(): return lax.ppermute(value, 'col', [(c, c + step) for c in sources])]
    ppermute x1, waiting for transfers between devices: 17 us -> 6.45 us  [per_device(): lax.ppermute(leaving, 'row', [(r, r + 1) for r in range(n_row - 1)])]
    pallas_call x21 -> x23, Pallas kernels: 52.2 us -> 44.6 us  [call(): pl.pallas_call(kernel, out_shape=out_shape, in_specs=in_specs, out_specs=...]
    ppermute x12, starting transfers between devices: 10.5 us -> 15.2 us  [to_row(): return lax.ppermute(value, 'row', [(r, r ^ step) for r in range(n_row)])]
    unnamed x20 -> x19, local copies, waits for them, and re-layouts: 5.88 us -> 8.64 us
    ppermute x24 -> x14, waiting for transfers between devices: 60.1 us -> 60 us  [along(): return lax.ppermute(value, 'col', [(c, c + step) for c in sources])]
  transfers between devices with their start and end apart: 48 -> 32, of which waited for: 17 -> 19; matrix products, arithmetic and copies ran while one was open for 0% -> 0% of each run, Pallas kernels for 20% -> 14%
where the time goes in v5:
time: 247 us; the launch traced here: 242 us
  waiting for transfers between devices  125 us (51%)
  starting transfers between devices  62.7 us (25%)
  Pallas kernels  44.6 us (18%)
  local copies, waits for them, and re-layouts  8.64 us (3%)
    ppermute x14, waiting for transfers between devices, along(): return lax.ppermute(value, 'col', [(c, c + step) for c in sources])  60 us
    ppermute x12, waiting for transfers between devices, to_row(): return lax.ppermute(value, 'row', [(r, r ^ step) for r in range(n_row)])  58.3 us
    pallas_call x23, Pallas kernels, call(): pl.pallas_call(kernel, out_shape=out_shape, in_specs=in_specs, out_specs=...  44.6 us
    ppermute x14, starting transfers between devices, along(): return lax.ppermute(value, 'col', [(c, c + step) for c in sources])  43.2 us
    ppermute x12, starting transfers between devices, to_row(): return lax.ppermute(value, 'row', [(r, r ^ step) for r in range(n_row)])  15.2 us
    unnamed x19, local copies, waits for them, and re-layouts  8.64 us
    ppermute x1, waiting for transfers between devices, per_device(): lax.ppermute(leaving, 'row', [(r, r + 1) for r in range(n_row - 1)])  6.45 us
  transfers between devices with their start and end apart: 32, of which 19 were waited for; matrix products, arithmetic and copies ran while one was open for 0% of the time, Pallas kernels for 14%

profile of v5, /device:TPU:18, one launch (start us, length us, event | category | flops | bytes accessed | tf_op | source)
XLA Modules:
  0.0 242.0 jit_solution(16159980052406409115)
XLA Ops:
  0.6 1.7 copy-done.5
  8.3 12.7 %collective-permute-done.refs_1_ = bf16[288,1024]{1,0:T(8,128)(2,1)S(1)} collective-permute-done((bf16[288,1024]{1,0:T(8,128)(2,1)S(1)}, bf16[288,1024]{1,0:T(8,128)(2,1)S(1)}, u32[]{:S(2)}, u32[]{:S(2)}) %collective-permute-start) | collective-permute-done | bytes 589856 | tf_op jit(solution)/shard_map/ppermute | solution.py:474
  21.1 10.8 %collective-permute-done.1.refs_2_ = bf16[288,1024]{1,0:T(8,128)(2,1)S(1)} collective-permute-done((bf16[288,1024]{1,0:T(8,128)(2,1)S(1)}, bf16[288,1024]{1,0:T(8,128)(2,1)S(1)}, u32[]{:S(2)}, u32[]{:S(2)}) %collective-permute-start.1) | collective-permute-done | bytes 589856 | tf_op jit(solution)/shard_map/ppermute | solution.py:474
  37.3 12.6 %collective-permute-done.4.refs_1_ = bf16[288,1024]{1,0:T(8,128)(2,1)S(1)} collective-permute-done((bf16[288,1024]{1,0:T(8,128)(2,1)S(1)}, bf16[288,1024]{1,0:T(8,128)(2,1)S(1)}, u32[]{:S(2)}, u32[]{:S(2)}) %collective-permute-start.4) | collective-permute-done | bytes 589856 | tf_op jit(solution)/shard_map/ppermute | solution.py:474
  50.0 12.7 %collective-permute-done.5.refs_2_ = bf16[288,1024]{1,0:T(8,128)(2,1)S(1)} collective-permute-done((bf16[288,1024]{1,0:T(8,128)(2,1)S(1)}, bf16[288,1024]{1,0:T(8,128)(2,1)S(1)}, u32[]{:S(2)}, u32[]{:S(2)}) %collective-permute-start.5) | collective-permute-done | bytes 589856 | tf_op jit(solution)/shard_map/ppermute | solution.py:474
  62.9 3.4 %collective-permute-start.8 = (bf16[1152,128]{1,0:T(8,128)(2,1)S(1)}, bf16[1152,128]{1,0:T(8,128)(2,1)S(1)}, u32[]{:S(2)}, u32[]{:S(2)}) collective-permute-start(bf16[1152,128]{1,0:T(8,128)(2,1)S(1)} %get-tuple-element.27.dep_ref.base_ref.refs_3_), channel_id=1, source_target_pairs={{0,4},{4,8},{8,12},{1,5},{5,9},{9,13},{2,6},{6,10},{10,14},{3,7},{... | collective-permute-start | bytes 884744 | tf_op jit(solution)/shard_map/ppermute | solution.py:491
  67.8 6.4 %collective-permute-done.8.arrived_ref = bf16[1152,128]{1,0:T(8,128)(2,1)S(1)} collective-permute-done((bf16[1152,128]{1,0:T(8,128)(2,1)S(1)}, bf16[1152,128]{1,0:T(8,128)(2,1)S(1)}, u32[]{:S(2)}, u32[]{:S(2)}) %collective-permute-start.8) | collective-permute-done | bytes 294944 | tf_op jit(solution)/shard_map/ppermute | solution.py:491
  74.3 2.4 collective-permute-start.10
  76.7 3.6 %collective-permute-start.9 = (bf16[1152,512]{1,0:T(8,128)(2,1)S(1)}, bf16[1152,512]{1,0:T(8,128)(2,1)S(1)}, u32[]{:S(2)}, u32[]{:S(2)}) collective-permute-start(bf16[1152,512]{1,0:T(8,128)(2,1)S(1)} %add_arrived.1.dep_ref.refs_3_.refs_5_), channel_id=1, source_target_pairs={{0,1},{1,2},{2,3},{4,5},{5,6},{6,7},{8,9},{9,10},{10,11},{12,13},{... | collective-permute-start | bytes 3538952 | tf_op jit(solution)/shard_map/ppermute | solution.py:480
  80.3 23.5 %collective-permute-done.10.came_l.refs_4_.refs_6_ = bf16[1152,512]{1,0:T(8,128)(2,1)S(1)} collective-permute-done((bf16[1152,512]{1,0:T(8,128)(2,1)S(1)}, bf16[1152,512]{1,0:T(8,128)(2,1)S(1)}, u32[]{:S(2)}, u32[]{:S(2)}) %collective-permute-start.10) | collective-permute-done | bytes 1179680 | tf_op jit(solution)/shard_map/ppermute | solution.py:480
  103.8 2.1 collective-permute-done.9.came_r.refs_2_.refs_4_
  106.0 4.8 %collective-permute-start.11 = (bf16[592,512]{1,0:T(8,128)(2,1)S(1)}, bf16[592,512]{1,0:T(8,128)(2,1)S(1)}, u32[]{:S(2)}, u32[]{:S(2)}) collective-permute-start(bf16[592,512]{1,0:T(8,128)(2,1)S(1)} %get-tuple-element.31.dep_ref.refs_1_), channel_id=1, source_target_pairs={{0,1},{1,2},{2,3},{4,5},{5,6},{6,7},{8,9},{9,10},{10,11},{12,13},{... | collective-permute-start | bytes 1818632 | tf_op jit(solution)/shard_map/ppermute | solution.py:480
  110.8 1.9 collective-permute-start.12
  112.9 5.2 %collective-permute-start.15 = (bf16[592,512]{1,0:T(8,128)(2,1)S(1)}, bf16[592,512]{1,0:T(8,128)(2,1)S(1)}, u32[]{:S(2)}, u32[]{:S(2)}) collective-permute-start(bf16[592,512]{1,0:T(8,128)(2,1)S(1)} %get-tuple-element.33.dep_ref), channel_id=1, source_target_pairs={{0,1},{1,2},{2,3},{4,5},{5,6},{6,7},{8,9},{9,10},{10,11},{12,13},{... | collective-permute-start | bytes 1818632 | tf_op jit(solution)/shard_map/ppermute | solution.py:480
  118.1 1.9 collective-permute-start.16
  120.1 4.9 %collective-permute-done.11.came_r.refs_1_.refs_8_ = bf16[592,512]{1,0:T(8,128)(2,1)S(1)} collective-permute-done((bf16[592,512]{1,0:T(8,128)(2,1)S(1)}, bf16[592,512]{1,0:T(8,128)(2,1)S(1)}, u32[]{:S(2)}, u32[]{:S(2)}) %collective-permute-start.11) | collective-permute-done | bytes 606240 | tf_op jit(solution)/shard_map/ppermute | solution.py:480
  125.0 4.4 %collective-permute-done.12.came_l.refs_5_.refs_9_ = bf16[592,512]{1,0:T(8,128)(2,1)S(1)} collective-permute-done((bf16[592,512]{1,0:T(8,128)(2,1)S(1)}, bf16[592,512]{1,0:T(8,128)(2,1)S(1)}, u32[]{:S(2)}, u32[]{:S(2)}) %collective-permute-start.12) | collective-permute-done | bytes 606240 | tf_op jit(solution)/shard_map/ppermute | solution.py:480
  129.3 2.3 line_step.8
  131.7 1.9 collective-permute-start.13
  133.6 3.9 %collective-permute-start.14 = (bf16[592,512]{1,0:T(8,128)(2,1)S(1)}, bf16[592,512]{1,0:T(8,128)(2,1)S(1)}, u32[]{:S(2)}, u32[]{:S(2)}) collective-permute-start(bf16[592,512]{1,0:T(8,128)(2,1)S(1)} %get-tuple-element.35), channel_id=1, source_target_pairs={{1,0},{2,1},{3,2},{5,4},{6,5},{7,6},{9,8},{10,9},{11,10},{13,12},{... | collective-permute-start | bytes 1818632 | tf_op jit(solution)/shard_map/ppermute | solution.py:480
  137.9 4.4 %collective-permute-done.16.came_l.refs_5_.refs_13_ = bf16[592,512]{1,0:T(8,128)(2,1)S(1)} collective-permute-done((bf16[592,512]{1,0:T(8,128)(2,1)S(1)}, bf16[592,512]{1,0:T(8,128)(2,1)S(1)}, u32[]{:S(2)}, u32[]{:S(2)}) %collective-permute-start.16) | collective-permute-done | bytes 606240 | tf_op jit(solution)/shard_map/ppermute | solution.py:480
  142.3 2.5 %line_step.9 = (bf16[592,512]{1,0:T(8,128)(2,1)S(1)}, bf16[592,512]{1,0:T(8,128)(2,1)S(1)}) custom-call(bf16[1152,1024]{1,0:T(8,128)(2,1)S(1)} %collect_rows.3.mine_ref.refs_2_, bf16[1152,1024]{1,0:T(8,128)(2,1)S(1)} %collective-permute-done.7.other_ref.refs_3_, bf16[1024,512]{1,0:T(8,128)(2,1)S(1)} %bitcast.7, ...), custom_call_target="tpu_custom_call" | custom-call | flops 1 | bytes 1 | tf_op jit(solution)/shard_map/line_step/pallas_call | solution.py:21
  144.8 3.6 %collective-permute-done.13.came_r.refs_0_.refs_7_ = bf16[592,512]{1,0:T(8,128)(2,1)S(1)} collective-permute-done((bf16[592,512]{1,0:T(8,128)(2,1)S(1)}, bf16[592,512]{1,0:T(8,128)(2,1)S(1)}, u32[]{:S(2)}, u32[]{:S(2)}) %collective-permute-start.13) | collective-permute-done | bytes 606240 | tf_op jit(solution)/shard_map/ppermute | solution.py:480
  148.4 4.1 %collective-permute-done.14.came_l.refs_6_.refs_10_ = bf16[592,512]{1,0:T(8,128)(2,1)S(1)} collective-permute-done((bf16[592,512]{1,0:T(8,128)(2,1)S(1)}, bf16[592,512]{1,0:T(8,128)(2,1)S(1)}, u32[]{:S(2)}, u32[]{:S(2)}) %collective-permute-start.14) | collective-permute-done | bytes 606240 | tf_op jit(solution)/shard_map/ppermute | solution.py:480
  152.5 4.5 %line_step.10 = (bf16[592,512]{1,0:T(8,128)(2,1)S(1)}, bf16[592,512]{1,0:T(8,128)(2,1)S(1)}) custom-call(bf16[1152,1024]{1,0:T(8,128)(2,1)S(1)} %collect_rows.2.refs_1_.mine_ref.refs_0_, bf16[1152,1024]{1,0:T(8,128)(2,1)S(1)} %collective-permute-done.3.other_ref.refs_1_, bf16[1024,512]{1,0:T(8,128)(2,1)S(1)} %bitcast.8, ...), custom_call_target="tpu_custom_call" | custom-call | flops 1 | bytes 1 | tf_op jit(solution)/shard_map/line_step/pallas_call | solution.py:21
  157.9 1.9 collective-permute-start.17
  159.8 3.9 %collective-permute-start.18 = (bf16[592,512]{1,0:T(8,128)(2,1)S(1)}, bf16[592,512]{1,0:T(8,128)(2,1)S(1)}, u32[]{:S(2)}, u32[]{:S(2)}) collective-permute-start(bf16[592,512]{1,0:T(8,128)(2,1)S(1)} %get-tuple-element.38), channel_id=1, source_target_pairs={{1,0},{2,1},{3,2},{5,4},{6,5},{7,6},{9,8},{10,9},{11,10},{13,12},{... | collective-permute-start | bytes 1818632 | tf_op jit(solution)/shard_map/ppermute | solution.py:480
  163.8 3.9 %grad_weight_partial.2 = (f32[288,1024]{1,0:T(8,128)S(1)}, bf16[304,1024]{1,0:T(8,128)(2,1)S(1)}, bf16[304,1024]{1,0:T(8,128)(2,1)S(1)}, bf16[304,1024]{1,0:T(8,128)(2,1)S(1)}) custom-call(bf16[1024,512]{1,0:T(8,128)(2,1)S(1)} %bitcast.10, bf16[1024,512]{1,0:T(8,128)(2,1)S(1)} %collective-permute-done.19.cot_other_ref, ...), custom_call_target="tpu_custom_call" | custom-call | flops 1 | bytes 1 | tf_op jit(solution)/shard_map/grad_weight_partial/pallas_call | solution.py:21
  167.7 7.7 %collective-permute-done.17.refs_0_.came_r.refs_11_ = bf16[592,512]{1,0:T(8,128)(2,1)S(1)} collective-permute-done((bf16[592,512]{1,0:T(8,128)(2,1)S(1)}, bf16[592,512]{1,0:T(8,128)(2,1)S(1)}, u32[]{:S(2)}, u32[]{:S(2)}) %collective-permute-start.17) | collective-permute-done | bytes 606240 | tf_op jit(solution)/shard_map/ppermute | solution.py:480
  175.4 1.9 collective-permute-done.18.refs_6_.came_l.refs_14_
  177.6 1.9 collective-permute-start.24
  179.5 3.0 %collective-permute-start.27 = (bf16[304,1024]{1,0:T(8,128)(2,1)S(1)}, bf16[304,1024]{1,0:T(8,128)(2,1)S(1)}, u32[]{:S(2)}, u32[]{:S(2)}) collective-permute-start(bf16[304,1024]{1,0:T(8,128)(2,1)S(1)} %get-tuple-element.46), channel_id=1, source_target_pairs={{0,8},{4,12},{8,0},{12,4},{1,9},{5,13},{9,1},{13,5},{2,10},{6,14},... | collective-permute-start | bytes 1867784 | tf_op jit(solution)/shard_map/ppermute | solution.py:474
  183.1 3.9 %collective-permute-start.25 = (bf16[592,512]{1,0:T(8,128)(2,1)S(1)}, bf16[592,512]{1,0:T(8,128)(2,1)S(1)}, u32[]{:S(2)}, u32[]{:S(2)}) collective-permute-start(bf16[592,512]{1,0:T(8,128)(2,1)S(1)} %get-tuple-element.44), channel_id=1, source_target_pairs={{1,0},{2,1},{3,2},{5,4},{6,5},{7,6},{9,8},{10,9},{11,10},{13,12},{... | collective-permute-start | bytes 1818632 | tf_op jit(solution)/shard_map/ppermute | solution.py:480
  187.0 4.5 %line_step.11 = (bf16[592,512]{1,0:T(8,128)(2,1)S(1)}, bf16[592,512]{1,0:T(8,128)(2,1)S(1)}) custom-call(bf16[1152,1024]{1,0:T(8,128)(2,1)S(1)} %collect_rows.3.mine_ref.refs_2_, bf16[1152,1024]{1,0:T(8,128)(2,1)S(1)} %collective-permute-done.7.other_ref.refs_3_, bf16[1024,512]{1,0:T(8,128)(2,1)S(1)} %bitcast.11, ...), custom_call_target="tpu_custom_call" | custom-call | flops 1 | bytes 1 | tf_op jit(solution)/shard_map/line_step/pallas_call | solution.py:21
  191.5 3.9 %grad_weight_partial.3 = (f32[288,1024]{1,0:T(8,128)S(1)}, bf16[304,1024]{1,0:T(8,128)(2,1)S(1)}, bf16[304,1024]{1,0:T(8,128)(2,1)S(1)}, bf16[304,1024]{1,0:T(8,128)(2,1)S(1)}) custom-call(bf16[1024,512]{1,0:T(8,128)(2,1)S(1)} %bitcast.12, bf16[1024,512]{1,0:T(8,128)(2,1)S(1)} %collective-permute-done.19.cot_other_ref, ...), custom_call_target="tpu_custom_call" | custom-call | flops 1 | bytes 1 | tf_op jit(solution)/shard_map/grad_weight_partial/pallas_call | solution.py:21
  195.5 1.7 collective-permute-start.29
  197.2 2.9 %collective-permute-done.25.l_ref = bf16[592,512]{1,0:T(8,128)(2,1)S(1)} collective-permute-done((bf16[592,512]{1,0:T(8,128)(2,1)S(1)}, bf16[592,512]{1,0:T(8,128)(2,1)S(1)}, u32[]{:S(2)}, u32[]{:S(2)}) %collective-permute-start.25) | collective-permute-done | bytes 606240 | tf_op jit(solution)/shard_map/ppermute | solution.py:480
  202.9 7.8 %collective-permute-done.27.refs_1_ = bf16[304,1024]{1,0:T(8,128)(2,1)S(1)} collective-permute-done((bf16[304,1024]{1,0:T(8,128)(2,1)S(1)}, bf16[304,1024]{1,0:T(8,128)(2,1)S(1)}, u32[]{:S(2)}, u32[]{:S(2)}) %collective-permute-start.27) | collective-permute-done | bytes 622624 | tf_op jit(solution)/shard_map/ppermute | solution.py:474
  210.7 1.9 collective-permute-start.22
  212.6 4.0 %collective-permute-start.23 = (bf16[592,512]{1,0:T(8,128)(2,1)S(1)}, bf16[592,512]{1,0:T(8,128)(2,1)S(1)}, u32[]{:S(2)}, u32[]{:S(2)}) collective-permute-start(bf16[592,512]{1,0:T(8,128)(2,1)S(1)} %get-tuple-element.43), channel_id=1, source_target_pairs={{1,0},{2,1},{3,2},{5,4},{6,5},{7,6},{9,8},{10,9},{11,10},{13,12},{... | collective-permute-start | bytes 1818632 | tf_op jit(solution)/shard_map/ppermute | solution.py:480
  216.6 7.0 %queries.1.dep_ref = bf16[1024,512]{1,0:T(8,128)(2,1)} custom-call(bf16[1152,1024]{1,0:T(8,128)(2,1)S(1)} %collect_rows.2.refs_1_.mine_ref.refs_0_, bf16[1152,1024]{1,0:T(8,128)(2,1)S(1)} %collective-permute-done.3.other_ref.refs_1_, bf16[1152,1024]{1,0:T(8,128)(2,1)S(1)} %collect_rows.3.mine_ref.refs_2_, ...), custom_call_target="tpu_custom_call" | custom-call | flops 1 | bytes 1 | tf_op jit(solution)/shard_map/queries/pallas_call | solution.py:21
  224.8 3.1 %grad_kept_last.2.refs_4_.base_ref = f32[1152,512]{1,0:T(8,128)} custom-call(bf16[1152,1024]{1,0:T(8,128)(2,1)S(1)} %collect_rows.2.refs_1_.mine_ref.refs_0_, bf16[1152,1024]{1,0:T(8,128)(2,1)S(1)} %collective-permute-done.3.other_ref.refs_1_, bf16[1024,512]{1,0:T(8,128)(2,1)S(1)} %bitcast.13, bf16[592,512]{1,0:T(8,128)(2,1)S(1)} %collective-permute-done.24.r_ref, ...), custom_call_target="tpu_custom_call" | custom-call | flops 1 | bytes 1 | tf_op jit(solution)/shard_map/grad_kept_last/pallas_call | solution.py:21
  227.9 1.7 copy-done.1
  229.6 2.8 %grad_weight_last.2.dep_ref.refs_3_ = f32[576,1024]{1,0:T(8,128)} custom-call(f32[288,1024]{1,0:T(8,128)S(1)} %get-tuple-element.40.refs_7_.own_ref, bf16[304,1024]{1,0:T(8,128)(2,1)S(1)} %collective-permute-done.26.refs_0_, bf16[304,1024]{1,0:T(8,128)(2,1)S(1)} %collective-permute-done.27.refs_1_, bf16[304,1024]{1,0:T(8,128)(2,1)S(1)} %collective-permute-done.28.refs_2_, ...), custom_call_target="tpu_custom_call" | custom-call | flops 1 | bytes 1 | tf_op jit(solution)/shard_map/grad_weight_last/pallas_call | solution.py:21
  232.5 1.7 copy-done.3
  234.1 3.1 %grad_kept_last.3.refs_4_ = f32[1152,512]{1,0:T(8,128)} custom-call(bf16[1152,1024]{1,0:T(8,128)(2,1)S(1)} %collect_rows.3.mine_ref.refs_2_, bf16[1152,1024]{1,0:T(8,128)(2,1)S(1)} %collective-permute-done.7.other_ref.refs_3_, bf16[1024,512]{1,0:T(8,128)(2,1)S(1)} %bitcast.14, ...), custom_call_target="tpu_custom_call", output_to_operand_aliasing={{}: (5, {})} | custom-call | flops 1 | bytes 1 | tf_op jit(solution)/shard_map/grad_kept_last/pallas_call | solution.py:21
  237.3 1.7 copy-done.2
  238.9 2.8 %grad_weight_last.3 = f32[576,1024]{1,0:T(8,128)} custom-call(f32[288,1024]{1,0:T(8,128)S(1)} %get-tuple-element.42.refs_15_.own_ref, bf16[304,1024]{1,0:T(8,128)(2,1)S(1)} %collective-permute-done.29.refs_0_, bf16[304,1024]{1,0:T(8,128)(2,1)S(1)} %collective-permute-done.30.refs_1_, ...), custom_call_target="tpu_custom_call", output_to_operand_aliasing={{}: (4, {})} | custom-call | flops 1 | bytes 1 | tf_op jit(solution)/shard_map/grad_weight_last/pallas_call | solution.py:21
  (58 shorter events, 19.5 us)
Async XLA Ops:
  0.6 1.7 copy-start.5
  2.3 0.7 copy-start.7
  3.0 1.5 copy-start.6
  4.8 16.3 %collective-permute-start = (bf16[288,1024]{1,0:T(8,128)(2,1)S(1)}, bf16[288,1024]{1,0:T(8,128)(2,1)S(1)}, u32[]{:S(2)}, u32[]{:S(2)}) collective-permute-start(bf16[288,1024]{1,0:T(8,128)(2,1)S(1)} %get-tuple-element.28.refs_0_), channel_id=1, source_target_pairs={{0,4},{4,0},{8,12},{12,8},{1,5},{5,1},{9,13},{13,9},{2,6},{6,2},{1... | collective-permute-start | bytes 1769480 | tf_op jit(solution)/shard_map/ppermute | solution.py:474
  5.4 26.5 %collective-permute-start.1 = (bf16[288,1024]{1,0:T(8,128)(2,1)S(1)}, bf16[288,1024]{1,0:T(8,128)(2,1)S(1)}, u32[]{:S(2)}, u32[]{:S(2)}) collective-permute-start(bf16[288,1024]{1,0:T(8,128)(2,1)S(1)} %get-tuple-element.28.refs_0_), channel_id=1, source_target_pairs={{0,8},{4,12},{8,0},{12,4},{1,9},{5,13},{9,1},{13,5},{2,10},{6,14},... | collective-permute-start | bytes 1769480 | tf_op jit(solution)/shard_map/ppermute | solution.py:474
  6.9 26.6 %collective-permute-start.2 = (bf16[288,1024]{1,0:T(8,128)(2,1)S(1)}, bf16[288,1024]{1,0:T(8,128)(2,1)S(1)}, u32[]{:S(2)}, u32[]{:S(2)}) collective-permute-start(bf16[288,1024]{1,0:T(8,128)(2,1)S(1)} %get-tuple-element.28.refs_0_), channel_id=1, source_target_pairs={{0,12},{4,8},{8,4},{12,0},{1,13},{5,9},{9,5},{13,1},{2,14},{6,10},... | collective-permute-start | bytes 1769480 | tf_op jit(solution)/shard_map/ppermute | solution.py:474
  33.7 72.2 %collective-permute-start.3 = (bf16[1152,1024]{1,0:T(8,128)(2,1)S(1)}, bf16[1152,1024]{1,0:T(8,128)(2,1)S(1)}, u32[]{:S(2)}, u32[]{:S(2)}) collective-permute-start(bf16[1152,1024]{1,0:T(8,128)(2,1)S(1)} %collect_rows.2.refs_1_.mine_ref.refs_0_), channel_id=1, source_target_pairs={{0,16},{16,0},{1,17},{17,1},{2,18},{18,2},{3,19},{19,3},{4,20},{20... | collective-permute-start | bytes 7077896 | tf_op jit(solution)/shard_map/ppermute | solution.py:477
  33.8 32.6 %copy-start.8 = (s32[1,2048]{1,0:T(1,128)S(1)}, s32[1,2048]{1,0:T(1,128)}, u32[]{:S(2)}) copy-start(s32[1,2048]{1,0:T(1,128)} %index_ref.3) | copy-start | bytes 24580
  33.8 16.2 %collective-permute-start.4 = (bf16[288,1024]{1,0:T(8,128)(2,1)S(1)}, bf16[288,1024]{1,0:T(8,128)(2,1)S(1)}, u32[]{:S(2)}, u32[]{:S(2)}) collective-permute-start(bf16[288,1024]{1,0:T(8,128)(2,1)S(1)} %after.2.refs_0_), channel_id=1, source_target_pairs={{0,4},{4,0},{8,12},{12,8},{1,5},{5,1},{9,13},{13,9},{2,6},{6,2},{1... | collective-permute-start | bytes 1769480 | tf_op jit(solution)/shard_map/ppermute | solution.py:474
  34.7 28.0 %collective-permute-start.5 = (bf16[288,1024]{1,0:T(8,128)(2,1)S(1)}, bf16[288,1024]{1,0:T(8,128)(2,1)S(1)}, u32[]{:S(2)}, u32[]{:S(2)}) collective-permute-start(bf16[288,1024]{1,0:T(8,128)(2,1)S(1)} %after.2.refs_0_), channel_id=1, source_target_pairs={{0,8},{4,12},{8,0},{12,4},{1,9},{5,13},{9,1},{13,5},{2,10},{6,14},... | collective-permute-start | bytes 1769480 | tf_op jit(solution)/shard_map/ppermute | solution.py:474
  36.2 26.5 %collective-permute-start.6 = (bf16[288,1024]{1,0:T(8,128)(2,1)S(1)}, bf16[288,1024]{1,0:T(8,128)(2,1)S(1)}, u32[]{:S(2)}, u32[]{:S(2)}) collective-permute-start(bf16[288,1024]{1,0:T(8,128)(2,1)S(1)} %after.2.refs_0_), channel_id=1, source_target_pairs={{0,12},{4,8},{8,4},{12,0},{1,13},{5,9},{9,5},{13,1},{2,14},{6,10},... | collective-permute-start | bytes 1769480 | tf_op jit(solution)/shard_map/ppermute | solution.py:474
  62.8 49.9 %collective-permute-start.7 = (bf16[1152,1024]{1,0:T(8,128)(2,1)S(1)}, bf16[1152,1024]{1,0:T(8,128)(2,1)S(1)}, u32[]{:S(2)}, u32[]{:S(2)}) collective-permute-start(bf16[1152,1024]{1,0:T(8,128)(2,1)S(1)} %collect_rows.3.mine_ref.refs_2_), channel_id=1, source_target_pairs={{0,16},{16,0},{1,17},{17,1},{2,18},{18,2},{3,19},{19,3},{4,20},{20... | collective-permute-start | bytes 7077896 | tf_op jit(solution)/shard_map/ppermute | solution.py:477
  62.9 11.3 %collective-permute-start.8 = (bf16[1152,128]{1,0:T(8,128)(2,1)S(1)}, bf16[1152,128]{1,0:T(8,128)(2,1)S(1)}, u32[]{:S(2)}, u32[]{:S(2)}) collective-permute-start(bf16[1152,128]{1,0:T(8,128)(2,1)S(1)} %get-tuple-element.27.dep_ref.base_ref.refs_3_), channel_id=1, source_target_pairs={{0,4},{4,8},{8,12},{1,5},{5,9},{9,13},{2,6},{6,10},{10,14},{3,7},{... | collective-permute-start | bytes 884744 | tf_op jit(solution)/shard_map/ppermute | solution.py:491
  67.8 38.1 %copy-start = (bf16[1,1024,512]{2,1,0:T(8,128)(2,1)S(1)}, bf16[1,1024,512]{2,1,0:T(8,128)(2,1)}, u32[]{:S(2)}) copy-start(bf16[1,1024,512]{2,1,0:T(8,128)(2,1)} %param.7) | copy-start | bytes 3145732
  74.3 29.5 %collective-permute-start.10 = (bf16[1152,512]{1,0:T(8,128)(2,1)S(1)}, bf16[1152,512]{1,0:T(8,128)(2,1)S(1)}, u32[]{:S(2)}, u32[]{:S(2)}) collective-permute-start(bf16[1152,512]{1,0:T(8,128)(2,1)S(1)} %add_arrived.1.dep_ref.refs_3_.refs_5_), channel_id=1, source_target_pairs={{1,0},{2,1},{3,2},{5,4},{6,5},{7,6},{9,8},{10,9},{11,10},{13,12},{... | collective-permute-start | bytes 3538952 | tf_op jit(solution)/shard_map/ppermute | solution.py:480
  76.7 29.2 %collective-permute-start.9 = (bf16[1152,512]{1,0:T(8,128)(2,1)S(1)}, bf16[1152,512]{1,0:T(8,128)(2,1)S(1)}, u32[]{:S(2)}, u32[]{:S(2)}) collective-permute-start(bf16[1152,512]{1,0:T(8,128)(2,1)S(1)} %add_arrived.1.dep_ref.refs_3_.refs_5_), channel_id=1, source_target_pairs={{0,1},{1,2},{2,3},{4,5},{5,6},{6,7},{8,9},{9,10},{10,11},{12,13},{... | collective-permute-start | bytes 3538952 | tf_op jit(solution)/shard_map/ppermute | solution.py:480
  106.0 19.0 %collective-permute-start.11 = (bf16[592,512]{1,0:T(8,128)(2,1)S(1)}, bf16[592,512]{1,0:T(8,128)(2,1)S(1)}, u32[]{:S(2)}, u32[]{:S(2)}) collective-permute-start(bf16[592,512]{1,0:T(8,128)(2,1)S(1)} %get-tuple-element.31.dep_ref.refs_1_), channel_id=1, source_target_pairs={{0,1},{1,2},{2,3},{4,5},{5,6},{6,7},{8,9},{9,10},{10,11},{12,13},{... | collective-permute-start | bytes 1818632 | tf_op jit(solution)/shard_map/ppermute | solution.py:480
  110.8 18.5 %collective-permute-start.12 = (bf16[592,512]{1,0:T(8,128)(2,1)S(1)}, bf16[592,512]{1,0:T(8,128)(2,1)S(1)}, u32[]{:S(2)}, u32[]{:S(2)}) collective-permute-start(bf16[592,512]{1,0:T(8,128)(2,1)S(1)} %get-tuple-element.32), channel_id=1, source_target_pairs={{1,0},{2,1},{3,2},{5,4},{6,5},{7,6},{9,8},{10,9},{11,10},{13,12},{... | collective-permute-start | bytes 1818632 | tf_op jit(solution)/shard_map/ppermute | solution.py:480
  112.9 25.1 %collective-permute-start.15 = (bf16[592,512]{1,0:T(8,128)(2,1)S(1)}, bf16[592,512]{1,0:T(8,128)(2,1)S(1)}, u32[]{:S(2)}, u32[]{:S(2)}) collective-permute-start(bf16[592,512]{1,0:T(8,128)(2,1)S(1)} %get-tuple-element.33.dep_ref), channel_id=1, source_target_pairs={{0,1},{1,2},{2,3},{4,5},{5,6},{6,7},{8,9},{9,10},{10,11},{12,13},{... | collective-permute-start | bytes 1818632 | tf_op jit(solution)/shard_map/ppermute | solution.py:480
  118.1 24.2 %collective-permute-start.16 = (bf16[592,512]{1,0:T(8,128)(2,1)S(1)}, bf16[592,512]{1,0:T(8,128)(2,1)S(1)}, u32[]{:S(2)}, u32[]{:S(2)}) collective-permute-start(bf16[592,512]{1,0:T(8,128)(2,1)S(1)} %get-tuple-element.36), channel_id=1, source_target_pairs={{1,0},{2,1},{3,2},{5,4},{6,5},{7,6},{9,8},{10,9},{11,10},{13,12},{... | collective-permute-start | bytes 1818632 | tf_op jit(solution)/shard_map/ppermute | solution.py:480
  131.7 16.8 %collective-permute-start.13 = (bf16[592,512]{1,0:T(8,128)(2,1)S(1)}, bf16[592,512]{1,0:T(8,128)(2,1)S(1)}, u32[]{:S(2)}, u32[]{:S(2)}) collective-permute-start(bf16[592,512]{1,0:T(8,128)(2,1)S(1)} %get-tuple-element.34.dep_ref), channel_id=1, source_target_pairs={{0,1},{1,2},{2,3},{4,5},{5,6},{6,7},{8,9},{9,10},{10,11},{12,13},{... | collective-permute-start | bytes 1818632 | tf_op jit(solution)/shard_map/ppermute | solution.py:480
  133.6 18.9 %collective-permute-start.14 = (bf16[592,512]{1,0:T(8,128)(2,1)S(1)}, bf16[592,512]{1,0:T(8,128)(2,1)S(1)}, u32[]{:S(2)}, u32[]{:S(2)}) collective-permute-start(bf16[592,512]{1,0:T(8,128)(2,1)S(1)} %get-tuple-element.35), channel_id=1, source_target_pairs={{1,0},{2,1},{3,2},{5,4},{6,5},{7,6},{9,8},{10,9},{11,10},{13,12},{... | collective-permute-start | bytes 1818632 | tf_op jit(solution)/shard_map/ppermute | solution.py:480
  157.2 6.6 %collective-permute-start.20 = (bf16[1152,512]{1,0:T(8,128)(2,1)S(1)}, bf16[1152,512]{1,0:T(8,128)(2,1)S(1)}, u32[]{:S(2)}, u32[]{:S(2)}) collective-permute-start(bf16[1152,512]{1,0:T(8,128)(2,1)S(1)} %half_for_other_core.2.refs_7_), channel_id=1, source_target_pairs={{0,16},{16,0},{1,17},{17,1},{2,18},{18,2},{3,19},{19,3},{4,20},{20... | collective-permute-start | bytes 3538952 | tf_op jit(solution)/shard_map/ppermute | solution.py:477
  157.4 6.4 %collective-permute-start.19 = (bf16[1024,512]{1,0:T(8,128)(2,1)S(1)}, bf16[1024,512]{1,0:T(8,128)(2,1)S(1)}, u32[]{:S(2)}, u32[]{:S(2)}) collective-permute-start(bf16[1024,512]{1,0:T(8,128)(2,1)S(1)} %after.3), channel_id=1, source_target_pairs={{0,16},{16,0},{1,17},{17,1},{2,18},{18,2},{3,19},{19,3},{4,20},{20... | collective-permute-start | bytes 3145736 | tf_op jit(solution)/shard_map/ppermute | solution.py:477
  157.9 17.5 %collective-permute-start.17 = (bf16[592,512]{1,0:T(8,128)(2,1)S(1)}, bf16[592,512]{1,0:T(8,128)(2,1)S(1)}, u32[]{:S(2)}, u32[]{:S(2)}) collective-permute-start(bf16[592,512]{1,0:T(8,128)(2,1)S(1)} %get-tuple-element.37.dep_ref), channel_id=1, source_target_pairs={{0,1},{1,2},{2,3},{4,5},{5,6},{6,7},{8,9},{9,10},{10,11},{12,13},{... | collective-permute-start | bytes 1818632 | tf_op jit(solution)/shard_map/ppermute | solution.py:480
  159.8 17.5 %collective-permute-start.18 = (bf16[592,512]{1,0:T(8,128)(2,1)S(1)}, bf16[592,512]{1,0:T(8,128)(2,1)S(1)}, u32[]{:S(2)}, u32[]{:S(2)}) collective-permute-start(bf16[592,512]{1,0:T(8,128)(2,1)S(1)} %get-tuple-element.38), channel_id=1, source_target_pairs={{1,0},{2,1},{3,2},{5,4},{6,5},{7,6},{9,8},{10,9},{11,10},{13,12},{... | collective-permute-start | bytes 1818632 | tf_op jit(solution)/shard_map/ppermute | solution.py:480
  177.4 5.6 %collective-permute-start.21 = (bf16[1152,512]{1,0:T(8,128)(2,1)S(1)}, bf16[1152,512]{1,0:T(8,128)(2,1)S(1)}, u32[]{:S(2)}, u32[]{:S(2)}) collective-permute-start(bf16[1152,512]{1,0:T(8,128)(2,1)S(1)} %half_for_other_core.3.dep_ref), channel_id=1, source_target_pairs={{0,16},{16,0},{1,17},{17,1},{2,18},{18,2},{3,19},{19,3},{4,20},{20... | collective-permute-start | bytes 3538952 | tf_op jit(solution)/shard_map/ppermute | solution.py:477
  177.5 24.1 %collective-permute-start.26 = (bf16[304,1024]{1,0:T(8,128)(2,1)S(1)}, bf16[304,1024]{1,0:T(8,128)(2,1)S(1)}, u32[]{:S(2)}, u32[]{:S(2)}) collective-permute-start(bf16[304,1024]{1,0:T(8,128)(2,1)S(1)} %get-tuple-element.45), channel_id=1, source_target_pairs={{0,4},{4,0},{8,12},{12,8},{1,5},{5,1},{9,13},{13,9},{2,6},{6,2},{1... | collective-permute-start | bytes 1867784 | tf_op jit(solution)/shard_map/ppermute | solution.py:474
  177.6 17.9 %collective-permute-start.24 = (bf16[592,512]{1,0:T(8,128)(2,1)S(1)}, bf16[592,512]{1,0:T(8,128)(2,1)S(1)}, u32[]{:S(2)}, u32[]{:S(2)}) collective-permute-start(bf16[592,512]{1,0:T(8,128)(2,1)S(1)} %get-tuple-element.39.refs_7_), channel_id=1, source_target_pairs={{0,1},{1,2},{2,3},{4,5},{5,6},{6,7},{8,9},{9,10},{10,11},{12,13},{... | collective-permute-start | bytes 1818632 | tf_op jit(solution)/shard_map/ppermute | solution.py:480
  179.5 31.1 %collective-permute-start.27 = (bf16[304,1024]{1,0:T(8,128)(2,1)S(1)}, bf16[304,1024]{1,0:T(8,128)(2,1)S(1)}, u32[]{:S(2)}, u32[]{:S(2)}) collective-permute-start(bf16[304,1024]{1,0:T(8,128)(2,1)S(1)} %get-tuple-element.46), channel_id=1, source_target_pairs={{0,8},{4,12},{8,0},{12,4},{1,9},{5,13},{9,1},{13,5},{2,10},{6,14},... | collective-permute-start | bytes 1867784 | tf_op jit(solution)/shard_map/ppermute | solution.py:474
  182.5 30.1 %collective-permute-start.28 = (bf16[304,1024]{1,0:T(8,128)(2,1)S(1)}, bf16[304,1024]{1,0:T(8,128)(2,1)S(1)}, u32[]{:S(2)}, u32[]{:S(2)}) collective-permute-start(bf16[304,1024]{1,0:T(8,128)(2,1)S(1)} %get-tuple-element.47), channel_id=1, source_target_pairs={{0,12},{4,8},{8,4},{12,0},{1,13},{5,9},{9,5},{13,1},{2,14},{6,10},... | collective-permute-start | bytes 1867784 | tf_op jit(solution)/shard_map/ppermute | solution.py:474
  183.1 17.1 %collective-permute-start.25 = (bf16[592,512]{1,0:T(8,128)(2,1)S(1)}, bf16[592,512]{1,0:T(8,128)(2,1)S(1)}, u32[]{:S(2)}, u32[]{:S(2)}) collective-permute-start(bf16[592,512]{1,0:T(8,128)(2,1)S(1)} %get-tuple-element.44), channel_id=1, source_target_pairs={{1,0},{2,1},{3,2},{5,4},{6,5},{7,6},{9,8},{10,9},{11,10},{13,12},{... | collective-permute-start | bytes 1818632 | tf_op jit(solution)/shard_map/ppermute | solution.py:480
  195.5 41.7 %collective-permute-start.29 = (bf16[304,1024]{1,0:T(8,128)(2,1)S(1)}, bf16[304,1024]{1,0:T(8,128)(2,1)S(1)}, u32[]{:S(2)}, u32[]{:S(2)}) collective-permute-start(bf16[304,1024]{1,0:T(8,128)(2,1)S(1)} %get-tuple-element.48), channel_id=1, source_target_pairs={{0,4},{4,0},{8,12},{12,8},{1,5},{5,1},{9,13},{13,9},{2,6},{6,2},{1... | collective-permute-start | bytes 1867784 | tf_op jit(solution)/shard_map/ppermute | solution.py:474
  200.1 37.1 %collective-permute-start.30 = (bf16[304,1024]{1,0:T(8,128)(2,1)S(1)}, bf16[304,1024]{1,0:T(8,128)(2,1)S(1)}, u32[]{:S(2)}, u32[]{:S(2)}) collective-permute-start(bf16[304,1024]{1,0:T(8,128)(2,1)S(1)} %get-tuple-element.49), channel_id=1, source_target_pairs={{0,8},{4,12},{8,0},{12,4},{1,9},{5,13},{9,1},{13,5},{2,10},{6,14},... | collective-permute-start | bytes 1867784 | tf_op jit(solution)/shard_map/ppermute | solution.py:474
  201.7 35.6 %collective-permute-start.31 = (bf16[304,1024]{1,0:T(8,128)(2,1)S(1)}, bf16[304,1024]{1,0:T(8,128)(2,1)S(1)}, u32[]{:S(2)}, u32[]{:S(2)}) collective-permute-start(bf16[304,1024]{1,0:T(8,128)(2,1)S(1)} %get-tuple-element.50), channel_id=1, source_target_pairs={{0,12},{4,8},{8,4},{12,0},{1,13},{5,9},{9,5},{13,1},{2,14},{6,10},... | collective-permute-start | bytes 1867784 | tf_op jit(solution)/shard_map/ppermute | solution.py:474
  210.7 21.8 %collective-permute-start.22 = (bf16[592,512]{1,0:T(8,128)(2,1)S(1)}, bf16[592,512]{1,0:T(8,128)(2,1)S(1)}, u32[]{:S(2)}, u32[]{:S(2)}) collective-permute-start(bf16[592,512]{1,0:T(8,128)(2,1)S(1)} %get-tuple-element.41.refs_7_), channel_id=1, source_target_pairs={{0,1},{1,2},{2,3},{4,5},{5,6},{6,7},{8,9},{9,10},{10,11},{12,13},{... | collective-permute-start | bytes 1818632 | tf_op jit(solution)/shard_map/ppermute | solution.py:480
  212.6 19.9 %collective-permute-start.23 = (bf16[592,512]{1,0:T(8,128)(2,1)S(1)}, bf16[592,512]{1,0:T(8,128)(2,1)S(1)}, u32[]{:S(2)}, u32[]{:S(2)}) collective-permute-start(bf16[592,512]{1,0:T(8,128)(2,1)S(1)} %get-tuple-element.43), channel_id=1, source_target_pairs={{1,0},{2,1},{3,2},{5,4},{6,5},{7,6},{9,8},{10,9},{11,10},{13,12},{... | collective-permute-start | bytes 1818632 | tf_op jit(solution)/shard_map/ppermute | solution.py:480
  223.6 1.2 copy-start.4
  227.9 1.7 copy-start.1
  232.5 1.7 copy-start.3
  237.3 1.7 copy-start.2

commit v6 on v5

v6 whole, which is shorter than its diff:
```python
import functools

import jax
import jax.numpy as jnp
from jax import lax
from jax.experimental import pallas as pl
from jax.experimental.pallas import tpu as pltpu
from jax.sharding import PartitionSpec as P

HEADER = 16
OFFSET = 128.0
F32 = jnp.float32
BF16 = jnp.bfloat16
ANY = pl.BlockSpec(memory_space=pl.ANY)
VMEM = pl.BlockSpec(memory_space=pltpu.VMEM)
HBM = pl.BlockSpec(memory_space=pltpu.HBM)


def call(kernel, name, out_shape, in_specs, args, out_specs=None, scratch=(), aliases=None, flops=0, mib=14):
    moved = sum(a.size * a.dtype.itemsize for a, s in zip(args, in_specs) if s is VMEM)
    return pl.pallas_call(
        kernel,
        out_shape=out_shape,
        in_specs=in_specs,
        out_specs=out_specs if out_specs is not None else [VMEM] * len(out_shape),
        scratch_shapes=scratch,
        input_output_aliases=aliases or {},
        compiler_params=pltpu.CompilerParams(vmem_limit_bytes=mib * 2**20),
        cost_estimate=pl.CostEstimate(flops=1, bytes_accessed=1, transcendentals=0),
        name=name,
    )(*args)


def shape(dims, dtype):
    return jax.ShapeDtypeStruct(dims, dtype)


TOKEN = shape((8, 128), F32)


def dot(a, b, ca, cb):
    return lax.dot_general(a, b, (((ca,), (cb,)), ((), ())), preferred_element_type=F32)


def span(start, size):
    return pl.ds(pl.multiple_of(start, 16), size)


def chunks(rows):
    size = 32 if rows % 32 == 0 else 16
    return size, rows // size


def exponent(bound):
    return jnp.clip(jnp.floor(14.99 - jnp.log2(jnp.maximum(bound, 1e-30))), -100.0, 100.0)


def power(values, scale):
    v = values * scale
    square = v * v
    fourth = square * square
    return (fourth * square * (v * jnp.abs(v))).astype(BF16)


def root(code, scale):
    y = code.astype(F32)
    quarter = lax.rsqrt(lax.rsqrt(jnp.maximum(jnp.abs(y), 1e-37)))
    size = quarter * lax.rsqrt(quarter) * scale
    return jnp.where(y > 0.0, size, jnp.where(y < 0.0, -size, 0.0))


def tile_max(values):
    most = jnp.max(jnp.abs(values), axis=0, keepdims=True)
    return jnp.broadcast_to(jnp.max(most, axis=1, keepdims=True), (8, 128))


def write_header(out_ref, expo):
    rows = out_ref.shape[0] - HEADER
    code = jnp.broadcast_to((expo + OFFSET)[0:1, 0:1], (HEADER, out_ref.shape[1]))
    out_ref[rows:, :] = code.astype(BF16)


def write_payload(out_ref, value_of, bound):
    expo = exponent(bound)
    scale = jnp.exp2(expo)[0:1, 0:1]
    size, count = chunks(out_ref.shape[0] - HEADER)

    @pl.loop(0, count)
    def _(i):
        out_ref[span(i * size, size), :] = power(value_of(i * size, size), scale)

    write_header(out_ref, expo)


def read_header(came_ref):
    rows = came_ref.shape[0] - HEADER
    code = came_ref[rows:, :][0:8, 0:128].astype(F32)
    came = code > 0.0
    expo = jnp.where(came, code - OFFSET, 0.0)
    return jnp.exp2(-expo)[0:1, 0:1], jnp.where(came, jnp.exp2(15.0 - expo), 0.0)


def part_rows(sizes, blocks):
    start = 0
    for size in sizes:
        yield start, size, start * blocks, size * blocks
        start += size


def onehot_of(index_ref, first, count, seq_dev):
    index = index_ref[:, pl.ds(pl.multiple_of(first, 128), count)] - lax.axis_index("row") * seq_dev
    positions = lax.broadcasted_iota(jnp.int32, (seq_dev, count), 0)
    return (positions == index).astype(F32).astype(BF16)


def pick_leaving_kernel(blocks, sizes, n_row, keep_dev, index_ref, x_ref, leaving_ref, rows_ref, onehot_ref, sem):
    d_dev, seq_dev = rows_ref.shape
    step = d_dev // blocks

    def copy(b):
        rows = pl.ds(b * step, step)
        return pltpu.make_async_copy(x_ref.at[rows, :], rows_ref.at[rows, :], sem.at[b])

    for b in range(blocks):
        copy(b).start()
    after = jnp.minimum(lax.axis_index("row") + 1, n_row - 1) * keep_dev
    onehot_ref[...] = onehot_of(index_ref, after, leaving_ref.shape[1], seq_dev)
    for b in range(blocks):
        copy(b).wait()
        for start, size, offset, _ in part_rows(sizes, blocks):
            picked = dot(rows_ref[pl.ds(b * step + start, size), :], onehot_ref[...], 1, 0)
            leaving_ref[pl.ds(offset + b * size, size), :] = picked.astype(BF16)


def pick_own_kernel(blocks, sizes, index_ref, rows_ref, kept_ref, onehot_ref):
    d_dev, seq_dev = rows_ref.shape
    keep_dev = kept_ref.shape[1]
    onehot_ref[...] = onehot_of(index_ref, lax.axis_index("row") * keep_dev, keep_dev, seq_dev)
    for b in range(blocks):
        for start, size, offset, _ in part_rows(sizes, blocks):
            picked = dot(rows_ref[pl.ds(b * (d_dev // blocks) + start, size), :], onehot_ref[...], 1, 0)
            kept_ref[pl.ds(offset + b * size, size), :] = picked.astype(BF16)


def add_arrived_kernel(arrived_ref, in_ref, dep_ref, out_ref):
    drift = arrived_ref.shape[1]
    out_ref[:, :drift] = in_ref[:, :drift] + arrived_ref[...]


def nothing_kernel(*refs):
    pass


def after(values, deps):
    return call(
        nothing_kernel,
        "after",
        [shape(v.shape, v.dtype) for v in values],
        [ANY] * (len(values) + len(deps)),
        (*values, *deps),
        out_specs=[ANY] * len(values),
        aliases={i: i for i in range(len(values))},
        mib=1,
    )


def split_kernel(sizes, w_ref, *refs):
    out_refs, sem = refs[:-1], refs[-1]
    copies = [
        pltpu.make_async_copy(w_ref.at[pl.ds(start, size), :], out_refs[p], sem.at[p])
        for p, (start, size, _, _) in enumerate(part_rows(sizes, 1))
    ]
    for copy in copies:
        copy.start()
    for copy in copies:
        copy.wait()


def join_kernel(*refs):
    count = len(refs) // 3
    for n in range(count):
        top, bottom, out_ref = refs[2 * n], refs[2 * n + 1], refs[2 * count + n]
        rows = top.shape[0]
        out_ref[:rows, :] = top[...]
        out_ref[rows:, :] = bottom[...]


def join(pairs):
    arrays = [array for pair in pairs for array in pair]
    return call(
        join_kernel,
        "join_rows",
        [shape((a.shape[0] + b.shape[0], a.shape[1]), a.dtype) for a, b in pairs],
        [VMEM] * len(arrays),
        arrays,
    )


def collect_kernel(plan, *refs):
    out_refs = refs[-len(plan) :]
    row = lax.axis_index("row")
    for out_ref, sources in zip(out_refs, plan):
        size = out_ref.shape[0] // len(sources)
        for step, piece, first in sources:
            out_ref[span((row ^ step) * size, size), :] = refs[piece][pl.ds(first, size), :]


def collect(pieces, plan, sizes, deps):
    heads = pieces[0].shape[1]
    return call(
        functools.partial(collect_kernel, plan),
        "collect_rows",
        [shape((len(sources) * size, heads), BF16) for sources, size in zip(plan, sizes)],
        [VMEM] * len(pieces) + [ANY] * len(deps),
        (*pieces, *deps),
    )


def copy_rows(out_ref, from_ref, first):
    size, count = chunks(out_ref.shape[0])

    @pl.loop(0, count)
    def _(i):
        out_ref[span(i * size, size), :] = from_ref[span(first + i * size, size), :]


def partial_into(out_ref, block, n_half, mine_ref, other_ref, cot_ref, rows_ref):
    shard = out_ref.shape[0]
    first = (block % n_half) * shard
    here = block // n_half == lax.axis_index("dp")
    pl.when(here)(lambda: copy_rows(rows_ref, mine_ref, first))
    pl.when(jnp.logical_not(here))(lambda: copy_rows(rows_ref, other_ref, first))
    out_ref[...] = dot(rows_ref[...], cot_ref[...], 1, 0)


def step_kernel(
    n_col, n_half, t, offset, mine_ref, other_ref, cot_ref, came_r, came_l, dep_ref, out_r, out_l, term_ref, rows_ref
):
    shard = out_r.shape[0] - HEADER
    col = lax.axis_index("col")

    @pl.loop(0, 2)
    def _(way):
        place = jnp.where(way == 0, col, n_col - 1 - col)

        @pl.when(place < t)
        def _():
            block = jnp.where(way == 0, n_col - t + col, t - n_col + col)
            partial_into(term_ref.at[way], block, n_half, mine_ref, other_ref, cot_ref, rows_ref)

    for way, (place, came, out) in enumerate(((col, came_r, out_r), (n_col - 1 - col, came_l, out_l))):
        pl.when(place >= t)(lambda: copy_rows(out.at[pl.ds(0, shard), :], came, offset))

        @pl.when(place < t)
        def _():
            bound = tile_max(term_ref[way])
            if t == 1:
                write_payload(out, lambda first, size: term_ref[way, span(first, size), :], bound)
            else:
                undo, came_bound = read_header(came)

                def total(first, size):
                    rows = span(first, size)
                    return term_ref[way, rows, :] + root(came[rows, :], undo)

                write_payload(out, total, bound + came_bound)


def line_step(n_col, n_half, t, offset, shard, mine, other, cot, came_r, came_l, dep):
    keep = cot.shape[1]
    payload = shape((shard + HEADER, keep), BF16)
    return call(
        functools.partial(step_kernel, n_col, n_half, t, offset),
        "line_step",
        [payload, payload],
        [VMEM] * 5 + [ANY],
        (mine, other, cot, came_r, came_l, dep),
        scratch=[pltpu.VMEM((2, shard, keep), F32), pltpu.VMEM((shard, cot.shape[0]), BF16)],
    )


def last_kernel(
    start, size, blocks, n_half, mine_ref, other_ref, cot_ref, r_ref, l_ref, base_ref, dep_ref, out_ref, *rest
):
    done_ref, total_ref, rows_ref, sem = rest
    done_ref[...] = jnp.zeros_like(done_ref)
    step = out_ref.shape[0] // blocks
    partial_into(total_ref, lax.axis_index("col"), n_half, mine_ref, other_ref, cot_ref, rows_ref)
    undo_r, _ = read_header(r_ref)
    undo_l, _ = read_header(l_ref)
    few, count = chunks(size)
    copies = []
    for b in range(blocks):

        @pl.loop(0, count)
        def _(i):
            rows = span(b * size + i * few, few)
            came = root(r_ref[rows, :], undo_r) + root(l_ref[rows, :], undo_l)
            total_ref[rows, :] = total_ref[rows, :] + came

        target = out_ref.at[pl.ds(b * step + start, size), :]
        copies.append(pltpu.make_async_copy(total_ref.at[pl.ds(b * size, size), :], target, sem.at[b]))
        copies[-1].start()
    for copy in copies:
        copy.wait()


def last_sums(mine, other, cot, came_r, came_l, base, dep, start, size, blocks, n_half, d_dev):
    shard, keep = came_r.shape[0] - HEADER, came_r.shape[1]
    return call(
        functools.partial(last_kernel, start, size, blocks, n_half),
        "grad_kept_last",
        [shape((d_dev, keep), F32), TOKEN],
        [VMEM] * 5 + [HBM if start else ANY, ANY],
        (mine, other, cot, came_r, came_l, base, dep),
        out_specs=[HBM, VMEM],
        scratch=[
            pltpu.VMEM((shard, keep), F32),
            pltpu.VMEM((shard, cot.shape[0]), BF16),
            pltpu.SemaphoreType.DMA((blocks,)),
        ],
        aliases={5: 0} if start else None,
    )


def each_shard(line, offset, rows):
    n_col = lax.axis_size("col")
    col = lax.axis_index("col")
    for n, ref in enumerate(line):
        away = n - len(line) // 2
        shard = col + away
        whole = abs(away) < 2
        yield (shard >= 0) & (shard < n_col), shard, ref.at[pl.ds(offset if whole else 0, rows), :]


def early(dp, n_half):
    return lax.axis_index("col") // n_half == dp


def wanted(when, dp, n_half):
    return None if when is None else early(dp, n_half) == when


def run_if(condition, body):
    if condition is None:
        body()
    else:
        pl.when(condition)(body)


def copy_half(dp, n_half, lines, layout, out_ref):
    base = 0
    for line, (_, _, offset, rows) in zip(lines, layout):
        for came, shard, ref in each_shard(line, offset, rows):

            @pl.when(came & (shard // n_half == dp))
            def _():
                out_ref[span(base + (shard % n_half) * rows, rows), :] = ref[...]

        base += n_half * rows


def half_kernel(n_half, layout, when, *refs):
    arrays, out_ref = refs[:-2], refs[-1]
    other = 1 - lax.axis_index("dp")
    run_if(
        wanted(when, other, n_half),
        lambda: copy_half(other, n_half, split_lines(arrays, len(layout)), layout, out_ref),
    )


def split_lines(arrays, parts):
    count = len(arrays) // parts
    return [arrays[p * count : (p + 1) * count] for p in range(parts)]


def other_half(lines, layout, n_half, when, dep):
    keep = lines[0][0].shape[1]
    arrays = [array for line in lines for array in line]
    return call(
        functools.partial(half_kernel, n_half, layout, when),
        "half_for_other_core",
        shape((n_half * sum(rows for _, _, _, rows in layout), keep), BF16),
        [VMEM] * len(arrays) + [ANY],
        (*arrays, dep),
        out_specs=VMEM,
    )


DIRECT, SQUARE = "direct", "square"


def weight_kernel(n_half, n_row, layout, when, form, count, cot_ref, cot_other_ref, other_ref, *refs):
    arrays, own_ref, send_refs = refs[:count], refs[count + 1], refs[count + 2 : -2]
    mine_ref, total_ref = refs[-2:]
    dp, row = lax.axis_index("dp"), lax.axis_index("row")
    sub = own_ref.shape[0]
    apart = (2,) if form == SQUARE else ()

    def body():
        copy_half(dp, n_half, split_lines(arrays, len(layout)), layout, mine_ref)
        base = start = 0
        for _, size, _, rows in layout:

            @pl.loop(0, n_row)
            def _(step):
                at = span(base + (row ^ step) * size, size)
                value = dot(mine_ref[at, :], cot_ref[...], 1, 1) + dot(other_ref[at, :], cot_other_ref[...], 1, 1)
                target = pl.ds(start, size)

                @pl.when(step == 0)
                def _():
                    own_ref[target, :] = value

                @pl.when(step > 0)
                def _():
                    total_ref[step - 1, target, :] = value

            start += size
            base += n_half * rows
        bound = tile_max(total_ref[0])
        for step in range(2, n_row):
            if step not in apart:
                bound = jnp.maximum(bound, tile_max(total_ref[step - 1]))
        for step in apart:
            send_refs[1][...] = total_ref[step - 1]
        if form == SQUARE:
            expo = exponent(bound)
            scale = jnp.exp2(expo)[0:1, 0:1]
            size, count = chunks(sub)
            for n, step in enumerate((1, 3)):

                @pl.loop(0, count)
                def _(i):
                    value = total_ref[step - 1, span(i * size, size), :]
                    send_refs[0][span(n * sub + i * size, size), :] = power(value, scale)

            write_header(send_refs[0], expo)
        else:
            for n, send_ref in enumerate(send_refs):
                write_payload(send_ref, lambda first, size: total_ref[n, span(first, size), :], bound)

    run_if(wanted(when, dp, n_half), body)


def weight_partial(cot, cot_other, other, lines, layout, n_half, n_row, when, form, dep):
    half, keep = other.shape
    heads = cot.shape[0]
    sub = sum(size for _, size, _, _ in layout)
    arrays = [array for line in lines for array in line]
    if form == SQUARE:
        outputs = [shape((2 * sub + HEADER, heads), BF16), shape((sub, heads), F32)]
    else:
        outputs = [shape((sub + HEADER, heads), BF16)] * (n_row - 1)
    return call(
        functools.partial(weight_kernel, n_half, n_row, layout, when, form, len(arrays)),
        "grad_weight_partial",
        [shape((sub, heads), F32)] + outputs,
        [VMEM] * (3 + len(arrays)) + [ANY],
        (cot, cot_other, other, *arrays, dep),
        scratch=[pltpu.VMEM((half, keep), BF16), pltpu.VMEM((n_row - 1, sub, heads), F32)],
        mib=24,
    )


def weight_middle_kernel(n_half, when, kept_ref, came_ref, dep_ref, out_ref):
    sub = kept_ref.shape[0]

    def body():
        undo, bound = read_header(came_ref)

        def total(first, size):
            return kept_ref[span(first, size), :] + root(came_ref[span(sub + first, size), :], undo)

        write_payload(out_ref, total, bound + tile_max(kept_ref[...]))

    run_if(wanted(when, lax.axis_index("dp"), n_half), body)


def weight_middle(kept, came, n_half, when, dep):
    sub, heads = kept.shape
    return call(
        functools.partial(weight_middle_kernel, n_half, when),
        "grad_weight_middle",
        shape((sub + HEADER, heads), BF16),
        [VMEM] * 2 + [ANY],
        (kept, came, dep),
        out_specs=VMEM,
    )


def weight_last_kernel(n_came, start, n_half, when, own_ref, *refs):
    came_refs, (out_ref, done_ref, total_ref, sem) = refs[:n_came], refs[-4:]
    sub = own_ref.shape[0]
    done_ref[...] = jnp.zeros_like(done_ref)

    def body():
        undo = [read_header(came)[0] for came in came_refs]
        size = 16
        steps = sub // size
        copies = []
        for first, last in ((0, steps // 2), (steps // 2, steps)):

            @pl.loop(first, last)
            def _(i):
                rows = span(i * size, size)
                total = own_ref[rows, :]
                for came, scale in zip(came_refs, undo):
                    total = total + root(came[rows, :], scale)
                total_ref[rows, :] = total

            rows = pl.ds(first * size, (last - first) * size)
            target = out_ref.at[pl.ds(start + first * size, (last - first) * size), :]
            copies.append(pltpu.make_async_copy(total_ref.at[rows, :], target, sem.at[len(copies)]))
            copies[-1].start()
        for copy in copies:
            copy.wait()

    run_if(wanted(when, lax.axis_index("dp"), n_half), body)


def weight_last(own, came, base, dep, start, w_rows, n_half, when):
    sub, heads = own.shape
    again = base.shape == (w_rows, heads) and base.dtype == F32
    return call(
        functools.partial(weight_last_kernel, len(came), start, n_half, when),
        "grad_weight_last",
        [shape((w_rows, heads), F32), TOKEN],
        [VMEM] * (1 + len(came)) + [HBM if again else ANY, ANY],
        (own, *came, base, dep),
        out_specs=[HBM, VMEM],
        scratch=[pltpu.VMEM((sub, heads), F32), pltpu.SemaphoreType.DMA((2,))],
        aliases={1 + len(came): 0} if again else None,
    )


def query_kernel(sizes, blocks, n_half, *refs):
    parts = len(sizes)
    w_refs = refs[: 2 * parts]
    out_ref, done_ref, tile_ref, sem, *panels = refs[-4 - parts :]
    done_ref[...] = jnp.zeros_like(done_ref)
    pieces = refs[2 * parts : -5 - parts]
    middle, outer = pieces[:3], pieces[3:]
    per_part = len(outer) // parts
    dp = lax.axis_index("dp")
    for p, (_, _, offset, rows) in enumerate(part_rows(sizes, blocks)):
        mine = outer[p * per_part : (p + 1) * per_part]
        line = mine[: per_part // 2] + middle + mine[per_part // 2 :]
        for came, shard, ref in each_shard(line, offset, rows):

            @pl.when(came)
            def _():
                place = (shard // n_half ^ dp) * n_half + shard % n_half
                panels[p][span(place * rows, rows), :] = ref[...]

    tile = tile_ref.shape[1]

    def copy(i):
        return pltpu.make_async_copy(tile_ref.at[i], out_ref.at[span(i * tile, tile), :], sem.at[i])

    count = out_ref.shape[0] // tile

    @pl.loop(0, count)
    def _(i):
        heads = pl.ds(pl.multiple_of(i * tile, tile), tile)
        total = jnp.zeros(tile_ref.shape[1:], F32)
        for p in range(parts):
            for n in range(2):
                w_ref = w_refs[2 * p + n]
                half = w_ref.shape[0]
                total = total + dot(w_ref[:, heads], panels[p][pl.ds(n * half, half), :], 0, 0)
        tile_ref[i] = total.astype(BF16)
        copy(i).start()

    for i in range(count):
        copy(i).wait()


def all_queries(w_halves, lines, sizes, blocks, n_half, dep):
    heads = w_halves[0].shape[1]
    keep = lines[0][0].shape[1]
    middle = len(lines[0]) // 2
    pieces = lines[0][middle - 1 : middle + 2]
    for line in lines:
        pieces = pieces + line[: middle - 1] + line[middle + 2 :]
    tile = 256
    return call(
        functools.partial(query_kernel, sizes, blocks, n_half),
        "queries",
        [shape((heads, keep), BF16), TOKEN],
        [VMEM] * (len(w_halves) + len(pieces)) + [ANY],
        (*w_halves, *pieces, dep),
        out_specs=[HBM, VMEM],
        scratch=[pltpu.VMEM((heads // tile, tile, keep), BF16), pltpu.SemaphoreType.DMA((heads // tile,))]
        + [pltpu.VMEM((2 * w.shape[0], keep), BF16) for w in w_halves[::2]],
        mib=20,
    )


def per_device(tokens, kept_index, w_query, cotangent):
    n_dp, n_row, n_col = (lax.axis_size(a) for a in ("dp", "row", "col"))
    seq_x = tokens[0]
    cot = cotangent[0]
    d_dev, seq_dev = seq_x.shape
    w_rows, heads = w_query.shape
    keep_dev = cot.shape[1]
    drift = keep_dev // 4
    sizes = part_sizes(w_rows)
    parts = len(sizes)
    blocks = d_dev // w_rows
    n_half = n_col // n_dp
    layout = list(part_rows(sizes, blocks))

    def to_row(value, step):
        return lax.ppermute(value, "row", [(r, r ^ step) for r in range(n_row)])

    def to_core(value):
        return lax.ppermute(value, "dp", [(i, i ^ 1) for i in range(n_dp)])

    def along(value, sources, step):
        return lax.ppermute(value, "col", [(c, c + step) for c in sources])

    if parts == 2 and n_row == 4:
        own_w = call(
            functools.partial(split_kernel, sizes),
            "split_rows",
            [shape((size, heads), BF16) for size in sizes],
            [HBM],
            (w_query,),
            scratch=[pltpu.SemaphoreType.DMA((parts,))],
        )
        ways = ((1, 2), (2, 1))
        pieces = join([(w, to_row(w, one)) for w, (one, _) in zip(own_w, ways)])
        pieces = [*pieces] + [to_row(pair, two) for pair, (_, two) in zip(pieces, ways)]
        plan = [
            ((0, p, 0), (one, p, size), (two, p + 2, 0), (3, p + 2, size))
            for p, ((one, two), size) in enumerate(zip(ways, sizes))
        ]
    else:
        pieces = [w_query] + [to_row(w_query, step) for step in range(1, n_row)]
        plan = [tuple((step, step, start) for step in range(n_row)) for start, _, _, _ in layout]

    leaving, rows = call(
        functools.partial(pick_leaving_kernel, blocks, sizes, n_row, keep_dev),
        "pick_leaving",
        [shape((d_dev, drift), BF16), shape((d_dev, seq_dev), BF16)],
        [VMEM, ANY],
        (kept_index, seq_x),
        scratch=[pltpu.VMEM((seq_dev, drift), BF16), pltpu.SemaphoreType.DMA((blocks,))],
        mib=40,
    )
    arrived = lax.ppermute(leaving, "row", [(r, r + 1) for r in range(n_row - 1)])
    cot_other = to_core(cot)
    picked = call(
        functools.partial(pick_own_kernel, blocks, sizes),
        "pick_own",
        shape((d_dev, keep_dev), BF16),
        [VMEM] * 2,
        (kept_index, rows),
        out_specs=VMEM,
        scratch=[pltpu.VMEM((seq_dev, keep_dev), BF16)],
    )
    kept = call(
        add_arrived_kernel,
        "add_arrived",
        shape((d_dev, keep_dev), BF16),
        [VMEM] * 2 + [ANY],
        (arrived, picked, cot_other),
        out_specs=VMEM,
        aliases={1: 0},
    )


    right = [[along(kept, range(n_col - 1), 1)] for _ in range(parts)]
    left = [[along(kept, range(1, n_col), -1)] for _ in range(parts)]
    for p in range(1, parts):
        right[p][0], left[p][0] = right[0][0], left[0][0]
    token = kept
    def line_of(p):
        return right[p][n_col - 2 :: -1] + [kept] + left[p][: n_col - 1]

    def step(p, t):
        nonlocal token
        offset = layout[p][2] if t == 1 else 0
        out_r, out_l = line_step(
            n_col, n_half, t, offset, layout[p][3], mine[p], other[p], cot, right[p][-1], left[p][-1], token
        )
        token = out_r
        right[p].append(along(out_r, range(n_col - 1), 1))
        left[p].append(along(out_l, range(1, n_col), -1))

    def device(s, r, c):
        return (s * n_row + r) * n_col + c

    def taking(when):
        return [
            (s, c) for s in range(n_dp) for c in range(n_col) if when is None or (c // n_half == s) == when
        ]

    def give(parts_of, when, lines):
        nonlocal token
        token = other_half(lines, [layout[p] for p in parts_of], n_half, when, token)
        pairs = [((1 - s) * n_col + c, s * n_col + c) for s, c in taking(when)]
        return lax.ppermute(token, ("dp", "col"), pairs)

    def to_rows(send, step, when):
        pairs = [(device(s, r, c), device(s, r ^ step, c)) for s, c in taking(when) for r in range(n_row)]
        return lax.ppermute(send, ("dp", "row", "col"), pairs)

    def weigh(parts_of, when, lines, theirs, form):
        nonlocal token
        own, *sends = weight_partial(
            cot, cot_other, theirs, lines, [layout[p] for p in parts_of], n_half, n_row, when, form, token
        )
        token = own
        return own, sends, layout[parts_of[0]][0], when

    def send_first(own, sends, start, when):
        return own, [to_rows(sends[0], 1, when), sends[1]], start, when

    def send_all(own, sends, start, when):
        return own, [to_rows(send, step, when) for step, send in enumerate(sends, 1)], start, when

    def second(own, came, start, when):
        nonlocal token
        token = weight_middle(came[1], came[0], n_half, when, token)
        return own, [came[0], to_rows(token, 2, when)], start, when

    grad_kept, grad_weight = leaving, leaving

    def finish_kept(p):
        nonlocal grad_kept, token
        start, size = layout[p][:2]
        grad_kept, token = last_sums(
            mine[p], other[p], cot, right[p][-1], left[p][-1], grad_kept, token, start, size, blocks, n_half, d_dev
        )

    def finish_weight(own, came, start, when):
        nonlocal grad_weight, token
        grad_weight, token = weight_last(own, came, grad_weight, token, start, w_rows, n_half, when)

    def collect_all():
        nonlocal token
        shares = collect(pieces, plan, sizes, [token, right[0][0], left[0][0]])
        token = shares[0]
        return shares, [to_core(share) for share in shares]

    def ask():
        nonlocal token
        halves = [h for p in range(parts) for h in (mine[p], other[p])]
        queries, token = all_queries(halves, [line_of(p) for p in range(parts)], sizes, blocks, n_half, token)
        return queries

    every = tuple(range(parts))
    if parts == 2 and n_half == 2 and n_row == 4:
        whole = [right[0][0], kept, left[0][0]]
        theirs = give(every, True, [whole, whole])
        mine, other = collect_all()
        step(0, 1)
        step(1, 1)
        first = send_first(*weigh(every, True, [whole, whole], theirs, SQUARE))
        step(0, 2)
        step(1, 2)
        step(0, 3)
        step(1, 3)
        finish_kept(0)
        theirs = give(every, False, [line_of(p) for p in every])
        first = second(*first)
        queries = ask()
        late = send_all(*weigh(every, False, [line_of(p) for p in every], theirs, DIRECT))
        finish_weight(*first)
        finish_kept(1)
        finish_weight(*late)
    else:
        mine, other = collect_all()
        for t in range(1, n_col):
            for p in every:
                step(p, t)
        theirs = give(every, None, [line_of(p) for p in every])
        late = send_all(*weigh(every, None, [line_of(p) for p in every], theirs, DIRECT))
        queries = ask()
        for p in every:
            finish_kept(p)
        finish_weight(*late)
    return (queries[None], grad_kept[None], grad_weight)


def part_sizes(w_rows):
    return (w_rows // 2, w_rows // 2) if w_rows % 32 == 0 else (w_rows,)


def solution(mesh):
    in_specs = (
        P("dp", "col", "row"),
        P("dp", None),
        P(("dp", "row"), "col"),
        P("dp", "col", "row"),
    )
    out_specs = (P("dp", "col", "row"), P("dp", "col", "row"), P(("dp", "row"), "col"))
    return jax.shard_map(
        per_device, mesh=mesh, in_specs=in_specs, out_specs=out_specs, check_vma=False
    )
```

time: 247 us -> 202 us (0.82); the launches traced: 242 us -> 201 us
  waiting for transfers between devices: 125 us -> 80.9 us
  local copies, waits for them, and re-layouts: 8.64 us -> 3.63 us
  starting transfers between devices: 62.7 us -> 67.2 us
  Pallas kernels: 44.6 us -> 48.5 us
    ppermute x12 -> x4, waiting for transfers between devices: 58.3 us -> 6.69 us  [to_row(): return lax.ppermute(value, 'row', [(r, r ^ step) for r in range(n_row)])]
    ppermute x0 -> x7, starting transfers between devices: none -> 14.2 us  [the longest x5 10.8 us: to_rows(): return lax.ppermute(send, ('dp', 'row', 'col'), pairs)]
    ppermute x12 -> x4, starting transfers between devices: 15.2 us -> 5.63 us  [to_row(): return lax.ppermute(value, 'row', [(r, r ^ step) for r in range(n_row)])]
    ppermute x0 -> x7, waiting for transfers between devices: none -> 8.1 us  [the longest x5 8.09 us: to_rows(): return lax.ppermute(send, ('dp', 'row', 'col'), pairs)]
    unnamed x19 -> x8, local copies, waits for them, and re-layouts: 8.64 us -> 3.63 us
    pallas_call x23 -> x22, Pallas kernels: 44.6 us -> 48.5 us  [call(): pl.pallas_call(kernel, out_shape=out_shape, in_specs=in_specs, out_specs=...]
  transfers between devices with their start and end apart: 32 -> 29, of which waited for: 19 -> 17; matrix products, arithmetic and copies ran while one was open for 0% -> 0% of each run, Pallas kernels for 14% -> 21%
where the time goes in v6:
time: 202 us; the launch traced here: 201 us
  waiting for transfers between devices  80.9 us (40%)
  starting transfers between devices  67.2 us (33%)
  Pallas kernels  48.5 us (24%)
  local copies, waits for them, and re-layouts  3.63 us (2%)
    ppermute x14, waiting for transfers between devices, along(): return lax.ppermute(value, 'col', [(c, c + step) for c in sources])  58.4 us
    pallas_call x22, Pallas kernels, call(): pl.pallas_call(kernel, out_shape=out_shape, in_specs=in_specs, out_specs=...  48.5 us
    ppermute x14, starting transfers between devices, along(): return lax.ppermute(value, 'col', [(c, c + step) for c in sources])  43.4 us
    ppermute x5, starting transfers between devices, to_rows(): return lax.ppermute(send, ('dp', 'row', 'col'), pairs)  10.8 us
    ppermute x5, waiting for transfers between devices, to_rows(): return lax.ppermute(send, ('dp', 'row', 'col'), pairs)  8.09 us
    ppermute x4, waiting for transfers between devices, to_row(): return lax.ppermute(value, 'row', [(r, r ^ step) for r in range(n_row)])  6.69 us
    ppermute x1, waiting for transfers between devices, per_device(): lax.ppermute(leaving, 'row', [(r, r + 1) for r in range(n_row - 1)])  5.76 us
    ppermute x4, starting transfers between devices, to_row(): return lax.ppermute(value, 'row', [(r, r ^ step) for r in range(n_row)])  5.63 us
  transfers between devices with their start and end apart: 29, of which 17 were waited for; matrix products, arithmetic and copies ran while one was open for 0% of the time, Pallas kernels for 21%

profile of v6, /device:TPU:18, one launch (start us, length us, event | category | flops | bytes accessed | tf_op | source)
XLA Modules:
  0.0 201.5 jit_solution(7964727368315325101)
XLA Ops:
  2.8 1.5 collective-permute-start.1
  4.4 1.7 copy-done.1
  6.7 1.5 pick_leaving.1
  8.2 3.3 %collective-permute-start.4 = (bf16[1152,128]{1,0:T(8,128)(2,1)S(1)}, bf16[1152,128]{1,0:T(8,128)(2,1)S(1)}, u32[]{:S(2)}, u32[]{:S(2)}) collective-permute-start(bf16[1152,128]{1,0:T(8,128)(2,1)S(1)} %get-tuple-element.43.base_ref.refs_2_), channel_id=1, source_target_pairs={{0,4},{4,8},{8,12},{1,5},{5,9},{9,13},{2,6},{6,10},{10,14},{3,7},{... | collective-permute-start | bytes 884744 | tf_op jit(solution)/shard_map/ppermute | solution.py:652
  11.6 1.4 pick_own.1.in_ref
  13.0 5.4 %collective-permute-done.refs_1_ = bf16[288,1024]{1,0:T(8,128)(2,1)S(1)} collective-permute-done((bf16[288,1024]{1,0:T(8,128)(2,1)S(1)}, bf16[288,1024]{1,0:T(8,128)(2,1)S(1)}, u32[]{:S(2)}, u32[]{:S(2)}) %collective-permute-start) | collective-permute-done | bytes 589856 | tf_op jit(solution)/shard_map/ppermute | solution.py:615
  18.6 5.8 %collective-permute-done.4.arrived_ref = bf16[1152,128]{1,0:T(8,128)(2,1)S(1)} collective-permute-done((bf16[1152,128]{1,0:T(8,128)(2,1)S(1)}, bf16[1152,128]{1,0:T(8,128)(2,1)S(1)}, u32[]{:S(2)}, u32[]{:S(2)}) %collective-permute-start.4) | collective-permute-done | bytes 294944 | tf_op jit(solution)/shard_map/ppermute | solution.py:652
  24.5 3.5 %collective-permute-start.6 = (bf16[1152,512]{1,0:T(8,128)(2,1)S(1)}, bf16[1152,512]{1,0:T(8,128)(2,1)S(1)}, u32[]{:S(2)}, u32[]{:S(2)}) collective-permute-start(bf16[1152,512]{1,0:T(8,128)(2,1)S(1)} %add_arrived.1.refs_1_.refs_4_.refs_6_.refs_3_.refs_10_.refs_5_), channel_id=1, source_target_pairs={{0,1},{1,2},{2,3},{4,5},{5,6},{6,7},{8,9},{9,10},{10,11},{12,13},{... | collective-permute-start | bytes 3538952 | tf_op jit(solution)/shard_map/ppermute | solution.py:621
  28.0 2.4 %collective-permute-start.7 = (bf16[1152,512]{1,0:T(8,128)(2,1)S(1)}, bf16[1152,512]{1,0:T(8,128)(2,1)S(1)}, u32[]{:S(2)}, u32[]{:S(2)}) collective-permute-start(bf16[1152,512]{1,0:T(8,128)(2,1)S(1)} %add_arrived.1.refs_1_.refs_4_.refs_6_.refs_3_.refs_10_.refs_5_), channel_id=1, source_target_pairs={{1,0},{2,1},{3,2},{5,4},{6,5},{7,6},{9,8},{10,9},{11,10},{13,12},{... | collective-permute-start | bytes 3538952 | tf_op jit(solution)/shard_map/ppermute | solution.py:621
  30.3 1.6 collective-permute-start.2
  31.9 1.9 collective-permute-start.3
  33.8 20.1 %collective-permute-done.6.refs_0_.refs_3_.refs_5_.came_r.refs_2_.refs_9_.refs_4_ = bf16[1152,512]{1,0:T(8,128)(2,1)S(1)} collective-permute-done((bf16[1152,512]{1,0:T(8,128)(2,1)S(1)}, bf16[1152,512]{1,0:T(8,128)(2,1)S(1)}, u32[]{:S(2)}, u32[]{:S(2)}) %collective-permute-start.6) | collective-permute-done | bytes 1179680 | tf_op jit(solution)/shard_map/ppermute | solution.py:621
  54.0 3.2 %collective-permute-done.7.refs_2_.refs_5_.refs_6_.came_l.refs_4_.refs_11_ = bf16[1152,512]{1,0:T(8,128)(2,1)S(1)} collective-permute-done((bf16[1152,512]{1,0:T(8,128)(2,1)S(1)}, bf16[1152,512]{1,0:T(8,128)(2,1)S(1)}, u32[]{:S(2)}, u32[]{:S(2)}) %collective-permute-start.7) | collective-permute-done | bytes 1179680 | tf_op jit(solution)/shard_map/ppermute | solution.py:621
  59.6 2.1 %collective-permute-start.12 = (bf16[2304,512]{1,0:T(8,128)(2,1)S(1)}, bf16[2304,512]{1,0:T(8,128)(2,1)S(1)}, u32[]{:S(2)}, u32[]{:S(2)}) collective-permute-start(bf16[2304,512]{1,0:T(8,128)(2,1)S(1)} %half_for_other_core.2.refs_4_), channel_id=1, source_target_pairs={{16,0},{17,1},{2,18},{3,19},{20,4},{21,5},{6,22},{7,23},{24,8},{25... | collective-permute-start | bytes 7077896 | tf_op jit(solution)/shard_map/ppermute | solution.py:704
  61.7 1.9 collective-permute-done.8.other_ref.refs_1_
  63.8 4.9 %collective-permute-start.10 = (bf16[592,512]{1,0:T(8,128)(2,1)S(1)}, bf16[592,512]{1,0:T(8,128)(2,1)S(1)}, u32[]{:S(2)}, u32[]{:S(2)}) collective-permute-start(bf16[592,512]{1,0:T(8,128)(2,1)S(1)} %get-tuple-element.47.dep_ref), channel_id=1, source_target_pairs={{0,1},{1,2},{2,3},{4,5},{5,6},{6,7},{8,9},{9,10},{10,11},{12,13},{... | collective-permute-start | bytes 1818632 | tf_op jit(solution)/shard_map/ppermute | solution.py:621
  68.7 1.9 collective-permute-start.11
  71.0 5.3 %collective-permute-start.15 = (bf16[592,512]{1,0:T(8,128)(2,1)S(1)}, bf16[592,512]{1,0:T(8,128)(2,1)S(1)}, u32[]{:S(2)}, u32[]{:S(2)}) collective-permute-start(bf16[592,512]{1,0:T(8,128)(2,1)S(1)} %get-tuple-element.49.refs_6_), channel_id=1, source_target_pairs={{0,1},{1,2},{2,3},{4,5},{5,6},{6,7},{8,9},{9,10},{10,11},{12,13},{... | collective-permute-start | bytes 1818632 | tf_op jit(solution)/shard_map/ppermute | solution.py:621
  76.3 1.9 collective-permute-start.16
  78.2 4.5 %collective-permute-done.10.came_r.refs_1_.refs_8_ = bf16[592,512]{1,0:T(8,128)(2,1)S(1)} collective-permute-done((bf16[592,512]{1,0:T(8,128)(2,1)S(1)}, bf16[592,512]{1,0:T(8,128)(2,1)S(1)}, u32[]{:S(2)}, u32[]{:S(2)}) %collective-permute-start.10) | collective-permute-done | bytes 606240 | tf_op jit(solution)/shard_map/ppermute | solution.py:621
  82.8 4.4 %collective-permute-done.11.came_l.refs_5_.refs_9_ = bf16[592,512]{1,0:T(8,128)(2,1)S(1)} collective-permute-done((bf16[592,512]{1,0:T(8,128)(2,1)S(1)}, bf16[592,512]{1,0:T(8,128)(2,1)S(1)}, u32[]{:S(2)}, u32[]{:S(2)}) %collective-permute-start.11) | collective-permute-done | bytes 606240 | tf_op jit(solution)/shard_map/ppermute | solution.py:621
  87.2 2.5 %line_step.8 = (bf16[592,512]{1,0:T(8,128)(2,1)S(1)}, bf16[592,512]{1,0:T(8,128)(2,1)S(1)}) custom-call(bf16[1152,1024]{1,0:T(8,128)(2,1)S(1)} %get-tuple-element.45.mine_ref.dep_ref.refs_0_, bf16[1152,1024]{1,0:T(8,128)(2,1)S(1)} %collective-permute-done.8.other_ref.refs_1_, bf16[1024,512]{1,0:T(8,128)(2,1)S(1)} %bitcast.8, ...), custom_call_target="tpu_custom_call" | custom-call | flops 1 | bytes 1 | tf_op jit(solution)/shard_map/line_step/pallas_call | solution.py:21
  89.7 1.9 collective-permute-start.13
  91.6 3.9 %collective-permute-start.14 = (bf16[592,512]{1,0:T(8,128)(2,1)S(1)}, bf16[592,512]{1,0:T(8,128)(2,1)S(1)}, u32[]{:S(2)}, u32[]{:S(2)}) collective-permute-start(bf16[592,512]{1,0:T(8,128)(2,1)S(1)} %get-tuple-element.52), channel_id=1, source_target_pairs={{1,0},{2,1},{3,2},{5,4},{6,5},{7,6},{9,8},{10,9},{11,10},{13,12},{... | collective-permute-start | bytes 1818632 | tf_op jit(solution)/shard_map/ppermute | solution.py:621
  96.4 3.8 %collective-permute-done.16.came_l.refs_12_.refs_13_ = bf16[592,512]{1,0:T(8,128)(2,1)S(1)} collective-permute-done((bf16[592,512]{1,0:T(8,128)(2,1)S(1)}, bf16[592,512]{1,0:T(8,128)(2,1)S(1)}, u32[]{:S(2)}, u32[]{:S(2)}) %collective-permute-start.16) | collective-permute-done | bytes 606240 | tf_op jit(solution)/shard_map/ppermute | solution.py:621
  100.2 2.5 %line_step.9 = (bf16[592,512]{1,0:T(8,128)(2,1)S(1)}, bf16[592,512]{1,0:T(8,128)(2,1)S(1)}) custom-call(bf16[1152,1024]{1,0:T(8,128)(2,1)S(1)} %get-tuple-element.46.mine_ref.refs_2_, bf16[1152,1024]{1,0:T(8,128)(2,1)S(1)} %collective-permute-done.9.other_ref.refs_3_, bf16[1024,512]{1,0:T(8,128)(2,1)S(1)} %bitcast.9, ...), custom_call_target="tpu_custom_call" | custom-call | flops 1 | bytes 1 | tf_op jit(solution)/shard_map/line_step/pallas_call | solution.py:21
  102.7 1.9 collective-permute-start.17
  104.6 3.9 %collective-permute-start.18 = (bf16[592,512]{1,0:T(8,128)(2,1)S(1)}, bf16[592,512]{1,0:T(8,128)(2,1)S(1)}, u32[]{:S(2)}, u32[]{:S(2)}) collective-permute-start(bf16[592,512]{1,0:T(8,128)(2,1)S(1)} %get-tuple-element.55), channel_id=1, source_target_pairs={{1,0},{2,1},{3,2},{5,4},{6,5},{7,6},{9,8},{10,9},{11,10},{13,12},{... | collective-permute-start | bytes 1818632 | tf_op jit(solution)/shard_map/ppermute | solution.py:621
  108.7 4.4 %collective-permute-done.14.came_l.refs_6_.refs_10_ = bf16[592,512]{1,0:T(8,128)(2,1)S(1)} collective-permute-done((bf16[592,512]{1,0:T(8,128)(2,1)S(1)}, bf16[592,512]{1,0:T(8,128)(2,1)S(1)}, u32[]{:S(2)}, u32[]{:S(2)}) %collective-permute-start.14) | collective-permute-done | bytes 606240 | tf_op jit(solution)/shard_map/ppermute | solution.py:621
  113.2 4.8 %line_step.10 = (bf16[592,512]{1,0:T(8,128)(2,1)S(1)}, bf16[592,512]{1,0:T(8,128)(2,1)S(1)}) custom-call(bf16[1152,1024]{1,0:T(8,128)(2,1)S(1)} %get-tuple-element.45.mine_ref.dep_ref.refs_0_, bf16[1152,1024]{1,0:T(8,128)(2,1)S(1)} %collective-permute-done.8.other_ref.refs_1_, bf16[1024,512]{1,0:T(8,128)(2,1)S(1)} %bitcast.10, ...), custom_call_target="tpu_custom_call" | custom-call | flops 1 | bytes 1 | tf_op jit(solution)/shard_map/line_step/pallas_call | solution.py:21
  118.0 1.9 collective-permute-start.20
  119.9 4.1 %collective-permute-start.21 = (bf16[592,512]{1,0:T(8,128)(2,1)S(1)}, bf16[592,512]{1,0:T(8,128)(2,1)S(1)}, u32[]{:S(2)}, u32[]{:S(2)}) collective-permute-start(bf16[592,512]{1,0:T(8,128)(2,1)S(1)} %get-tuple-element.59), channel_id=1, source_target_pairs={{1,0},{2,1},{3,2},{5,4},{6,5},{7,6},{9,8},{10,9},{11,10},{13,12},{... | collective-permute-start | bytes 1818632 | tf_op jit(solution)/shard_map/ppermute | solution.py:621
  124.0 2.2 %collective-permute-done.18.came_l.refs_13_.refs_14_ = bf16[592,512]{1,0:T(8,128)(2,1)S(1)} collective-permute-done((bf16[592,512]{1,0:T(8,128)(2,1)S(1)}, bf16[592,512]{1,0:T(8,128)(2,1)S(1)}, u32[]{:S(2)}, u32[]{:S(2)}) %collective-permute-start.18) | collective-permute-done | bytes 606240 | tf_op jit(solution)/shard_map/ppermute | solution.py:621
  126.2 4.8 %line_step.11 = (bf16[592,512]{1,0:T(8,128)(2,1)S(1)}, bf16[592,512]{1,0:T(8,128)(2,1)S(1)}) custom-call(bf16[1152,1024]{1,0:T(8,128)(2,1)S(1)} %get-tuple-element.46.mine_ref.refs_2_, bf16[1152,1024]{1,0:T(8,128)(2,1)S(1)} %collective-permute-done.9.other_ref.refs_3_, bf16[1024,512]{1,0:T(8,128)(2,1)S(1)} %bitcast.11, ...), custom_call_target="tpu_custom_call" | custom-call | flops 1 | bytes 1 | tf_op jit(solution)/shard_map/line_step/pallas_call | solution.py:21
  130.9 3.0 %collective-permute-done.20.r_ref = bf16[592,512]{1,0:T(8,128)(2,1)S(1)} collective-permute-done((bf16[592,512]{1,0:T(8,128)(2,1)S(1)}, bf16[592,512]{1,0:T(8,128)(2,1)S(1)}, u32[]{:S(2)}, u32[]{:S(2)}) %collective-permute-start.20) | collective-permute-done | bytes 606240 | tf_op jit(solution)/shard_map/ppermute | solution.py:621
  133.9 4.1 %collective-permute-done.21.l_ref = bf16[592,512]{1,0:T(8,128)(2,1)S(1)} collective-permute-done((bf16[592,512]{1,0:T(8,128)(2,1)S(1)}, bf16[592,512]{1,0:T(8,128)(2,1)S(1)}, u32[]{:S(2)}, u32[]{:S(2)}) %collective-permute-start.21) | collective-permute-done | bytes 606240 | tf_op jit(solution)/shard_map/ppermute | solution.py:621
  138.0 3.2 %grad_kept_last.2 = (f32[1152,512]{1,0:T(8,128)}, f32[8,128]{1,0:T(8,128)S(1)}) custom-call(bf16[1152,1024]{1,0:T(8,128)(2,1)S(1)} %get-tuple-element.45.mine_ref.dep_ref.refs_0_, bf16[1152,1024]{1,0:T(8,128)(2,1)S(1)} %collective-permute-done.8.other_ref.refs_1_, bf16[1024,512]{1,0:T(8,128)(2,1)S(1)} %bitcast.12, ...), custom_call_target="tpu_custom_call" | custom-call | flops 1 | bytes 1 | tf_op jit(solution)/shard_map/grad_kept_last/pallas_call | solution.py:21
  143.4 7.5 %queries.1 = (bf16[1024,512]{1,0:T(8,128)(2,1)}, f32[8,128]{1,0:T(8,128)S(1)}) custom-call(bf16[1152,1024]{1,0:T(8,128)(2,1)S(1)} %get-tuple-element.45.mine_ref.dep_ref.refs_0_, bf16[1152,1024]{1,0:T(8,128)(2,1)S(1)} %collective-permute-done.8.other_ref.refs_1_, bf16[1152,1024]{1,0:T(8,128)(2,1)S(1)} %get-tuple-element.46.mine_ref.refs_2_, ...), custom_call_target="tpu_custom_call" | custom-call | flops 1 | bytes 1 | tf_op jit(solution)/shard_map/queries/pallas_call | solution.py:21
  150.9 9.8 %grad_weight_partial.3 = (f32[576,1024]{1,0:T(8,128)S(1)}, bf16[592,1024]{1,0:T(8,128)(2,1)S(1)}, bf16[592,1024]{1,0:T(8,128)(2,1)S(1)}, bf16[592,1024]{1,0:T(8,128)(2,1)S(1)}) custom-call(bf16[1024,512]{1,0:T(8,128)(2,1)S(1)} %bitcast.13, bf16[1024,512]{1,0:T(8,128)(2,1)S(1)} %collective-permute-done.5.dep_ref.cot_other_ref, ...), custom_call_target="tpu_custom_call" | custom-call | flops 1 | bytes 1 | tf_op jit(solution)/shard_map/grad_weight_partial/pallas_call | solution.py:21
  160.7 3.5 %collective-permute-start.26 = (bf16[592,1024]{1,0:T(8,128)(2,1)S(1)}, bf16[592,1024]{1,0:T(8,128)(2,1)S(1)}, u32[]{:S(2)}, u32[]{:S(2)}) collective-permute-start(bf16[592,1024]{1,0:T(8,128)(2,1)S(1)} %get-tuple-element.69), channel_id=1, source_target_pairs={{2,6},{6,2},{10,14},{14,10},{3,7},{7,3},{11,15},{15,11},{16,20},{2... | collective-permute-start | bytes 3637256 | tf_op jit(solution)/shard_map/ppermute | solution.py:708
  164.2 2.3 %collective-permute-start.27 = (bf16[592,1024]{1,0:T(8,128)(2,1)S(1)}, bf16[592,1024]{1,0:T(8,128)(2,1)S(1)}, u32[]{:S(2)}, u32[]{:S(2)}) collective-permute-start(bf16[592,1024]{1,0:T(8,128)(2,1)S(1)} %get-tuple-element.70), channel_id=1, source_target_pairs={{2,10},{6,14},{10,2},{14,6},{3,11},{7,15},{11,3},{15,7},{16,24},{2... | collective-permute-start | bytes 3637256 | tf_op jit(solution)/shard_map/ppermute | solution.py:708
  166.5 3.4 %collective-permute-start.28 = (bf16[592,1024]{1,0:T(8,128)(2,1)S(1)}, bf16[592,1024]{1,0:T(8,128)(2,1)S(1)}, u32[]{:S(2)}, u32[]{:S(2)}) collective-permute-start(bf16[592,1024]{1,0:T(8,128)(2,1)S(1)} %get-tuple-element.71), channel_id=1, source_target_pairs={{2,14},{6,10},{10,6},{14,2},{3,15},{7,11},{11,7},{15,3},{16,28},{2... | collective-permute-start | bytes 3637256 | tf_op jit(solution)/shard_map/ppermute | solution.py:708
  169.9 1.9 collective-permute-start.22
  171.9 3.9 %collective-permute-start.23 = (bf16[592,512]{1,0:T(8,128)(2,1)S(1)}, bf16[592,512]{1,0:T(8,128)(2,1)S(1)}, u32[]{:S(2)}, u32[]{:S(2)}) collective-permute-start(bf16[592,512]{1,0:T(8,128)(2,1)S(1)} %get-tuple-element.63), channel_id=1, source_target_pairs={{1,0},{2,1},{3,2},{5,4},{6,5},{7,6},{9,8},{10,9},{11,10},{13,12},{... | collective-permute-start | bytes 1818632 | tf_op jit(solution)/shard_map/ppermute | solution.py:621
  175.9 7.3 %collective-permute-done.22.r_ref = bf16[592,512]{1,0:T(8,128)(2,1)S(1)} collective-permute-done((bf16[592,512]{1,0:T(8,128)(2,1)S(1)}, bf16[592,512]{1,0:T(8,128)(2,1)S(1)}, u32[]{:S(2)}, u32[]{:S(2)}) %collective-permute-start.22) | collective-permute-done | bytes 606240 | tf_op jit(solution)/shard_map/ppermute | solution.py:621
  184.3 3.2 %grad_kept_last.3 = (f32[1152,512]{1,0:T(8,128)}, f32[8,128]{1,0:T(8,128)S(1)}) custom-call(bf16[1152,1024]{1,0:T(8,128)(2,1)S(1)} %get-tuple-element.46.mine_ref.refs_2_, bf16[1152,1024]{1,0:T(8,128)(2,1)S(1)} %collective-permute-done.9.other_ref.refs_3_, bf16[1024,512]{1,0:T(8,128)(2,1)S(1)} %bitcast.14, ...), custom_call_target="tpu_custom_call", output_to_operand_aliasing={{0}: (5, {})} | custom-call | flops 1 | bytes 1 | tf_op jit(solution)/shard_map/grad_kept_last/pallas_call | solution.py:21
  187.6 8.1 %collective-permute-done.27.refs_1_ = bf16[592,1024]{1,0:T(8,128)(2,1)S(1)} collective-permute-done((bf16[592,1024]{1,0:T(8,128)(2,1)S(1)}, bf16[592,1024]{1,0:T(8,128)(2,1)S(1)}, u32[]{:S(2)}, u32[]{:S(2)}) %collective-permute-start.27) | collective-permute-done | bytes 1212448 | tf_op jit(solution)/shard_map/ppermute | solution.py:708
  195.7 5.6 %grad_weight_last.3 = (f32[576,1024]{1,0:T(8,128)}, f32[8,128]{1,0:T(8,128)}) custom-call(f32[576,1024]{1,0:T(8,128)S(1)} %get-tuple-element.66.refs_3_.own_ref, bf16[592,1024]{1,0:T(8,128)(2,1)S(1)} %collective-permute-done.26.refs_0_, bf16[592,1024]{1,0:T(8,128)(2,1)S(1)} %collective-permute-done.27.refs_1_, ...), custom_call_target="tpu_custom_call", output_to_operand_aliasing={{0}: (4, {})} | custom-call | flops 1 | bytes 1 | tf_op jit(solution)/shard_map/grad_weight_last/pallas_call | solution.py:21
  (40 shorter events, 10.4 us)
Async XLA Ops:
  0.6 23.7 %collective-permute-start.5 = (bf16[1024,512]{1,0:T(8,128)(2,1)}, bf16[1024,512]{1,0:T(8,128)(2,1)S(1)}, u32[]{:S(2)}, u32[]{:S(2)}) collective-permute-start(bf16[1024,512]{1,0:T(8,128)(2,1)} %bitcast.4), channel_id=1, source_target_pairs={{0,16},{16,0},{1,17},{17,1},{2,18},{18,2},{3,19},{19,3},{4,20},{20... | collective-permute-start | bytes 3145736 | tf_op jit(solution)/shard_map/ppermute | solution.py:618
  0.7 1.3 copy-start.2
  2.2 16.2 %collective-permute-start = (bf16[288,1024]{1,0:T(8,128)(2,1)S(1)}, bf16[288,1024]{1,0:T(8,128)(2,1)S(1)}, u32[]{:S(2)}, u32[]{:S(2)}) collective-permute-start(bf16[288,1024]{1,0:T(8,128)(2,1)S(1)} %get-tuple-element.39.refs_0_), channel_id=1, source_target_pairs={{0,4},{4,0},{8,12},{12,8},{1,5},{5,1},{9,13},{13,9},{2,6},{6,2},{1... | collective-permute-start | bytes 1769480 | tf_op jit(solution)/shard_map/ppermute | solution.py:615
  2.8 15.6 %collective-permute-start.1 = (bf16[288,1024]{1,0:T(8,128)(2,1)S(1)}, bf16[288,1024]{1,0:T(8,128)(2,1)S(1)}, u32[]{:S(2)}, u32[]{:S(2)}) collective-permute-start(bf16[288,1024]{1,0:T(8,128)(2,1)S(1)} %get-tuple-element.40.refs_2_), channel_id=1, source_target_pairs={{0,8},{4,12},{8,0},{12,4},{1,9},{5,13},{9,1},{13,5},{2,10},{6,14},... | collective-permute-start | bytes 1769480 | tf_op jit(solution)/shard_map/ppermute | solution.py:615
  4.4 1.7 copy-start.1
  6.0 0.7 copy-start.3
  8.2 16.1 %collective-permute-start.4 = (bf16[1152,128]{1,0:T(8,128)(2,1)S(1)}, bf16[1152,128]{1,0:T(8,128)(2,1)S(1)}, u32[]{:S(2)}, u32[]{:S(2)}) collective-permute-start(bf16[1152,128]{1,0:T(8,128)(2,1)S(1)} %get-tuple-element.43.base_ref.refs_2_), channel_id=1, source_target_pairs={{0,4},{4,8},{8,12},{1,5},{5,9},{9,13},{2,6},{6,10},{10,14},{3,7},{... | collective-permute-start | bytes 884744 | tf_op jit(solution)/shard_map/ppermute | solution.py:652
  24.5 29.5 %collective-permute-start.6 = (bf16[1152,512]{1,0:T(8,128)(2,1)S(1)}, bf16[1152,512]{1,0:T(8,128)(2,1)S(1)}, u32[]{:S(2)}, u32[]{:S(2)}) collective-permute-start(bf16[1152,512]{1,0:T(8,128)(2,1)S(1)} %add_arrived.1.refs_1_.refs_4_.refs_6_.refs_3_.refs_10_.refs_5_), channel_id=1, source_target_pairs={{0,1},{1,2},{2,3},{4,5},{5,6},{6,7},{8,9},{9,10},{10,11},{12,13},{... | collective-permute-start | bytes 3538952 | tf_op jit(solution)/shard_map/ppermute | solution.py:621
  28.0 29.2 %collective-permute-start.7 = (bf16[1152,512]{1,0:T(8,128)(2,1)S(1)}, bf16[1152,512]{1,0:T(8,128)(2,1)S(1)}, u32[]{:S(2)}, u32[]{:S(2)}) collective-permute-start(bf16[1152,512]{1,0:T(8,128)(2,1)S(1)} %add_arrived.1.refs_1_.refs_4_.refs_6_.refs_3_.refs_10_.refs_5_), channel_id=1, source_target_pairs={{1,0},{2,1},{3,2},{5,4},{6,5},{7,6},{9,8},{10,9},{11,10},{13,12},{... | collective-permute-start | bytes 3538952 | tf_op jit(solution)/shard_map/ppermute | solution.py:621
  30.3 27.1 %collective-permute-start.2 = (bf16[576,1024]{1,0:T(8,128)(2,1)S(1)}, bf16[576,1024]{1,0:T(8,128)(2,1)S(1)}, u32[]{:S(2)}, u32[]{:S(2)}) collective-permute-start(bf16[576,1024]{1,0:T(8,128)(2,1)S(1)} %get-tuple-element.41.refs_0_), channel_id=1, source_target_pairs={{0,8},{4,12},{8,0},{12,4},{1,9},{5,13},{9,1},{13,5},{2,10},{6,14},... | collective-permute-start | bytes 3538952 | tf_op jit(solution)/shard_map/ppermute | solution.py:615
  31.9 26.7 %collective-permute-start.3 = (bf16[576,1024]{1,0:T(8,128)(2,1)S(1)}, bf16[576,1024]{1,0:T(8,128)(2,1)S(1)}, u32[]{:S(2)}, u32[]{:S(2)}) collective-permute-start(bf16[576,1024]{1,0:T(8,128)(2,1)S(1)} %get-tuple-element.42.refs_1_), channel_id=1, source_target_pairs={{0,4},{4,0},{8,12},{12,8},{1,5},{5,1},{9,13},{13,9},{2,6},{6,2},{1... | collective-permute-start | bytes 3538952 | tf_op jit(solution)/shard_map/ppermute | solution.py:615
  57.4 6.2 %copy-start = (bf16[1,1024,512]{2,1,0:T(8,128)(2,1)S(1)}, bf16[1,1024,512]{2,1,0:T(8,128)(2,1)}, u32[]{:S(2)}) copy-start(bf16[1,1024,512]{2,1,0:T(8,128)(2,1)} %param.7) | copy-start | bytes 3145732
  59.0 4.6 %collective-permute-start.8 = (bf16[1152,1024]{1,0:T(8,128)(2,1)S(1)}, bf16[1152,1024]{1,0:T(8,128)(2,1)S(1)}, u32[]{:S(2)}, u32[]{:S(2)}) collective-permute-start(bf16[1152,1024]{1,0:T(8,128)(2,1)S(1)} %get-tuple-element.45.mine_ref.dep_ref.refs_0_), channel_id=1, source_target_pairs={{0,16},{16,0},{1,17},{17,1},{2,18},{18,2},{3,19},{19,3},{4,20},{20... | collective-permute-start | bytes 7077896 | tf_op jit(solution)/shard_map/ppermute | solution.py:618
  59.1 11.6 %collective-permute-start.9 = (bf16[1152,1024]{1,0:T(8,128)(2,1)S(1)}, bf16[1152,1024]{1,0:T(8,128)(2,1)S(1)}, u32[]{:S(2)}, u32[]{:S(2)}) collective-permute-start(bf16[1152,1024]{1,0:T(8,128)(2,1)S(1)} %get-tuple-element.46.mine_ref.refs_2_), channel_id=1, source_target_pairs={{0,16},{16,0},{1,17},{17,1},{2,18},{18,2},{3,19},{19,3},{4,20},{20... | collective-permute-start | bytes 7077896 | tf_op jit(solution)/shard_map/ppermute | solution.py:618
  59.6 18.6 %collective-permute-start.12 = (bf16[2304,512]{1,0:T(8,128)(2,1)S(1)}, bf16[2304,512]{1,0:T(8,128)(2,1)S(1)}, u32[]{:S(2)}, u32[]{:S(2)}) collective-permute-start(bf16[2304,512]{1,0:T(8,128)(2,1)S(1)} %half_for_other_core.2.refs_4_), channel_id=1, source_target_pairs={{16,0},{17,1},{2,18},{3,19},{20,4},{21,5},{6,22},{7,23},{24,8},{25... | collective-permute-start | bytes 7077896 | tf_op jit(solution)/shard_map/ppermute | solution.py:704
  63.8 18.9 %collective-permute-start.10 = (bf16[592,512]{1,0:T(8,128)(2,1)S(1)}, bf16[592,512]{1,0:T(8,128)(2,1)S(1)}, u32[]{:S(2)}, u32[]{:S(2)}) collective-permute-start(bf16[592,512]{1,0:T(8,128)(2,1)S(1)} %get-tuple-element.47.dep_ref), channel_id=1, source_target_pairs={{0,1},{1,2},{2,3},{4,5},{5,6},{6,7},{8,9},{9,10},{10,11},{12,13},{... | collective-permute-start | bytes 1818632 | tf_op jit(solution)/shard_map/ppermute | solution.py:621
  68.7 18.5 %collective-permute-start.11 = (bf16[592,512]{1,0:T(8,128)(2,1)S(1)}, bf16[592,512]{1,0:T(8,128)(2,1)S(1)}, u32[]{:S(2)}, u32[]{:S(2)}) collective-permute-start(bf16[592,512]{1,0:T(8,128)(2,1)S(1)} %get-tuple-element.48), channel_id=1, source_target_pairs={{1,0},{2,1},{3,2},{5,4},{6,5},{7,6},{9,8},{10,9},{11,10},{13,12},{... | collective-permute-start | bytes 1818632 | tf_op jit(solution)/shard_map/ppermute | solution.py:621
  71.0 25.4 %collective-permute-start.15 = (bf16[592,512]{1,0:T(8,128)(2,1)S(1)}, bf16[592,512]{1,0:T(8,128)(2,1)S(1)}, u32[]{:S(2)}, u32[]{:S(2)}) collective-permute-start(bf16[592,512]{1,0:T(8,128)(2,1)S(1)} %get-tuple-element.49.refs_6_), channel_id=1, source_target_pairs={{0,1},{1,2},{2,3},{4,5},{5,6},{6,7},{8,9},{9,10},{10,11},{12,13},{... | collective-permute-start | bytes 1818632 | tf_op jit(solution)/shard_map/ppermute | solution.py:621
  76.3 23.9 %collective-permute-start.16 = (bf16[592,512]{1,0:T(8,128)(2,1)S(1)}, bf16[592,512]{1,0:T(8,128)(2,1)S(1)}, u32[]{:S(2)}, u32[]{:S(2)}) collective-permute-start(bf16[592,512]{1,0:T(8,128)(2,1)S(1)} %get-tuple-element.53), channel_id=1, source_target_pairs={{1,0},{2,1},{3,2},{5,4},{6,5},{7,6},{9,8},{10,9},{11,10},{13,12},{... | collective-permute-start | bytes 1818632 | tf_op jit(solution)/shard_map/ppermute | solution.py:621
  89.7 19.0 %collective-permute-start.13 = (bf16[592,512]{1,0:T(8,128)(2,1)S(1)}, bf16[592,512]{1,0:T(8,128)(2,1)S(1)}, u32[]{:S(2)}, u32[]{:S(2)}) collective-permute-start(bf16[592,512]{1,0:T(8,128)(2,1)S(1)} %get-tuple-element.51.dep_ref), channel_id=1, source_target_pairs={{0,1},{1,2},{2,3},{4,5},{5,6},{6,7},{8,9},{9,10},{10,11},{12,13},{... | collective-permute-start | bytes 1818632 | tf_op jit(solution)/shard_map/ppermute | solution.py:621
  91.6 21.6 %collective-permute-start.14 = (bf16[592,512]{1,0:T(8,128)(2,1)S(1)}, bf16[592,512]{1,0:T(8,128)(2,1)S(1)}, u32[]{:S(2)}, u32[]{:S(2)}) collective-permute-start(bf16[592,512]{1,0:T(8,128)(2,1)S(1)} %get-tuple-element.52), channel_id=1, source_target_pairs={{1,0},{2,1},{3,2},{5,4},{6,5},{7,6},{9,8},{10,9},{11,10},{13,12},{... | collective-permute-start | bytes 1818632 | tf_op jit(solution)/shard_map/ppermute | solution.py:621
  95.5 47.0 %collective-permute-start.19 = (bf16[1168,1024]{1,0:T(8,128)(2,1)S(1)}, bf16[1168,1024]{1,0:T(8,128)(2,1)S(1)}, u32[]{:S(2)}, u32[]{:S(2)}) collective-permute-start(bf16[1168,1024]{1,0:T(8,128)(2,1)S(1)} %get-tuple-element.57), channel_id=1, source_target_pairs={{0,4},{4,0},{8,12},{12,8},{1,5},{5,1},{9,13},{13,9},{18,22},{22,18... | collective-permute-start | bytes 7176200 | tf_op jit(solution)/shard_map/ppermute | solution.py:708
  102.7 21.3 %collective-permute-start.17 = (bf16[592,512]{1,0:T(8,128)(2,1)S(1)}, bf16[592,512]{1,0:T(8,128)(2,1)S(1)}, u32[]{:S(2)}, u32[]{:S(2)}) collective-permute-start(bf16[592,512]{1,0:T(8,128)(2,1)S(1)} %get-tuple-element.54.dep_ref), channel_id=1, source_target_pairs={{0,1},{1,2},{2,3},{4,5},{5,6},{6,7},{8,9},{9,10},{10,11},{12,13},{... | collective-permute-start | bytes 1818632 | tf_op jit(solution)/shard_map/ppermute | solution.py:621
  104.6 21.6 %collective-permute-start.18 = (bf16[592,512]{1,0:T(8,128)(2,1)S(1)}, bf16[592,512]{1,0:T(8,128)(2,1)S(1)}, u32[]{:S(2)}, u32[]{:S(2)}) collective-permute-start(bf16[592,512]{1,0:T(8,128)(2,1)S(1)} %get-tuple-element.55), channel_id=1, source_target_pairs={{1,0},{2,1},{3,2},{5,4},{6,5},{7,6},{9,8},{10,9},{11,10},{13,12},{... | collective-permute-start | bytes 1818632 | tf_op jit(solution)/shard_map/ppermute | solution.py:621
  118.0 15.9 %collective-permute-start.20 = (bf16[592,512]{1,0:T(8,128)(2,1)S(1)}, bf16[592,512]{1,0:T(8,128)(2,1)S(1)}, u32[]{:S(2)}, u32[]{:S(2)}) collective-permute-start(bf16[592,512]{1,0:T(8,128)(2,1)S(1)} %get-tuple-element.58.dep_ref), channel_id=1, source_target_pairs={{0,1},{1,2},{2,3},{4,5},{5,6},{6,7},{8,9},{9,10},{10,11},{12,13},{... | collective-permute-start | bytes 1818632 | tf_op jit(solution)/shard_map/ppermute | solution.py:621
  119.9 18.1 %collective-permute-start.21 = (bf16[592,512]{1,0:T(8,128)(2,1)S(1)}, bf16[592,512]{1,0:T(8,128)(2,1)S(1)}, u32[]{:S(2)}, u32[]{:S(2)}) collective-permute-start(bf16[592,512]{1,0:T(8,128)(2,1)S(1)} %get-tuple-element.59), channel_id=1, source_target_pairs={{1,0},{2,1},{3,2},{5,4},{6,5},{7,6},{9,8},{10,9},{11,10},{13,12},{... | collective-permute-start | bytes 1818632 | tf_op jit(solution)/shard_map/ppermute | solution.py:621
  141.3 9.6 %collective-permute-start.25 = (bf16[2304,512]{1,0:T(8,128)(2,1)S(1)}, bf16[2304,512]{1,0:T(8,128)(2,1)S(1)}, u32[]{:S(2)}, u32[]{:S(2)}) collective-permute-start(bf16[2304,512]{1,0:T(8,128)(2,1)S(1)} %half_for_other_core.3.dep_ref), channel_id=1, source_target_pairs={{18,2},{19,3},{0,16},{1,17},{22,6},{23,7},{4,20},{5,21},{26,10},{2... | collective-permute-start | bytes 7077896 | tf_op jit(solution)/shard_map/ppermute | solution.py:704
  142.6 29.3 %collective-permute-start.24 = (bf16[592,1024]{1,0:T(8,128)(2,1)S(1)}, bf16[592,1024]{1,0:T(8,128)(2,1)S(1)}, u32[]{:S(2)}, u32[]{:S(2)}) collective-permute-start(bf16[592,1024]{1,0:T(8,128)(2,1)S(1)} %grad_weight_middle.1.refs_15_), channel_id=1, source_target_pairs={{0,8},{4,12},{8,0},{12,4},{1,9},{5,13},{9,1},{13,5},{18,26},{22,30... | collective-permute-start | bytes 3637256 | tf_op jit(solution)/shard_map/ppermute | solution.py:708
  160.7 26.9 %collective-permute-start.26 = (bf16[592,1024]{1,0:T(8,128)(2,1)S(1)}, bf16[592,1024]{1,0:T(8,128)(2,1)S(1)}, u32[]{:S(2)}, u32[]{:S(2)}) collective-permute-start(bf16[592,1024]{1,0:T(8,128)(2,1)S(1)} %get-tuple-element.69), channel_id=1, source_target_pairs={{2,6},{6,2},{10,14},{14,10},{3,7},{7,3},{11,15},{15,11},{16,20},{2... | collective-permute-start | bytes 3637256 | tf_op jit(solution)/shard_map/ppermute | solution.py:708
  164.2 31.4 %collective-permute-start.27 = (bf16[592,1024]{1,0:T(8,128)(2,1)S(1)}, bf16[592,1024]{1,0:T(8,128)(2,1)S(1)}, u32[]{:S(2)}, u32[]{:S(2)}) collective-permute-start(bf16[592,1024]{1,0:T(8,128)(2,1)S(1)} %get-tuple-element.70), channel_id=1, source_target_pairs={{2,10},{6,14},{10,2},{14,6},{3,11},{7,15},{11,3},{15,7},{16,24},{2... | collective-permute-start | bytes 3637256 | tf_op jit(solution)/shard_map/ppermute | solution.py:708
  166.5 29.2 %collective-permute-start.28 = (bf16[592,1024]{1,0:T(8,128)(2,1)S(1)}, bf16[592,1024]{1,0:T(8,128)(2,1)S(1)}, u32[]{:S(2)}, u32[]{:S(2)}) collective-permute-start(bf16[592,1024]{1,0:T(8,128)(2,1)S(1)} %get-tuple-element.71), channel_id=1, source_target_pairs={{2,14},{6,10},{10,6},{14,2},{3,15},{7,11},{11,7},{15,3},{16,28},{2... | collective-permute-start | bytes 3637256 | tf_op jit(solution)/shard_map/ppermute | solution.py:708
  169.9 13.2 %collective-permute-start.22 = (bf16[592,512]{1,0:T(8,128)(2,1)S(1)}, bf16[592,512]{1,0:T(8,128)(2,1)S(1)}, u32[]{:S(2)}, u32[]{:S(2)}) collective-permute-start(bf16[592,512]{1,0:T(8,128)(2,1)S(1)} %get-tuple-element.60.dep_ref), channel_id=1, source_target_pairs={{0,1},{1,2},{2,3},{4,5},{5,6},{6,7},{8,9},{9,10},{10,11},{12,13},{... | collective-permute-start | bytes 1818632 | tf_op jit(solution)/shard_map/ppermute | solution.py:621
  171.9 12.5 %collective-permute-start.23 = (bf16[592,512]{1,0:T(8,128)(2,1)S(1)}, bf16[592,512]{1,0:T(8,128)(2,1)S(1)}, u32[]{:S(2)}, u32[]{:S(2)}) collective-permute-start(bf16[592,512]{1,0:T(8,128)(2,1)S(1)} %get-tuple-element.63), channel_id=1, source_target_pairs={{1,0},{2,1},{3,2},{5,4},{6,5},{7,6},{9,8},{10,9},{11,10},{13,12},{... | collective-permute-start | bytes 1818632 | tf_op jit(solution)/shard_map/ppermute | solution.py:621

commit v7 on v6

--- a/solution.py
+++ b/solution.py
@@ -766,9 +766,9 @@
         finish_kept(0)
         theirs = give(every, False, [line_of(p) for p in every])
         first = second(*first)
-        queries = ask()
         late = send_all(*weigh(every, False, [line_of(p) for p in every], theirs, DIRECT))
         finish_weight(*first)
+        queries = ask()
         finish_kept(1)
         finish_weight(*late)
     else:

time: 202 us -> 199 us (0.985)
  waiting for transfers between devices: 80.9 us -> 77.7 us
    ppermute x14, waiting for transfers between devices: 58.4 us -> 52.6 us  [along(): return lax.ppermute(value, 'col', [(c, c + step) for c in sources])]
    ppermute x2, waiting for transfers between devices: 0.01 us -> 4.35 us  [give(): return lax.ppermute(token, ('dp', 'col'), pairs)]
  transfers between devices with their start and end apart: 29 -> 29, of which waited for: 17 -> 18; matrix products, arithmetic and copies ran while one was open for 0% -> 0% of each run, Pallas kernels for 21% -> 21%
where the time goes in v7:
time: 199 us; the launch traced here: 198 us
  waiting for transfers between devices  77.7 us (39%)
  starting transfers between devices  67.2 us (34%)
  Pallas kernels  48.4 us (24%)
  local copies, waits for them, and re-layouts  3.63 us (2%)
    ppermute x14, waiting for transfers between devices, along(): return lax.ppermute(value, 'col', [(c, c + step) for c in sources])  52.6 us
    pallas_call x22, Pallas kernels, call(): pl.pallas_call(kernel, out_shape=out_shape, in_specs=in_specs, out_specs=...  48.4 us
    ppermute x14, starting transfers between devices, along(): return lax.ppermute(value, 'col', [(c, c + step) for c in sources])  43.4 us
    ppermute x5, starting transfers between devices, to_rows(): return lax.ppermute(send, ('dp', 'row', 'col'), pairs)  10.8 us
    ppermute x4, waiting for transfers between devices, to_row(): return lax.ppermute(value, 'row', [(r, r ^ step) for r in range(n_row)])  6.69 us
    ppermute x5, waiting for transfers between devices, to_rows(): return lax.ppermute(send, ('dp', 'row', 'col'), pairs)  6.48 us
    ppermute x1, waiting for transfers between devices, per_device(): lax.ppermute(leaving, 'row', [(r, r + 1) for r in range(n_row - 1)])  5.76 us
    ppermute x4, starting transfers between devices, to_row(): return lax.ppermute(value, 'row', [(r, r ^ step) for r in range(n_row)])  5.63 us
  transfers between devices with their start and end apart: 29, of which 18 were waited for; matrix products, arithmetic and copies ran while one was open for 0% of the time, Pallas kernels for 21%

profile of v7, /device:TPU:18, one launch (start us, length us, event | category | flops | bytes accessed | tf_op | source)
XLA Modules:
  0.0 198.2 jit_solution(857335621207691110)
XLA Ops:
  2.8 1.5 collective-permute-start.1
  4.4 1.7 copy-done.1
  6.7 1.5 pick_leaving.1
  8.2 3.3 %collective-permute-start.4 = (bf16[1152,128]{1,0:T(8,128)(2,1)S(1)}, bf16[1152,128]{1,0:T(8,128)(2,1)S(1)}, u32[]{:S(2)}, u32[]{:S(2)}) collective-permute-start(bf16[1152,128]{1,0:T(8,128)(2,1)S(1)} %get-tuple-element.43.base_ref.refs_2_), channel_id=1, source_target_pairs={{0,4},{4,8},{8,12},{1,5},{5,9},{9,13},{2,6},{6,10},{10,14},{3,7},{... | collective-permute-start | bytes 884744 | tf_op jit(solution)/shard_map/ppermute | solution.py:652
  11.6 1.4 pick_own.1.in_ref
  13.0 5.4 %collective-permute-done.refs_1_ = bf16[288,1024]{1,0:T(8,128)(2,1)S(1)} collective-permute-done((bf16[288,1024]{1,0:T(8,128)(2,1)S(1)}, bf16[288,1024]{1,0:T(8,128)(2,1)S(1)}, u32[]{:S(2)}, u32[]{:S(2)}) %collective-permute-start) | collective-permute-done | bytes 589856 | tf_op jit(solution)/shard_map/ppermute | solution.py:615
  18.6 5.8 %collective-permute-done.4.arrived_ref = bf16[1152,128]{1,0:T(8,128)(2,1)S(1)} collective-permute-done((bf16[1152,128]{1,0:T(8,128)(2,1)S(1)}, bf16[1152,128]{1,0:T(8,128)(2,1)S(1)}, u32[]{:S(2)}, u32[]{:S(2)}) %collective-permute-start.4) | collective-permute-done | bytes 294944 | tf_op jit(solution)/shard_map/ppermute | solution.py:652
  24.5 3.5 %collective-permute-start.6 = (bf16[1152,512]{1,0:T(8,128)(2,1)S(1)}, bf16[1152,512]{1,0:T(8,128)(2,1)S(1)}, u32[]{:S(2)}, u32[]{:S(2)}) collective-permute-start(bf16[1152,512]{1,0:T(8,128)(2,1)S(1)} %add_arrived.1.refs_1_.refs_4_.refs_6_.refs_3_.refs_10_.refs_5_), channel_id=1, source_target_pairs={{0,1},{1,2},{2,3},{4,5},{5,6},{6,7},{8,9},{9,10},{10,11},{12,13},{... | collective-permute-start | bytes 3538952 | tf_op jit(solution)/shard_map/ppermute | solution.py:621
  28.0 2.4 %collective-permute-start.7 = (bf16[1152,512]{1,0:T(8,128)(2,1)S(1)}, bf16[1152,512]{1,0:T(8,128)(2,1)S(1)}, u32[]{:S(2)}, u32[]{:S(2)}) collective-permute-start(bf16[1152,512]{1,0:T(8,128)(2,1)S(1)} %add_arrived.1.refs_1_.refs_4_.refs_6_.refs_3_.refs_10_.refs_5_), channel_id=1, source_target_pairs={{1,0},{2,1},{3,2},{5,4},{6,5},{7,6},{9,8},{10,9},{11,10},{13,12},{... | collective-permute-start | bytes 3538952 | tf_op jit(solution)/shard_map/ppermute | solution.py:621
  30.3 1.6 collective-permute-start.2
  31.9 1.9 collective-permute-start.3
  33.8 20.1 %collective-permute-done.6.refs_0_.refs_3_.refs_5_.came_r.refs_2_.refs_9_.refs_4_ = bf16[1152,512]{1,0:T(8,128)(2,1)S(1)} collective-permute-done((bf16[1152,512]{1,0:T(8,128)(2,1)S(1)}, bf16[1152,512]{1,0:T(8,128)(2,1)S(1)}, u32[]{:S(2)}, u32[]{:S(2)}) %collective-permute-start.6) | collective-permute-done | bytes 1179680 | tf_op jit(solution)/shard_map/ppermute | solution.py:621
  54.0 3.2 %collective-permute-done.7.refs_2_.refs_5_.refs_6_.came_l.refs_4_.refs_11_ = bf16[1152,512]{1,0:T(8,128)(2,1)S(1)} collective-permute-done((bf16[1152,512]{1,0:T(8,128)(2,1)S(1)}, bf16[1152,512]{1,0:T(8,128)(2,1)S(1)}, u32[]{:S(2)}, u32[]{:S(2)}) %collective-permute-start.7) | collective-permute-done | bytes 1179680 | tf_op jit(solution)/shard_map/ppermute | solution.py:621
  59.6 2.1 %collective-permute-start.12 = (bf16[2304,512]{1,0:T(8,128)(2,1)S(1)}, bf16[2304,512]{1,0:T(8,128)(2,1)S(1)}, u32[]{:S(2)}, u32[]{:S(2)}) collective-permute-start(bf16[2304,512]{1,0:T(8,128)(2,1)S(1)} %half_for_other_core.2.refs_4_), channel_id=1, source_target_pairs={{16,0},{17,1},{2,18},{3,19},{20,4},{21,5},{6,22},{7,23},{24,8},{25... | collective-permute-start | bytes 7077896 | tf_op jit(solution)/shard_map/ppermute | solution.py:704
  61.7 1.9 collective-permute-done.8.other_ref.refs_1_
  63.8 4.9 %collective-permute-start.10 = (bf16[592,512]{1,0:T(8,128)(2,1)S(1)}, bf16[592,512]{1,0:T(8,128)(2,1)S(1)}, u32[]{:S(2)}, u32[]{:S(2)}) collective-permute-start(bf16[592,512]{1,0:T(8,128)(2,1)S(1)} %get-tuple-element.47.dep_ref), channel_id=1, source_target_pairs={{0,1},{1,2},{2,3},{4,5},{5,6},{6,7},{8,9},{9,10},{10,11},{12,13},{... | collective-permute-start | bytes 1818632 | tf_op jit(solution)/shard_map/ppermute | solution.py:621
  68.7 1.9 collective-permute-start.11
  71.0 5.3 %collective-permute-start.15 = (bf16[592,512]{1,0:T(8,128)(2,1)S(1)}, bf16[592,512]{1,0:T(8,128)(2,1)S(1)}, u32[]{:S(2)}, u32[]{:S(2)}) collective-permute-start(bf16[592,512]{1,0:T(8,128)(2,1)S(1)} %get-tuple-element.49.refs_6_), channel_id=1, source_target_pairs={{0,1},{1,2},{2,3},{4,5},{5,6},{6,7},{8,9},{9,10},{10,11},{12,13},{... | collective-permute-start | bytes 1818632 | tf_op jit(solution)/shard_map/ppermute | solution.py:621
  76.3 1.9 collective-permute-start.16
  78.2 4.5 %collective-permute-done.10.came_r.refs_1_.refs_8_ = bf16[592,512]{1,0:T(8,128)(2,1)S(1)} collective-permute-done((bf16[592,512]{1,0:T(8,128)(2,1)S(1)}, bf16[592,512]{1,0:T(8,128)(2,1)S(1)}, u32[]{:S(2)}, u32[]{:S(2)}) %collective-permute-start.10) | collective-permute-done | bytes 606240 | tf_op jit(solution)/shard_map/ppermute | solution.py:621
  82.7 4.4 %collective-permute-done.11.came_l.refs_5_.refs_9_ = bf16[592,512]{1,0:T(8,128)(2,1)S(1)} collective-permute-done((bf16[592,512]{1,0:T(8,128)(2,1)S(1)}, bf16[592,512]{1,0:T(8,128)(2,1)S(1)}, u32[]{:S(2)}, u32[]{:S(2)}) %collective-permute-start.11) | collective-permute-done | bytes 606240 | tf_op jit(solution)/shard_map/ppermute | solution.py:621
  87.2 2.5 %line_step.8 = (bf16[592,512]{1,0:T(8,128)(2,1)S(1)}, bf16[592,512]{1,0:T(8,128)(2,1)S(1)}) custom-call(bf16[1152,1024]{1,0:T(8,128)(2,1)S(1)} %get-tuple-element.45.mine_ref.dep_ref.refs_0_, bf16[1152,1024]{1,0:T(8,128)(2,1)S(1)} %collective-permute-done.8.other_ref.refs_1_, bf16[1024,512]{1,0:T(8,128)(2,1)S(1)} %bitcast.8, ...), custom_call_target="tpu_custom_call" | custom-call | flops 1 | bytes 1 | tf_op jit(solution)/shard_map/line_step/pallas_call | solution.py:21
  89.7 1.9 collective-permute-start.13
  91.6 3.9 %collective-permute-start.14 = (bf16[592,512]{1,0:T(8,128)(2,1)S(1)}, bf16[592,512]{1,0:T(8,128)(2,1)S(1)}, u32[]{:S(2)}, u32[]{:S(2)}) collective-permute-start(bf16[592,512]{1,0:T(8,128)(2,1)S(1)} %get-tuple-element.52), channel_id=1, source_target_pairs={{1,0},{2,1},{3,2},{5,4},{6,5},{7,6},{9,8},{10,9},{11,10},{13,12},{... | collective-permute-start | bytes 1818632 | tf_op jit(solution)/shard_map/ppermute | solution.py:621
  96.4 3.8 %collective-permute-done.16.came_l.refs_12_.refs_13_ = bf16[592,512]{1,0:T(8,128)(2,1)S(1)} collective-permute-done((bf16[592,512]{1,0:T(8,128)(2,1)S(1)}, bf16[592,512]{1,0:T(8,128)(2,1)S(1)}, u32[]{:S(2)}, u32[]{:S(2)}) %collective-permute-start.16) | collective-permute-done | bytes 606240 | tf_op jit(solution)/shard_map/ppermute | solution.py:621
  100.2 2.5 %line_step.9 = (bf16[592,512]{1,0:T(8,128)(2,1)S(1)}, bf16[592,512]{1,0:T(8,128)(2,1)S(1)}) custom-call(bf16[1152,1024]{1,0:T(8,128)(2,1)S(1)} %get-tuple-element.46.mine_ref.refs_2_, bf16[1152,1024]{1,0:T(8,128)(2,1)S(1)} %collective-permute-done.9.other_ref.refs_3_, bf16[1024,512]{1,0:T(8,128)(2,1)S(1)} %bitcast.9, ...), custom_call_target="tpu_custom_call" | custom-call | flops 1 | bytes 1 | tf_op jit(solution)/shard_map/line_step/pallas_call | solution.py:21
  102.7 1.9 collective-permute-start.17
  104.6 3.9 %collective-permute-start.18 = (bf16[592,512]{1,0:T(8,128)(2,1)S(1)}, bf16[592,512]{1,0:T(8,128)(2,1)S(1)}, u32[]{:S(2)}, u32[]{:S(2)}) collective-permute-start(bf16[592,512]{1,0:T(8,128)(2,1)S(1)} %get-tuple-element.55), channel_id=1, source_target_pairs={{1,0},{2,1},{3,2},{5,4},{6,5},{7,6},{9,8},{10,9},{11,10},{13,12},{... | collective-permute-start | bytes 1818632 | tf_op jit(solution)/shard_map/ppermute | solution.py:621
  108.7 4.4 %collective-permute-done.14.came_l.refs_6_.refs_10_ = bf16[592,512]{1,0:T(8,128)(2,1)S(1)} collective-permute-done((bf16[592,512]{1,0:T(8,128)(2,1)S(1)}, bf16[592,512]{1,0:T(8,128)(2,1)S(1)}, u32[]{:S(2)}, u32[]{:S(2)}) %collective-permute-start.14) | collective-permute-done | bytes 606240 | tf_op jit(solution)/shard_map/ppermute | solution.py:621
  113.2 4.8 %line_step.10 = (bf16[592,512]{1,0:T(8,128)(2,1)S(1)}, bf16[592,512]{1,0:T(8,128)(2,1)S(1)}) custom-call(bf16[1152,1024]{1,0:T(8,128)(2,1)S(1)} %get-tuple-element.45.mine_ref.dep_ref.refs_0_, bf16[1152,1024]{1,0:T(8,128)(2,1)S(1)} %collective-permute-done.8.other_ref.refs_1_, bf16[1024,512]{1,0:T(8,128)(2,1)S(1)} %bitcast.10, ...), custom_call_target="tpu_custom_call" | custom-call | flops 1 | bytes 1 | tf_op jit(solution)/shard_map/line_step/pallas_call | solution.py:21
  117.9 1.9 collective-permute-start.20
  119.9 4.1 %collective-permute-start.21 = (bf16[592,512]{1,0:T(8,128)(2,1)S(1)}, bf16[592,512]{1,0:T(8,128)(2,1)S(1)}, u32[]{:S(2)}, u32[]{:S(2)}) collective-permute-start(bf16[592,512]{1,0:T(8,128)(2,1)S(1)} %get-tuple-element.59), channel_id=1, source_target_pairs={{1,0},{2,1},{3,2},{5,4},{6,5},{7,6},{9,8},{10,9},{11,10},{13,12},{... | collective-permute-start | bytes 1818632 | tf_op jit(solution)/shard_map/ppermute | solution.py:621
  124.0 2.2 %collective-permute-done.18.came_l.refs_13_.refs_14_ = bf16[592,512]{1,0:T(8,128)(2,1)S(1)} collective-permute-done((bf16[592,512]{1,0:T(8,128)(2,1)S(1)}, bf16[592,512]{1,0:T(8,128)(2,1)S(1)}, u32[]{:S(2)}, u32[]{:S(2)}) %collective-permute-start.18) | collective-permute-done | bytes 606240 | tf_op jit(solution)/shard_map/ppermute | solution.py:621
  126.2 4.8 %line_step.11 = (bf16[592,512]{1,0:T(8,128)(2,1)S(1)}, bf16[592,512]{1,0:T(8,128)(2,1)S(1)}) custom-call(bf16[1152,1024]{1,0:T(8,128)(2,1)S(1)} %get-tuple-element.46.mine_ref.refs_2_, bf16[1152,1024]{1,0:T(8,128)(2,1)S(1)} %collective-permute-done.9.other_ref.refs_3_, bf16[1024,512]{1,0:T(8,128)(2,1)S(1)} %bitcast.11, ...), custom_call_target="tpu_custom_call" | custom-call | flops 1 | bytes 1 | tf_op jit(solution)/shard_map/line_step/pallas_call | solution.py:21
  130.9 3.0 %collective-permute-done.20.r_ref = bf16[592,512]{1,0:T(8,128)(2,1)S(1)} collective-permute-done((bf16[592,512]{1,0:T(8,128)(2,1)S(1)}, bf16[592,512]{1,0:T(8,128)(2,1)S(1)}, u32[]{:S(2)}, u32[]{:S(2)}) %collective-permute-start.20) | collective-permute-done | bytes 606240 | tf_op jit(solution)/shard_map/ppermute | solution.py:621
  133.9 4.1 %collective-permute-done.21.l_ref = bf16[592,512]{1,0:T(8,128)(2,1)S(1)} collective-permute-done((bf16[592,512]{1,0:T(8,128)(2,1)S(1)}, bf16[592,512]{1,0:T(8,128)(2,1)S(1)}, u32[]{:S(2)}, u32[]{:S(2)}) %collective-permute-start.21) | collective-permute-done | bytes 606240 | tf_op jit(solution)/shard_map/ppermute | solution.py:621
  138.0 3.2 %grad_kept_last.2 = (f32[1152,512]{1,0:T(8,128)}, f32[8,128]{1,0:T(8,128)S(1)}) custom-call(bf16[1152,1024]{1,0:T(8,128)(2,1)S(1)} %get-tuple-element.45.mine_ref.dep_ref.refs_0_, bf16[1152,1024]{1,0:T(8,128)(2,1)S(1)} %collective-permute-done.8.other_ref.refs_1_, bf16[1024,512]{1,0:T(8,128)(2,1)S(1)} %bitcast.12, ...), custom_call_target="tpu_custom_call" | custom-call | flops 1 | bytes 1 | tf_op jit(solution)/shard_map/grad_kept_last/pallas_call | solution.py:21
  143.4 4.3 %collective-permute-done.23.other_ref = bf16[2304,512]{1,0:T(8,128)(2,1)S(1)} collective-permute-done((bf16[2304,512]{1,0:T(8,128)(2,1)S(1)}, bf16[2304,512]{1,0:T(8,128)(2,1)S(1)}, u32[]{:S(2)}, u32[]{:S(2)}) %collective-permute-start.23) | collective-permute-done | bytes 2359328 | tf_op jit(solution)/shard_map/ppermute | solution.py:704
  147.7 9.8 %grad_weight_partial.3 = (f32[576,1024]{1,0:T(8,128)S(1)}, bf16[592,1024]{1,0:T(8,128)(2,1)S(1)}, bf16[592,1024]{1,0:T(8,128)(2,1)S(1)}, bf16[592,1024]{1,0:T(8,128)(2,1)S(1)}) custom-call(bf16[1024,512]{1,0:T(8,128)(2,1)S(1)} %bitcast.13, bf16[1024,512]{1,0:T(8,128)(2,1)S(1)} %collective-permute-done.5.dep_ref.cot_other_ref, ...), custom_call_target="tpu_custom_call" | custom-call | flops 1 | bytes 1 | tf_op jit(solution)/shard_map/grad_weight_partial/pallas_call | solution.py:21
  157.5 3.5 %collective-permute-start.26 = (bf16[592,1024]{1,0:T(8,128)(2,1)S(1)}, bf16[592,1024]{1,0:T(8,128)(2,1)S(1)}, u32[]{:S(2)}, u32[]{:S(2)}) collective-permute-start(bf16[592,1024]{1,0:T(8,128)(2,1)S(1)} %get-tuple-element.69), channel_id=1, source_target_pairs={{2,6},{6,2},{10,14},{14,10},{3,7},{7,3},{11,15},{15,11},{16,20},{2... | collective-permute-start | bytes 3637256 | tf_op jit(solution)/shard_map/ppermute | solution.py:708
  161.0 2.3 %collective-permute-start.27 = (bf16[592,1024]{1,0:T(8,128)(2,1)S(1)}, bf16[592,1024]{1,0:T(8,128)(2,1)S(1)}, u32[]{:S(2)}, u32[]{:S(2)}) collective-permute-start(bf16[592,1024]{1,0:T(8,128)(2,1)S(1)} %get-tuple-element.70), channel_id=1, source_target_pairs={{2,10},{6,14},{10,2},{14,6},{3,11},{7,15},{11,3},{15,7},{16,24},{2... | collective-permute-start | bytes 3637256 | tf_op jit(solution)/shard_map/ppermute | solution.py:708
  163.3 3.4 %collective-permute-start.28 = (bf16[592,1024]{1,0:T(8,128)(2,1)S(1)}, bf16[592,1024]{1,0:T(8,128)(2,1)S(1)}, u32[]{:S(2)}, u32[]{:S(2)}) collective-permute-start(bf16[592,1024]{1,0:T(8,128)(2,1)S(1)} %get-tuple-element.71), channel_id=1, source_target_pairs={{2,14},{6,10},{10,6},{14,2},{3,15},{7,11},{11,7},{15,3},{16,28},{2... | collective-permute-start | bytes 3637256 | tf_op jit(solution)/shard_map/ppermute | solution.py:708
  166.7 1.9 collective-permute-start.24
  168.6 3.9 %collective-permute-start.25 = (bf16[592,512]{1,0:T(8,128)(2,1)S(1)}, bf16[592,512]{1,0:T(8,128)(2,1)S(1)}, u32[]{:S(2)}, u32[]{:S(2)}) collective-permute-start(bf16[592,512]{1,0:T(8,128)(2,1)S(1)} %get-tuple-element.65), channel_id=1, source_target_pairs={{1,0},{2,1},{3,2},{5,4},{6,5},{7,6},{9,8},{10,9},{11,10},{13,12},{... | collective-permute-start | bytes 1818632 | tf_op jit(solution)/shard_map/ppermute | solution.py:621
  172.6 7.5 %queries.1 = (bf16[1024,512]{1,0:T(8,128)(2,1)}, f32[8,128]{1,0:T(8,128)S(1)}) custom-call(bf16[1152,1024]{1,0:T(8,128)(2,1)S(1)} %get-tuple-element.45.mine_ref.dep_ref.refs_0_, bf16[1152,1024]{1,0:T(8,128)(2,1)S(1)} %collective-permute-done.8.other_ref.refs_1_, bf16[1152,1024]{1,0:T(8,128)(2,1)S(1)} %get-tuple-element.46.mine_ref.refs_2_, ...), custom_call_target="tpu_custom_call" | custom-call | flops 1 | bytes 1 | tf_op jit(solution)/shard_map/queries/pallas_call | solution.py:21
  182.7 3.2 %grad_kept_last.3 = (f32[1152,512]{1,0:T(8,128)}, f32[8,128]{1,0:T(8,128)S(1)}) custom-call(bf16[1152,1024]{1,0:T(8,128)(2,1)S(1)} %get-tuple-element.46.mine_ref.refs_2_, bf16[1152,1024]{1,0:T(8,128)(2,1)S(1)} %collective-permute-done.9.other_ref.refs_3_, bf16[1024,512]{1,0:T(8,128)(2,1)S(1)} %bitcast.14, ...), custom_call_target="tpu_custom_call", output_to_operand_aliasing={{0}: (5, {})} | custom-call | flops 1 | bytes 1 | tf_op jit(solution)/shard_map/grad_kept_last/pallas_call | solution.py:21
  186.0 6.5 %collective-permute-done.27.refs_1_ = bf16[592,1024]{1,0:T(8,128)(2,1)S(1)} collective-permute-done((bf16[592,1024]{1,0:T(8,128)(2,1)S(1)}, bf16[592,1024]{1,0:T(8,128)(2,1)S(1)}, u32[]{:S(2)}, u32[]{:S(2)}) %collective-permute-start.27) | collective-permute-done | bytes 1212448 | tf_op jit(solution)/shard_map/ppermute | solution.py:708
  192.4 5.6 %grad_weight_last.3 = (f32[576,1024]{1,0:T(8,128)}, f32[8,128]{1,0:T(8,128)}) custom-call(f32[576,1024]{1,0:T(8,128)S(1)} %get-tuple-element.62.refs_3_.own_ref, bf16[592,1024]{1,0:T(8,128)(2,1)S(1)} %collective-permute-done.26.refs_0_, bf16[592,1024]{1,0:T(8,128)(2,1)S(1)} %collective-permute-done.27.refs_1_, ...), custom_call_target="tpu_custom_call", output_to_operand_aliasing={{0}: (4, {})} | custom-call | flops 1 | bytes 1 | tf_op jit(solution)/shard_map/grad_weight_last/pallas_call | solution.py:21
  (40 shorter events, 11.8 us)
Async XLA Ops:
  0.6 23.7 %collective-permute-start.5 = (bf16[1024,512]{1,0:T(8,128)(2,1)}, bf16[1024,512]{1,0:T(8,128)(2,1)S(1)}, u32[]{:S(2)}, u32[]{:S(2)}) collective-permute-start(bf16[1024,512]{1,0:T(8,128)(2,1)} %bitcast.4), channel_id=1, source_target_pairs={{0,16},{16,0},{1,17},{17,1},{2,18},{18,2},{3,19},{19,3},{4,20},{20... | collective-permute-start | bytes 3145736 | tf_op jit(solution)/shard_map/ppermute | solution.py:618
  0.7 1.3 copy-start.2
  2.2 16.2 %collective-permute-start = (bf16[288,1024]{1,0:T(8,128)(2,1)S(1)}, bf16[288,1024]{1,0:T(8,128)(2,1)S(1)}, u32[]{:S(2)}, u32[]{:S(2)}) collective-permute-start(bf16[288,1024]{1,0:T(8,128)(2,1)S(1)} %get-tuple-element.39.refs_0_), channel_id=1, source_target_pairs={{0,4},{4,0},{8,12},{12,8},{1,5},{5,1},{9,13},{13,9},{2,6},{6,2},{1... | collective-permute-start | bytes 1769480 | tf_op jit(solution)/shard_map/ppermute | solution.py:615
  2.8 15.6 %collective-permute-start.1 = (bf16[288,1024]{1,0:T(8,128)(2,1)S(1)}, bf16[288,1024]{1,0:T(8,128)(2,1)S(1)}, u32[]{:S(2)}, u32[]{:S(2)}) collective-permute-start(bf16[288,1024]{1,0:T(8,128)(2,1)S(1)} %get-tuple-element.40.refs_2_), channel_id=1, source_target_pairs={{0,8},{4,12},{8,0},{12,4},{1,9},{5,13},{9,1},{13,5},{2,10},{6,14},... | collective-permute-start | bytes 1769480 | tf_op jit(solution)/shard_map/ppermute | solution.py:615
  4.4 1.7 copy-start.1
  6.0 0.7 copy-start.3
  8.2 16.1 %collective-permute-start.4 = (bf16[1152,128]{1,0:T(8,128)(2,1)S(1)}, bf16[1152,128]{1,0:T(8,128)(2,1)S(1)}, u32[]{:S(2)}, u32[]{:S(2)}) collective-permute-start(bf16[1152,128]{1,0:T(8,128)(2,1)S(1)} %get-tuple-element.43.base_ref.refs_2_), channel_id=1, source_target_pairs={{0,4},{4,8},{8,12},{1,5},{5,9},{9,13},{2,6},{6,10},{10,14},{3,7},{... | collective-permute-start | bytes 884744 | tf_op jit(solution)/shard_map/ppermute | solution.py:652
  24.5 29.5 %collective-permute-start.6 = (bf16[1152,512]{1,0:T(8,128)(2,1)S(1)}, bf16[1152,512]{1,0:T(8,128)(2,1)S(1)}, u32[]{:S(2)}, u32[]{:S(2)}) collective-permute-start(bf16[1152,512]{1,0:T(8,128)(2,1)S(1)} %add_arrived.1.refs_1_.refs_4_.refs_6_.refs_3_.refs_10_.refs_5_), channel_id=1, source_target_pairs={{0,1},{1,2},{2,3},{4,5},{5,6},{6,7},{8,9},{9,10},{10,11},{12,13},{... | collective-permute-start | bytes 3538952 | tf_op jit(solution)/shard_map/ppermute | solution.py:621
  28.0 29.2 %collective-permute-start.7 = (bf16[1152,512]{1,0:T(8,128)(2,1)S(1)}, bf16[1152,512]{1,0:T(8,128)(2,1)S(1)}, u32[]{:S(2)}, u32[]{:S(2)}) collective-permute-start(bf16[1152,512]{1,0:T(8,128)(2,1)S(1)} %add_arrived.1.refs_1_.refs_4_.refs_6_.refs_3_.refs_10_.refs_5_), channel_id=1, source_target_pairs={{1,0},{2,1},{3,2},{5,4},{6,5},{7,6},{9,8},{10,9},{11,10},{13,12},{... | collective-permute-start | bytes 3538952 | tf_op jit(solution)/shard_map/ppermute | solution.py:621
  30.3 27.1 %collective-permute-start.2 = (bf16[576,1024]{1,0:T(8,128)(2,1)S(1)}, bf16[576,1024]{1,0:T(8,128)(2,1)S(1)}, u32[]{:S(2)}, u32[]{:S(2)}) collective-permute-start(bf16[576,1024]{1,0:T(8,128)(2,1)S(1)} %get-tuple-element.41.refs_0_), channel_id=1, source_target_pairs={{0,8},{4,12},{8,0},{12,4},{1,9},{5,13},{9,1},{13,5},{2,10},{6,14},... | collective-permute-start | bytes 3538952 | tf_op jit(solution)/shard_map/ppermute | solution.py:615
  31.9 26.7 %collective-permute-start.3 = (bf16[576,1024]{1,0:T(8,128)(2,1)S(1)}, bf16[576,1024]{1,0:T(8,128)(2,1)S(1)}, u32[]{:S(2)}, u32[]{:S(2)}) collective-permute-start(bf16[576,1024]{1,0:T(8,128)(2,1)S(1)} %get-tuple-element.42.refs_1_), channel_id=1, source_target_pairs={{0,4},{4,0},{8,12},{12,8},{1,5},{5,1},{9,13},{13,9},{2,6},{6,2},{1... | collective-permute-start | bytes 3538952 | tf_op jit(solution)/shard_map/ppermute | solution.py:615
  57.4 6.2 %copy-start = (bf16[1,1024,512]{2,1,0:T(8,128)(2,1)S(1)}, bf16[1,1024,512]{2,1,0:T(8,128)(2,1)}, u32[]{:S(2)}) copy-start(bf16[1,1024,512]{2,1,0:T(8,128)(2,1)} %param.7) | copy-start | bytes 3145732
  59.0 4.6 %collective-permute-start.8 = (bf16[1152,1024]{1,0:T(8,128)(2,1)S(1)}, bf16[1152,1024]{1,0:T(8,128)(2,1)S(1)}, u32[]{:S(2)}, u32[]{:S(2)}) collective-permute-start(bf16[1152,1024]{1,0:T(8,128)(2,1)S(1)} %get-tuple-element.45.mine_ref.dep_ref.refs_0_), channel_id=1, source_target_pairs={{0,16},{16,0},{1,17},{17,1},{2,18},{18,2},{3,19},{19,3},{4,20},{20... | collective-permute-start | bytes 7077896 | tf_op jit(solution)/shard_map/ppermute | solution.py:618
  59.1 11.6 %collective-permute-start.9 = (bf16[1152,1024]{1,0:T(8,128)(2,1)S(1)}, bf16[1152,1024]{1,0:T(8,128)(2,1)S(1)}, u32[]{:S(2)}, u32[]{:S(2)}) collective-permute-start(bf16[1152,1024]{1,0:T(8,128)(2,1)S(1)} %get-tuple-element.46.mine_ref.refs_2_), channel_id=1, source_target_pairs={{0,16},{16,0},{1,17},{17,1},{2,18},{18,2},{3,19},{19,3},{4,20},{20... | collective-permute-start | bytes 7077896 | tf_op jit(solution)/shard_map/ppermute | solution.py:618
  59.6 18.6 %collective-permute-start.12 = (bf16[2304,512]{1,0:T(8,128)(2,1)S(1)}, bf16[2304,512]{1,0:T(8,128)(2,1)S(1)}, u32[]{:S(2)}, u32[]{:S(2)}) collective-permute-start(bf16[2304,512]{1,0:T(8,128)(2,1)S(1)} %half_for_other_core.2.refs_4_), channel_id=1, source_target_pairs={{16,0},{17,1},{2,18},{3,19},{20,4},{21,5},{6,22},{7,23},{24,8},{25... | collective-permute-start | bytes 7077896 | tf_op jit(solution)/shard_map/ppermute | solution.py:704
  63.8 18.9 %collective-permute-start.10 = (bf16[592,512]{1,0:T(8,128)(2,1)S(1)}, bf16[592,512]{1,0:T(8,128)(2,1)S(1)}, u32[]{:S(2)}, u32[]{:S(2)}) collective-permute-start(bf16[592,512]{1,0:T(8,128)(2,1)S(1)} %get-tuple-element.47.dep_ref), channel_id=1, source_target_pairs={{0,1},{1,2},{2,3},{4,5},{5,6},{6,7},{8,9},{9,10},{10,11},{12,13},{... | collective-permute-start | bytes 1818632 | tf_op jit(solution)/shard_map/ppermute | solution.py:621
  68.7 18.5 %collective-permute-start.11 = (bf16[592,512]{1,0:T(8,128)(2,1)S(1)}, bf16[592,512]{1,0:T(8,128)(2,1)S(1)}, u32[]{:S(2)}, u32[]{:S(2)}) collective-permute-start(bf16[592,512]{1,0:T(8,128)(2,1)S(1)} %get-tuple-element.48), channel_id=1, source_target_pairs={{1,0},{2,1},{3,2},{5,4},{6,5},{7,6},{9,8},{10,9},{11,10},{13,12},{... | collective-permute-start | bytes 1818632 | tf_op jit(solution)/shard_map/ppermute | solution.py:621
  71.0 25.4 %collective-permute-start.15 = (bf16[592,512]{1,0:T(8,128)(2,1)S(1)}, bf16[592,512]{1,0:T(8,128)(2,1)S(1)}, u32[]{:S(2)}, u32[]{:S(2)}) collective-permute-start(bf16[592,512]{1,0:T(8,128)(2,1)S(1)} %get-tuple-element.49.refs_6_), channel_id=1, source_target_pairs={{0,1},{1,2},{2,3},{4,5},{5,6},{6,7},{8,9},{9,10},{10,11},{12,13},{... | collective-permute-start | bytes 1818632 | tf_op jit(solution)/shard_map/ppermute | solution.py:621
  76.3 23.9 %collective-permute-start.16 = (bf16[592,512]{1,0:T(8,128)(2,1)S(1)}, bf16[592,512]{1,0:T(8,128)(2,1)S(1)}, u32[]{:S(2)}, u32[]{:S(2)}) collective-permute-start(bf16[592,512]{1,0:T(8,128)(2,1)S(1)} %get-tuple-element.53), channel_id=1, source_target_pairs={{1,0},{2,1},{3,2},{5,4},{6,5},{7,6},{9,8},{10,9},{11,10},{13,12},{... | collective-permute-start | bytes 1818632 | tf_op jit(solution)/shard_map/ppermute | solution.py:621
  89.7 19.1 %collective-permute-start.13 = (bf16[592,512]{1,0:T(8,128)(2,1)S(1)}, bf16[592,512]{1,0:T(8,128)(2,1)S(1)}, u32[]{:S(2)}, u32[]{:S(2)}) collective-permute-start(bf16[592,512]{1,0:T(8,128)(2,1)S(1)} %get-tuple-element.51.dep_ref), channel_id=1, source_target_pairs={{0,1},{1,2},{2,3},{4,5},{5,6},{6,7},{8,9},{9,10},{10,11},{12,13},{... | collective-permute-start | bytes 1818632 | tf_op jit(solution)/shard_map/ppermute | solution.py:621
  91.6 21.6 %collective-permute-start.14 = (bf16[592,512]{1,0:T(8,128)(2,1)S(1)}, bf16[592,512]{1,0:T(8,128)(2,1)S(1)}, u32[]{:S(2)}, u32[]{:S(2)}) collective-permute-start(bf16[592,512]{1,0:T(8,128)(2,1)S(1)} %get-tuple-element.52), channel_id=1, source_target_pairs={{1,0},{2,1},{3,2},{5,4},{6,5},{7,6},{9,8},{10,9},{11,10},{13,12},{... | collective-permute-start | bytes 1818632 | tf_op jit(solution)/shard_map/ppermute | solution.py:621
  95.5 47.0 %collective-permute-start.19 = (bf16[1168,1024]{1,0:T(8,128)(2,1)S(1)}, bf16[1168,1024]{1,0:T(8,128)(2,1)S(1)}, u32[]{:S(2)}, u32[]{:S(2)}) collective-permute-start(bf16[1168,1024]{1,0:T(8,128)(2,1)S(1)} %get-tuple-element.56), channel_id=1, source_target_pairs={{0,4},{4,0},{8,12},{12,8},{1,5},{5,1},{9,13},{13,9},{18,22},{22,18... | collective-permute-start | bytes 7176200 | tf_op jit(solution)/shard_map/ppermute | solution.py:708
  102.7 21.3 %collective-permute-start.17 = (bf16[592,512]{1,0:T(8,128)(2,1)S(1)}, bf16[592,512]{1,0:T(8,128)(2,1)S(1)}, u32[]{:S(2)}, u32[]{:S(2)}) collective-permute-start(bf16[592,512]{1,0:T(8,128)(2,1)S(1)} %get-tuple-element.54.dep_ref), channel_id=1, source_target_pairs={{0,1},{1,2},{2,3},{4,5},{5,6},{6,7},{8,9},{9,10},{10,11},{12,13},{... | collective-permute-start | bytes 1818632 | tf_op jit(solution)/shard_map/ppermute | solution.py:621
  104.6 21.6 %collective-permute-start.18 = (bf16[592,512]{1,0:T(8,128)(2,1)S(1)}, bf16[592,512]{1,0:T(8,128)(2,1)S(1)}, u32[]{:S(2)}, u32[]{:S(2)}) collective-permute-start(bf16[592,512]{1,0:T(8,128)(2,1)S(1)} %get-tuple-element.55), channel_id=1, source_target_pairs={{1,0},{2,1},{3,2},{5,4},{6,5},{7,6},{9,8},{10,9},{11,10},{13,12},{... | collective-permute-start | bytes 1818632 | tf_op jit(solution)/shard_map/ppermute | solution.py:621
  117.9 16.0 %collective-permute-start.20 = (bf16[592,512]{1,0:T(8,128)(2,1)S(1)}, bf16[592,512]{1,0:T(8,128)(2,1)S(1)}, u32[]{:S(2)}, u32[]{:S(2)}) collective-permute-start(bf16[592,512]{1,0:T(8,128)(2,1)S(1)} %get-tuple-element.58.dep_ref), channel_id=1, source_target_pairs={{0,1},{1,2},{2,3},{4,5},{5,6},{6,7},{8,9},{9,10},{10,11},{12,13},{... | collective-permute-start | bytes 1818632 | tf_op jit(solution)/shard_map/ppermute | solution.py:621
  119.9 18.1 %collective-permute-start.21 = (bf16[592,512]{1,0:T(8,128)(2,1)S(1)}, bf16[592,512]{1,0:T(8,128)(2,1)S(1)}, u32[]{:S(2)}, u32[]{:S(2)}) collective-permute-start(bf16[592,512]{1,0:T(8,128)(2,1)S(1)} %get-tuple-element.59), channel_id=1, source_target_pairs={{1,0},{2,1},{3,2},{5,4},{6,5},{7,6},{9,8},{10,9},{11,10},{13,12},{... | collective-permute-start | bytes 1818632 | tf_op jit(solution)/shard_map/ppermute | solution.py:621
  141.3 6.4 %collective-permute-start.23 = (bf16[2304,512]{1,0:T(8,128)(2,1)S(1)}, bf16[2304,512]{1,0:T(8,128)(2,1)S(1)}, u32[]{:S(2)}, u32[]{:S(2)}) collective-permute-start(bf16[2304,512]{1,0:T(8,128)(2,1)S(1)} %half_for_other_core.3.dep_ref), channel_id=1, source_target_pairs={{18,2},{19,3},{0,16},{1,17},{22,6},{23,7},{4,20},{5,21},{26,10},{2... | collective-permute-start | bytes 7077896 | tf_op jit(solution)/shard_map/ppermute | solution.py:704
  142.6 26.0 %collective-permute-start.22 = (bf16[592,1024]{1,0:T(8,128)(2,1)S(1)}, bf16[592,1024]{1,0:T(8,128)(2,1)S(1)}, u32[]{:S(2)}, u32[]{:S(2)}) collective-permute-start(bf16[592,1024]{1,0:T(8,128)(2,1)S(1)} %grad_weight_middle.1.refs_14_), channel_id=1, source_target_pairs={{0,8},{4,12},{8,0},{12,4},{1,9},{5,13},{9,1},{13,5},{18,26},{22,30... | collective-permute-start | bytes 3637256 | tf_op jit(solution)/shard_map/ppermute | solution.py:708
  157.5 28.5 %collective-permute-start.26 = (bf16[592,1024]{1,0:T(8,128)(2,1)S(1)}, bf16[592,1024]{1,0:T(8,128)(2,1)S(1)}, u32[]{:S(2)}, u32[]{:S(2)}) collective-permute-start(bf16[592,1024]{1,0:T(8,128)(2,1)S(1)} %get-tuple-element.69), channel_id=1, source_target_pairs={{2,6},{6,2},{10,14},{14,10},{3,7},{7,3},{11,15},{15,11},{16,20},{2... | collective-permute-start | bytes 3637256 | tf_op jit(solution)/shard_map/ppermute | solution.py:708
  161.0 31.4 %collective-permute-start.27 = (bf16[592,1024]{1,0:T(8,128)(2,1)S(1)}, bf16[592,1024]{1,0:T(8,128)(2,1)S(1)}, u32[]{:S(2)}, u32[]{:S(2)}) collective-permute-start(bf16[592,1024]{1,0:T(8,128)(2,1)S(1)} %get-tuple-element.70), channel_id=1, source_target_pairs={{2,10},{6,14},{10,2},{14,6},{3,11},{7,15},{11,3},{15,7},{16,24},{2... | collective-permute-start | bytes 3637256 | tf_op jit(solution)/shard_map/ppermute | solution.py:708
  163.3 29.2 %collective-permute-start.28 = (bf16[592,1024]{1,0:T(8,128)(2,1)S(1)}, bf16[592,1024]{1,0:T(8,128)(2,1)S(1)}, u32[]{:S(2)}, u32[]{:S(2)}) collective-permute-start(bf16[592,1024]{1,0:T(8,128)(2,1)S(1)} %get-tuple-element.71), channel_id=1, source_target_pairs={{2,14},{6,10},{10,6},{14,2},{3,15},{7,11},{11,7},{15,3},{16,28},{2... | collective-permute-start | bytes 3637256 | tf_op jit(solution)/shard_map/ppermute | solution.py:708
  166.7 14.8 %collective-permute-start.24 = (bf16[592,512]{1,0:T(8,128)(2,1)S(1)}, bf16[592,512]{1,0:T(8,128)(2,1)S(1)}, u32[]{:S(2)}, u32[]{:S(2)}) collective-permute-start(bf16[592,512]{1,0:T(8,128)(2,1)S(1)} %get-tuple-element.60.dep_ref), channel_id=1, source_target_pairs={{0,1},{1,2},{2,3},{4,5},{5,6},{6,7},{8,9},{9,10},{10,11},{12,13},{... | collective-permute-start | bytes 1818632 | tf_op jit(solution)/shard_map/ppermute | solution.py:621
  168.6 14.1 %collective-permute-start.25 = (bf16[592,512]{1,0:T(8,128)(2,1)S(1)}, bf16[592,512]{1,0:T(8,128)(2,1)S(1)}, u32[]{:S(2)}, u32[]{:S(2)}) collective-permute-start(bf16[592,512]{1,0:T(8,128)(2,1)S(1)} %get-tuple-element.65), channel_id=1, source_target_pairs={{1,0},{2,1},{3,2},{5,4},{6,5},{7,6},{9,8},{10,9},{11,10},{13,12},{... | collective-permute-start | bytes 1818632 | tf_op jit(solution)/shard_map/ppermute | solution.py:621

commit v8 on v7

--- a/solution.py
+++ b/solution.py
@@ -763,12 +763,12 @@
         step(1, 2)
         step(0, 3)
         step(1, 3)
+        queries = ask()
         finish_kept(0)
         theirs = give(every, False, [line_of(p) for p in every])
         first = second(*first)
         late = send_all(*weigh(every, False, [line_of(p) for p in every], theirs, DIRECT))
         finish_weight(*first)
-        queries = ask()
         finish_kept(1)
         finish_weight(*late)
     else:

time: 199 us -> 197 us (0.990)
  starting transfers between devices: 67.2 us -> 65.1 us
    ppermute x5, waiting for transfers between devices: 6.48 us -> 2.69 us  [to_rows(): return lax.ppermute(send, ('dp', 'row', 'col'), pairs)]
    ppermute x14, waiting for transfers between devices: 52.6 us -> 55.1 us  [along(): return lax.ppermute(value, 'col', [(c, c + step) for c in sources])]
    ppermute x14, starting transfers between devices: 43.4 us -> 41.4 us  [along(): return lax.ppermute(value, 'col', [(c, c + step) for c in sources])]
  transfers between devices with their start and end apart: 29 -> 29, of which waited for: 18 -> 18; matrix products, arithmetic and copies ran while one was open for 0% -> 0% of each run, Pallas kernels for 21% -> 22%
where the time goes in v8:
time: 197 us; the launch traced here: 196 us
  waiting for transfers between devices  77.7 us (39%)
  starting transfers between devices  65.1 us (33%)
  Pallas kernels  48.4 us (25%)
  local copies, waits for them, and re-layouts  3.63 us (2%)
    ppermute x14, waiting for transfers between devices, along(): return lax.ppermute(value, 'col', [(c, c + step) for c in sources])  55.1 us
    pallas_call x22, Pallas kernels, call(): pl.pallas_call(kernel, out_shape=out_shape, in_specs=in_specs, out_specs=...  48.4 us
    ppermute x14, starting transfers between devices, along(): return lax.ppermute(value, 'col', [(c, c + step) for c in sources])  41.4 us
    ppermute x5, starting transfers between devices, to_rows(): return lax.ppermute(send, ('dp', 'row', 'col'), pairs)  10.8 us
    ppermute x4, waiting for transfers between devices, to_row(): return lax.ppermute(value, 'row', [(r, r ^ step) for r in range(n_row)])  7.89 us
    ppermute x1, waiting for transfers between devices, per_device(): lax.ppermute(leaving, 'row', [(r, r + 1) for r in range(n_row - 1)])  5.76 us
    ppermute x4, starting transfers between devices, to_row(): return lax.ppermute(value, 'row', [(r, r ^ step) for r in range(n_row)])  5.63 us
    ppermute x2, waiting for transfers between devices, give(): return lax.ppermute(token, ('dp', 'col'), pairs)  4.35 us
  transfers between devices with their start and end apart: 29, of which 18 were waited for; matrix products, arithmetic and copies ran while one was open for 0% of the time, Pallas kernels for 22%

profile of v8, /device:TPU:18, one launch (start us, length us, event | category | flops | bytes accessed | tf_op | source)
XLA Modules:
  0.0 196.1 jit_solution(13357307273448063162)
XLA Ops:
  2.8 1.5 collective-permute-start.1
  4.4 1.7 copy-done.1
  6.7 1.5 pick_leaving.1
  8.2 3.3 %collective-permute-start.4 = (bf16[1152,128]{1,0:T(8,128)(2,1)S(1)}, bf16[1152,128]{1,0:T(8,128)(2,1)S(1)}, u32[]{:S(2)}, u32[]{:S(2)}) collective-permute-start(bf16[1152,128]{1,0:T(8,128)(2,1)S(1)} %get-tuple-element.43.base_ref.refs_2_), channel_id=1, source_target_pairs={{0,4},{4,8},{8,12},{1,5},{5,9},{9,13},{2,6},{6,10},{10,14},{3,7},{... | collective-permute-start | bytes 884744 | tf_op jit(solution)/shard_map/ppermute | solution.py:652
  13.0 5.4 %collective-permute-done.refs_1_ = bf16[288,1024]{1,0:T(8,128)(2,1)S(1)} collective-permute-done((bf16[288,1024]{1,0:T(8,128)(2,1)S(1)}, bf16[288,1024]{1,0:T(8,128)(2,1)S(1)}, u32[]{:S(2)}, u32[]{:S(2)}) %collective-permute-start) | collective-permute-done | bytes 589856 | tf_op jit(solution)/shard_map/ppermute | solution.py:615
  18.6 5.8 %collective-permute-done.4.arrived_ref = bf16[1152,128]{1,0:T(8,128)(2,1)S(1)} collective-permute-done((bf16[1152,128]{1,0:T(8,128)(2,1)S(1)}, bf16[1152,128]{1,0:T(8,128)(2,1)S(1)}, u32[]{:S(2)}, u32[]{:S(2)}) %collective-permute-start.4) | collective-permute-done | bytes 294944 | tf_op jit(solution)/shard_map/ppermute | solution.py:652
  24.5 2.4 %collective-permute-start.7 = (bf16[1152,512]{1,0:T(8,128)(2,1)S(1)}, bf16[1152,512]{1,0:T(8,128)(2,1)S(1)}, u32[]{:S(2)}, u32[]{:S(2)}) collective-permute-start(bf16[1152,512]{1,0:T(8,128)(2,1)S(1)} %add_arrived.1.refs_1_.refs_4_.refs_6_.refs_5_.refs_3_.refs_10_), channel_id=1, source_target_pairs={{1,0},{2,1},{3,2},{5,4},{6,5},{7,6},{9,8},{10,9},{11,10},{13,12},{... | collective-permute-start | bytes 3538952 | tf_op jit(solution)/shard_map/ppermute | solution.py:621
  26.8 3.6 %collective-permute-start.6 = (bf16[1152,512]{1,0:T(8,128)(2,1)S(1)}, bf16[1152,512]{1,0:T(8,128)(2,1)S(1)}, u32[]{:S(2)}, u32[]{:S(2)}) collective-permute-start(bf16[1152,512]{1,0:T(8,128)(2,1)S(1)} %add_arrived.1.refs_1_.refs_4_.refs_6_.refs_5_.refs_3_.refs_10_), channel_id=1, source_target_pairs={{0,1},{1,2},{2,3},{4,5},{5,6},{6,7},{8,9},{9,10},{10,11},{12,13},{... | collective-permute-start | bytes 3538952 | tf_op jit(solution)/shard_map/ppermute | solution.py:621
  30.4 1.6 collective-permute-start.2
  32.0 1.9 collective-permute-start.3
  33.9 20.0 %collective-permute-done.7.refs_2_.refs_5_.refs_6_.came_l.refs_4_.refs_11_ = bf16[1152,512]{1,0:T(8,128)(2,1)S(1)} collective-permute-done((bf16[1152,512]{1,0:T(8,128)(2,1)S(1)}, bf16[1152,512]{1,0:T(8,128)(2,1)S(1)}, u32[]{:S(2)}, u32[]{:S(2)}) %collective-permute-start.7) | collective-permute-done | bytes 1179680 | tf_op jit(solution)/shard_map/ppermute | solution.py:621
  54.0 2.1 %collective-permute-done.6.refs_0_.refs_3_.refs_5_.came_r.refs_4_.refs_2_.refs_9_ = bf16[1152,512]{1,0:T(8,128)(2,1)S(1)} collective-permute-done((bf16[1152,512]{1,0:T(8,128)(2,1)S(1)}, bf16[1152,512]{1,0:T(8,128)(2,1)S(1)}, u32[]{:S(2)}, u32[]{:S(2)}) %collective-permute-start.6) | collective-permute-done | bytes 1179680 | tf_op jit(solution)/shard_map/ppermute | solution.py:621
  59.6 2.1 %collective-permute-start.12 = (bf16[2304,512]{1,0:T(8,128)(2,1)S(1)}, bf16[2304,512]{1,0:T(8,128)(2,1)S(1)}, u32[]{:S(2)}, u32[]{:S(2)}) collective-permute-start(bf16[2304,512]{1,0:T(8,128)(2,1)S(1)} %half_for_other_core.2.refs_4_), channel_id=1, source_target_pairs={{16,0},{17,1},{2,18},{3,19},{20,4},{21,5},{6,22},{7,23},{24,8},{25... | collective-permute-start | bytes 7077896 | tf_op jit(solution)/shard_map/ppermute | solution.py:704
  61.8 1.9 collective-permute-done.8.other_ref.refs_1_
  63.9 2.3 %collective-permute-start.11 = (bf16[592,512]{1,0:T(8,128)(2,1)S(1)}, bf16[592,512]{1,0:T(8,128)(2,1)S(1)}, u32[]{:S(2)}, u32[]{:S(2)}) collective-permute-start(bf16[592,512]{1,0:T(8,128)(2,1)S(1)} %get-tuple-element.48), channel_id=1, source_target_pairs={{1,0},{2,1},{3,2},{5,4},{6,5},{7,6},{9,8},{10,9},{11,10},{13,12},{... | collective-permute-start | bytes 1818632 | tf_op jit(solution)/shard_map/ppermute | solution.py:621
  66.2 3.6 %collective-permute-start.10 = (bf16[592,512]{1,0:T(8,128)(2,1)S(1)}, bf16[592,512]{1,0:T(8,128)(2,1)S(1)}, u32[]{:S(2)}, u32[]{:S(2)}) collective-permute-start(bf16[592,512]{1,0:T(8,128)(2,1)S(1)} %get-tuple-element.47.dep_ref), channel_id=1, source_target_pairs={{0,1},{1,2},{2,3},{4,5},{5,6},{6,7},{8,9},{9,10},{10,11},{12,13},{... | collective-permute-start | bytes 1818632 | tf_op jit(solution)/shard_map/ppermute | solution.py:621
  70.1 2.3 %collective-permute-start.16 = (bf16[592,512]{1,0:T(8,128)(2,1)S(1)}, bf16[592,512]{1,0:T(8,128)(2,1)S(1)}, u32[]{:S(2)}, u32[]{:S(2)}) collective-permute-start(bf16[592,512]{1,0:T(8,128)(2,1)S(1)} %get-tuple-element.53), channel_id=1, source_target_pairs={{1,0},{2,1},{3,2},{5,4},{6,5},{7,6},{9,8},{10,9},{11,10},{13,12},{... | collective-permute-start | bytes 1818632 | tf_op jit(solution)/shard_map/ppermute | solution.py:621
  72.3 3.6 %collective-permute-start.15 = (bf16[592,512]{1,0:T(8,128)(2,1)S(1)}, bf16[592,512]{1,0:T(8,128)(2,1)S(1)}, u32[]{:S(2)}, u32[]{:S(2)}) collective-permute-start(bf16[592,512]{1,0:T(8,128)(2,1)S(1)} %get-tuple-element.49.refs_6_), channel_id=1, source_target_pairs={{0,1},{1,2},{2,3},{4,5},{5,6},{6,7},{8,9},{9,10},{10,11},{12,13},{... | collective-permute-start | bytes 1818632 | tf_op jit(solution)/shard_map/ppermute | solution.py:621
  76.0 6.3 %collective-permute-done.11.came_l.refs_9_.refs_5_ = bf16[592,512]{1,0:T(8,128)(2,1)S(1)} collective-permute-done((bf16[592,512]{1,0:T(8,128)(2,1)S(1)}, bf16[592,512]{1,0:T(8,128)(2,1)S(1)}, u32[]{:S(2)}, u32[]{:S(2)}) %collective-permute-start.11) | collective-permute-done | bytes 606240 | tf_op jit(solution)/shard_map/ppermute | solution.py:621
  82.3 2.3 %collective-permute-done.10.came_r.refs_8_.refs_1_ = bf16[592,512]{1,0:T(8,128)(2,1)S(1)} collective-permute-done((bf16[592,512]{1,0:T(8,128)(2,1)S(1)}, bf16[592,512]{1,0:T(8,128)(2,1)S(1)}, u32[]{:S(2)}, u32[]{:S(2)}) %collective-permute-start.10) | collective-permute-done | bytes 606240 | tf_op jit(solution)/shard_map/ppermute | solution.py:621
  84.6 2.5 %line_step.8 = (bf16[592,512]{1,0:T(8,128)(2,1)S(1)}, bf16[592,512]{1,0:T(8,128)(2,1)S(1)}) custom-call(bf16[1152,1024]{1,0:T(8,128)(2,1)S(1)} %get-tuple-element.45.mine_ref.dep_ref.refs_0_, bf16[1152,1024]{1,0:T(8,128)(2,1)S(1)} %collective-permute-done.8.other_ref.refs_1_, bf16[1024,512]{1,0:T(8,128)(2,1)S(1)} %bitcast.8, ...), custom_call_target="tpu_custom_call" | custom-call | flops 1 | bytes 1 | tf_op jit(solution)/shard_map/line_step/pallas_call | solution.py:21
  87.1 3.8 %collective-permute-start.14 = (bf16[592,512]{1,0:T(8,128)(2,1)S(1)}, bf16[592,512]{1,0:T(8,128)(2,1)S(1)}, u32[]{:S(2)}, u32[]{:S(2)}) collective-permute-start(bf16[592,512]{1,0:T(8,128)(2,1)S(1)} %get-tuple-element.52), channel_id=1, source_target_pairs={{1,0},{2,1},{3,2},{5,4},{6,5},{7,6},{9,8},{10,9},{11,10},{13,12},{... | collective-permute-start | bytes 1818632 | tf_op jit(solution)/shard_map/ppermute | solution.py:621
  91.0 2.0 %collective-permute-start.13 = (bf16[592,512]{1,0:T(8,128)(2,1)S(1)}, bf16[592,512]{1,0:T(8,128)(2,1)S(1)}, u32[]{:S(2)}, u32[]{:S(2)}) collective-permute-start(bf16[592,512]{1,0:T(8,128)(2,1)S(1)} %get-tuple-element.51.dep_ref), channel_id=1, source_target_pairs={{0,1},{1,2},{2,3},{4,5},{5,6},{6,7},{8,9},{9,10},{10,11},{12,13},{... | collective-permute-start | bytes 1818632 | tf_op jit(solution)/shard_map/ppermute | solution.py:621
  95.3 2.3 %collective-permute-done.15.came_r.refs_12_.refs_8_ = bf16[592,512]{1,0:T(8,128)(2,1)S(1)} collective-permute-done((bf16[592,512]{1,0:T(8,128)(2,1)S(1)}, bf16[592,512]{1,0:T(8,128)(2,1)S(1)}, u32[]{:S(2)}, u32[]{:S(2)}) %collective-permute-start.15) | collective-permute-done | bytes 606240 | tf_op jit(solution)/shard_map/ppermute | solution.py:621
  97.6 2.5 %line_step.9 = (bf16[592,512]{1,0:T(8,128)(2,1)S(1)}, bf16[592,512]{1,0:T(8,128)(2,1)S(1)}) custom-call(bf16[1152,1024]{1,0:T(8,128)(2,1)S(1)} %get-tuple-element.46.mine_ref.refs_2_, bf16[1152,1024]{1,0:T(8,128)(2,1)S(1)} %collective-permute-done.9.other_ref.refs_3_, bf16[1024,512]{1,0:T(8,128)(2,1)S(1)} %bitcast.9, ...), custom_call_target="tpu_custom_call" | custom-call | flops 1 | bytes 1 | tf_op jit(solution)/shard_map/line_step/pallas_call | solution.py:21
  100.1 3.8 %collective-permute-start.18 = (bf16[592,512]{1,0:T(8,128)(2,1)S(1)}, bf16[592,512]{1,0:T(8,128)(2,1)S(1)}, u32[]{:S(2)}, u32[]{:S(2)}) collective-permute-start(bf16[592,512]{1,0:T(8,128)(2,1)S(1)} %get-tuple-element.55), channel_id=1, source_target_pairs={{1,0},{2,1},{3,2},{5,4},{6,5},{7,6},{9,8},{10,9},{11,10},{13,12},{... | collective-permute-start | bytes 1818632 | tf_op jit(solution)/shard_map/ppermute | solution.py:621
  103.9 2.1 %collective-permute-start.17 = (bf16[592,512]{1,0:T(8,128)(2,1)S(1)}, bf16[592,512]{1,0:T(8,128)(2,1)S(1)}, u32[]{:S(2)}, u32[]{:S(2)}) collective-permute-start(bf16[592,512]{1,0:T(8,128)(2,1)S(1)} %get-tuple-element.54.dep_ref), channel_id=1, source_target_pairs={{0,1},{1,2},{2,3},{4,5},{5,6},{6,7},{8,9},{9,10},{10,11},{12,13},{... | collective-permute-start | bytes 1818632 | tf_op jit(solution)/shard_map/ppermute | solution.py:621
  106.0 2.3 %collective-permute-done.14.came_l.refs_10_.refs_6_ = bf16[592,512]{1,0:T(8,128)(2,1)S(1)} collective-permute-done((bf16[592,512]{1,0:T(8,128)(2,1)S(1)}, bf16[592,512]{1,0:T(8,128)(2,1)S(1)}, u32[]{:S(2)}, u32[]{:S(2)}) %collective-permute-start.14) | collective-permute-done | bytes 606240 | tf_op jit(solution)/shard_map/ppermute | solution.py:621
  108.3 2.3 %collective-permute-done.13.came_r.refs_7_.refs_0_ = bf16[592,512]{1,0:T(8,128)(2,1)S(1)} collective-permute-done((bf16[592,512]{1,0:T(8,128)(2,1)S(1)}, bf16[592,512]{1,0:T(8,128)(2,1)S(1)}, u32[]{:S(2)}, u32[]{:S(2)}) %collective-permute-start.13) | collective-permute-done | bytes 606240 | tf_op jit(solution)/shard_map/ppermute | solution.py:621
  110.6 4.8 %line_step.10 = (bf16[592,512]{1,0:T(8,128)(2,1)S(1)}, bf16[592,512]{1,0:T(8,128)(2,1)S(1)}) custom-call(bf16[1152,1024]{1,0:T(8,128)(2,1)S(1)} %get-tuple-element.45.mine_ref.dep_ref.refs_0_, bf16[1152,1024]{1,0:T(8,128)(2,1)S(1)} %collective-permute-done.8.other_ref.refs_1_, bf16[1024,512]{1,0:T(8,128)(2,1)S(1)} %bitcast.10, ...), custom_call_target="tpu_custom_call" | custom-call | flops 1 | bytes 1 | tf_op jit(solution)/shard_map/line_step/pallas_call | solution.py:21
  115.4 3.8 %collective-permute-start.22 = (bf16[592,512]{1,0:T(8,128)(2,1)S(1)}, bf16[592,512]{1,0:T(8,128)(2,1)S(1)}, u32[]{:S(2)}, u32[]{:S(2)}) collective-permute-start(bf16[592,512]{1,0:T(8,128)(2,1)S(1)} %get-tuple-element.60), channel_id=1, source_target_pairs={{1,0},{2,1},{3,2},{5,4},{6,5},{7,6},{9,8},{10,9},{11,10},{13,12},{... | collective-permute-start | bytes 1818632 | tf_op jit(solution)/shard_map/ppermute | solution.py:621
  119.2 2.3 %collective-permute-start.21 = (bf16[592,512]{1,0:T(8,128)(2,1)S(1)}, bf16[592,512]{1,0:T(8,128)(2,1)S(1)}, u32[]{:S(2)}, u32[]{:S(2)}) collective-permute-start(bf16[592,512]{1,0:T(8,128)(2,1)S(1)} %get-tuple-element.56.dep_ref), channel_id=1, source_target_pairs={{0,1},{1,2},{2,3},{4,5},{5,6},{6,7},{8,9},{9,10},{10,11},{12,13},{... | collective-permute-start | bytes 1818632 | tf_op jit(solution)/shard_map/ppermute | solution.py:621
  121.5 2.1 %collective-permute-done.17.came_r.refs_11_.refs_7_ = bf16[592,512]{1,0:T(8,128)(2,1)S(1)} collective-permute-done((bf16[592,512]{1,0:T(8,128)(2,1)S(1)}, bf16[592,512]{1,0:T(8,128)(2,1)S(1)}, u32[]{:S(2)}, u32[]{:S(2)}) %collective-permute-start.17) | collective-permute-done | bytes 606240 | tf_op jit(solution)/shard_map/ppermute | solution.py:621
  123.6 4.8 %line_step.11 = (bf16[592,512]{1,0:T(8,128)(2,1)S(1)}, bf16[592,512]{1,0:T(8,128)(2,1)S(1)}) custom-call(bf16[1152,1024]{1,0:T(8,128)(2,1)S(1)} %get-tuple-element.46.mine_ref.refs_2_, bf16[1152,1024]{1,0:T(8,128)(2,1)S(1)} %collective-permute-done.9.other_ref.refs_3_, bf16[1024,512]{1,0:T(8,128)(2,1)S(1)} %bitcast.11, ...), custom_call_target="tpu_custom_call" | custom-call | flops 1 | bytes 1 | tf_op jit(solution)/shard_map/line_step/pallas_call | solution.py:21
  128.4 7.5 %queries.1 = (bf16[1024,512]{1,0:T(8,128)(2,1)}, f32[8,128]{1,0:T(8,128)S(1)}) custom-call(bf16[1152,1024]{1,0:T(8,128)(2,1)S(1)} %get-tuple-element.45.mine_ref.dep_ref.refs_0_, bf16[1152,1024]{1,0:T(8,128)(2,1)S(1)} %collective-permute-done.8.other_ref.refs_1_, bf16[1152,1024]{1,0:T(8,128)(2,1)S(1)} %get-tuple-element.46.mine_ref.refs_2_, ...), custom_call_target="tpu_custom_call" | custom-call | flops 1 | bytes 1 | tf_op jit(solution)/shard_map/queries/pallas_call | solution.py:21
  135.9 3.3 %grad_kept_last.2 = (f32[1152,512]{1,0:T(8,128)}, f32[8,128]{1,0:T(8,128)S(1)}) custom-call(bf16[1152,1024]{1,0:T(8,128)(2,1)S(1)} %get-tuple-element.45.mine_ref.dep_ref.refs_0_, bf16[1152,1024]{1,0:T(8,128)(2,1)S(1)} %collective-permute-done.8.other_ref.refs_1_, bf16[1024,512]{1,0:T(8,128)(2,1)S(1)} %bitcast.12, ...), custom_call_target="tpu_custom_call" | custom-call | flops 1 | bytes 1 | tf_op jit(solution)/shard_map/grad_kept_last/pallas_call | solution.py:21
  141.3 4.3 %collective-permute-done.25.other_ref = bf16[2304,512]{1,0:T(8,128)(2,1)S(1)} collective-permute-done((bf16[2304,512]{1,0:T(8,128)(2,1)S(1)}, bf16[2304,512]{1,0:T(8,128)(2,1)S(1)}, u32[]{:S(2)}, u32[]{:S(2)}) %collective-permute-start.25) | collective-permute-done | bytes 2359328 | tf_op jit(solution)/shard_map/ppermute | solution.py:704
  145.6 9.8 %grad_weight_partial.3 = (f32[576,1024]{1,0:T(8,128)S(1)}, bf16[592,1024]{1,0:T(8,128)(2,1)S(1)}, bf16[592,1024]{1,0:T(8,128)(2,1)S(1)}, bf16[592,1024]{1,0:T(8,128)(2,1)S(1)}) custom-call(bf16[1024,512]{1,0:T(8,128)(2,1)S(1)} %bitcast.13, bf16[1024,512]{1,0:T(8,128)(2,1)S(1)} %collective-permute-done.5.dep_ref.cot_other_ref, ...), custom_call_target="tpu_custom_call" | custom-call | flops 1 | bytes 1 | tf_op jit(solution)/shard_map/grad_weight_partial/pallas_call | solution.py:21
  155.4 3.5 %collective-permute-start.26 = (bf16[592,1024]{1,0:T(8,128)(2,1)S(1)}, bf16[592,1024]{1,0:T(8,128)(2,1)S(1)}, u32[]{:S(2)}, u32[]{:S(2)}) collective-permute-start(bf16[592,1024]{1,0:T(8,128)(2,1)S(1)} %get-tuple-element.69), channel_id=1, source_target_pairs={{2,6},{6,2},{10,14},{14,10},{3,7},{7,3},{11,15},{15,11},{16,20},{2... | collective-permute-start | bytes 3637256 | tf_op jit(solution)/shard_map/ppermute | solution.py:708
  158.9 2.3 %collective-permute-start.27 = (bf16[592,1024]{1,0:T(8,128)(2,1)S(1)}, bf16[592,1024]{1,0:T(8,128)(2,1)S(1)}, u32[]{:S(2)}, u32[]{:S(2)}) collective-permute-start(bf16[592,1024]{1,0:T(8,128)(2,1)S(1)} %get-tuple-element.70), channel_id=1, source_target_pairs={{2,10},{6,14},{10,2},{14,6},{3,11},{7,15},{11,3},{15,7},{16,24},{2... | collective-permute-start | bytes 3637256 | tf_op jit(solution)/shard_map/ppermute | solution.py:708
  161.2 3.4 %collective-permute-start.28 = (bf16[592,1024]{1,0:T(8,128)(2,1)S(1)}, bf16[592,1024]{1,0:T(8,128)(2,1)S(1)}, u32[]{:S(2)}, u32[]{:S(2)}) collective-permute-start(bf16[592,1024]{1,0:T(8,128)(2,1)S(1)} %get-tuple-element.71), channel_id=1, source_target_pairs={{2,14},{6,10},{10,6},{14,2},{3,15},{7,11},{11,7},{15,3},{16,28},{2... | collective-permute-start | bytes 3637256 | tf_op jit(solution)/shard_map/ppermute | solution.py:708
  164.6 1.9 collective-permute-start.20
  166.6 4.0 %collective-permute-start.19 = (bf16[592,512]{1,0:T(8,128)(2,1)S(1)}, bf16[592,512]{1,0:T(8,128)(2,1)S(1)}, u32[]{:S(2)}, u32[]{:S(2)}) collective-permute-start(bf16[592,512]{1,0:T(8,128)(2,1)S(1)} %get-tuple-element.57.refs_15_), channel_id=1, source_target_pairs={{0,1},{1,2},{2,3},{4,5},{5,6},{6,7},{8,9},{9,10},{10,11},{12,13},{... | collective-permute-start | bytes 1818632 | tf_op jit(solution)/shard_map/ppermute | solution.py:621
  170.6 9.7 %collective-permute-done.20.l_ref = bf16[592,512]{1,0:T(8,128)(2,1)S(1)} collective-permute-done((bf16[592,512]{1,0:T(8,128)(2,1)S(1)}, bf16[592,512]{1,0:T(8,128)(2,1)S(1)}, u32[]{:S(2)}, u32[]{:S(2)}) %collective-permute-start.20) | collective-permute-done | bytes 606240 | tf_op jit(solution)/shard_map/ppermute | solution.py:621
  180.3 4.1 %collective-permute-done.19.r_ref = bf16[592,512]{1,0:T(8,128)(2,1)S(1)} collective-permute-done((bf16[592,512]{1,0:T(8,128)(2,1)S(1)}, bf16[592,512]{1,0:T(8,128)(2,1)S(1)}, u32[]{:S(2)}, u32[]{:S(2)}) %collective-permute-start.19) | collective-permute-done | bytes 606240 | tf_op jit(solution)/shard_map/ppermute | solution.py:621
  184.4 3.2 %grad_kept_last.3 = (f32[1152,512]{1,0:T(8,128)}, f32[8,128]{1,0:T(8,128)S(1)}) custom-call(bf16[1152,1024]{1,0:T(8,128)(2,1)S(1)} %get-tuple-element.46.mine_ref.refs_2_, bf16[1152,1024]{1,0:T(8,128)(2,1)S(1)} %collective-permute-done.9.other_ref.refs_3_, bf16[1024,512]{1,0:T(8,128)(2,1)S(1)} %bitcast.14, ...), custom_call_target="tpu_custom_call", output_to_operand_aliasing={{0}: (5, {})} | custom-call | flops 1 | bytes 1 | tf_op jit(solution)/shard_map/grad_kept_last/pallas_call | solution.py:21
  187.7 2.7 %collective-permute-done.27.refs_1_ = bf16[592,1024]{1,0:T(8,128)(2,1)S(1)} collective-permute-done((bf16[592,1024]{1,0:T(8,128)(2,1)S(1)}, bf16[592,1024]{1,0:T(8,128)(2,1)S(1)}, u32[]{:S(2)}, u32[]{:S(2)}) %collective-permute-start.27) | collective-permute-done | bytes 1212448 | tf_op jit(solution)/shard_map/ppermute | solution.py:708
  190.4 5.6 %grad_weight_last.3 = (f32[576,1024]{1,0:T(8,128)}, f32[8,128]{1,0:T(8,128)}) custom-call(f32[576,1024]{1,0:T(8,128)S(1)} %get-tuple-element.66.refs_3_.own_ref, bf16[592,1024]{1,0:T(8,128)(2,1)S(1)} %collective-permute-done.26.refs_0_, bf16[592,1024]{1,0:T(8,128)(2,1)S(1)} %collective-permute-done.27.refs_1_, ...), custom_call_target="tpu_custom_call", output_to_operand_aliasing={{0}: (4, {})} | custom-call | flops 1 | bytes 1 | tf_op jit(solution)/shard_map/grad_weight_last/pallas_call | solution.py:21
  (40 shorter events, 13.1 us)
Async XLA Ops:
  0.6 23.7 %collective-permute-start.5 = (bf16[1024,512]{1,0:T(8,128)(2,1)}, bf16[1024,512]{1,0:T(8,128)(2,1)S(1)}, u32[]{:S(2)}, u32[]{:S(2)}) collective-permute-start(bf16[1024,512]{1,0:T(8,128)(2,1)} %bitcast.4), channel_id=1, source_target_pairs={{0,16},{16,0},{1,17},{17,1},{2,18},{18,2},{3,19},{19,3},{4,20},{20... | collective-permute-start | bytes 3145736 | tf_op jit(solution)/shard_map/ppermute | solution.py:618
  0.7 1.3 copy-start.2
  2.2 16.2 %collective-permute-start = (bf16[288,1024]{1,0:T(8,128)(2,1)S(1)}, bf16[288,1024]{1,0:T(8,128)(2,1)S(1)}, u32[]{:S(2)}, u32[]{:S(2)}) collective-permute-start(bf16[288,1024]{1,0:T(8,128)(2,1)S(1)} %get-tuple-element.39.refs_0_), channel_id=1, source_target_pairs={{0,4},{4,0},{8,12},{12,8},{1,5},{5,1},{9,13},{13,9},{2,6},{6,2},{1... | collective-permute-start | bytes 1769480 | tf_op jit(solution)/shard_map/ppermute | solution.py:615
  2.8 15.6 %collective-permute-start.1 = (bf16[288,1024]{1,0:T(8,128)(2,1)S(1)}, bf16[288,1024]{1,0:T(8,128)(2,1)S(1)}, u32[]{:S(2)}, u32[]{:S(2)}) collective-permute-start(bf16[288,1024]{1,0:T(8,128)(2,1)S(1)} %get-tuple-element.40.refs_2_), channel_id=1, source_target_pairs={{0,8},{4,12},{8,0},{12,4},{1,9},{5,13},{9,1},{13,5},{2,10},{6,14},... | collective-permute-start | bytes 1769480 | tf_op jit(solution)/shard_map/ppermute | solution.py:615
  4.4 1.7 copy-start.1
  6.0 0.7 copy-start.3
  8.2 16.1 %collective-permute-start.4 = (bf16[1152,128]{1,0:T(8,128)(2,1)S(1)}, bf16[1152,128]{1,0:T(8,128)(2,1)S(1)}, u32[]{:S(2)}, u32[]{:S(2)}) collective-permute-start(bf16[1152,128]{1,0:T(8,128)(2,1)S(1)} %get-tuple-element.43.base_ref.refs_2_), channel_id=1, source_target_pairs={{0,4},{4,8},{8,12},{1,5},{5,9},{9,13},{2,6},{6,10},{10,14},{3,7},{... | collective-permute-start | bytes 884744 | tf_op jit(solution)/shard_map/ppermute | solution.py:652
  24.5 29.5 %collective-permute-start.7 = (bf16[1152,512]{1,0:T(8,128)(2,1)S(1)}, bf16[1152,512]{1,0:T(8,128)(2,1)S(1)}, u32[]{:S(2)}, u32[]{:S(2)}) collective-permute-start(bf16[1152,512]{1,0:T(8,128)(2,1)S(1)} %add_arrived.1.refs_1_.refs_4_.refs_6_.refs_5_.refs_3_.refs_10_), channel_id=1, source_target_pairs={{1,0},{2,1},{3,2},{5,4},{6,5},{7,6},{9,8},{10,9},{11,10},{13,12},{... | collective-permute-start | bytes 3538952 | tf_op jit(solution)/shard_map/ppermute | solution.py:621
  26.8 29.2 %collective-permute-start.6 = (bf16[1152,512]{1,0:T(8,128)(2,1)S(1)}, bf16[1152,512]{1,0:T(8,128)(2,1)S(1)}, u32[]{:S(2)}, u32[]{:S(2)}) collective-permute-start(bf16[1152,512]{1,0:T(8,128)(2,1)S(1)} %add_arrived.1.refs_1_.refs_4_.refs_6_.refs_5_.refs_3_.refs_10_), channel_id=1, source_target_pairs={{0,1},{1,2},{2,3},{4,5},{5,6},{6,7},{8,9},{9,10},{10,11},{12,13},{... | collective-permute-start | bytes 3538952 | tf_op jit(solution)/shard_map/ppermute | solution.py:621
  30.4 27.1 %collective-permute-start.2 = (bf16[576,1024]{1,0:T(8,128)(2,1)S(1)}, bf16[576,1024]{1,0:T(8,128)(2,1)S(1)}, u32[]{:S(2)}, u32[]{:S(2)}) collective-permute-start(bf16[576,1024]{1,0:T(8,128)(2,1)S(1)} %get-tuple-element.41.refs_0_), channel_id=1, source_target_pairs={{0,8},{4,12},{8,0},{12,4},{1,9},{5,13},{9,1},{13,5},{2,10},{6,14},... | collective-permute-start | bytes 3538952 | tf_op jit(solution)/shard_map/ppermute | solution.py:615
  32.0 26.7 %collective-permute-start.3 = (bf16[576,1024]{1,0:T(8,128)(2,1)S(1)}, bf16[576,1024]{1,0:T(8,128)(2,1)S(1)}, u32[]{:S(2)}, u32[]{:S(2)}) collective-permute-start(bf16[576,1024]{1,0:T(8,128)(2,1)S(1)} %get-tuple-element.42.refs_1_), channel_id=1, source_target_pairs={{0,4},{4,0},{8,12},{12,8},{1,5},{5,1},{9,13},{13,9},{2,6},{6,2},{1... | collective-permute-start | bytes 3538952 | tf_op jit(solution)/shard_map/ppermute | solution.py:615
  56.2 7.4 %copy-start = (bf16[1,1024,512]{2,1,0:T(8,128)(2,1)S(1)}, bf16[1,1024,512]{2,1,0:T(8,128)(2,1)}, u32[]{:S(2)}) copy-start(bf16[1,1024,512]{2,1,0:T(8,128)(2,1)} %param.7) | copy-start | bytes 3145732
  59.1 4.6 %collective-permute-start.8 = (bf16[1152,1024]{1,0:T(8,128)(2,1)S(1)}, bf16[1152,1024]{1,0:T(8,128)(2,1)S(1)}, u32[]{:S(2)}, u32[]{:S(2)}) collective-permute-start(bf16[1152,1024]{1,0:T(8,128)(2,1)S(1)} %get-tuple-element.45.mine_ref.dep_ref.refs_0_), channel_id=1, source_target_pairs={{0,16},{16,0},{1,17},{17,1},{2,18},{18,2},{3,19},{19,3},{4,20},{20... | collective-permute-start | bytes 7077896 | tf_op jit(solution)/shard_map/ppermute | solution.py:618
  59.1 10.6 %collective-permute-start.9 = (bf16[1152,1024]{1,0:T(8,128)(2,1)S(1)}, bf16[1152,1024]{1,0:T(8,128)(2,1)S(1)}, u32[]{:S(2)}, u32[]{:S(2)}) collective-permute-start(bf16[1152,1024]{1,0:T(8,128)(2,1)S(1)} %get-tuple-element.46.mine_ref.refs_2_), channel_id=1, source_target_pairs={{0,16},{16,0},{1,17},{17,1},{2,18},{18,2},{3,19},{19,3},{4,20},{20... | collective-permute-start | bytes 7077896 | tf_op jit(solution)/shard_map/ppermute | solution.py:618
  59.6 16.3 %collective-permute-start.12 = (bf16[2304,512]{1,0:T(8,128)(2,1)S(1)}, bf16[2304,512]{1,0:T(8,128)(2,1)S(1)}, u32[]{:S(2)}, u32[]{:S(2)}) collective-permute-start(bf16[2304,512]{1,0:T(8,128)(2,1)S(1)} %half_for_other_core.2.refs_4_), channel_id=1, source_target_pairs={{16,0},{17,1},{2,18},{3,19},{20,4},{21,5},{6,22},{7,23},{24,8},{25... | collective-permute-start | bytes 7077896 | tf_op jit(solution)/shard_map/ppermute | solution.py:704
  63.9 18.4 %collective-permute-start.11 = (bf16[592,512]{1,0:T(8,128)(2,1)S(1)}, bf16[592,512]{1,0:T(8,128)(2,1)S(1)}, u32[]{:S(2)}, u32[]{:S(2)}) collective-permute-start(bf16[592,512]{1,0:T(8,128)(2,1)S(1)} %get-tuple-element.48), channel_id=1, source_target_pairs={{1,0},{2,1},{3,2},{5,4},{6,5},{7,6},{9,8},{10,9},{11,10},{13,12},{... | collective-permute-start | bytes 1818632 | tf_op jit(solution)/shard_map/ppermute | solution.py:621
  66.2 18.4 %collective-permute-start.10 = (bf16[592,512]{1,0:T(8,128)(2,1)S(1)}, bf16[592,512]{1,0:T(8,128)(2,1)S(1)}, u32[]{:S(2)}, u32[]{:S(2)}) collective-permute-start(bf16[592,512]{1,0:T(8,128)(2,1)S(1)} %get-tuple-element.47.dep_ref), channel_id=1, source_target_pairs={{0,1},{1,2},{2,3},{4,5},{5,6},{6,7},{8,9},{9,10},{10,11},{12,13},{... | collective-permute-start | bytes 1818632 | tf_op jit(solution)/shard_map/ppermute | solution.py:621
  70.1 25.2 %collective-permute-start.16 = (bf16[592,512]{1,0:T(8,128)(2,1)S(1)}, bf16[592,512]{1,0:T(8,128)(2,1)S(1)}, u32[]{:S(2)}, u32[]{:S(2)}) collective-permute-start(bf16[592,512]{1,0:T(8,128)(2,1)S(1)} %get-tuple-element.53), channel_id=1, source_target_pairs={{1,0},{2,1},{3,2},{5,4},{6,5},{7,6},{9,8},{10,9},{11,10},{13,12},{... | collective-permute-start | bytes 1818632 | tf_op jit(solution)/shard_map/ppermute | solution.py:621
  72.3 25.3 %collective-permute-start.15 = (bf16[592,512]{1,0:T(8,128)(2,1)S(1)}, bf16[592,512]{1,0:T(8,128)(2,1)S(1)}, u32[]{:S(2)}, u32[]{:S(2)}) collective-permute-start(bf16[592,512]{1,0:T(8,128)(2,1)S(1)} %get-tuple-element.49.refs_6_), channel_id=1, source_target_pairs={{0,1},{1,2},{2,3},{4,5},{5,6},{6,7},{8,9},{9,10},{10,11},{12,13},{... | collective-permute-start | bytes 1818632 | tf_op jit(solution)/shard_map/ppermute | solution.py:621
  87.1 21.2 %collective-permute-start.14 = (bf16[592,512]{1,0:T(8,128)(2,1)S(1)}, bf16[592,512]{1,0:T(8,128)(2,1)S(1)}, u32[]{:S(2)}, u32[]{:S(2)}) collective-permute-start(bf16[592,512]{1,0:T(8,128)(2,1)S(1)} %get-tuple-element.52), channel_id=1, source_target_pairs={{1,0},{2,1},{3,2},{5,4},{6,5},{7,6},{9,8},{10,9},{11,10},{13,12},{... | collective-permute-start | bytes 1818632 | tf_op jit(solution)/shard_map/ppermute | solution.py:621
  91.0 19.6 %collective-permute-start.13 = (bf16[592,512]{1,0:T(8,128)(2,1)S(1)}, bf16[592,512]{1,0:T(8,128)(2,1)S(1)}, u32[]{:S(2)}, u32[]{:S(2)}) collective-permute-start(bf16[592,512]{1,0:T(8,128)(2,1)S(1)} %get-tuple-element.51.dep_ref), channel_id=1, source_target_pairs={{0,1},{1,2},{2,3},{4,5},{5,6},{6,7},{8,9},{9,10},{10,11},{12,13},{... | collective-permute-start | bytes 1818632 | tf_op jit(solution)/shard_map/ppermute | solution.py:621
  93.0 47.5 %collective-permute-start.23 = (bf16[1168,1024]{1,0:T(8,128)(2,1)S(1)}, bf16[1168,1024]{1,0:T(8,128)(2,1)S(1)}, u32[]{:S(2)}, u32[]{:S(2)}) collective-permute-start(bf16[1168,1024]{1,0:T(8,128)(2,1)S(1)} %get-tuple-element.63), channel_id=1, source_target_pairs={{0,4},{4,0},{8,12},{12,8},{1,5},{5,1},{9,13},{13,9},{18,22},{22,18... | collective-permute-start | bytes 7176200 | tf_op jit(solution)/shard_map/ppermute | solution.py:708
  100.1 21.4 %collective-permute-start.18 = (bf16[592,512]{1,0:T(8,128)(2,1)S(1)}, bf16[592,512]{1,0:T(8,128)(2,1)S(1)}, u32[]{:S(2)}, u32[]{:S(2)}) collective-permute-start(bf16[592,512]{1,0:T(8,128)(2,1)S(1)} %get-tuple-element.55), channel_id=1, source_target_pairs={{1,0},{2,1},{3,2},{5,4},{6,5},{7,6},{9,8},{10,9},{11,10},{13,12},{... | collective-permute-start | bytes 1818632 | tf_op jit(solution)/shard_map/ppermute | solution.py:621
  103.9 19.7 %collective-permute-start.17 = (bf16[592,512]{1,0:T(8,128)(2,1)S(1)}, bf16[592,512]{1,0:T(8,128)(2,1)S(1)}, u32[]{:S(2)}, u32[]{:S(2)}) collective-permute-start(bf16[592,512]{1,0:T(8,128)(2,1)S(1)} %get-tuple-element.54.dep_ref), channel_id=1, source_target_pairs={{0,1},{1,2},{2,3},{4,5},{5,6},{6,7},{8,9},{9,10},{10,11},{12,13},{... | collective-permute-start | bytes 1818632 | tf_op jit(solution)/shard_map/ppermute | solution.py:621
  115.4 20.5 %collective-permute-start.22 = (bf16[592,512]{1,0:T(8,128)(2,1)S(1)}, bf16[592,512]{1,0:T(8,128)(2,1)S(1)}, u32[]{:S(2)}, u32[]{:S(2)}) collective-permute-start(bf16[592,512]{1,0:T(8,128)(2,1)S(1)} %get-tuple-element.60), channel_id=1, source_target_pairs={{1,0},{2,1},{3,2},{5,4},{6,5},{7,6},{9,8},{10,9},{11,10},{13,12},{... | collective-permute-start | bytes 1818632 | tf_op jit(solution)/shard_map/ppermute | solution.py:621
  119.2 16.7 %collective-permute-start.21 = (bf16[592,512]{1,0:T(8,128)(2,1)S(1)}, bf16[592,512]{1,0:T(8,128)(2,1)S(1)}, u32[]{:S(2)}, u32[]{:S(2)}) collective-permute-start(bf16[592,512]{1,0:T(8,128)(2,1)S(1)} %get-tuple-element.56.dep_ref), channel_id=1, source_target_pairs={{0,1},{1,2},{2,3},{4,5},{5,6},{6,7},{8,9},{9,10},{10,11},{12,13},{... | collective-permute-start | bytes 1818632 | tf_op jit(solution)/shard_map/ppermute | solution.py:621
  139.2 6.4 %collective-permute-start.25 = (bf16[2304,512]{1,0:T(8,128)(2,1)S(1)}, bf16[2304,512]{1,0:T(8,128)(2,1)S(1)}, u32[]{:S(2)}, u32[]{:S(2)}) collective-permute-start(bf16[2304,512]{1,0:T(8,128)(2,1)S(1)} %half_for_other_core.3.dep_ref), channel_id=1, source_target_pairs={{18,2},{19,3},{0,16},{1,17},{22,6},{23,7},{4,20},{5,21},{26,10},{2... | collective-permute-start | bytes 7077896 | tf_op jit(solution)/shard_map/ppermute | solution.py:704
  140.5 26.0 %collective-permute-start.24 = (bf16[592,1024]{1,0:T(8,128)(2,1)S(1)}, bf16[592,1024]{1,0:T(8,128)(2,1)S(1)}, u32[]{:S(2)}, u32[]{:S(2)}) collective-permute-start(bf16[592,1024]{1,0:T(8,128)(2,1)S(1)} %grad_weight_middle.1.refs_14_), channel_id=1, source_target_pairs={{0,8},{4,12},{8,0},{12,4},{1,9},{5,13},{9,1},{13,5},{18,26},{22,30... | collective-permute-start | bytes 3637256 | tf_op jit(solution)/shard_map/ppermute | solution.py:708
  155.4 32.3 %collective-permute-start.26 = (bf16[592,1024]{1,0:T(8,128)(2,1)S(1)}, bf16[592,1024]{1,0:T(8,128)(2,1)S(1)}, u32[]{:S(2)}, u32[]{:S(2)}) collective-permute-start(bf16[592,1024]{1,0:T(8,128)(2,1)S(1)} %get-tuple-element.69), channel_id=1, source_target_pairs={{2,6},{6,2},{10,14},{14,10},{3,7},{7,3},{11,15},{15,11},{16,20},{2... | collective-permute-start | bytes 3637256 | tf_op jit(solution)/shard_map/ppermute | solution.py:708
  158.9 31.4 %collective-permute-start.27 = (bf16[592,1024]{1,0:T(8,128)(2,1)S(1)}, bf16[592,1024]{1,0:T(8,128)(2,1)S(1)}, u32[]{:S(2)}, u32[]{:S(2)}) collective-permute-start(bf16[592,1024]{1,0:T(8,128)(2,1)S(1)} %get-tuple-element.70), channel_id=1, source_target_pairs={{2,10},{6,14},{10,2},{14,6},{3,11},{7,15},{11,3},{15,7},{16,24},{2... | collective-permute-start | bytes 3637256 | tf_op jit(solution)/shard_map/ppermute | solution.py:708
  161.2 29.2 %collective-permute-start.28 = (bf16[592,1024]{1,0:T(8,128)(2,1)S(1)}, bf16[592,1024]{1,0:T(8,128)(2,1)S(1)}, u32[]{:S(2)}, u32[]{:S(2)}) collective-permute-start(bf16[592,1024]{1,0:T(8,128)(2,1)S(1)} %get-tuple-element.71), channel_id=1, source_target_pairs={{2,14},{6,10},{10,6},{14,2},{3,15},{7,11},{11,7},{15,3},{16,28},{2... | collective-permute-start | bytes 3637256 | tf_op jit(solution)/shard_map/ppermute | solution.py:708
  164.6 15.7 %collective-permute-start.20 = (bf16[592,512]{1,0:T(8,128)(2,1)S(1)}, bf16[592,512]{1,0:T(8,128)(2,1)S(1)}, u32[]{:S(2)}, u32[]{:S(2)}) collective-permute-start(bf16[592,512]{1,0:T(8,128)(2,1)S(1)} %get-tuple-element.59), channel_id=1, source_target_pairs={{1,0},{2,1},{3,2},{5,4},{6,5},{7,6},{9,8},{10,9},{11,10},{13,12},{... | collective-permute-start | bytes 1818632 | tf_op jit(solution)/shard_map/ppermute | solution.py:621
  166.6 17.9 %collective-permute-start.19 = (bf16[592,512]{1,0:T(8,128)(2,1)S(1)}, bf16[592,512]{1,0:T(8,128)(2,1)S(1)}, u32[]{:S(2)}, u32[]{:S(2)}) collective-permute-start(bf16[592,512]{1,0:T(8,128)(2,1)S(1)} %get-tuple-element.57.refs_15_), channel_id=1, source_target_pairs={{0,1},{1,2},{2,3},{4,5},{5,6},{6,7},{8,9},{9,10},{10,11},{12,13},{... | collective-permute-start | bytes 1818632 | tf_op jit(solution)/shard_map/ppermute | solution.py:621
